TPU v7x, 128 devices: a whole 4x4x4 slice. The times are simulated.
128 devices in a mesh: dirs: 4 (over z), slab: 32 (over y, x, core).
Axes of the slice: x: 4, y: 4, z: 4, core: 2. Of those that a mesh axis runs over, the one named last changes fastest.
Arguments:
- perturbations: float32 [16, 128, 128, 256], P('dirs', 'slab'), may hold values from -6 to 6
- background_now: float32 [128, 128, 256], P('slab'), may hold values from -9 to 9
- background_prev: float32 [128, 128, 256], P('slab'), may hold values from -9 to 9
- stiffness: float32 [128, 128, 256], P('slab'), may hold values from 0.06 to 0.3
- buoyancy: float32 [128, 128, 256], P('slab'), may hold values from 0.5 to 0.9
- absorb_mask: int32 [128, 128, 256], P('slab'), may hold values 0 or 1
- source_cells: int32 [512], P('slab'), may hold values from 0 to 131071
- source_amp: float32 [512], P('slab'), may hold values from -12 to 12
- receiver_cells: int32 [32768], P('slab'), may hold values from 0 to 131071
- column_order: int32 [16], replicated, may hold values from 0 to 15, each once
Outputs:
- basis: float32 [16, 128, 128, 256], P(None, 'slab', 'dirs')
- triangle: float32 [16, 16], replicated
Inputs may be any that keep to these rules, and one draw needn't show every extreme that they name: `source_cells`: entry i names a cell of depth slab i // 16, numbered (layer * 128 + row) * 256 + column inside that slab; cells may repeat. `receiver_cells`: entry i names a cell of depth slab i // 1024, numbered (layer * 128 + row) * 256 + column inside that slab; cells may repeat. `column_order`: each number of 0 to 15 appears once.
All inputs are finite; a program needn't handle non-finite values. No bound on the sum of `absorb_mask` on one device may be relied on, other than what follows from the above.
Results may differ from a plain program's by a relative error of at most 0.0003.
Values sent between devices are 32-bit elements; how exact they have to be, the bound alone decides.
No kernel may reach another device: no remote copies, remote signals or barrier semaphores. Data moves between devices by JAX's collectives and lax.ppermute only.
A program may use at most 256 MiB of HBM per device.

v0:
```python
import math

import jax
import jax.numpy as jnp
from jax import lax
from jax.sharding import PartitionSpec as P

STEPS = 4


COEFFS = (1.6, -0.2, 8.0 / 315.0, -1.0 / 560.0)
DAMPING = 0.3


def extended(block, sides, width):
    for axis, dim in sides:
        count = lax.axis_size(axis)
        forward = [(i, i + 1) for i in range(count - 1)]
        backward = [(target, source) for source, target in forward]
        low = lax.ppermute(
            lax.slice_in_dim(block, block.shape[dim] - width, None, axis=dim), axis, forward
        )
        high = lax.ppermute(lax.slice_in_dim(block, 0, width, axis=dim), axis, backward)
        block = jnp.concatenate([low, block, high], axis=dim)
    return block


def source_weight(t):
    return (1.0 - 0.4 * t) * math.exp(-0.125 * t * t)


def along_columns(values, k):
    if k > 0:
        return jnp.concatenate(
            [values[..., k:], jnp.zeros(values.shape[:-1] + (k,), values.dtype)], -1
        )
    return jnp.concatenate(
        [jnp.zeros(values.shape[:-1] + (-k,), values.dtype), values[..., :k]], -1
    )


def laplace(fields, buoy_padded):
    layers = fields.shape[1]
    width = fields.shape[2]
    padded = extended(fields, (("slab", 1),), 4)
    padded = jnp.pad(padded, ((0, 0), (0, 0), (4, 4), (0, 0)))
    centre = padded[:, 4 : 4 + layers, 4 : 4 + width]
    buoy_centre = buoy_padded[4 : 4 + layers, 4 : 4 + width]
    summed = jnp.zeros(fields.shape, jnp.float32)
    for k in range(1, 5):
        beyond = padded[:, 4 + k : 4 + k + layers, 4 : 4 + width]
        behind = padded[:, 4 - k : 4 - k + layers, 4 : 4 + width]
        buoy_beyond = buoy_padded[4 + k : 4 + k + layers, 4 : 4 + width]
        buoy_behind = buoy_padded[4 - k : 4 - k + layers, 4 : 4 + width]
        partial_value = (buoy_centre + buoy_beyond) * (beyond - centre) - (
            buoy_centre + buoy_behind
        ) * (centre - behind)
        beyond = padded[:, 4 : 4 + layers, 4 + k : 4 + k + width]
        behind = padded[:, 4 : 4 + layers, 4 - k : 4 - k + width]
        buoy_beyond = buoy_padded[4 : 4 + layers, 4 + k : 4 + k + width]
        buoy_behind = buoy_padded[4 : 4 + layers, 4 - k : 4 - k + width]
        partial_value = partial_value + (
            (buoy_centre + buoy_beyond) * (beyond - centre)
            - (buoy_centre + buoy_behind) * (centre - behind)
        )
        beyond = along_columns(centre, k)
        behind = along_columns(centre, -k)
        buoy_beyond = along_columns(buoy_centre, k)
        buoy_behind = along_columns(buoy_centre, -k)
        partial_value = partial_value + (
            (buoy_centre + buoy_beyond) * (beyond - centre)
            - (buoy_centre + buoy_behind) * (centre - behind)
        )
        summed = summed + 0.5 * COEFFS[k - 1] * partial_value
    return summed


def factor(gram):
    count = gram.shape[0]
    identity = jnp.eye(count, dtype=gram.dtype)
    lower = jnp.zeros_like(gram)
    for column in range(count):
        values = gram[:, column] - jnp.sum(lower * lower[column][None, :], 1)
        pivot = jnp.sqrt(values[column])
        below = jnp.arange(count) >= column
        lower = lower + jnp.where(below, values / pivot, 0.0)[:, None] * identity[column][None, :]
    inverse_lower = jnp.zeros_like(gram)
    for row in range(count):
        solved = (identity[row] - jnp.sum(lower[row][:, None] * inverse_lower, 0)) / lower[row, row]
        inverse_lower = inverse_lower + identity[row][:, None] * solved[None, :]
    return (lower.T, inverse_lower.T)


def product(left, right):
    return jnp.dot(left, right, precision=lax.Precision.HIGHEST, preferred_element_type=jnp.float32)


def shards(
    perturbations,
    background_now,
    background_prev,
    stiffness,
    buoyancy,
    absorb_mask,
    source_cells,
    source_amp,
    receiver_cells,
    column_order,
):
    layers = buoyancy.shape[0]
    rows_all = buoyancy.shape[1]
    columns_all = buoyancy.shape[2]
    buoy_rim = extended(buoyancy, (("slab", 0),), 4)
    buoy_rim = jnp.pad(buoy_rim, ((0, 0), (4, 4), (0, 0)))
    tapering = 1.0 - DAMPING * absorb_mask.astype(jnp.float32)
    older = background_prev
    current = background_now
    window_cells = layers * rows_all * columns_all
    plane_cells = rows_all * columns_all

    def locate(cells):
        depth_index = cells // plane_cells
        within = cells % plane_cells
        row_local = within // columns_all
        inside = (row_local >= 0) & (row_local < rows_all)
        local_cell = (depth_index * rows_all + row_local) * columns_all + within % columns_all
        return (jnp.where(inside, local_cell, window_cells), inside)

    source_local, source_inside = locate(source_cells)
    source_field = (
        jnp.zeros((window_cells,), jnp.float32)
        .at[source_local]
        .add(source_amp, mode="drop")
        .reshape(layers, rows_all, columns_all)
    )
    receiver_local, receiver_inside = locate(receiver_cells)
    receiver_safe = jnp.where(receiver_inside, receiver_local, 0)
    sketch_count = perturbations.shape[0]
    field_shape = (sketch_count, layers, rows_all, columns_all)
    born_old = jnp.zeros(field_shape, jnp.float32)
    born_now = jnp.zeros(field_shape, jnp.float32)
    laplace_back = []
    records = []
    for t in range(STEPS):
        lapped = laplace(jnp.concatenate([current[None], born_now], 0), buoy_rim)
        back_lap = lapped[0]
        laplace_back.append(back_lap)
        newer = (
            tapering * (2.0 * current - older + stiffness * back_lap)
            + source_weight(t) * source_field
        )
        born_new = tapering * (
            2.0 * born_now - born_old + stiffness * lapped[1:] + perturbations * back_lap
        )
        records.append(
            jnp.where(
                receiver_inside[None, :],
                born_new.reshape(sketch_count, window_cells)[:, receiver_safe],
                0.0,
            )
        )
        older, current = (current, newer)
        born_old, born_now = (born_now, born_new)
    adjoint_far = jnp.zeros(field_shape, jnp.float32)
    adjoint_near = jnp.zeros(field_shape, jnp.float32)
    images = jnp.zeros(field_shape, jnp.float32)
    for t in reversed(range(STEPS)):
        injected = (
            jnp.zeros((sketch_count, window_cells), jnp.float32)
            .at[:, receiver_local]
            .add(records[t], mode="drop")
            .reshape(field_shape)
        )
        if t == STEPS - 1:
            adjoint_now = injected
        else:
            adjoint_now = (
                tapering
                * (2.0 * adjoint_near - adjoint_far + stiffness * laplace(adjoint_near, buoy_rim))
                + injected
            )
        images = images + laplace_back[t] * adjoint_now
        adjoint_far, adjoint_near = (adjoint_near, adjoint_now)
    sketch = lax.all_to_all(images, "dirs", split_axis=2, concat_axis=0, tiled=True)
    total_dirs = sketch.shape[0]
    local_cells = sketch.shape[1] * sketch.shape[2] * sketch.shape[3]
    selector = (column_order[:, None] == jnp.arange(total_dirs, dtype=jnp.int32)[None, :]).astype(
        jnp.float32
    )
    ordered = product(selector, sketch.reshape(total_dirs, local_cells))
    grid_cells = layers * lax.axis_size("slab") * rows_all * columns_all
    factor_cells = math.sqrt(grid_cells)
    half_count = total_dirs // 2
    first_rows = ordered[:half_count]
    second_rows = ordered[half_count:]
    first_gram = lax.psum(product(first_rows, first_rows.T), ("dirs", "slab"))
    upper_first, inverse_first = factor(first_gram)
    first_basis = product(inverse_first.T, first_rows)
    coupling = lax.psum(product(first_basis, second_rows.T), ("dirs", "slab"))
    remainder = second_rows - product(coupling.T, first_basis)
    second_gram = lax.psum(product(remainder, remainder.T), ("dirs", "slab"))
    upper_second, inverse_second = factor(second_gram)
    second_basis = product(inverse_second.T, remainder)
    basis = jnp.concatenate([first_basis, second_basis], 0)
    top_rows = jnp.concatenate([upper_first, coupling], 1)
    low_rows = jnp.concatenate([jnp.zeros((half_count, half_count), jnp.float32), upper_second], 1)
    triangle = jnp.concatenate([top_rows, low_rows], 0)
    basis = (basis * factor_cells).reshape(
        total_dirs, sketch.shape[1], sketch.shape[2], sketch.shape[3]
    )
    return (basis, triangle / factor_cells)


def solution(mesh):
    return jax.shard_map(
        shards,
        mesh=mesh,
        in_specs=(
            P("dirs", "slab", None, None),
            P("slab", None, None),
            P("slab", None, None),
            P("slab", None, None),
            P("slab", None, None),
            P("slab", None, None),
            P("slab"),
            P("slab"),
            P("slab"),
            P(),
        ),
        out_specs=(P(None, "slab", "dirs", None), P()),
        check_vma=False,
    )
```

profile of v0, /device:TPU:14, one launch (start us, length us, event | category | flops | bytes accessed | tf_op | source)
XLA Modules:
  0.0 1290.5 jit_solution(13211733280376505228)
XLA Ops:
  58.9 29.9 %fusion.49 = f32[5,4,128,256]{3,2,1,0:T(8,128)} fusion(f32[1,4,128,256]{3,2,1,0:T(8,128)S(1)} %bitcast.291, f32[5,4,128,256]{3,2,1,0:T(8,128)} %collective-permute-done.1, f32[5,4,128,256]{3,2,1,0:T(8,128)} %concatenate.374, f32[5,4,128,256]{3,2,1,0:T(8,128)} %collective-permute-done.3, f32[5,12,136,256]{3,2,1,0:T(8,128)} %select_maximum_fusion.9, ...), kind=kLoop, calls=%fused_computation.201 | loop fusion | flops 53084160 | bytes 65331200 | tf_op jit(solution)/shard_map/add | solution.py:74
  136.7 26.9 %fusion.170 = f32[5,4,128,256]{3,2,1,0:T(8,128)} fusion(f32[5,12,136,256]{3,2,1,0:T(8,128)} %select_maximum_fusion.6, f32[5,8,128,256]{3,2,1,0:T(8,128)} %get-tuple-element.58, f32[5,8,128,256]{3,2,1,0:T(8,128)} %get-tuple-element.57, f32[5,4,128,252]{3,2,1,0:T(8,128)} %get-tuple-element.56, f32[5,4,128,252]{3,2,1,0:T(8,128)} %get-tuple-element.55, ...), kind=kLoop, calls=%fused_computation.351 | loop fusion | flops 49807360 | bytes 80535552 | tf_op jit(solution)/shard_map/add | solution.py:74
  211.7 27.3 %fusion.134 = f32[5,4,128,256]{3,2,1,0:T(8,128)} fusion(f32[5,12,136,256]{3,2,1,0:T(8,128)} %select_maximum_fusion.3, f32[5,8,128,256]{3,2,1,0:T(8,128)} %get-tuple-element.48, f32[5,8,128,256]{3,2,1,0:T(8,128)} %get-tuple-element.47, f32[5,4,128,252]{3,2,1,0:T(8,128)} %get-tuple-element.46, f32[5,4,128,252]{3,2,1,0:T(8,128)} %get-tuple-element.45, ...), kind=kLoop, calls=%fused_computation.301 | loop fusion | flops 49807360 | bytes 80535552 | tf_op jit(solution)/shard_map/add | solution.py:74
  258.9 32.5 %copy.314 = f32[4,4,128,256]{0,3,2,1:T(8,128)} copy(f32[4,4,128,256]{3,2,1,0:T(8,128)S(1)} %fusion.361) | data formatting | bytes 4194304 | tf_op jit(solution)/shard_map/mul | solution.py:152
  306.6 33.6 %copy.312 = f32[4,4,128,256]{0,3,2,1:T(8,128)} copy(f32[4,4,128,256]{3,2,1,0:T(8,128)} %copy-done.2) | data formatting | bytes 4194304 | tf_op jit(solution)/shard_map/mul | solution.py:152
  355.5 32.5 %copy.309 = f32[4,4,128,256]{0,3,2,1:T(8,128)} copy(f32[4,4,128,256]{3,2,1,0:T(8,128)S(1)} %copy-done.6) | data formatting | bytes 4194304 | tf_op jit(solution)/shard_map/mul | solution.py:152
  388.0 15.3 %gather_fusion.1 = f32[1024,4]{1,0:T(8,128)} fusion(f32[4,131072]{0,1:T(8,128)} %bitcast.11, s32[1024]{0:T(1024)S(1)} %get-tuple-element.26), kind=kCustom, calls=%fused_computation.1 | custom fusion | bytes 36864 | tf_op jit(solution)/shard_map/gather | solution.py:158
  428.1 27.3 %fusion.98 = f32[5,4,128,256]{3,2,1,0:T(8,128)} fusion(f32[5,12,136,256]{3,2,1,0:T(8,128)} %select_maximum_fusion, f32[5,8,128,256]{3,2,1,0:T(8,128)} %get-tuple-element.38, f32[5,8,128,256]{3,2,1,0:T(8,128)} %get-tuple-element.37, f32[5,4,128,252]{3,2,1,0:T(8,128)} %get-tuple-element.36, f32[5,4,128,252]{3,2,1,0:T(8,128)} %get-tuple-element.35, ...), kind=kLoop, calls=%fused_computation.251 | loop fusion | flops 49807360 | bytes 80535552 | tf_op jit(solution)/shard_map/add | solution.py:74
  461.8 33.6 %copy.269 = f32[4,4,128,256]{0,3,2,1:T(8,128)} copy(f32[4,4,128,256]{3,2,1,0:T(8,128)} %fusion.353) | data formatting | bytes 4194304 | tf_op jit(solution)/shard_map/mul | solution.py:152
  507.8 44.9 %scatter_custom_fusion.1 = f32[4,131072]{0,1:T(8,128)} fusion(s32[1024]{0:T(1024)S(1)} %get-tuple-element.2, f32[]{:T(128)} %constant.127.clone.1, f32[1024,4]{1,0:T(8,128)} %get-tuple-element.180, s32[1024]{0:T(1024)S(1)} %broadcast_clamp_fusion), kind=kCustom, calls=%fused_computation.20 | custom fusion | flops 4096 | bytes 2097664 | tf_op jit(solution)/shard_map/scatter-add | solution.py:171
  552.7 38.4 %copy.270 = f32[4,4,128,256]{3,2,1,0:T(8,128)S(1)} copy(f32[4,4,128,256]{0,3,2,1:T(8,128)} %bitcast.10) | data formatting | bytes 4194304 | tf_op jit(solution)/shard_map/reshape | solution.py:172
  599.3 42.5 %scatter_custom_fusion.2 = f32[4,131072]{0,1:T(8,128)} fusion(s32[1024]{0:T(1024)S(1)} %get-tuple-element.2, f32[]{:T(128)} %constant.127.clone.1, f32[1024,4]{1,0:T(8,128)S(1)} %get-tuple-element.181, s32[1024]{0:T(1024)S(1)} %broadcast_clamp_fusion), kind=kCustom, calls=%fused_computation.18 | custom fusion | flops 4096 | bytes 2097156 | tf_op jit(solution)/shard_map/scatter-add | solution.py:171
  641.8 39.4 %copy.310 = f32[4,4,128,256]{3,2,1,0:T(8,128)} copy(f32[4,4,128,256]{0,3,2,1:T(8,128)} %bitcast.12) | data formatting | bytes 4194304 | tf_op jit(solution)/shard_map/reshape | solution.py:172
  696.9 27.4 %fusion.268 = f32[4,4,128,256]{3,2,1,0:T(8,128)} fusion(f32[4,4,128,256]{3,2,1,0:T(8,128)} %copy.310, f32[4,4,128,256]{3,2,1,0:T(8,128)S(1)} %copy.270, f32[4,4,128,256]{3,2,1,0:T(8,128)} %collective-permute-done.11, f32[4,4,128,256]{3,2,1,0:T(8,128)} %collective-permute-done.10, f32[4,12,136,256]{3,2,1,0:T(8,128)} %select_maximum_fusion.15, ...), kind=kLoop, calls=%fused_computation.466 | loop fusion | flops 45088768 | bytes 57507840 | tf_op jit(solution)/shard_map/add | solution.py:178
  730.3 44.7 %scatter_custom_fusion.3 = f32[4,131072]{0,1:T(8,128)} fusion(s32[1024]{0:T(1024)S(1)} %get-tuple-element.2, f32[]{:T(128)} %constant.127.clone.1, f32[1024,4]{1,0:T(8,128)} %get-tuple-element.179, s32[1024]{0:T(1024)S(1)} %broadcast_clamp_fusion), kind=kCustom, calls=%fused_computation.16 | custom fusion | flops 4096 | bytes 2097664 | tf_op jit(solution)/shard_map/scatter-add | solution.py:171
  775.0 39.4 %copy.313 = f32[4,4,128,256]{3,2,1,0:T(8,128)} copy(f32[4,4,128,256]{0,3,2,1:T(8,128)} %bitcast.14) | data formatting | bytes 4194304 | tf_op jit(solution)/shard_map/reshape | solution.py:172
  832.3 29.9 %fusion.241 = f32[4,4,128,256]{3,2,1,0:T(8,128)} fusion(f32[4,4,128,256]{3,2,1,0:T(8,128)} %copy.313, f32[4,4,128,256]{3,2,1,0:T(8,128)} %fusion.268, f32[4,4,128,256]{3,2,1,0:T(8,128)} %collective-permute-done.13, f32[4,4,128,256]{3,2,1,0:T(8,128)} %collective-permute-done.12, f32[4,12,136,256]{3,2,1,0:T(8,128)} %select_maximum_fusion.13, ...), kind=kLoop, calls=%fused_computation.439 | loop fusion | flops 45613056 | bytes 59604992 | tf_op jit(solution)/shard_map/add | solution.py:178
  869.1 44.9 %scatter_custom_fusion.4 = f32[4,131072]{0,1:T(8,128)} fusion(s32[1024]{0:T(1024)S(1)} %get-tuple-element.2, f32[]{:T(128)} %constant.127.clone.1, f32[1024,4]{1,0:T(8,128)} %get-tuple-element.178, s32[1024]{0:T(1024)S(1)} %broadcast_clamp_fusion), kind=kCustom, calls=%fused_computation.14 | custom fusion | flops 4096 | bytes 2097664 | tf_op jit(solution)/shard_map/scatter-add | solution.py:171
  914.0 39.3 %copy.315 = f32[4,4,128,256]{3,2,1,0:T(8,128)} copy(f32[4,4,128,256]{0,3,2,1:T(8,128)} %bitcast.16) | data formatting | bytes 4194304 | tf_op jit(solution)/shard_map/reshape | solution.py:172
  971.6 24.3 %multiply_add_fusion = f32[4,4,128,256]{3,2,1,0:T(8,128)} fusion(f32[4,4,128,256]{3,2,1,0:T(8,128)S(1)} %copy-done.4, f32[4,4,128,256]{3,2,1,0:T(8,128)S(1)} %copy-done.1, f32[4,4,128,256]{3,2,1,0:T(8,128)S(1)} %copy.270, f32[4,4,128,256]{3,2,1,0:T(8,128)} %copy.315, f32[4,4,128,252]{3,2,1,0:T(8,128)} %get-tuple-element.74, ...), kind=kLoop, calls=%fused_computation.596 | loop fusion | flops 49283072 | bytes 63799296 | tf_op jit(solution)/shard_map/add | solution.py:182
  1005.7 25.0 %all-to-all-done = f32[4,4,128,256]{3,1,0,2:T(4,128)S(1)} async-done(((f32[4,4,128,256]{3,1,0,2:T(4,128)}), f32[4,4,128,256]{3,1,0,2:T(4,128)S(1)}, u32[]{:S(2)}, u32[]{:S(2)}) %all-to-all-start) | async-done | bytes 2097184 | tf_op jit(solution)/shard_map/all_to_all | solution.py:184
  1041.2 65.8 %psum.21 = f32[8,8]{1,0:T(8,128)S(1)} all-reduce(f32[8,8]{1,0:T(8,128)S(1)} %fusion.367), channel_id=1, replica_groups=mesh['dirs'=4,'slab'=32] {'dirs','slab'}, use_global_device_ids=true, to_apply=%region_5.6 | all-reduce | flops 64 | bytes 512 | tf_op jit(solution)/shard_map/psum | solution.py:196
  1132.5 63.6 %psum.22 = f32[8,8]{1,0:T(8,128)S(1)} all-reduce(f32[8,8]{1,0:T(8,128)S(1)} %fusion.363), channel_id=1, replica_groups=mesh['dirs'=4,'slab'=32] {'dirs','slab'}, use_global_device_ids=true, to_apply=%region_21.22 | all-reduce | flops 64 | bytes 512 | tf_op jit(solution)/shard_map/psum | solution.py:199
  1200.5 62.4 %psum.23 = f32[8,8]{1,0:T(8,128)S(1)} all-reduce(f32[8,8]{1,0:T(8,128)S(1)} %fusion.486), channel_id=1, replica_groups=mesh['dirs'=4,'slab'=32] {'dirs','slab'}, use_global_device_ids=true, to_apply=%region_22.23 | all-reduce | flops 64 | bytes 512 | tf_op jit(solution)/shard_map/psum | solution.py:201
  (376 shorter events, 386.7 us)
Async XLA Ops:
  3.6 49.2 %collective-permute-start.1 = (f32[5,4,128,256]{3,2,1,0:T(8,128)}, f32[5,4,128,256]{3,2,1,0:T(8,128)}, u32[]{:S(2)}, u32[]{:S(2)}) collective-permute-start(f32[5,4,128,256]{3,2,1,0:T(8,128)} %concatenate.374), channel_id=1, source_target_pairs={{1,0},{2,1},{3,2},{4,3},{5,4},{6,5},{7,6},{8,7},{9,8},{10,9},{11,1... | collective-permute-start | bytes 7864328 | tf_op jit(solution)/shard_map/ppermute | solution.py:23
  5.8 47.1 %collective-permute-start.3 = (f32[5,4,128,256]{3,2,1,0:T(8,128)}, f32[5,4,128,256]{3,2,1,0:T(8,128)}, u32[]{:S(2)}, u32[]{:S(2)}) collective-permute-start(f32[5,4,128,256]{3,2,1,0:T(8,128)} %concatenate.374), channel_id=1, source_target_pairs={{0,1},{1,2},{2,3},{3,4},{4,5},{5,6},{6,7},{7,8},{8,9},{9,10},{10,1... | collective-permute-start | bytes 7864328 | tf_op jit(solution)/shard_map/ppermute | solution.py:20
  8.0 32.8 %collective-permute-start = (f32[4,128,256]{2,1,0:T(8,128)S(1)}, f32[4,128,256]{2,1,0:T(8,128)S(1)}, u32[]{:S(2)}, u32[]{:S(2)}) collective-permute-start(f32[4,128,256]{2,1,0:T(8,128)S(1)} %copy-done.7), channel_id=1, source_target_pairs={{1,0},{2,1},{3,2},{4,3},{5,4},{6,5},{7,6},{8,7},{9,8},{10,9},{11,1... | collective-permute-start | bytes 1572872 | tf_op jit(solution)/shard_map/ppermute | solution.py:23
  11.4 33.2 %collective-permute-start.2 = (f32[4,128,256]{2,1,0:T(8,128)S(1)}, f32[4,128,256]{2,1,0:T(8,128)S(1)}, u32[]{:S(2)}, u32[]{:S(2)}) collective-permute-start(f32[4,128,256]{2,1,0:T(8,128)S(1)} %copy-done.7), channel_id=1, source_target_pairs={{0,1},{1,2},{2,3},{3,4},{4,5},{5,6},{6,7},{7,8},{8,9},{9,10},{10,1... | collective-permute-start | bytes 1572872 | tf_op jit(solution)/shard_map/ppermute | solution.py:20
  58.9 31.2 %copy-start.8 = (f32[4,128,256]{2,1,0:T(8,128)S(1)}, f32[4,128,256]{2,1,0:T(8,128)}, u32[]{:S(2)}) copy-start(f32[4,128,256]{2,1,0:T(8,128)} %param.13) | copy-start | bytes 1572868
  93.4 31.1 %collective-permute-start.4 = (f32[5,4,128,256]{3,2,1,0:T(8,128)S(1)}, f32[5,4,128,256]{3,2,1,0:T(8,128)S(1)}, u32[]{:S(2)}, u32[]{:S(2)}) collective-permute-start(f32[5,4,128,256]{3,2,1,0:T(8,128)S(1)} %pad_maximum_fusion), channel_id=1, source_target_pairs={{1,0},{2,1},{3,2},{4,3},{5,4},{6,5},{7,6},{8,7},{9,8},{10,9},{11,1... | collective-permute-start | bytes 7864328 | tf_op jit(solution)/shard_map/ppermute | solution.py:23
  95.3 33.0 %collective-permute-start.5 = (f32[5,4,128,256]{3,2,1,0:T(8,128)S(1)}, f32[5,4,128,256]{3,2,1,0:T(8,128)S(1)}, u32[]{:S(2)}, u32[]{:S(2)}) collective-permute-start(f32[5,4,128,256]{3,2,1,0:T(8,128)S(1)} %pad_maximum_fusion), channel_id=1, source_target_pairs={{0,1},{1,2},{2,3},{3,4},{4,5},{5,6},{6,7},{7,8},{8,9},{9,10},{10,1... | collective-permute-start | bytes 7864328 | tf_op jit(solution)/shard_map/ppermute | solution.py:20
  168.1 74.7 %copy-start.2 = (f32[4,4,128,256]{3,2,1,0:T(8,128)}, f32[4,4,128,256]{3,2,1,0:T(8,128)S(1)}, u32[]{:S(2)}) copy-start(f32[4,4,128,256]{3,2,1,0:T(8,128)S(1)} %fusion.359) | copy-start | bytes 6291460
  168.4 31.1 %collective-permute-start.6 = (f32[5,4,128,256]{3,2,1,0:T(8,128)S(1)}, f32[5,4,128,256]{3,2,1,0:T(8,128)S(1)}, u32[]{:S(2)}, u32[]{:S(2)}) collective-permute-start(f32[5,4,128,256]{3,2,1,0:T(8,128)S(1)} %pad_maximum_fusion.1), channel_id=1, source_target_pairs={{1,0},{2,1},{3,2},{4,3},{5,4},{6,5},{7,6},{8,7},{9,8},{10,9},{11,1... | collective-permute-start | bytes 7864328 | tf_op jit(solution)/shard_map/ppermute | solution.py:23
  170.3 33.0 %collective-permute-start.7 = (f32[5,4,128,256]{3,2,1,0:T(8,128)S(1)}, f32[5,4,128,256]{3,2,1,0:T(8,128)S(1)}, u32[]{:S(2)}, u32[]{:S(2)}) collective-permute-start(f32[5,4,128,256]{3,2,1,0:T(8,128)S(1)} %pad_maximum_fusion.1), channel_id=1, source_target_pairs={{0,1},{1,2},{2,3},{3,4},{4,5},{5,6},{6,7},{7,8},{8,9},{9,10},{10,1... | collective-permute-start | bytes 7864328 | tf_op jit(solution)/shard_map/ppermute | solution.py:20
  245.8 170.4 %collective-permute-start.8 = (f32[5,4,128,256]{3,2,1,0:T(8,128)}, f32[5,4,128,256]{3,2,1,0:T(8,128)}, u32[]{:S(2)}, u32[]{:S(2)}) collective-permute-start(f32[5,4,128,256]{3,2,1,0:T(8,128)} %pad_maximum_fusion.2), channel_id=1, source_target_pairs={{1,0},{2,1},{3,2},{4,3},{5,4},{6,5},{7,6},{8,7},{9,8},{10,9},{11,1... | collective-permute-start | bytes 7864328 | tf_op jit(solution)/shard_map/ppermute | solution.py:23
  247.8 168.5 %collective-permute-start.9 = (f32[5,4,128,256]{3,2,1,0:T(8,128)}, f32[5,4,128,256]{3,2,1,0:T(8,128)}, u32[]{:S(2)}, u32[]{:S(2)}) collective-permute-start(f32[5,4,128,256]{3,2,1,0:T(8,128)} %pad_maximum_fusion.2), channel_id=1, source_target_pairs={{0,1},{1,2},{2,3},{3,4},{4,5},{5,6},{6,7},{7,8},{8,9},{9,10},{10,1... | collective-permute-start | bytes 7864328 | tf_op jit(solution)/shard_map/ppermute | solution.py:20
  306.6 48.9 %copy-start.6 = (f32[4,4,128,256]{3,2,1,0:T(8,128)S(1)}, f32[4,4,128,256]{3,2,1,0:T(8,128)}, u32[]{:S(2)}) copy-start(f32[4,4,128,256]{3,2,1,0:T(8,128)} %copy-done.5) | copy-start | bytes 6291460
  355.5 47.8 %copy-start.11 = (f32[1,4,128,256]{3,2,1,0:T(8,128)S(1)}, f32[1,4,128,256]{3,2,1,0:T(8,128)}, u32[]{:S(2)}) copy-start(f32[1,4,128,256]{3,2,1,0:T(8,128)} %copy-done.10) | copy-start | bytes 1572868
  461.8 44.5 %copy-start.51 = (f32[1024,4]{1,0:T(8,128)S(1)}, f32[1024,4]{1,0:T(8,128)}, u32[]{:S(2)}) copy-start(f32[1024,4]{1,0:T(8,128)} %gather_fusion.3) | copy-start | bytes 49156
  461.8 44.6 %copy-start.52 = (f32[1024,4]{1,0:T(8,128)S(1)}, f32[1024,4]{1,0:T(8,128)}, u32[]{:S(2)}) copy-start(f32[1024,4]{1,0:T(8,128)} %gather_fusion.2) | copy-start | bytes 49156
  461.8 44.6 %copy-start.53 = (f32[1024,4]{1,0:T(8,128)S(1)}, f32[1024,4]{1,0:T(8,128)}, u32[]{:S(2)}) copy-start(f32[1024,4]{1,0:T(8,128)} %gather_fusion.1) | copy-start | bytes 49156
  591.1 101.0 %collective-permute-start.11 = (f32[4,4,128,256]{3,2,1,0:T(8,128)S(1)}, f32[4,4,128,256]{3,2,1,0:T(8,128)}, u32[]{:S(2)}, u32[]{:S(2)}) collective-permute-start(f32[4,4,128,256]{3,2,1,0:T(8,128)S(1)} %copy.270), channel_id=1, source_target_pairs={{0,1},{1,2},{2,3},{3,4},{4,5},{5,6},{6,7},{7,8},{8,9},{9,10},{10,1... | collective-permute-start | bytes 6291464 | tf_op jit(solution)/shard_map/ppermute | solution.py:20
  597.3 94.8 %collective-permute-start.10 = (f32[4,4,128,256]{3,2,1,0:T(8,128)S(1)}, f32[4,4,128,256]{3,2,1,0:T(8,128)}, u32[]{:S(2)}, u32[]{:S(2)}) collective-permute-start(f32[4,4,128,256]{3,2,1,0:T(8,128)S(1)} %copy.270), channel_id=1, source_target_pairs={{1,0},{2,1},{3,2},{4,3},{5,4},{6,5},{7,6},{8,7},{9,8},{10,9},{11,1... | collective-permute-start | bytes 6291464 | tf_op jit(solution)/shard_map/ppermute | solution.py:23
  724.3 103.4 %collective-permute-start.13 = (f32[4,4,128,256]{3,2,1,0:T(8,128)}, f32[4,4,128,256]{3,2,1,0:T(8,128)}, u32[]{:S(2)}, u32[]{:S(2)}) collective-permute-start(f32[4,4,128,256]{3,2,1,0:T(8,128)} %fusion.268), channel_id=1, source_target_pairs={{0,1},{1,2},{2,3},{3,4},{4,5},{5,6},{6,7},{7,8},{8,9},{9,10},{10,1... | collective-permute-start | bytes 6291464 | tf_op jit(solution)/shard_map/ppermute | solution.py:20
  726.9 100.8 %collective-permute-start.12 = (f32[4,4,128,256]{3,2,1,0:T(8,128)}, f32[4,4,128,256]{3,2,1,0:T(8,128)}, u32[]{:S(2)}, u32[]{:S(2)}) collective-permute-start(f32[4,4,128,256]{3,2,1,0:T(8,128)} %fusion.268), channel_id=1, source_target_pairs={{1,0},{2,1},{3,2},{4,3},{5,4},{6,5},{7,6},{8,7},{9,8},{10,9},{11,1... | collective-permute-start | bytes 6291464 | tf_op jit(solution)/shard_map/ppermute | solution.py:23
  862.3 104.5 %collective-permute-start.14 = (f32[4,4,128,256]{3,2,1,0:T(8,128)}, f32[4,4,128,256]{3,2,1,0:T(8,128)}, u32[]{:S(2)}, u32[]{:S(2)}) collective-permute-start(f32[4,4,128,256]{3,2,1,0:T(8,128)} %fusion.241), channel_id=1, source_target_pairs={{1,0},{2,1},{3,2},{4,3},{5,4},{6,5},{7,6},{8,7},{9,8},{10,9},{11,1... | collective-permute-start | bytes 6291464 | tf_op jit(solution)/shard_map/ppermute | solution.py:23
  864.2 102.6 %collective-permute-start.15 = (f32[4,4,128,256]{3,2,1,0:T(8,128)}, f32[4,4,128,256]{3,2,1,0:T(8,128)}, u32[]{:S(2)}, u32[]{:S(2)}) collective-permute-start(f32[4,4,128,256]{3,2,1,0:T(8,128)} %fusion.241), channel_id=1, source_target_pairs={{0,1},{1,2},{2,3},{3,4},{4,5},{5,6},{6,7},{7,8},{8,9},{9,10},{10,1... | collective-permute-start | bytes 6291464 | tf_op jit(solution)/shard_map/ppermute | solution.py:20
  1000.2 30.6 %all-to-all-start = ((f32[4,4,128,256]{3,1,0,2:T(4,128)}), f32[4,4,128,256]{3,1,0,2:T(4,128)S(1)}, u32[]{:S(2)}, u32[]{:S(2)}) async-start(f32[4,4,128,256]{3,1,0,2:T(4,128)} %copy.316), calls=%async_computation | async-start | bytes 4194304 | tf_op jit(solution)/shard_map/all_to_all | solution.py:184
  (50 other events, 311.8 us)
where the time goes:
time: 1310 us; the launch traced here: 1290 us
  other arithmetic  510 us (39%)
  local copies, waits for them, and re-layouts  433 us (33%)
  blocking collectives  192 us (15%)
  waiting for transfers between devices  68.6 us (5%)
  starting transfers between devices  59.4 us (5%)
  matrix products  14.3 us (1%)
  between operations  13.1 us (1%)
    scatter-add x6, other arithmetic, shards(): injected = jnp.zeros((sketch_count, window_cells), jnp.float32).at[:, rec...  181 us
    reshape x4, local copies, waits for them, and re-layouts, shards(): injected = jnp.zeros((sketch_count, window_cells), jnp.float32).at[:, rec...  156 us
    mul x4, local copies, waits for them, and re-layouts, shards(): tapering * (2.0 * born_now - born_old + stiffness * lapped[1:] + perturba...  132 us
    add x4, other arithmetic, laplace(): summed = summed + 0.5 * COEFFS[k - 1] * partial_value  111 us
    psum x1, blocking collectives, shards(): first_gram = lax.psum(product(first_rows, first_rows.T), ('dirs', 'slab'))  65.8 us
    psum x1, blocking collectives, shards(): coupling = lax.psum(product(first_basis, second_rows.T), ('dirs', 'slab'))  63.6 us
    psum x1, blocking collectives, shards(): second_gram = lax.psum(product(remainder, remainder.T), ('dirs', 'slab'))  62.4 us
    add x2, other arithmetic, shards(): tapering * (2.0 * adjoint_near - adjoint_far + stiffness * laplace(adjoin...  57.3 us
  transfers between devices with their start and end apart: 17, of which 7 were waited for; matrix products, arithmetic and copies ran while one was open for 39% of the time, Pallas kernels for 0%

commit v1 on v0

v1 whole, which is shorter than its diff:
```python
import functools
import math

import jax
import jax.numpy as jnp
import ml_dtypes
import numpy as np
from jax import lax
from jax.experimental import pallas as pl
from jax.experimental.pallas import tpu as pltpu
from jax.sharding import PartitionSpec as P

STEPS = 4
DAMPING = 0.3
TAPS = (8064.0, -1008.0, 128.0, -9.0)
CENTRE = 6.0 * sum(TAPS)
HALF = 0.5 / 5040.0
GROUPS = 2
VMEM = 40 * 1024 * 1024
LANE = 128


def band(size):
    matrix = np.zeros((size, size), np.float32)
    for k, tap in enumerate(TAPS, 1):
        matrix += tap * (np.eye(size, k=k) + np.eye(size, k=-k))
    return matrix.astype(ml_dtypes.bfloat16)


def source_weight(t):
    return (1.0 - 0.4 * t) * math.exp(-0.125 * t * t)


def params(**more):
    return pltpu.CompilerParams(vmem_limit_bytes=VMEM, **more)


def split_rows(y_ref, slot, layer, row, values, parts, rows):
    size = values.shape[0]
    for s in range(parts):
        part = values.astype(jnp.bfloat16)
        y_ref[slot, layer, s * rows + row : s * rows + row + size, :] = part
        if s < parts - 1:
            values = values - part.astype(jnp.float32)


def plane_part(functions, y_ref, a_ref, mx_ref, my_ref, parts):
    _, layers, rows, _ = a_ref.shape
    for layer in range(layers):
        for row in range(0, rows, 32):
            for slot, values in enumerate(functions(layer, row, 32)):
                split_rows(y_ref, slot, layer, row, values, parts, rows)
    for slot in range(a_ref.shape[0]):
        for layer in range(layers):
            y = y_ref[slot, layer]
            along = jnp.dot(y, mx_ref[...], preferred_element_type=jnp.float32)
            total = jnp.dot(my_ref[...], y, preferred_element_type=jnp.float32)
            for s in range(parts):
                total = total + along[s * rows : (s + 1) * rows]
            a_ref[slot, layer] = total


def depth_part(tall, layer):
    total = None
    for k, tap in enumerate(TAPS, 1):
        term = tap * (tall[layer + 4 + k] + tall[layer + 4 - k])
        total = term if total is None else total + term
    return total


def tall_of(refs, rows, columns):
    low, mid, high = refs
    return [ref[layer, rows, columns] for ref in (low, mid, high) for layer in range(4)]


def tiles(shape, body):
    _, rows, columns = shape

    def step(i, carry):
        at = pl.ds(pl.multiple_of(i * 8, 8), 8)
        for column in range(0, columns, LANE):
            body(i, at, slice(column, column + LANE))
        return carry

    lax.fori_loop(0, rows // 8, step, 0)


def place_kernel(rc_ref, sc_ref, amp_ref, mask_ref, m_ref, src_ref, taper_ref):
    layers, rows, columns = m_ref.shape
    count = rc_ref.shape[1]
    lines = layers * rows
    chunk = min(256, count)
    total = None
    for start in range(0, count, chunk):
        cells = rc_ref[:, start : start + chunk]
        line = lax.broadcasted_iota(jnp.int32, (lines, chunk), 0) == cells // columns
        column = lax.broadcasted_iota(jnp.int32, (columns, chunk), 0) == cells % columns
        part = lax.dot_general(
            jnp.where(line, 1.0, 0.0).astype(jnp.bfloat16),
            jnp.where(column, 1.0, 0.0).astype(jnp.bfloat16),
            (((1,), (1,)), ((), ())),
            preferred_element_type=jnp.float32,
        )
        total = part if total is None else total + part
    m_ref[...] = total.reshape(m_ref.shape)
    cells = sc_ref[...]
    count = cells.shape[1]
    line = lax.broadcasted_iota(jnp.int32, (lines, count), 0) == cells // columns
    column = lax.broadcasted_iota(jnp.int32, (columns, count), 0) == cells % columns
    part = lax.dot_general(
        jnp.where(line, 1.0, 0.0),
        jnp.where(column, amp_ref[...], 0.0),
        (((1,), (1,)), ((), ())),
        precision=lax.Precision.HIGHEST,
        preferred_element_type=jnp.float32,
    )
    src_ref[...] = part.reshape(src_ref.shape)
    taper_ref[...] = 1.0 - DAMPING * mask_ref[...].astype(jnp.float32)


def background_kernel(weight, first, last, *refs):
    refs = list(refs)
    u = [refs.pop(0) for _ in range(3)]
    b = [refs.pop(0) for _ in range(3)]
    stiff_ref = refs.pop(0)
    dg_ref = None if first else refs.pop(0)
    taper_ref = src_ref = older_ref = new_ref = None
    if not last:
        taper_ref, src_ref, older_ref = (refs.pop(0) for _ in range(3))
    mx_ref, my_ref = refs.pop(0), refs.pop(0)
    lap_ref = refs.pop(0)
    if not last:
        new_ref = refs.pop(0)
    if first:
        dg_ref = refs.pop(0)
    y_ref, a_ref = refs

    def functions(layer, row, size):
        value = u[1][layer, row : row + size]
        buoy = b[1][layer, row : row + size]
        return [value, value * buoy] + ([buoy] if first else [])

    plane_part(functions, y_ref, a_ref, mx_ref, my_ref, 3)

    def body(i, at, columns):
        value = tall_of(u, at, columns)
        buoy = tall_of(b, at, columns)
        both = [x * y for x, y in zip(value, buoy)]
        for layer in range(4):
            here, b_here = value[layer + 4], buoy[layer + 4]
            if first:
                dg = depth_part(buoy, layer) + a_ref[2, layer, at, columns] + CENTRE * b_here
                dg_ref[layer, at, columns] = dg
            else:
                dg = dg_ref[layer, at, columns]
            plain = depth_part(value, layer) + a_ref[0, layer, at, columns]
            times = depth_part(both, layer) + a_ref[1, layer, at, columns]
            lap = HALF * (b_here * plain + times - here * dg)
            lap_ref[layer, at, columns] = lap
            if not last:
                new_ref[layer, at, columns] = (
                    taper_ref[layer, at, columns]
                    * (
                        2.0 * here
                        - older_ref[layer, at, columns]
                        + stiff_ref[layer, at, columns] * lap
                    )
                    + weight * src_ref[layer, at, columns]
                )

    tiles(lap_ref.shape, body)


def wave_kernel(mode, has_old, *refs):
    refs = list(refs)
    p = [refs.pop(0) for _ in range(3)]
    old_ref = refs.pop(0) if has_old else None
    add_ref, lap_ref = refs.pop(0), refs.pop(0)
    b = [refs.pop(0) for _ in range(3)]
    dg_ref, stiff_ref, taper_ref = (refs.pop(0) for _ in range(3))
    count_ref = refs.pop(0) if mode == "turn" else None
    if mode == "image":
        first_ref = refs.pop(0)
        laps = [refs.pop(0) for _ in range(4)]
    mx_ref, my_ref, out_ref, y_ref, a_ref = refs

    def functions(layer, row, size):
        value = p[1][layer, row : row + size]
        return value, value * b[1][layer, row : row + size]

    plane_part(functions, y_ref, a_ref, mx_ref, my_ref, 2)

    def body(i, at, columns):
        value = tall_of(p, at, columns)
        buoy = tall_of(b, at, columns)
        both = [x * y for x, y in zip(value, buoy)]
        for layer in range(4):
            here = value[layer + 4]
            spot = (layer, at, columns)
            plain = depth_part(value, layer) + a_ref[0, layer, at, columns]
            times = depth_part(both, layer) + a_ref[1, layer, at, columns]
            lb = buoy[layer + 4] * plain + times - here * dg_ref[spot]
            total = 2.0 * here + (HALF * stiff_ref[spot]) * lb
            old = old_ref[spot] if has_old else None
            if has_old:
                total = total - old
            added = add_ref[spot] * lap_ref[spot]
            if mode in ("born", "turn"):
                new = taper_ref[spot] * (total + added)
            else:
                new = taper_ref[spot] * total + added
            if mode == "turn":
                new = count_ref[spot] * new
            if mode == "image":
                image = laps[3][spot] * first_ref[spot] + laps[2][spot] * old
                image = image + laps[1][spot] * here + laps[0][spot] * new
                per = out_ref.shape[2] // 8
                inner = pl.ds(pl.multiple_of((i % per) * 8, 8), 8)
                out_ref[i // per, layer, inner, columns] = image
            else:
                out_ref[spot] = new

    tiles(p[1].shape, body)


def gram_kernel(parts, *refs):
    pieces, out_ref = refs[:parts], refs[parts]
    owners, each, rows, columns = pieces[0].shape
    count = owners * parts * each

    def piece(c, at, column):
        owner, rest = divmod(c, parts * each)
        group, inner = divmod(rest, each)
        return pieces[group][owner, inner, at, column : column + LANE]

    for i0 in range(0, count, 4):
        for j0 in range(0, count, 8):

            def step(r, accs, i0=i0, j0=j0):
                at = pl.ds(pl.multiple_of(r * 8, 8), 8)
                accs = list(accs)
                for column in range(0, columns, LANE):
                    left = [piece(i0 + i, at, column) for i in range(4)]
                    for j in range(8):
                        right = piece(j0 + j, at, column)
                        for i in range(4):
                            accs[i * 8 + j] = accs[i * 8 + j] + left[i] * right
                return tuple(accs)

            zero = jnp.zeros((8, LANE), jnp.float32)
            accs = lax.fori_loop(0, rows // 8, step, (zero,) * 32)
            for i in range(4):
                for j in range(8):
                    out_ref[i0 + i, j0 + j : j0 + j + 1, :] = jnp.sum(
                        accs[i * 8 + j], axis=0, keepdims=True
                    )


def exact(left, right):
    return jnp.dot(left, right, precision=lax.Precision.HIGHEST, preferred_element_type=jnp.float32)


def basis_kernel(parts, scale, gram_ref, sel_ref, selt_ref, *refs):
    pieces = refs[:parts]
    out_ref, triangle_ref, spread_ref = refs[parts:]
    count = gram_ref.shape[0]
    owners, each, layers, rows, columns = pieces[0].shape

    @pl.when(pl.program_id(0) == 0)
    def _():
        row = lax.broadcasted_iota(jnp.int32, (count, count), 0)
        column = lax.broadcasted_iota(jnp.int32, (count, count), 1)
        left = exact(exact(sel_ref[...], gram_ref[...]), selt_ref[...])
        unit = jnp.where(row == column, 1.0, 0.0)
        for i in range(count):
            pivot = jnp.sqrt(left[i : i + 1, i : i + 1])
            upper = left[i : i + 1, :] / pivot
            solved = unit[i : i + 1, :] / pivot
            below = left[:, i : i + 1] / pivot
            is_row = row == i
            left = jnp.where(is_row, upper, jnp.where(row > i, left - below * upper, left))
            unit = jnp.where(is_row, solved, jnp.where(row > i, unit - below * solved, unit))
        triangle_ref[...] = jnp.where(column >= row, left, 0.0) / scale
        weights = exact(unit, sel_ref[...]) * scale
        for i in range(count):
            for c in range(count):
                spread_ref[i * count + c] = jnp.broadcast_to(
                    weights[i : i + 1, c : c + 1], (8, LANE)
                )

    def piece(c, at, columns):
        owner, rest = divmod(c, parts * each)
        group, inner = divmod(rest, each)
        return pieces[group][owner, inner, 0, at, columns]

    for r in range(0, rows, 8):
        at = slice(r, r + 8)
        halves = [slice(column, column + LANE) for column in range(0, columns, LANE)]
        values = [[piece(c, at, half) for half in halves] for c in range(count)]

        def step(i, carry, values=values, at=at):
            totals = [None] * len(halves)
            for c in range(count):
                weight = spread_ref[i * count + c]
                for h in range(len(halves)):
                    term = weight * values[c][h]
                    totals[h] = term if totals[h] is None else totals[h] + term
            for h, half in enumerate(halves):
                out_ref[i, 0, at, half] = totals[h]
            return carry

        for i in range(count):
            step(i, 0)


def halo(block):
    count = lax.axis_size("slab")
    forward = [(i, i + 1) for i in range(count - 1)]
    backward = [(target, source) for source, target in forward]
    return lax.ppermute(block, "slab", forward), lax.ppermute(block, "slab", backward)


def whole(shape):
    zeros = (0,) * len(shape)
    return pl.BlockSpec(tuple(shape), lambda *_: zeros)


def add_up(value):
    for axis in ("slab", "dirs"):
        size, stride = lax.axis_size(axis), 1
        while stride < size:
            value = value + lax.ppermute(value, axis, [(i, i ^ stride) for i in range(size)])
            stride *= 2
    return value


def shards(
    perturbations,
    background_now,
    background_prev,
    stiffness,
    buoyancy,
    absorb_mask,
    source_cells,
    source_amp,
    receiver_cells,
    column_order,
):
    shape = buoyancy.shape
    layers, rows, columns = shape
    sketch_count = perturbations.shape[0]
    each = sketch_count // GROUPS
    owners = lax.axis_size("dirs")
    f32 = jnp.float32
    field = jax.ShapeDtypeStruct(shape, f32)
    cells_here = layers * rows * columns
    mx = jnp.asarray(band(columns))
    my = band(rows)
    my2 = jnp.asarray(np.concatenate([my] * 2, 1))
    my3 = jnp.asarray(np.concatenate([my] * 3, 1))

    b_low, b_high = halo(buoyancy)
    buoy = (b_low, buoyancy, b_high)
    current = background_now
    u_low, u_high = halo(current)

    counts, source_field, taper = pl.pallas_call(
        place_kernel,
        out_shape=(field, field, field),
        compiler_params=params(),
        cost_estimate=pl.CostEstimate(
            flops=40 * cells_here, bytes_accessed=16 * cells_here, transcendentals=0
        ),
        name="place",
    )(
        receiver_cells.reshape(1, -1),
        source_cells.reshape(1, -1),
        source_amp.reshape(1, -1),
        absorb_mask,
    )

    older = background_prev
    laps = []
    dg = None
    for t in range(STEPS):
        first, last = t == 0, t == STEPS - 1
        if not first:
            u_low, u_high = halo(current)
        operands = [u_low, current, u_high, *buoy, stiffness]
        if not first:
            operands.append(dg)
        if not last:
            operands += [taper, source_field, older]
        operands += [mx, my3]
        slots = 3 if first else 2
        results = pl.pallas_call(
            functools.partial(background_kernel, source_weight(t), first, last),
            out_shape=(field,) * (1 + (not last) + first),
            scratch_shapes=[
                pltpu.VMEM((slots, layers, 3 * rows, columns), jnp.bfloat16),
                pltpu.VMEM((slots, layers, rows, columns), f32),
            ],
            compiler_params=params(),
            cost_estimate=pl.CostEstimate(
                flops=60 * cells_here, bytes_accessed=56 * cells_here, transcendentals=0
            ),
            name=f"background{t}",
        )(*operands)
        results = list(results)
        laps.append(results.pop(0))
        if not last:
            older, current = current, results.pop(0)
        if first:
            dg = results.pop(0)

    def wave(mode, group, p, old, add, lap, extra=()):
        low, high = halo(p)
        one = pl.BlockSpec((None, *shape), lambda d: (d, 0, 0, 0))
        shifted = pl.BlockSpec((None, *shape), lambda d: (d + group * each, 0, 0, 0))
        same = whole(shape)
        operands, specs = [low, p, high], [one] * 3
        if old is not None:
            operands.append(old)
            specs.append(one)
        if mode in ("born", "turn"):
            operands += [add, lap]
            specs += [shifted, same]
        else:
            operands += [add, lap]
            specs += [one, same]
        operands += [*buoy, dg, stiffness, taper]
        specs += [same] * 6
        if mode == "turn":
            operands.append(counts)
            specs.append(same)
        if mode == "image":
            operands += list(extra)
            specs += [one] + [same] * 4
        operands += [mx, my2]
        specs += [whole(mx.shape), whole(my2.shape)]
        if mode == "image":
            split = (owners, each, layers, rows // owners, columns)
            out_shape = jax.ShapeDtypeStruct(split, f32)
            out_spec = pl.BlockSpec((owners, None, *split[2:]), lambda d: (0, d, 0, 0, 0))
        else:
            out_shape = jax.ShapeDtypeStruct((each, *shape), f32)
            out_spec = one
        return pl.pallas_call(
            functools.partial(wave_kernel, mode, old is not None),
            grid=(each,),
            in_specs=specs,
            out_specs=out_spec,
            out_shape=out_shape,
            scratch_shapes=[
                pltpu.VMEM((2, layers, 2 * rows, columns), jnp.bfloat16),
                pltpu.VMEM((2, layers, rows, columns), f32),
            ],
            compiler_params=params(),
            cost_estimate=pl.CostEstimate(
                flops=60 * each * cells_here,
                bytes_accessed=28 * each * cells_here,
                transcendentals=0,
            ),
            name=mode,
        )(*operands)

    born = [[None] * GROUPS for _ in range(STEPS + 1)]
    for g in range(GROUPS):
        mine = perturbations[g * each : (g + 1) * each]
        born[1][g] = taper * (mine * laps[0])
    for t in (1, 2):
        for g in range(GROUPS):
            old = born[t - 1][g] if t > 1 else None
            born[t + 1][g] = wave("born", g, born[t][g], old, perturbations, laps[t])
    adjoint = [[None] * GROUPS for _ in range(STEPS + 1)]
    for g in range(GROUPS):
        adjoint[3][g] = wave("turn", g, born[3][g], born[2][g], perturbations, laps[3])
    for t in (2, 1):
        for g in range(GROUPS):
            old = adjoint[t + 2][g] if t < 2 else None
            adjoint[t][g] = wave("adjoint", g, adjoint[t + 1][g], old, born[t + 1][g], counts)
    sketch = []
    for g in range(GROUPS):
        image = wave(
            "image", g, adjoint[1][g], adjoint[2][g], born[1][g], counts, (adjoint[3][g], *laps)
        )
        sketch.append(lax.all_to_all(image, "dirs", split_axis=0, concat_axis=0, tiled=True))

    total_dirs = owners * sketch_count
    local_rows = rows // owners
    spread = pl.pallas_call(
        functools.partial(gram_kernel, GROUPS),
        out_shape=jax.ShapeDtypeStruct((total_dirs, total_dirs, LANE), f32),
        compiler_params=params(),
        name="gram",
    )(*[s.reshape(owners, each, layers * local_rows, columns) for s in sketch])
    gram = add_up(jnp.sum(spread, -1))
    selector = (column_order[:, None] == jnp.arange(total_dirs, dtype=jnp.int32)[None, :]).astype(
        f32
    )
    grid_cells = layers * lax.axis_size("slab") * rows * columns
    square = (total_dirs, total_dirs)
    part = (owners, each, 1, local_rows, columns)
    basis, triangle = pl.pallas_call(
        functools.partial(basis_kernel, GROUPS, math.sqrt(grid_cells)),
        grid=(layers,),
        in_specs=[whole(square)] * 3
        + [pl.BlockSpec(part, lambda l: (0, 0, l, 0, 0))] * GROUPS,
        out_specs=[
            pl.BlockSpec((total_dirs, 1, local_rows, columns), lambda l: (0, l, 0, 0)),
            whole(square),
        ],
        out_shape=(
            jax.ShapeDtypeStruct((total_dirs, layers, local_rows, columns), f32),
            jax.ShapeDtypeStruct(square, f32),
        ),
        scratch_shapes=[pltpu.VMEM((total_dirs * total_dirs, 8, LANE), f32)],
        compiler_params=params(),
        name="basis",
    )(gram, selector, selector.T, *sketch)
    return basis, triangle


def solution(mesh):
    return jax.shard_map(
        shards,
        mesh=mesh,
        in_specs=(
            P("dirs", "slab", None, None),
            P("slab", None, None),
            P("slab", None, None),
            P("slab", None, None),
            P("slab", None, None),
            P("slab", None, None),
            P("slab"),
            P("slab"),
            P("slab"),
            P(),
        ),
        out_specs=(P(None, "slab", "dirs", None), P()),
        check_vma=False,
    )
```

time: 1310 us -> 279 us (0.21); the launches traced: 1290 us -> 277 us
  other arithmetic: 510 us -> 0.41 us
  local copies, waits for them, and re-layouts: 433 us -> 19.9 us
  blocking collectives: 192 us -> 18.8 us
  starting transfers between devices: 59.4 us -> 131 us
  Pallas kernels: 0 us -> 59.4 us
  waiting for transfers between devices: 68.6 us -> 45.3 us
  matrix products: 14.3 us -> 0 us
    add x24 -> x7, other arithmetic: 201 us -> 0.02 us  [add_up(): value + lax.ppermute(value, axis, [(i, i ^ stride) for i in range(size)])]
    psum x3 -> x0, blocking collectives: 192 us -> none  [the longest x1 65.8 us: shards(): first_gram = lax.psum(product(first_rows, first_rows.T), ('dirs', 'slab'))]
    scatter-add x7 -> x0, other arithmetic: 182 us -> none  [the longest x6 181 us: shards(): injected = jnp.zeros((sketch_count, window_cells), jnp.float32).at[:, rec...]
    reshape x6 -> x0, local copies, waits for them, and re-layouts: 160 us -> none  [the longest x4 156 us: shards(): injected = jnp.zeros((sketch_count, window_cells), jnp.float32).at[:, rec...]
    mul x20 -> x0, local copies, waits for them, and re-layouts: 133 us -> none  [the longest x4 132 us: shards(): tapering * (2.0 * born_now - born_old + stiffness * lapped[1:] + perturba...]
    concatenate x26 -> x0, other arithmetic: 90.2 us -> none  [the longest x11 49.1 us: extended(): block = jnp.concatenate([low, block, high], axis=dim)]
    ppermute x16 -> x41, starting transfers between devices: 53.9 us -> 126 us  [the longest x17 80.4 us: halo(): lax.ppermute(block, 'slab', forward)]
    slice x38 -> x0, local copies, waits for them, and re-layouts: 63.7 us -> none  [the longest x20 53.1 us: along_columns(): values[..., k:]]
  transfers between devices with their start and end apart: 17 -> 42, of which waited for: 7 -> 20; matrix products, arithmetic and copies ran while one was open for 39% -> 0% of each run, Pallas kernels for 0% -> 16%
where the time goes in v1:
time: 279 us; the launch traced here: 277 us
  starting transfers between devices  131 us (47%)
  Pallas kernels  59.4 us (21%)
  waiting for transfers between devices  45.3 us (16%)
  local copies, waits for them, and re-layouts  19.9 us (7%)
  blocking collectives  18.8 us (7%)
    ppermute x17, starting transfers between devices, halo(): lax.ppermute(block, 'slab', forward)  80.4 us
    ppermute x17, starting transfers between devices, halo(): lax.ppermute(block, 'slab', backward)  40 us
    pallas_call x12, Pallas kernels, wave(): pl.pallas_call(functools.partial(wave_kernel, mode, old is not None), gri...  39.4 us
    ppermute x7, waiting for transfers between devices, add_up(): lax.ppermute(value, axis, [(i, i ^ stride) for i in range(size)])  24.6 us
    unnamed x72, local copies, waits for them, and re-layouts  19.9 us
    all_to_all x1, blocking collectives, shards(): lax.all_to_all(image, 'dirs', split_axis=0, concat_axis=0, tiled=True)  18.8 us
    ppermute x17, waiting for transfers between devices, halo(): lax.ppermute(block, 'slab', backward)  14 us
    pallas_call x4, Pallas kernels, shards(): pl.pallas_call(functools.partial(background_kernel, source_weight(t), fir...  7.41 us
  transfers between devices with their start and end apart: 42, of which 20 were waited for; matrix products, arithmetic and copies ran while one was open for 0% of the time, Pallas kernels for 16%

profile of v1, /device:TPU:14, one launch (start us, length us, event | category | flops | bytes accessed | tf_op | source)
XLA Modules:
  0.0 276.6 jit_solution(887121159629634533)
XLA Ops:
  27.4 8.0 %collective-permute-start.22 = (f32[2,4,128,256]{3,2,1,0:T(8,128)S(1)}, f32[2,4,128,256]{3,2,1,0:T(8,128)S(1)}, u32[]{:S(2)}, u32[]{:S(2)}) collective-permute-start(f32[2,4,128,256]{3,2,1,0:T(8,128)S(1)} %get-tuple-element.22.refs_1_.refs_3_.refs_4_), channel_id=1, source_target_pairs={{0,1},{1,2},{2,3},{3,4},{4,5},{5,6},{6,7},{7,8},{8,9},{9,10},{10,1... | collective-permute-start | bytes 3145736 | tf_op jit(solution)/shard_map/ppermute | solution.py:320
  42.9 4.0 %collective-permute-start.4 = (f32[2,4,128,256]{3,2,1,0:T(8,128)S(1)}, f32[2,4,128,256]{3,2,1,0:T(8,128)S(1)}, u32[]{:S(2)}, u32[]{:S(2)}) collective-permute-start(f32[2,4,128,256]{3,2,1,0:T(8,128)S(1)} %get-tuple-element.23.refs_1_.refs_3_.refs_4_), channel_id=1, source_target_pairs={{0,1},{1,2},{2,3},{3,4},{4,5},{5,6},{6,7},{7,8},{8,9},{9,10},{10,1... | collective-permute-start | bytes 3145736 | tf_op jit(solution)/shard_map/ppermute | solution.py:320
  51.4 3.9 %collective-permute-done.7.refs_2_ = f32[4,128,256]{2,1,0:T(8,128)S(1)} collective-permute-done((f32[4,128,256]{2,1,0:T(8,128)S(1)}, f32[4,128,256]{2,1,0:T(8,128)S(1)}, u32[]{:S(2)}, u32[]{:S(2)}) %collective-permute-start.7) | collective-permute-done | bytes 524320 | tf_op jit(solution)/shard_map/ppermute | solution.py:320
  60.1 5.9 %collective-permute-start.24 = (f32[2,4,128,256]{3,2,1,0:T(8,128)S(1)}, f32[2,4,128,256]{3,2,1,0:T(8,128)S(1)}, u32[]{:S(2)}, u32[]{:S(2)}) collective-permute-start(f32[2,4,128,256]{3,2,1,0:T(8,128)S(1)} %born.6.refs_1_.refs_3_.refs_4_), channel_id=1, source_target_pairs={{0,1},{1,2},{2,3},{3,4},{4,5},{5,6},{6,7},{7,8},{8,9},{9,10},{10,1... | collective-permute-start | bytes 3145736 | tf_op jit(solution)/shard_map/ppermute | solution.py:320
  76.5 4.1 %collective-permute-start.8 = (f32[2,4,128,256]{3,2,1,0:T(8,128)S(1)}, f32[2,4,128,256]{3,2,1,0:T(8,128)S(1)}, u32[]{:S(2)}, u32[]{:S(2)}) collective-permute-start(f32[2,4,128,256]{3,2,1,0:T(8,128)S(1)} %born.4.refs_1_.refs_3_.refs_4_), channel_id=1, source_target_pairs={{0,1},{1,2},{2,3},{3,4},{4,5},{5,6},{6,7},{7,8},{8,9},{9,10},{10,1... | collective-permute-start | bytes 3145736 | tf_op jit(solution)/shard_map/ppermute | solution.py:320
  90.6 5.9 %collective-permute-start.26 = (f32[2,4,128,256]{3,2,1,0:T(8,128)S(1)}, f32[2,4,128,256]{3,2,1,0:T(8,128)S(1)}, u32[]{:S(2)}, u32[]{:S(2)}) collective-permute-start(f32[2,4,128,256]{3,2,1,0:T(8,128)S(1)} %born.7.refs_1_.refs_3_), channel_id=1, source_target_pairs={{0,1},{1,2},{2,3},{3,4},{4,5},{5,6},{6,7},{7,8},{8,9},{9,10},{10,1... | collective-permute-start | bytes 3145736 | tf_op jit(solution)/shard_map/ppermute | solution.py:320
  107.3 4.3 %collective-permute-start.12 = (f32[2,4,128,256]{3,2,1,0:T(8,128)S(1)}, f32[2,4,128,256]{3,2,1,0:T(8,128)S(1)}, u32[]{:S(2)}, u32[]{:S(2)}) collective-permute-start(f32[2,4,128,256]{3,2,1,0:T(8,128)S(1)} %born.5.refs_1_.refs_3_), channel_id=1, source_target_pairs={{0,1},{1,2},{2,3},{3,4},{4,5},{5,6},{6,7},{7,8},{8,9},{9,10},{10,1... | collective-permute-start | bytes 3145736 | tf_op jit(solution)/shard_map/ppermute | solution.py:320
  121.1 6.2 %collective-permute-start.28 = (f32[2,4,128,256]{3,2,1,0:T(8,128)S(1)}, f32[2,4,128,256]{3,2,1,0:T(8,128)S(1)}, u32[]{:S(2)}, u32[]{:S(2)}) collective-permute-start(f32[2,4,128,256]{3,2,1,0:T(8,128)S(1)} %turn.3.refs_1_.refs_3_.refs_12_), channel_id=1, source_target_pairs={{0,1},{1,2},{2,3},{3,4},{4,5},{5,6},{6,7},{7,8},{8,9},{9,10},{10,1... | collective-permute-start | bytes 3145736 | tf_op jit(solution)/shard_map/ppermute | solution.py:320
  132.4 6.3 %collective-permute-start.16 = (f32[2,4,128,256]{3,2,1,0:T(8,128)S(1)}, f32[2,4,128,256]{3,2,1,0:T(8,128)S(1)}, u32[]{:S(2)}, u32[]{:S(2)}) collective-permute-start(f32[2,4,128,256]{3,2,1,0:T(8,128)S(1)} %turn.2.refs_1_.refs_3_.refs_12_), channel_id=1, source_target_pairs={{0,1},{1,2},{2,3},{3,4},{4,5},{5,6},{6,7},{7,8},{8,9},{9,10},{10,1... | collective-permute-start | bytes 3145736 | tf_op jit(solution)/shard_map/ppermute | solution.py:320
  144.5 6.4 %collective-permute-start.30 = (f32[2,4,128,256]{3,2,1,0:T(8,128)S(1)}, f32[2,4,128,256]{3,2,1,0:T(8,128)S(1)}, u32[]{:S(2)}, u32[]{:S(2)}) collective-permute-start(f32[2,4,128,256]{3,2,1,0:T(8,128)S(1)} %adjoint.6.refs_1_.refs_3_), channel_id=1, source_target_pairs={{0,1},{1,2},{2,3},{3,4},{4,5},{5,6},{6,7},{7,8},{8,9},{9,10},{10,1... | collective-permute-start | bytes 3145736 | tf_op jit(solution)/shard_map/ppermute | solution.py:320
  156.0 6.2 %collective-permute-start.18 = (f32[2,4,128,256]{3,2,1,0:T(8,128)S(1)}, f32[2,4,128,256]{3,2,1,0:T(8,128)S(1)}, u32[]{:S(2)}, u32[]{:S(2)}) collective-permute-start(f32[2,4,128,256]{3,2,1,0:T(8,128)S(1)} %adjoint.4.refs_1_.refs_3_), channel_id=1, source_target_pairs={{0,1},{1,2},{2,3},{3,4},{4,5},{5,6},{6,7},{7,8},{8,9},{9,10},{10,1... | collective-permute-start | bytes 3145736 | tf_op jit(solution)/shard_map/ppermute | solution.py:320
  168.2 5.9 %collective-permute-start.32 = (f32[2,4,128,256]{3,2,1,0:T(8,128)S(1)}, f32[2,4,128,256]{3,2,1,0:T(8,128)S(1)}, u32[]{:S(2)}, u32[]{:S(2)}) collective-permute-start(f32[2,4,128,256]{3,2,1,0:T(8,128)S(1)} %adjoint.7.refs_1_), channel_id=1, source_target_pairs={{0,1},{1,2},{2,3},{3,4},{4,5},{5,6},{6,7},{7,8},{8,9},{9,10},{10,1... | collective-permute-start | bytes 3145736 | tf_op jit(solution)/shard_map/ppermute | solution.py:320
  176.4 3.8 %adjoint.5.refs_1_ = f32[2,4,128,256]{3,2,1,0:T(8,128)} custom-call(f32[2,4,128,256]{3,2,1,0:T(8,128)S(1)} %collective-permute-done.18.refs_0_, f32[2,4,128,256]{3,2,1,0:T(8,128)S(1)} %adjoint.4.refs_1_.refs_3_, f32[2,4,128,256]{3,2,1,0:T(8,128)S(1)} %collective-permute-done.19.refs_2_, f32[2,4,128,256]{3,2,1,0:T(8,128)S(1)} %turn.2.refs_1_.refs_3_.refs_12_, ...), custom_call_target="tpu_custom_call" | custom-call | flops 15728640 | bytes 7340032 | tf_op jit(solution)/shard_map/adjoint/pallas_call | solution.py:448
  180.2 5.9 %collective-permute-start.20 = (f32[2,4,128,256]{3,2,1,0:T(8,128)}, f32[2,4,128,256]{3,2,1,0:T(8,128)}, u32[]{:S(2)}, u32[]{:S(2)}) collective-permute-start(f32[2,4,128,256]{3,2,1,0:T(8,128)} %adjoint.5.refs_1_), channel_id=1, source_target_pairs={{0,1},{1,2},{2,3},{3,4},{4,5},{5,6},{6,7},{7,8},{8,9},{9,10},{10,1... | collective-permute-start | bytes 3145736 | tf_op jit(solution)/shard_map/ppermute | solution.py:320
  188.3 3.7 %image.3 = f32[4,2,4,32,256]{4,3,2,1,0:T(8,128)S(1)} custom-call(f32[2,4,128,256]{3,2,1,0:T(8,128)S(1)} %collective-permute-done.32.refs_0_, f32[2,4,128,256]{3,2,1,0:T(8,128)S(1)} %adjoint.7.refs_1_, f32[2,4,128,256]{3,2,1,0:T(8,128)S(1)} %collective-permute-done.33.refs_2_, f32[2,4,128,256]{3,2,1,0:T(8,128)S(1)} %adjoint.6.refs_1_.refs_3_, ...), custom_call_target="tpu_custom_call" | custom-call | flops 15728640 | bytes 7340032 | tf_op jit(solution)/shard_map/image/pallas_call | solution.py:448
  193.1 5.3 %all-to-all-start.1 = ((f32[4,2,4,32,256]{4,3,2,1,0:T(8,128)}), f32[4,2,4,32,256]{4,3,2,1,0:T(8,128)}, u32[]{:S(2)}, u32[]{:S(2)}) async-start(f32[4,2,4,32,256]{4,3,2,1,0:T(8,128)} %copy-done.24), calls=%async_computation.1 | async-start | bytes 2097152 | tf_op jit(solution)/shard_map/all_to_all | solution.py:487
  209.6 5.1 %image.2 = f32[4,2,4,32,256]{4,3,2,1,0:T(8,128)S(1)} custom-call(f32[2,4,128,256]{3,2,1,0:T(8,128)} %collective-permute-done.20.refs_0_, f32[2,4,128,256]{3,2,1,0:T(8,128)} %adjoint.5.refs_1_, f32[2,4,128,256]{3,2,1,0:T(8,128)} %collective-permute-done.21.refs_2_, f32[2,4,128,256]{3,2,1,0:T(8,128)S(1)} %copy-done.17, f32[2,4,128,256]{3,2,1,0:T(8,128)S(1)} %copy-done.12, ...), custom_call_target="tpu_custom_call" | custom-call | flops 15728640 | bytes 7340032 | tf_op jit(solution)/shard_map/image/pallas_call | solution.py:448
  215.6 18.8 %all_to_all.10.refs_0_ = f32[4,2,4,32,256]{4,3,2,1,0:T(8,128)S(1)} all-to-all(f32[4,2,4,32,256]{4,3,2,1,0:T(8,128)} %copy-done.25), channel_id=1, replica_groups=mesh['dirs'=4,'slab'=32] {'dirs'}, dimensions={0} | all-to-all | bytes 2097152 | tf_op jit(solution)/shard_map/all_to_all | solution.py:487
  234.5 4.8 %gram.1 = f32[16,16,128]{2,1,0:T(8,128)S(1)} custom-call(f32[4,2,128,256]{3,2,1,0:T(8,128)S(1)} %bitcast.5, f32[4,2,128,256]{3,2,1,0:T(8,128)} %bitcast.4.refs_1_), custom_call_target="tpu_custom_call" | custom-call | tf_op jit(solution)/shard_map/gram/pallas_call | solution.py:491
  243.2 3.6 %collective-permute-done.35 = f32[16,16]{1,0:T(8,128)S(1)} collective-permute-done((f32[16,16]{1,0:T(8,128)S(1)}, f32[16,16]{1,0:T(8,128)S(1)}, u32[]{:S(2)}, u32[]{:S(2)}) %collective-permute-start.35) | collective-permute-done | bytes 1056 | tf_op jit(solution)/shard_map/ppermute | solution.py:332
  246.9 5.2 %collective-permute-done.36 = f32[16,16]{1,0:T(8,128)S(1)} collective-permute-done((f32[16,16]{1,0:T(8,128)S(1)}, f32[16,16]{1,0:T(8,128)S(1)}, u32[]{:S(2)}, u32[]{:S(2)}) %collective-permute-start.36) | collective-permute-done | bytes 1056 | tf_op jit(solution)/shard_map/ppermute | solution.py:332
  256.4 4.4 %collective-permute-done.38 = f32[16,16]{1,0:T(8,128)S(1)} collective-permute-done((f32[16,16]{1,0:T(8,128)S(1)}, f32[16,16]{1,0:T(8,128)S(1)}, u32[]{:S(2)}, u32[]{:S(2)}) %collective-permute-start.38) | collective-permute-done | bytes 1056 | tf_op jit(solution)/shard_map/ppermute | solution.py:332
  265.4 4.3 %collective-permute-done.40 = f32[16,16]{1,0:T(8,128)S(1)} collective-permute-done((f32[16,16]{1,0:T(8,128)S(1)}, f32[16,16]{1,0:T(8,128)S(1)}, u32[]{:S(2)}, u32[]{:S(2)}) %collective-permute-start.40) | collective-permute-done | bytes 1056 | tf_op jit(solution)/shard_map/ppermute | solution.py:332
  269.6 6.9 %basis.1 = (f32[16,4,32,256]{3,2,1,0:T(8,128)}, f32[16,16]{1,0:T(8,128)}) custom-call(f32[16,16]{1,0:T(8,128)S(1)} %add.27.gram_ref, f32[16,16]{1,0:T(8,128)S(1)} %get-tuple-element.25.sel_ref, f32[16,16]{1,0:T(8,128)S(1)} %get-tuple-element.24.selt_ref, f32[4,2,4,32,256]{4,3,2,1,0:T(8,128)S(1)} %all_to_all.10.refs_0_, ...), custom_call_target="tpu_custom_call" | custom-call | tf_op jit(solution)/shard_map/basis/pallas_call | solution.py:504
  (162 shorter events, 136.1 us)
Async XLA Ops:
  0.6 15.1 %collective-permute-start.2 = (f32[4,128,256]{2,1,0:T(8,128)}, f32[4,128,256]{2,1,0:T(8,128)S(1)}, u32[]{:S(2)}, u32[]{:S(2)}) collective-permute-start(f32[4,128,256]{2,1,0:T(8,128)} %refs_7_.15), channel_id=1, source_target_pairs={{0,1},{1,2},{2,3},{3,4},{4,5},{5,6},{6,7},{7,8},{8,9},{9,10},{10,1... | collective-permute-start | bytes 1572872 | tf_op jit(solution)/shard_map/ppermute | solution.py:320
  27.4 29.7 %collective-permute-start.22 = (f32[2,4,128,256]{3,2,1,0:T(8,128)S(1)}, f32[2,4,128,256]{3,2,1,0:T(8,128)S(1)}, u32[]{:S(2)}, u32[]{:S(2)}) collective-permute-start(f32[2,4,128,256]{3,2,1,0:T(8,128)S(1)} %get-tuple-element.22.refs_1_.refs_3_.refs_4_), channel_id=1, source_target_pairs={{0,1},{1,2},{2,3},{3,4},{4,5},{5,6},{6,7},{7,8},{8,9},{9,10},{10,1... | collective-permute-start | bytes 3145736 | tf_op jit(solution)/shard_map/ppermute | solution.py:320
  35.4 21.6 %collective-permute-start.23 = (f32[2,4,128,256]{3,2,1,0:T(8,128)S(1)}, f32[2,4,128,256]{3,2,1,0:T(8,128)S(1)}, u32[]{:S(2)}, u32[]{:S(2)}) collective-permute-start(f32[2,4,128,256]{3,2,1,0:T(8,128)S(1)} %get-tuple-element.22.refs_1_.refs_3_.refs_4_), channel_id=1, source_target_pairs={{1,0},{2,1},{3,2},{4,3},{5,4},{6,5},{7,6},{8,7},{9,8},{10,9},{11,1... | collective-permute-start | bytes 3145736 | tf_op jit(solution)/shard_map/ppermute | solution.py:320
  39.8 15.5 %collective-permute-start.7 = (f32[4,128,256]{2,1,0:T(8,128)S(1)}, f32[4,128,256]{2,1,0:T(8,128)S(1)}, u32[]{:S(2)}, u32[]{:S(2)}) collective-permute-start(f32[4,128,256]{2,1,0:T(8,128)S(1)} %get-tuple-element.15.refs_1_.refs_10_), channel_id=1, source_target_pairs={{1,0},{2,1},{3,2},{4,3},{5,4},{6,5},{7,6},{8,7},{9,8},{10,9},{11,1... | collective-permute-start | bytes 1572872 | tf_op jit(solution)/shard_map/ppermute | solution.py:320
  42.9 27.4 %collective-permute-start.4 = (f32[2,4,128,256]{3,2,1,0:T(8,128)S(1)}, f32[2,4,128,256]{3,2,1,0:T(8,128)S(1)}, u32[]{:S(2)}, u32[]{:S(2)}) collective-permute-start(f32[2,4,128,256]{3,2,1,0:T(8,128)S(1)} %get-tuple-element.23.refs_1_.refs_3_.refs_4_), channel_id=1, source_target_pairs={{0,1},{1,2},{2,3},{3,4},{4,5},{5,6},{6,7},{7,8},{8,9},{9,10},{10,1... | collective-permute-start | bytes 3145736 | tf_op jit(solution)/shard_map/ppermute | solution.py:320
  49.5 24.0 %collective-permute-start.5 = (f32[2,4,128,256]{3,2,1,0:T(8,128)S(1)}, f32[2,4,128,256]{3,2,1,0:T(8,128)S(1)}, u32[]{:S(2)}, u32[]{:S(2)}) collective-permute-start(f32[2,4,128,256]{3,2,1,0:T(8,128)S(1)} %get-tuple-element.23.refs_1_.refs_3_.refs_4_), channel_id=1, source_target_pairs={{1,0},{2,1},{3,2},{4,3},{5,4},{6,5},{7,6},{8,7},{9,8},{10,9},{11,1... | collective-permute-start | bytes 3145736 | tf_op jit(solution)/shard_map/ppermute | solution.py:320
  60.1 27.5 %collective-permute-start.24 = (f32[2,4,128,256]{3,2,1,0:T(8,128)S(1)}, f32[2,4,128,256]{3,2,1,0:T(8,128)S(1)}, u32[]{:S(2)}, u32[]{:S(2)}) collective-permute-start(f32[2,4,128,256]{3,2,1,0:T(8,128)S(1)} %born.6.refs_1_.refs_3_.refs_4_), channel_id=1, source_target_pairs={{0,1},{1,2},{2,3},{3,4},{4,5},{5,6},{6,7},{7,8},{8,9},{9,10},{10,1... | collective-permute-start | bytes 3145736 | tf_op jit(solution)/shard_map/ppermute | solution.py:320
  66.0 21.6 %collective-permute-start.25 = (f32[2,4,128,256]{3,2,1,0:T(8,128)S(1)}, f32[2,4,128,256]{3,2,1,0:T(8,128)S(1)}, u32[]{:S(2)}, u32[]{:S(2)}) collective-permute-start(f32[2,4,128,256]{3,2,1,0:T(8,128)S(1)} %born.6.refs_1_.refs_3_.refs_4_), channel_id=1, source_target_pairs={{1,0},{2,1},{3,2},{4,3},{5,4},{6,5},{7,6},{8,7},{9,8},{10,9},{11,1... | collective-permute-start | bytes 3145736 | tf_op jit(solution)/shard_map/ppermute | solution.py:320
  70.4 15.5 %collective-permute-start.11 = (f32[4,128,256]{2,1,0:T(8,128)S(1)}, f32[4,128,256]{2,1,0:T(8,128)S(1)}, u32[]{:S(2)}, u32[]{:S(2)}) collective-permute-start(f32[4,128,256]{2,1,0:T(8,128)S(1)} %get-tuple-element.18.refs_1_), channel_id=1, source_target_pairs={{1,0},{2,1},{3,2},{4,3},{5,4},{6,5},{7,6},{8,7},{9,8},{10,9},{11,1... | collective-permute-start | bytes 1572872 | tf_op jit(solution)/shard_map/ppermute | solution.py:320
  76.5 24.6 %collective-permute-start.8 = (f32[2,4,128,256]{3,2,1,0:T(8,128)S(1)}, f32[2,4,128,256]{3,2,1,0:T(8,128)S(1)}, u32[]{:S(2)}, u32[]{:S(2)}) collective-permute-start(f32[2,4,128,256]{3,2,1,0:T(8,128)S(1)} %born.4.refs_1_.refs_3_.refs_4_), channel_id=1, source_target_pairs={{0,1},{1,2},{2,3},{3,4},{4,5},{5,6},{6,7},{7,8},{8,9},{9,10},{10,1... | collective-permute-start | bytes 3145736 | tf_op jit(solution)/shard_map/ppermute | solution.py:320
  82.3 22.0 %collective-permute-start.9 = (f32[2,4,128,256]{3,2,1,0:T(8,128)S(1)}, f32[2,4,128,256]{3,2,1,0:T(8,128)S(1)}, u32[]{:S(2)}, u32[]{:S(2)}) collective-permute-start(f32[2,4,128,256]{3,2,1,0:T(8,128)S(1)} %born.4.refs_1_.refs_3_.refs_4_), channel_id=1, source_target_pairs={{1,0},{2,1},{3,2},{4,3},{5,4},{6,5},{7,6},{8,7},{9,8},{10,9},{11,1... | collective-permute-start | bytes 3145736 | tf_op jit(solution)/shard_map/ppermute | solution.py:320
  90.6 27.4 %collective-permute-start.26 = (f32[2,4,128,256]{3,2,1,0:T(8,128)S(1)}, f32[2,4,128,256]{3,2,1,0:T(8,128)S(1)}, u32[]{:S(2)}, u32[]{:S(2)}) collective-permute-start(f32[2,4,128,256]{3,2,1,0:T(8,128)S(1)} %born.7.refs_1_.refs_3_), channel_id=1, source_target_pairs={{0,1},{1,2},{2,3},{3,4},{4,5},{5,6},{6,7},{7,8},{8,9},{9,10},{10,1... | collective-permute-start | bytes 3145736 | tf_op jit(solution)/shard_map/ppermute | solution.py:320
  96.6 21.5 %collective-permute-start.27 = (f32[2,4,128,256]{3,2,1,0:T(8,128)S(1)}, f32[2,4,128,256]{3,2,1,0:T(8,128)S(1)}, u32[]{:S(2)}, u32[]{:S(2)}) collective-permute-start(f32[2,4,128,256]{3,2,1,0:T(8,128)S(1)} %born.7.refs_1_.refs_3_), channel_id=1, source_target_pairs={{1,0},{2,1},{3,2},{4,3},{5,4},{6,5},{7,6},{8,7},{9,8},{10,9},{11,1... | collective-permute-start | bytes 3145736 | tf_op jit(solution)/shard_map/ppermute | solution.py:320
  101.1 15.3 %collective-permute-start.15 = (f32[4,128,256]{2,1,0:T(8,128)S(1)}, f32[4,128,256]{2,1,0:T(8,128)S(1)}, u32[]{:S(2)}, u32[]{:S(2)}) collective-permute-start(f32[4,128,256]{2,1,0:T(8,128)S(1)} %get-tuple-element.20.refs_1_), channel_id=1, source_target_pairs={{1,0},{2,1},{3,2},{4,3},{5,4},{6,5},{7,6},{8,7},{9,8},{10,9},{11,1... | collective-permute-start | bytes 1572872 | tf_op jit(solution)/shard_map/ppermute | solution.py:320
  107.3 22.0 %collective-permute-start.12 = (f32[2,4,128,256]{3,2,1,0:T(8,128)S(1)}, f32[2,4,128,256]{3,2,1,0:T(8,128)S(1)}, u32[]{:S(2)}, u32[]{:S(2)}) collective-permute-start(f32[2,4,128,256]{3,2,1,0:T(8,128)S(1)} %born.5.refs_1_.refs_3_), channel_id=1, source_target_pairs={{0,1},{1,2},{2,3},{3,4},{4,5},{5,6},{6,7},{7,8},{8,9},{9,10},{10,1... | collective-permute-start | bytes 3145736 | tf_op jit(solution)/shard_map/ppermute | solution.py:320
  112.8 16.5 %collective-permute-start.13 = (f32[2,4,128,256]{3,2,1,0:T(8,128)S(1)}, f32[2,4,128,256]{3,2,1,0:T(8,128)S(1)}, u32[]{:S(2)}, u32[]{:S(2)}) collective-permute-start(f32[2,4,128,256]{3,2,1,0:T(8,128)S(1)} %born.5.refs_1_.refs_3_), channel_id=1, source_target_pairs={{1,0},{2,1},{3,2},{4,3},{5,4},{6,5},{7,6},{8,7},{9,8},{10,9},{11,1... | collective-permute-start | bytes 3145736 | tf_op jit(solution)/shard_map/ppermute | solution.py:320
  121.1 19.5 %collective-permute-start.28 = (f32[2,4,128,256]{3,2,1,0:T(8,128)S(1)}, f32[2,4,128,256]{3,2,1,0:T(8,128)S(1)}, u32[]{:S(2)}, u32[]{:S(2)}) collective-permute-start(f32[2,4,128,256]{3,2,1,0:T(8,128)S(1)} %turn.3.refs_1_.refs_3_.refs_12_), channel_id=1, source_target_pairs={{0,1},{1,2},{2,3},{3,4},{4,5},{5,6},{6,7},{7,8},{8,9},{9,10},{10,1... | collective-permute-start | bytes 3145736 | tf_op jit(solution)/shard_map/ppermute | solution.py:320
  132.4 20.7 %collective-permute-start.16 = (f32[2,4,128,256]{3,2,1,0:T(8,128)S(1)}, f32[2,4,128,256]{3,2,1,0:T(8,128)S(1)}, u32[]{:S(2)}, u32[]{:S(2)}) collective-permute-start(f32[2,4,128,256]{3,2,1,0:T(8,128)S(1)} %turn.2.refs_1_.refs_3_.refs_12_), channel_id=1, source_target_pairs={{0,1},{1,2},{2,3},{3,4},{4,5},{5,6},{6,7},{7,8},{8,9},{9,10},{10,1... | collective-permute-start | bytes 3145736 | tf_op jit(solution)/shard_map/ppermute | solution.py:320
  144.5 19.6 %collective-permute-start.30 = (f32[2,4,128,256]{3,2,1,0:T(8,128)S(1)}, f32[2,4,128,256]{3,2,1,0:T(8,128)S(1)}, u32[]{:S(2)}, u32[]{:S(2)}) collective-permute-start(f32[2,4,128,256]{3,2,1,0:T(8,128)S(1)} %adjoint.6.refs_1_.refs_3_), channel_id=1, source_target_pairs={{0,1},{1,2},{2,3},{3,4},{4,5},{5,6},{6,7},{7,8},{8,9},{9,10},{10,1... | collective-permute-start | bytes 3145736 | tf_op jit(solution)/shard_map/ppermute | solution.py:320
  156.0 20.0 %collective-permute-start.18 = (f32[2,4,128,256]{3,2,1,0:T(8,128)S(1)}, f32[2,4,128,256]{3,2,1,0:T(8,128)S(1)}, u32[]{:S(2)}, u32[]{:S(2)}) collective-permute-start(f32[2,4,128,256]{3,2,1,0:T(8,128)S(1)} %adjoint.4.refs_1_.refs_3_), channel_id=1, source_target_pairs={{0,1},{1,2},{2,3},{3,4},{4,5},{5,6},{6,7},{7,8},{8,9},{9,10},{10,1... | collective-permute-start | bytes 3145736 | tf_op jit(solution)/shard_map/ppermute | solution.py:320
  168.2 19.9 %collective-permute-start.32 = (f32[2,4,128,256]{3,2,1,0:T(8,128)S(1)}, f32[2,4,128,256]{3,2,1,0:T(8,128)S(1)}, u32[]{:S(2)}, u32[]{:S(2)}) collective-permute-start(f32[2,4,128,256]{3,2,1,0:T(8,128)S(1)} %adjoint.7.refs_1_), channel_id=1, source_target_pairs={{0,1},{1,2},{2,3},{3,4},{4,5},{5,6},{6,7},{7,8},{8,9},{9,10},{10,1... | collective-permute-start | bytes 3145736 | tf_op jit(solution)/shard_map/ppermute | solution.py:320
  180.2 18.2 %collective-permute-start.20 = (f32[2,4,128,256]{3,2,1,0:T(8,128)}, f32[2,4,128,256]{3,2,1,0:T(8,128)}, u32[]{:S(2)}, u32[]{:S(2)}) collective-permute-start(f32[2,4,128,256]{3,2,1,0:T(8,128)} %adjoint.5.refs_1_), channel_id=1, source_target_pairs={{0,1},{1,2},{2,3},{3,4},{4,5},{5,6},{6,7},{7,8},{8,9},{9,10},{10,1... | collective-permute-start | bytes 3145736 | tf_op jit(solution)/shard_map/ppermute | solution.py:320
  186.1 14.5 %collective-permute-start.21 = (f32[2,4,128,256]{3,2,1,0:T(8,128)}, f32[2,4,128,256]{3,2,1,0:T(8,128)}, u32[]{:S(2)}, u32[]{:S(2)}) collective-permute-start(f32[2,4,128,256]{3,2,1,0:T(8,128)} %adjoint.5.refs_1_), channel_id=1, source_target_pairs={{1,0},{2,1},{3,2},{4,3},{5,4},{6,5},{7,6},{8,7},{9,8},{10,9},{11,1... | collective-permute-start | bytes 3145736 | tf_op jit(solution)/shard_map/ppermute | solution.py:320
  193.1 22.6 %all-to-all-start.1 = ((f32[4,2,4,32,256]{4,3,2,1,0:T(8,128)}), f32[4,2,4,32,256]{4,3,2,1,0:T(8,128)}, u32[]{:S(2)}, u32[]{:S(2)}) async-start(f32[4,2,4,32,256]{4,3,2,1,0:T(8,128)} %copy-done.24), calls=%async_computation.1 | async-start | bytes 2097152 | tf_op jit(solution)/shard_map/all_to_all | solution.py:487
  (54 other events, 1158.5 us)

commit v2 on v1

--- a/solution.py
+++ b/solution.py
@@ -3,8 +3,6 @@
 
 import jax
 import jax.numpy as jnp
-import ml_dtypes
-import numpy as np
 from jax import lax
 from jax.experimental import pallas as pl
 from jax.experimental.pallas import tpu as pltpu
@@ -16,23 +14,26 @@
 CENTRE = 6.0 * sum(TAPS)
 HALF = 0.5 / 5040.0
 GROUPS = 2
-VMEM = 40 * 1024 * 1024
+VMEM = 22 * 1024 * 1024
 LANE = 128
 
 
-def band(size):
-    matrix = np.zeros((size, size), np.float32)
+def band(shape, period):
+    row = lax.broadcasted_iota(jnp.int32, shape, 0)
+    column = lax.broadcasted_iota(jnp.int32, shape, 1) % period
+    distance = jnp.abs(row - column)
+    matrix = jnp.zeros(shape, jnp.float32)
     for k, tap in enumerate(TAPS, 1):
-        matrix += tap * (np.eye(size, k=k) + np.eye(size, k=-k))
-    return matrix.astype(ml_dtypes.bfloat16)
+        matrix = jnp.where(distance == k, tap, matrix)
+    return matrix.astype(jnp.bfloat16)
 
 
 def source_weight(t):
     return (1.0 - 0.4 * t) * math.exp(-0.125 * t * t)
 
 
-def params(**more):
-    return pltpu.CompilerParams(vmem_limit_bytes=VMEM, **more)
+def params():
+    return pltpu.CompilerParams(vmem_limit_bytes=VMEM)
 
 
 def split_rows(y_ref, slot, layer, row, values, parts, rows):
@@ -73,11 +74,9 @@
     return [ref[layer, rows, columns] for ref in (low, mid, high) for layer in range(4)]
 
 
-def tiles(shape, body):
-    _, rows, columns = shape
-
+def tiles(rows, columns, body, start=0):
     def step(i, carry):
-        at = pl.ds(pl.multiple_of(i * 8, 8), 8)
+        at = pl.ds(pl.multiple_of(start + i * 8, 8), 8)
         for column in range(0, columns, LANE):
             body(i, at, slice(column, column + LANE))
         return carry
@@ -85,8 +84,14 @@
     lax.fori_loop(0, rows // 8, step, 0)
 
 
-def place_kernel(rc_ref, sc_ref, amp_ref, mask_ref, m_ref, src_ref, taper_ref):
+def place_kernel(copies, rc_ref, sc_ref, amp_ref, mask_ref, *refs):
+    sources, refs = refs[:copies], refs[copies:]
+    m_ref, src_ref, taper_ref, mx_ref, my2_ref, my3_ref = refs[:6]
+    for source, target in zip(sources, refs[6:]):
+        target[...] = source[...]
     layers, rows, columns = m_ref.shape
+    for matrix in (mx_ref, my2_ref, my3_ref):
+        matrix[...] = band(matrix.shape, matrix.shape[0])
     count = rc_ref.shape[1]
     lines = layers * rows
     chunk = min(256, count)
@@ -168,21 +173,26 @@
                     + weight * src_ref[layer, at, columns]
                 )
 
-    tiles(lap_ref.shape, body)
+    tiles(*lap_ref.shape[1:], body)
 
 
 def wave_kernel(mode, has_old, *refs):
     refs = list(refs)
     p = [refs.pop(0) for _ in range(3)]
     old_ref = refs.pop(0) if has_old else None
-    add_ref, lap_ref = refs.pop(0), refs.pop(0)
     b = [refs.pop(0) for _ in range(3)]
-    dg_ref, stiff_ref, taper_ref = (refs.pop(0) for _ in range(3))
+    dg_ref, stiff_ref = refs.pop(0), refs.pop(0)
+    if mode == "image":
+        sum_ref, me_ref, weight_ref, near_ref = (refs.pop(0) for _ in range(4))
+    else:
+        taper_ref, add_ref, lap_ref = (refs.pop(0) for _ in range(3))
     count_ref = refs.pop(0) if mode == "turn" else None
-    if mode == "image":
+    if mode == "fold":
         first_ref = refs.pop(0)
         laps = [refs.pop(0) for _ in range(4)]
-    mx_ref, my_ref, out_ref, y_ref, a_ref = refs
+    mx_ref, my_ref = refs.pop(0), refs.pop(0)
+    y_ref, a_ref = refs[-2:]
+    outs = refs[:-2]
 
     def functions(layer, row, size):
         value = p[1][layer, row : row + size]
@@ -190,7 +200,7 @@
 
     plane_part(functions, y_ref, a_ref, mx_ref, my_ref, 2)
 
-    def body(i, at, columns):
+    def body(block, i, at, columns):
         value = tall_of(p, at, columns)
         buoy = tall_of(b, at, columns)
         both = [x * y for x, y in zip(value, buoy)]
@@ -201,40 +211,61 @@
             times = depth_part(both, layer) + a_ref[1, layer, at, columns]
             lb = buoy[layer + 4] * plain + times - here * dg_ref[spot]
             total = 2.0 * here + (HALF * stiff_ref[spot]) * lb
-            old = old_ref[spot] if has_old else None
+            if mode == "image":
+                inner = pl.ds(pl.multiple_of(i * 8, 8), 8)
+                outs[block][layer, inner, columns] = (
+                    sum_ref[spot] + near_ref[spot] * here + weight_ref[spot] * total
+                )
+                continue
             if has_old:
+                old = old_ref[spot]
                 total = total - old
+            taper = taper_ref[spot]
             added = add_ref[spot] * lap_ref[spot]
             if mode in ("born", "turn"):
-                new = taper_ref[spot] * (total + added)
+                new = taper * (total + added)
             else:
-                new = taper_ref[spot] * total + added
+                new = taper * total + added
             if mode == "turn":
                 new = count_ref[spot] * new
-            if mode == "image":
-                image = laps[3][spot] * first_ref[spot] + laps[2][spot] * old
-                image = image + laps[1][spot] * here + laps[0][spot] * new
-                per = out_ref.shape[2] // 8
-                inner = pl.ds(pl.multiple_of((i % per) * 8, 8), 8)
-                out_ref[i // per, layer, inner, columns] = image
-            else:
-                out_ref[spot] = new
-
-    tiles(p[1].shape, body)
-
-
-def gram_kernel(parts, *refs):
-    pieces, out_ref = refs[:parts], refs[parts]
-    owners, each, rows, columns = pieces[0].shape
-    count = owners * parts * each
+            outs[0][spot] = new
+            if mode == "fold":
+                weight = laps[0][spot] * taper
+                known = laps[3][spot] * old + laps[2][spot] * here
+                known = known + laps[0][spot] * (lap_ref[spot] * first_ref[spot])
+                outs[1][spot] = known - weight * here
+                if len(outs) > 2:
+                    outs[2][spot] = weight
+                    outs[3][spot] = laps[1][spot]
+
+    _, rows, columns = p[1].shape
+    if mode == "image":
+        per = rows // len(outs)
+        for block in range(len(outs)):
+            owner = lax.rem(me_ref[0] + block, len(outs))
+            tiles(per, columns, functools.partial(body, block), owner * per)
+    else:
+        tiles(rows, columns, functools.partial(body, 0))
+
+
+def piece_of(pieces, parts, c):
+    each = pieces[0].shape[0]
+    block, rest = divmod(c, parts * each)
+    group, inner = divmod(rest, each)
+    return pieces[group * (len(pieces) // parts) + block], inner
+
+
+def gram_kernel(parts, sel_ref, selt_ref, *refs):
+    *pieces, out_ref, lanes_ref = refs
+    count = sel_ref.shape[0]
+    _, rows, columns = pieces[0].shape
 
     def piece(c, at, column):
-        owner, rest = divmod(c, parts * each)
-        group, inner = divmod(rest, each)
-        return pieces[group][owner, inner, at, column : column + LANE]
+        ref, inner = piece_of(pieces, parts, c)
+        return ref[inner, at, column : column + LANE]
 
     for i0 in range(0, count, 4):
-        for j0 in range(0, count, 8):
+        for j0 in range(i0 // 8 * 8, count, 8):
 
             def step(r, accs, i0=i0, j0=j0):
                 at = pl.ds(pl.multiple_of(r * 8, 8), 8)
@@ -251,26 +282,30 @@
             accs = lax.fori_loop(0, rows // 8, step, (zero,) * 32)
             for i in range(4):
                 for j in range(8):
-                    out_ref[i0 + i, j0 + j : j0 + j + 1, :] = jnp.sum(
+                    lanes_ref[i0 + i, j0 + j : j0 + j + 1, :] = jnp.sum(
                         accs[i * 8 + j], axis=0, keepdims=True
                     )
+    local = jnp.sum(lanes_ref[...], axis=-1)
+    row = lax.broadcasted_iota(jnp.int32, local.shape, 0)
+    column = lax.broadcasted_iota(jnp.int32, local.shape, 1)
+    local = jnp.where(row // 8 > column // 8, local.T, local)
+    out_ref[...] = exact(exact(sel_ref[...], local), selt_ref[...])
 
 
 def exact(left, right):
     return jnp.dot(left, right, precision=lax.Precision.HIGHEST, preferred_element_type=jnp.float32)
 
 
-def basis_kernel(parts, scale, gram_ref, sel_ref, selt_ref, *refs):
-    pieces = refs[:parts]
-    out_ref, triangle_ref, spread_ref = refs[parts:]
+def basis_kernel(parts, scale, gram_ref, sel_ref, *refs):
+    *pieces, out_ref, triangle_ref, spread_ref = refs
     count = gram_ref.shape[0]
-    owners, each, layers, rows, columns = pieces[0].shape
+    _, _, rows, columns = pieces[0].shape
 
     @pl.when(pl.program_id(0) == 0)
     def _():
         row = lax.broadcasted_iota(jnp.int32, (count, count), 0)
         column = lax.broadcasted_iota(jnp.int32, (count, count), 1)
-        left = exact(exact(sel_ref[...], gram_ref[...]), selt_ref[...])
+        left = gram_ref[...]
         unit = jnp.where(row == column, 1.0, 0.0)
         for i in range(count):
             pivot = jnp.sqrt(left[i : i + 1, i : i + 1])
@@ -289,16 +324,14 @@
                 )
 
     def piece(c, at, columns):
-        owner, rest = divmod(c, parts * each)
-        group, inner = divmod(rest, each)
-        return pieces[group][owner, inner, 0, at, columns]
-
+        ref, inner = piece_of(pieces, parts, c)
+        return ref[inner, 0, at, columns]
+
+    halves = [slice(column, column + LANE) for column in range(0, columns, LANE)]
     for r in range(0, rows, 8):
         at = slice(r, r + 8)
-        halves = [slice(column, column + LANE) for column in range(0, columns, LANE)]
         values = [[piece(c, at, half) for half in halves] for c in range(count)]
-
-        def step(i, carry, values=values, at=at):
+        for i in range(count):
             totals = [None] * len(halves)
             for c in range(count):
                 weight = spread_ref[i * count + c]
@@ -307,10 +340,6 @@
                     totals[h] = term if totals[h] is None else totals[h] + term
             for h, half in enumerate(halves):
                 out_ref[i, 0, at, half] = totals[h]
-            return carry
-
-        for i in range(count):
-            step(i, 0)
 
 
 def halo(block):
@@ -351,22 +380,23 @@
     sketch_count = perturbations.shape[0]
     each = sketch_count // GROUPS
     owners = lax.axis_size("dirs")
+    me = lax.axis_index("dirs").astype(jnp.int32).reshape(1)
     f32 = jnp.float32
     field = jax.ShapeDtypeStruct(shape, f32)
     cells_here = layers * rows * columns
-    mx = jnp.asarray(band(columns))
-    my = band(rows)
-    my2 = jnp.asarray(np.concatenate([my] * 2, 1))
-    my3 = jnp.asarray(np.concatenate([my] * 3, 1))
-
     b_low, b_high = halo(buoyancy)
-    buoy = (b_low, buoyancy, b_high)
-    current = background_now
-    u_low, u_high = halo(current)
-
-    counts, source_field, taper = pl.pallas_call(
-        place_kernel,
-        out_shape=(field, field, field),
+    u_low, u_high = halo(background_now)
+
+    def matrix(*size):
+        return jax.ShapeDtypeStruct(size, jnp.bfloat16)
+
+    copied = (stiffness, buoyancy, background_now, background_prev)
+    matrices = (matrix(columns, columns), matrix(rows, 2 * rows), matrix(rows, 3 * rows))
+    (
+        counts, source_field, taper, mx, my2, my3, stiffness, b_mid, current, older
+    ) = pl.pallas_call(
+        functools.partial(place_kernel, len(copied)),
+        out_shape=(field,) * 3 + matrices + (field,) * len(copied),
         compiler_params=params(),
         cost_estimate=pl.CostEstimate(
             flops=40 * cells_here, bytes_accessed=16 * cells_here, transcendentals=0
@@ -377,9 +407,11 @@
         source_cells.reshape(1, -1),
         source_amp.reshape(1, -1),
         absorb_mask,
+        *copied,
     )
 
-    older = background_prev
+    buoy = (b_low, b_mid, b_high)
+    fields = [current]
     laps = []
     dg = None
     for t in range(STEPS):
@@ -410,6 +442,7 @@
         laps.append(results.pop(0))
         if not last:
             older, current = current, results.pop(0)
+            fields.append(current)
         if first:
             dg = results.pop(0)
 
@@ -422,30 +455,30 @@
         if old is not None:
             operands.append(old)
             specs.append(one)
-        if mode in ("born", "turn"):
-            operands += [add, lap]
-            specs += [shifted, same]
-        else:
-            operands += [add, lap]
-            specs += [one, same]
-        operands += [*buoy, dg, stiffness, taper]
-        specs += [same] * 6
+        operands += [*buoy, dg, stiffness]
+        specs += [same] * 5
+        if mode != "image":
+            operands += [taper, add, lap]
+            specs += [same, shifted if mode in ("born", "turn") else one, same]
         if mode == "turn":
             operands.append(counts)
             specs.append(same)
+        if mode == "fold":
+            specs += [one] + [same] * 4
         if mode == "image":
-            operands += list(extra)
-            specs += [one] + [same] * 4
-        operands += [mx, my2]
+            specs += [one, pl.BlockSpec(memory_space=pltpu.SMEM)] + [same] * 2
+        operands += [*extra, mx, my2]
         specs += [whole(mx.shape), whole(my2.shape)]
-        if mode == "image":
-            split = (owners, each, layers, rows // owners, columns)
-            out_shape = jax.ShapeDtypeStruct(split, f32)
-            out_spec = pl.BlockSpec((owners, None, *split[2:]), lambda d: (0, d, 0, 0, 0))
-        else:
-            out_shape = jax.ShapeDtypeStruct((each, *shape), f32)
-            out_spec = one
-        return pl.pallas_call(
+        out_shape, out_spec = (jax.ShapeDtypeStruct((each, *shape), f32),), [one]
+        if mode == "fold":
+            out_shape, out_spec = out_shape * 2, out_spec * 2
+            if group == 0:
+                out_shape, out_spec = out_shape + (field,) * 2, out_spec + [same] * 2
+        elif mode == "image":
+            split = (layers, rows // owners, columns)
+            out_shape = (jax.ShapeDtypeStruct((each, *split), f32),) * owners
+            out_spec = [pl.BlockSpec((None, *split), lambda d: (d, 0, 0, 0))] * owners
+        results = pl.pallas_call(
             functools.partial(wave_kernel, mode, old is not None),
             grid=(each,),
             in_specs=specs,
@@ -463,49 +496,68 @@
             ),
             name=mode,
         )(*operands)
+        return results[0] if len(results) == 1 else results
+
+    def after(value, earlier):
+        return lax.optimization_barrier((value, earlier))[0]
 
     born = [[None] * GROUPS for _ in range(STEPS + 1)]
     for g in range(GROUPS):
         mine = perturbations[g * each : (g + 1) * each]
         born[1][g] = taper * (mine * laps[0])
+    born[1][1] = after(born[1][1], fields[2])
+    ahead = {(2, 1): fields[3]}
     for t in (1, 2):
         for g in range(GROUPS):
             old = born[t - 1][g] if t > 1 else None
-            born[t + 1][g] = wave("born", g, born[t][g], old, perturbations, laps[t])
+            new = wave("born", g, born[t][g], old, perturbations, laps[t])
+            if (t + 1, g) in ahead:
+                new = after(new, ahead[t + 1, g])
+            born[t + 1][g] = new
     adjoint = [[None] * GROUPS for _ in range(STEPS + 1)]
     for g in range(GROUPS):
         adjoint[3][g] = wave("turn", g, born[3][g], born[2][g], perturbations, laps[3])
-    for t in (2, 1):
-        for g in range(GROUPS):
-            old = adjoint[t + 2][g] if t < 2 else None
-            adjoint[t][g] = wave("adjoint", g, adjoint[t + 1][g], old, born[t + 1][g], counts)
+    for g in range(GROUPS):
+        adjoint[2][g] = wave("adjoint", g, adjoint[3][g], None, born[3][g], counts)
+    known = [None] * GROUPS
+    for g in range(GROUPS):
+        adjoint[1][g], known[g], *rest = wave(
+            "fold", g, adjoint[2][g], adjoint[3][g], born[2][g], counts, (born[1][g], *laps)
+        )
+        if g == 0:
+            weight, near = rest
     sketch = []
     for g in range(GROUPS):
-        image = wave(
-            "image", g, adjoint[1][g], adjoint[2][g], born[1][g], counts, (adjoint[3][g], *laps)
+        blocks = wave(
+            "image", g, adjoint[1][g], None, None, None, (known[g], me, weight, near)
         )
-        sketch.append(lax.all_to_all(image, "dirs", split_axis=0, concat_axis=0, tiled=True))
+        sketch.append(blocks[0])
+        for s in range(1, owners):
+            ring = [(i, (i + s) % owners) for i in range(owners)]
+            sketch.append(lax.ppermute(blocks[s], "dirs", ring))
 
     total_dirs = owners * sketch_count
     local_rows = rows // owners
-    spread = pl.pallas_call(
+    square = (total_dirs, total_dirs)
+    place = jnp.arange(total_dirs, dtype=jnp.int32)
+    owner = (me[0] - place // sketch_count + owners) % owners
+    local = owner * sketch_count + place % sketch_count
+    selector = (column_order[:, None] == local[None, :]).astype(f32)
+    gram = pl.pallas_call(
         functools.partial(gram_kernel, GROUPS),
-        out_shape=jax.ShapeDtypeStruct((total_dirs, total_dirs, LANE), f32),
+        out_shape=jax.ShapeDtypeStruct(square, f32),
+        scratch_shapes=[pltpu.VMEM((*square, LANE), f32)],
         compiler_params=params(),
         name="gram",
-    )(*[s.reshape(owners, each, layers * local_rows, columns) for s in sketch])
-    gram = add_up(jnp.sum(spread, -1))
-    selector = (column_order[:, None] == jnp.arange(total_dirs, dtype=jnp.int32)[None, :]).astype(
-        f32
-    )
+    )(selector, selector.T, *[s.reshape(each, layers * local_rows, columns) for s in sketch])
+    gram = add_up(gram)
     grid_cells = layers * lax.axis_size("slab") * rows * columns
-    square = (total_dirs, total_dirs)
-    part = (owners, each, 1, local_rows, columns)
+    part = (each, 1, local_rows, columns)
     basis, triangle = pl.pallas_call(
         functools.partial(basis_kernel, GROUPS, math.sqrt(grid_cells)),
         grid=(layers,),
-        in_specs=[whole(square)] * 3
-        + [pl.BlockSpec(part, lambda l: (0, 0, l, 0, 0))] * GROUPS,
+        in_specs=[whole(square)] * 2
+        + [pl.BlockSpec(part, lambda l: (0, l, 0, 0))] * len(sketch),
         out_specs=[
             pl.BlockSpec((total_dirs, 1, local_rows, columns), lambda l: (0, l, 0, 0)),
             whole(square),
@@ -517,7 +569,7 @@
         scratch_shapes=[pltpu.VMEM((total_dirs * total_dirs, 8, LANE), f32)],
         compiler_params=params(),
         name="basis",
-    )(gram, selector, selector.T, *sketch)
+    )(gram, selector, *sketch)
     return basis, triangle
 
 

time: 279 us -> 270 us (0.968)
  blocking collectives: 18.8 us -> 0 us
  waiting for transfers between devices: 45.3 us -> 58.3 us
  local copies, waits for them, and re-layouts: 19.9 us -> 10.5 us
  starting transfers between devices: 131 us -> 139 us
    all_to_all x1 -> x0, blocking collectives: 18.8 us -> none  [shards(): lax.all_to_all(image, 'dirs', split_axis=0, concat_axis=0, tiled=True)]
    ppermute x0 -> x6, starting transfers between devices: none -> 11.9 us  [shards(): sketch.append(lax.ppermute(blocks[s], 'dirs', ring))]
    ppermute x0 -> x6, waiting for transfers between devices: none -> 10.9 us  [shards(): sketch.append(lax.ppermute(blocks[s], 'dirs', ring))]
    unnamed x72 -> x34, local copies, waits for them, and re-layouts: 19.9 us -> 10.5 us
    ppermute x17, waiting for transfers between devices: 14 us -> 23.4 us  [halo(): lax.ppermute(block, 'slab', backward)]
    all_to_all x1 -> x0, starting transfers between devices: 5.31 us -> none  [shards(): lax.all_to_all(image, 'dirs', split_axis=0, concat_axis=0, tiled=True)]
    ppermute x17, waiting for transfers between devices: 6.63 us -> 1.9 us  [halo(): lax.ppermute(block, 'slab', forward)]
  transfers between devices with their start and end apart: 42 -> 47, of which waited for: 20 -> 18; matrix products, arithmetic and copies ran while one was open for 0% -> 0% of each run, Pallas kernels for 16% -> 18%
where the time goes in v2:
time: 270 us; the launch traced here: 268 us
  starting transfers between devices  139 us (51%)
  Pallas kernels  58.7 us (22%)
  waiting for transfers between devices  58.3 us (22%)
  local copies, waits for them, and re-layouts  10.5 us (4%)
    ppermute x17, starting transfers between devices, halo(): lax.ppermute(block, 'slab', forward)  81.7 us
    pallas_call x12, Pallas kernels, wave(): pl.pallas_call(functools.partial(wave_kernel, mode, old is not None), gri...  41.6 us
    ppermute x17, starting transfers between devices, halo(): lax.ppermute(block, 'slab', backward)  38.5 us
    ppermute x17, waiting for transfers between devices, halo(): lax.ppermute(block, 'slab', backward)  23.4 us
    ppermute x7, waiting for transfers between devices, add_up(): lax.ppermute(value, axis, [(i, i ^ stride) for i in range(size)])  22 us
    ppermute x6, starting transfers between devices, shards(): sketch.append(lax.ppermute(blocks[s], 'dirs', ring))  11.9 us
    ppermute x6, waiting for transfers between devices, shards(): sketch.append(lax.ppermute(blocks[s], 'dirs', ring))  10.9 us
    unnamed x34, local copies, waits for them, and re-layouts  10.5 us
  transfers between devices with their start and end apart: 47, of which 18 were waited for; matrix products, arithmetic and copies ran while one was open for 0% of the time, Pallas kernels for 18%

profile of v2, /device:TPU:14, one launch (start us, length us, event | category | flops | bytes accessed | tf_op | source)
XLA Modules:
  0.0 268.5 jit_solution(10315116399899164933)
XLA Ops:
  2.6 3.6 %collective-permute-start.1 = (f32[4,128,256]{2,1,0:T(8,128)}, f32[4,128,256]{2,1,0:T(8,128)S(1)}, u32[]{:S(2)}, u32[]{:S(2)}) collective-permute-start(f32[4,128,256]{2,1,0:T(8,128)} %refs_2_.1), channel_id=1, source_target_pairs={{1,0},{2,1},{3,2},{4,3},{5,4},{6,5},{7,6},{8,7},{9,8},{10,9},{11,1... | collective-permute-start | bytes 1572872 | tf_op jit(solution)/shard_map/ppermute | solution.py:349
  8.1 3.6 %collective-permute-start.3 = (f32[4,128,256]{2,1,0:T(8,128)}, f32[4,128,256]{2,1,0:T(8,128)S(1)}, u32[]{:S(2)}, u32[]{:S(2)}) collective-permute-start(f32[4,128,256]{2,1,0:T(8,128)} %refs_1_.1), channel_id=1, source_target_pairs={{1,0},{2,1},{3,2},{4,3},{5,4},{6,5},{7,6},{8,7},{9,8},{10,9},{11,1... | collective-permute-start | bytes 1572872 | tf_op jit(solution)/shard_map/ppermute | solution.py:349
  22.5 6.4 %collective-permute-start.6 = (f32[4,128,256]{2,1,0:T(8,128)S(1)}, f32[4,128,256]{2,1,0:T(8,128)S(1)}, u32[]{:S(2)}, u32[]{:S(2)}) collective-permute-start(f32[4,128,256]{2,1,0:T(8,128)S(1)} %get-tuple-element.45.refs_1_.refs_10_), channel_id=1, source_target_pairs={{0,1},{1,2},{2,3},{3,4},{4,5},{5,6},{6,7},{7,8},{8,9},{9,10},{10,1... | collective-permute-start | bytes 1572872 | tf_op jit(solution)/shard_map/ppermute | solution.py:349
  39.3 7.3 %collective-permute-start.25 = (f32[2,4,128,256]{3,2,1,0:T(8,128)S(1)}, f32[2,4,128,256]{3,2,1,0:T(8,128)S(1)}, u32[]{:S(2)}, u32[]{:S(2)}) collective-permute-start(f32[2,4,128,256]{3,2,1,0:T(8,128)S(1)} %get-tuple-element.60.refs_1_.refs_3_.refs_12_), channel_id=1, source_target_pairs={{0,1},{1,2},{2,3},{3,4},{4,5},{5,6},{6,7},{7,8},{8,9},{9,10},{10,1... | collective-permute-start | bytes 3145736 | tf_op jit(solution)/shard_map/ppermute | solution.py:349
  57.0 5.1 %collective-permute-start.8 = (f32[2,4,128,256]{3,2,1,0:T(8,128)S(1)}, f32[2,4,128,256]{3,2,1,0:T(8,128)S(1)}, u32[]{:S(2)}, u32[]{:S(2)}) collective-permute-start(f32[2,4,128,256]{3,2,1,0:T(8,128)S(1)} %born.4.refs_1_.refs_3_.refs_10_), channel_id=1, source_target_pairs={{0,1},{1,2},{2,3},{3,4},{4,5},{5,6},{6,7},{7,8},{8,9},{9,10},{10,1... | collective-permute-start | bytes 3145736 | tf_op jit(solution)/shard_map/ppermute | solution.py:349
  71.1 8.8 %collective-permute-start.27 = (f32[2,4,128,256]{3,2,1,0:T(8,128)S(1)}, f32[2,4,128,256]{3,2,1,0:T(8,128)S(1)}, u32[]{:S(2)}, u32[]{:S(2)}) collective-permute-start(f32[2,4,128,256]{3,2,1,0:T(8,128)S(1)} %born.6.refs_1_.refs_3_.refs_10_), channel_id=1, source_target_pairs={{0,1},{1,2},{2,3},{3,4},{4,5},{5,6},{6,7},{7,8},{8,9},{9,10},{10,1... | collective-permute-start | bytes 3145736 | tf_op jit(solution)/shard_map/ppermute | solution.py:349
  87.3 5.3 %collective-permute-start.12 = (f32[2,4,128,256]{3,2,1,0:T(8,128)S(1)}, f32[2,4,128,256]{3,2,1,0:T(8,128)S(1)}, u32[]{:S(2)}, u32[]{:S(2)}) collective-permute-start(f32[2,4,128,256]{3,2,1,0:T(8,128)S(1)} %born.5.refs_1_.refs_9_), channel_id=1, source_target_pairs={{0,1},{1,2},{2,3},{3,4},{4,5},{5,6},{6,7},{7,8},{8,9},{9,10},{10,1... | collective-permute-start | bytes 3145736 | tf_op jit(solution)/shard_map/ppermute | solution.py:349
  97.5 5.5 %collective-permute-start.29 = (f32[2,4,128,256]{3,2,1,0:T(8,128)S(1)}, f32[2,4,128,256]{3,2,1,0:T(8,128)S(1)}, u32[]{:S(2)}, u32[]{:S(2)}) collective-permute-start(f32[2,4,128,256]{3,2,1,0:T(8,128)S(1)} %born.7.refs_1_.refs_9_), channel_id=1, source_target_pairs={{0,1},{1,2},{2,3},{3,4},{4,5},{5,6},{6,7},{7,8},{8,9},{9,10},{10,1... | collective-permute-start | bytes 3145736 | tf_op jit(solution)/shard_map/ppermute | solution.py:349
  106.9 16.7 %collective-permute-done.15.refs_2_ = f32[4,128,256]{2,1,0:T(8,128)S(1)} collective-permute-done((f32[4,128,256]{2,1,0:T(8,128)S(1)}, f32[4,128,256]{2,1,0:T(8,128)S(1)}, u32[]{:S(2)}, u32[]{:S(2)}) %collective-permute-start.15) | collective-permute-done | bytes 524320 | tf_op jit(solution)/shard_map/ppermute | solution.py:349
  128.3 5.9 %collective-permute-start.16 = (f32[2,4,128,256]{3,2,1,0:T(8,128)S(1)}, f32[2,4,128,256]{3,2,1,0:T(8,128)S(1)}, u32[]{:S(2)}, u32[]{:S(2)}) collective-permute-start(f32[2,4,128,256]{3,2,1,0:T(8,128)S(1)} %turn.2.refs_1_.refs_3_), channel_id=1, source_target_pairs={{0,1},{1,2},{2,3},{3,4},{4,5},{5,6},{6,7},{7,8},{8,9},{9,10},{10,1... | collective-permute-start | bytes 3145736 | tf_op jit(solution)/shard_map/ppermute | solution.py:349
  144.9 3.6 %collective-permute-done.17.refs_2_ = f32[2,4,128,256]{3,2,1,0:T(8,128)S(1)} collective-permute-done((f32[2,4,128,256]{3,2,1,0:T(8,128)S(1)}, f32[2,4,128,256]{3,2,1,0:T(8,128)S(1)}, u32[]{:S(2)}, u32[]{:S(2)}) %collective-permute-start.17) | collective-permute-done | bytes 1048608 | tf_op jit(solution)/shard_map/ppermute | solution.py:349
  151.4 5.9 %collective-permute-start.18 = (f32[2,4,128,256]{3,2,1,0:T(8,128)S(1)}, f32[2,4,128,256]{3,2,1,0:T(8,128)S(1)}, u32[]{:S(2)}, u32[]{:S(2)}) collective-permute-start(f32[2,4,128,256]{3,2,1,0:T(8,128)S(1)} %adjoint.2.refs_1_), channel_id=1, source_target_pairs={{0,1},{1,2},{2,3},{3,4},{4,5},{5,6},{6,7},{7,8},{8,9},{9,10},{10,1... | collective-permute-start | bytes 3145736 | tf_op jit(solution)/shard_map/ppermute | solution.py:349
  162.6 5.9 %collective-permute-start.33 = (f32[2,4,128,256]{3,2,1,0:T(8,128)S(1)}, f32[2,4,128,256]{3,2,1,0:T(8,128)S(1)}, u32[]{:S(2)}, u32[]{:S(2)}) collective-permute-start(f32[2,4,128,256]{3,2,1,0:T(8,128)S(1)} %adjoint.3.refs_1_), channel_id=1, source_target_pairs={{0,1},{1,2},{2,3},{3,4},{4,5},{5,6},{6,7},{7,8},{8,9},{9,10},{10,1... | collective-permute-start | bytes 3145736 | tf_op jit(solution)/shard_map/ppermute | solution.py:349
  171.6 4.5 %fold.2 = (f32[2,4,128,256]{3,2,1,0:T(8,128)}, f32[2,4,128,256]{3,2,1,0:T(8,128)S(1)}, f32[4,128,256]{2,1,0:T(8,128)S(1)}, f32[4,128,256]{2,1,0:T(8,128)S(1)}) custom-call(f32[2,4,128,256]{3,2,1,0:T(8,128)S(1)} %collective-permute-done.18.refs_0_, f32[2,4,128,256]{3,2,1,0:T(8,128)S(1)} %adjoint.2.refs_1_, ...), custom_call_target="tpu_custom_call" | custom-call | flops 15728640 | bytes 7340032 | tf_op jit(solution)/shard_map/fold/pallas_call | solution.py:481
  176.1 5.9 %collective-permute-start.20 = (f32[2,4,128,256]{3,2,1,0:T(8,128)}, f32[2,4,128,256]{3,2,1,0:T(8,128)}, u32[]{:S(2)}, u32[]{:S(2)}) collective-permute-start(f32[2,4,128,256]{3,2,1,0:T(8,128)} %get-tuple-element.52.refs_1_), channel_id=1, source_target_pairs={{0,1},{1,2},{2,3},{3,4},{4,5},{5,6},{6,7},{7,8},{8,9},{9,10},{10,1... | collective-permute-start | bytes 3145736 | tf_op jit(solution)/shard_map/ppermute | solution.py:349
  184.0 4.4 %fold.3 = (f32[2,4,128,256]{3,2,1,0:T(8,128)}, f32[2,4,128,256]{3,2,1,0:T(8,128)S(1)}) custom-call(f32[2,4,128,256]{3,2,1,0:T(8,128)S(1)} %collective-permute-done.33.refs_0_, f32[2,4,128,256]{3,2,1,0:T(8,128)S(1)} %adjoint.3.refs_1_, f32[2,4,128,256]{3,2,1,0:T(8,128)S(1)} %collective-permute-done.34.refs_2_, f32[2,4,128,256]{3,2,1,0:T(8,128)S(1)} %turn.3.refs_1_.refs_3_, ...), custom_call_target="tpu_custom_call" | custom-call | flops 15728640 | bytes 7340032 | tf_op jit(solution)/shard_map/fold/pallas_call | solution.py:481
  189.4 4.7 %collective-permute-start.35 = (f32[2,4,128,256]{3,2,1,0:T(8,128)}, f32[2,4,128,256]{3,2,1,0:T(8,128)}, u32[]{:S(2)}, u32[]{:S(2)}) collective-permute-start(f32[2,4,128,256]{3,2,1,0:T(8,128)} %get-tuple-element.62.refs_1_), channel_id=1, source_target_pairs={{0,1},{1,2},{2,3},{3,4},{4,5},{5,6},{6,7},{7,8},{8,9},{9,10},{10,1... | collective-permute-start | bytes 3145736 | tf_op jit(solution)/shard_map/ppermute | solution.py:349
  198.8 4.5 %image.2 = (f32[2,4,32,256]{3,2,1,0:T(8,128)S(1)}, f32[2,4,32,256]{3,2,1,0:T(8,128)S(1)}, f32[2,4,32,256]{3,2,1,0:T(8,128)S(1)}, f32[2,4,32,256]{3,2,1,0:T(8,128)S(1)}) custom-call(f32[2,4,128,256]{3,2,1,0:T(8,128)} %collective-permute-done.20.refs_0_, f32[2,4,128,256]{3,2,1,0:T(8,128)} %get-tuple-element.52.refs_1_, ...), custom_call_target="tpu_custom_call" | custom-call | flops 15728640 | bytes 7340032 | tf_op jit(solution)/shard_map/image/pallas_call | solution.py:481
  209.9 4.4 %image.3 = (f32[2,4,32,256]{3,2,1,0:T(8,128)S(1)}, f32[2,4,32,256]{3,2,1,0:T(8,128)S(1)}, f32[2,4,32,256]{3,2,1,0:T(8,128)S(1)}, f32[2,4,32,256]{3,2,1,0:T(8,128)S(1)}) custom-call(f32[2,4,128,256]{3,2,1,0:T(8,128)} %collective-permute-done.35.refs_0_, f32[2,4,128,256]{3,2,1,0:T(8,128)} %get-tuple-element.62.refs_1_, ...), custom_call_target="tpu_custom_call" | custom-call | flops 15728640 | bytes 7340032 | tf_op jit(solution)/shard_map/image/pallas_call | solution.py:481
  219.7 7.2 %collective-permute-done.37.refs_5_ = f32[2,4,32,256]{3,2,1,0:T(8,128)S(1)} collective-permute-done((f32[2,4,32,256]{3,2,1,0:T(8,128)S(1)}, f32[2,4,32,256]{3,2,1,0:T(8,128)S(1)}, u32[]{:S(2)}, u32[]{:S(2)}) %collective-permute-start.37) | collective-permute-done | bytes 262176 | tf_op jit(solution)/shard_map/ppermute | solution.py:537
  236.5 3.6 %collective-permute-done.41 = f32[16,16]{1,0:T(8,128)S(1)} collective-permute-done((f32[16,16]{1,0:T(8,128)S(1)}, f32[16,16]{1,0:T(8,128)S(1)}, u32[]{:S(2)}, u32[]{:S(2)}) %collective-permute-start.41) | collective-permute-done | bytes 1056 | tf_op jit(solution)/shard_map/ppermute | solution.py:361
  240.2 5.2 %collective-permute-done.42 = f32[16,16]{1,0:T(8,128)S(1)} collective-permute-done((f32[16,16]{1,0:T(8,128)S(1)}, f32[16,16]{1,0:T(8,128)S(1)}, u32[]{:S(2)}, u32[]{:S(2)}) %collective-permute-start.42) | collective-permute-done | bytes 1056 | tf_op jit(solution)/shard_map/ppermute | solution.py:361
  249.7 4.4 %collective-permute-done.44 = f32[16,16]{1,0:T(8,128)S(1)} collective-permute-done((f32[16,16]{1,0:T(8,128)S(1)}, f32[16,16]{1,0:T(8,128)S(1)}, u32[]{:S(2)}, u32[]{:S(2)}) %collective-permute-start.44) | collective-permute-done | bytes 1056 | tf_op jit(solution)/shard_map/ppermute | solution.py:361
  263.0 5.5 %basis.1 = (f32[16,4,32,256]{3,2,1,0:T(8,128)}, f32[16,16]{1,0:T(8,128)}) custom-call(f32[16,16]{1,0:T(8,128)S(1)} %add.68.gram_ref, f32[16,16]{1,0:T(8,128)S(1)} %get-tuple-element.71.sel_ref, f32[2,4,32,256]{3,2,1,0:T(8,128)S(1)} %get-tuple-element.56.refs_0_, f32[2,4,32,256]{3,2,1,0:T(8,128)S(1)} %collective-permute-done.22.refs_1_, ...), custom_call_target="tpu_custom_call" | custom-call | tf_op jit(solution)/shard_map/basis/pallas_call | solution.py:556
  (133 shorter events, 129.1 us)
Async XLA Ops:
  0.6 19.5 %collective-permute-start = (f32[4,128,256]{2,1,0:T(8,128)}, f32[4,128,256]{2,1,0:T(8,128)S(1)}, u32[]{:S(2)}, u32[]{:S(2)}) collective-permute-start(f32[4,128,256]{2,1,0:T(8,128)} %refs_2_.1), channel_id=1, source_target_pairs={{0,1},{1,2},{2,3},{3,4},{4,5},{5,6},{6,7},{7,8},{8,9},{9,10},{10,1... | collective-permute-start | bytes 1572872 | tf_op jit(solution)/shard_map/ppermute | solution.py:349
  2.6 17.6 %collective-permute-start.1 = (f32[4,128,256]{2,1,0:T(8,128)}, f32[4,128,256]{2,1,0:T(8,128)S(1)}, u32[]{:S(2)}, u32[]{:S(2)}) collective-permute-start(f32[4,128,256]{2,1,0:T(8,128)} %refs_2_.1), channel_id=1, source_target_pairs={{1,0},{2,1},{3,2},{4,3},{5,4},{6,5},{7,6},{8,7},{9,8},{10,9},{11,1... | collective-permute-start | bytes 1572872 | tf_op jit(solution)/shard_map/ppermute | solution.py:349
  31.1 20.4 %collective-permute-start.4 = (f32[2,4,128,256]{3,2,1,0:T(8,128)S(1)}, f32[2,4,128,256]{3,2,1,0:T(8,128)S(1)}, u32[]{:S(2)}, u32[]{:S(2)}) collective-permute-start(f32[2,4,128,256]{3,2,1,0:T(8,128)S(1)} %get-tuple-element.69.refs_1_.refs_3_.refs_12_), channel_id=1, source_target_pairs={{0,1},{1,2},{2,3},{3,4},{4,5},{5,6},{6,7},{7,8},{8,9},{9,10},{10,1... | collective-permute-start | bytes 3145736 | tf_op jit(solution)/shard_map/ppermute | solution.py:349
  34.3 19.7 %collective-permute-start.5 = (f32[2,4,128,256]{3,2,1,0:T(8,128)S(1)}, f32[2,4,128,256]{3,2,1,0:T(8,128)S(1)}, u32[]{:S(2)}, u32[]{:S(2)}) collective-permute-start(f32[2,4,128,256]{3,2,1,0:T(8,128)S(1)} %get-tuple-element.69.refs_1_.refs_3_.refs_12_), channel_id=1, source_target_pairs={{1,0},{2,1},{3,2},{4,3},{5,4},{6,5},{7,6},{8,7},{9,8},{10,9},{11,1... | collective-permute-start | bytes 3145736 | tf_op jit(solution)/shard_map/ppermute | solution.py:349
  39.3 28.9 %collective-permute-start.25 = (f32[2,4,128,256]{3,2,1,0:T(8,128)S(1)}, f32[2,4,128,256]{3,2,1,0:T(8,128)S(1)}, u32[]{:S(2)}, u32[]{:S(2)}) collective-permute-start(f32[2,4,128,256]{3,2,1,0:T(8,128)S(1)} %get-tuple-element.60.refs_1_.refs_3_.refs_12_), channel_id=1, source_target_pairs={{0,1},{1,2},{2,3},{3,4},{4,5},{5,6},{6,7},{7,8},{8,9},{9,10},{10,1... | collective-permute-start | bytes 3145736 | tf_op jit(solution)/shard_map/ppermute | solution.py:349
  46.5 21.6 %collective-permute-start.26 = (f32[2,4,128,256]{3,2,1,0:T(8,128)S(1)}, f32[2,4,128,256]{3,2,1,0:T(8,128)S(1)}, u32[]{:S(2)}, u32[]{:S(2)}) collective-permute-start(f32[2,4,128,256]{3,2,1,0:T(8,128)S(1)} %get-tuple-element.60.refs_1_.refs_3_.refs_12_), channel_id=1, source_target_pairs={{1,0},{2,1},{3,2},{4,3},{5,4},{6,5},{7,6},{8,7},{9,8},{10,9},{11,1... | collective-permute-start | bytes 3145736 | tf_op jit(solution)/shard_map/ppermute | solution.py:349
  48.5 15.6 %collective-permute-start.10 = (f32[4,128,256]{2,1,0:T(8,128)S(1)}, f32[4,128,256]{2,1,0:T(8,128)S(1)}, u32[]{:S(2)}, u32[]{:S(2)}) collective-permute-start(f32[4,128,256]{2,1,0:T(8,128)S(1)} %get-tuple-element.48.refs_1_), channel_id=1, source_target_pairs={{0,1},{1,2},{2,3},{3,4},{4,5},{5,6},{6,7},{7,8},{8,9},{9,10},{10,1... | collective-permute-start | bytes 1572872 | tf_op jit(solution)/shard_map/ppermute | solution.py:349
  57.0 27.2 %collective-permute-start.8 = (f32[2,4,128,256]{3,2,1,0:T(8,128)S(1)}, f32[2,4,128,256]{3,2,1,0:T(8,128)S(1)}, u32[]{:S(2)}, u32[]{:S(2)}) collective-permute-start(f32[2,4,128,256]{3,2,1,0:T(8,128)S(1)} %born.4.refs_1_.refs_3_.refs_10_), channel_id=1, source_target_pairs={{0,1},{1,2},{2,3},{3,4},{4,5},{5,6},{6,7},{7,8},{8,9},{9,10},{10,1... | collective-permute-start | bytes 3145736 | tf_op jit(solution)/shard_map/ppermute | solution.py:349
  64.0 20.2 %collective-permute-start.9 = (f32[2,4,128,256]{3,2,1,0:T(8,128)S(1)}, f32[2,4,128,256]{3,2,1,0:T(8,128)S(1)}, u32[]{:S(2)}, u32[]{:S(2)}) collective-permute-start(f32[2,4,128,256]{3,2,1,0:T(8,128)S(1)} %born.4.refs_1_.refs_3_.refs_10_), channel_id=1, source_target_pairs={{1,0},{2,1},{3,2},{4,3},{5,4},{6,5},{7,6},{8,7},{9,8},{10,9},{11,1... | collective-permute-start | bytes 3145736 | tf_op jit(solution)/shard_map/ppermute | solution.py:349
  71.1 23.4 %collective-permute-start.27 = (f32[2,4,128,256]{3,2,1,0:T(8,128)S(1)}, f32[2,4,128,256]{3,2,1,0:T(8,128)S(1)}, u32[]{:S(2)}, u32[]{:S(2)}) collective-permute-start(f32[2,4,128,256]{3,2,1,0:T(8,128)S(1)} %born.6.refs_1_.refs_3_.refs_10_), channel_id=1, source_target_pairs={{0,1},{1,2},{2,3},{3,4},{4,5},{5,6},{6,7},{7,8},{8,9},{9,10},{10,1... | collective-permute-start | bytes 3145736 | tf_op jit(solution)/shard_map/ppermute | solution.py:349
  81.9 23.2 %collective-permute-start.14 = (f32[4,128,256]{2,1,0:T(8,128)S(1)}, f32[4,128,256]{2,1,0:T(8,128)S(1)}, u32[]{:S(2)}, u32[]{:S(2)}) collective-permute-start(f32[4,128,256]{2,1,0:T(8,128)S(1)} %get-tuple-element.50.refs_1_), channel_id=1, source_target_pairs={{0,1},{1,2},{2,3},{3,4},{4,5},{5,6},{6,7},{7,8},{8,9},{9,10},{10,1... | collective-permute-start | bytes 1572872 | tf_op jit(solution)/shard_map/ppermute | solution.py:349
  87.3 38.0 %collective-permute-start.12 = (f32[2,4,128,256]{3,2,1,0:T(8,128)S(1)}, f32[2,4,128,256]{3,2,1,0:T(8,128)S(1)}, u32[]{:S(2)}, u32[]{:S(2)}) collective-permute-start(f32[2,4,128,256]{3,2,1,0:T(8,128)S(1)} %born.5.refs_1_.refs_9_), channel_id=1, source_target_pairs={{0,1},{1,2},{2,3},{3,4},{4,5},{5,6},{6,7},{7,8},{8,9},{9,10},{10,1... | collective-permute-start | bytes 3145736 | tf_op jit(solution)/shard_map/ppermute | solution.py:349
  92.6 32.7 %collective-permute-start.13 = (f32[2,4,128,256]{3,2,1,0:T(8,128)S(1)}, f32[2,4,128,256]{3,2,1,0:T(8,128)S(1)}, u32[]{:S(2)}, u32[]{:S(2)}) collective-permute-start(f32[2,4,128,256]{3,2,1,0:T(8,128)S(1)} %born.5.refs_1_.refs_9_), channel_id=1, source_target_pairs={{1,0},{2,1},{3,2},{4,3},{5,4},{6,5},{7,6},{8,7},{9,8},{10,9},{11,1... | collective-permute-start | bytes 3145736 | tf_op jit(solution)/shard_map/ppermute | solution.py:349
  97.5 38.7 %collective-permute-start.29 = (f32[2,4,128,256]{3,2,1,0:T(8,128)S(1)}, f32[2,4,128,256]{3,2,1,0:T(8,128)S(1)}, u32[]{:S(2)}, u32[]{:S(2)}) collective-permute-start(f32[2,4,128,256]{3,2,1,0:T(8,128)S(1)} %born.7.refs_1_.refs_9_), channel_id=1, source_target_pairs={{0,1},{1,2},{2,3},{3,4},{4,5},{5,6},{6,7},{7,8},{8,9},{9,10},{10,1... | collective-permute-start | bytes 3145736 | tf_op jit(solution)/shard_map/ppermute | solution.py:349
  103.1 33.1 %collective-permute-start.30 = (f32[2,4,128,256]{3,2,1,0:T(8,128)S(1)}, f32[2,4,128,256]{3,2,1,0:T(8,128)S(1)}, u32[]{:S(2)}, u32[]{:S(2)}) collective-permute-start(f32[2,4,128,256]{3,2,1,0:T(8,128)S(1)} %born.7.refs_1_.refs_9_), channel_id=1, source_target_pairs={{1,0},{2,1},{3,2},{4,3},{5,4},{6,5},{7,6},{8,7},{9,8},{10,9},{11,1... | collective-permute-start | bytes 3145736 | tf_op jit(solution)/shard_map/ppermute | solution.py:349
  105.0 18.6 %collective-permute-start.15 = (f32[4,128,256]{2,1,0:T(8,128)S(1)}, f32[4,128,256]{2,1,0:T(8,128)S(1)}, u32[]{:S(2)}, u32[]{:S(2)}) collective-permute-start(f32[4,128,256]{2,1,0:T(8,128)S(1)} %get-tuple-element.50.refs_1_), channel_id=1, source_target_pairs={{1,0},{2,1},{3,2},{4,3},{5,4},{6,5},{7,6},{8,7},{9,8},{10,9},{11,1... | collective-permute-start | bytes 1572872 | tf_op jit(solution)/shard_map/ppermute | solution.py:349
  128.3 16.5 %collective-permute-start.16 = (f32[2,4,128,256]{3,2,1,0:T(8,128)S(1)}, f32[2,4,128,256]{3,2,1,0:T(8,128)S(1)}, u32[]{:S(2)}, u32[]{:S(2)}) collective-permute-start(f32[2,4,128,256]{3,2,1,0:T(8,128)S(1)} %turn.2.refs_1_.refs_3_), channel_id=1, source_target_pairs={{0,1},{1,2},{2,3},{3,4},{4,5},{5,6},{6,7},{7,8},{8,9},{9,10},{10,1... | collective-permute-start | bytes 3145736 | tf_op jit(solution)/shard_map/ppermute | solution.py:349
  139.3 20.2 %collective-permute-start.31 = (f32[2,4,128,256]{3,2,1,0:T(8,128)S(1)}, f32[2,4,128,256]{3,2,1,0:T(8,128)S(1)}, u32[]{:S(2)}, u32[]{:S(2)}) collective-permute-start(f32[2,4,128,256]{3,2,1,0:T(8,128)S(1)} %turn.3.refs_1_.refs_3_), channel_id=1, source_target_pairs={{0,1},{1,2},{2,3},{3,4},{4,5},{5,6},{6,7},{7,8},{8,9},{9,10},{10,1... | collective-permute-start | bytes 3145736 | tf_op jit(solution)/shard_map/ppermute | solution.py:349
  141.7 18.0 %collective-permute-start.32 = (f32[2,4,128,256]{3,2,1,0:T(8,128)S(1)}, f32[2,4,128,256]{3,2,1,0:T(8,128)S(1)}, u32[]{:S(2)}, u32[]{:S(2)}) collective-permute-start(f32[2,4,128,256]{3,2,1,0:T(8,128)S(1)} %turn.3.refs_1_.refs_3_), channel_id=1, source_target_pairs={{1,0},{2,1},{3,2},{4,3},{5,4},{6,5},{7,6},{8,7},{9,8},{10,9},{11,1... | collective-permute-start | bytes 3145736 | tf_op jit(solution)/shard_map/ppermute | solution.py:349
  151.4 19.1 %collective-permute-start.18 = (f32[2,4,128,256]{3,2,1,0:T(8,128)S(1)}, f32[2,4,128,256]{3,2,1,0:T(8,128)S(1)}, u32[]{:S(2)}, u32[]{:S(2)}) collective-permute-start(f32[2,4,128,256]{3,2,1,0:T(8,128)S(1)} %adjoint.2.refs_1_), channel_id=1, source_target_pairs={{0,1},{1,2},{2,3},{3,4},{4,5},{5,6},{6,7},{7,8},{8,9},{9,10},{10,1... | collective-permute-start | bytes 3145736 | tf_op jit(solution)/shard_map/ppermute | solution.py:349
  162.6 21.3 %collective-permute-start.33 = (f32[2,4,128,256]{3,2,1,0:T(8,128)S(1)}, f32[2,4,128,256]{3,2,1,0:T(8,128)S(1)}, u32[]{:S(2)}, u32[]{:S(2)}) collective-permute-start(f32[2,4,128,256]{3,2,1,0:T(8,128)S(1)} %adjoint.3.refs_1_), channel_id=1, source_target_pairs={{0,1},{1,2},{2,3},{3,4},{4,5},{5,6},{6,7},{7,8},{8,9},{9,10},{10,1... | collective-permute-start | bytes 3145736 | tf_op jit(solution)/shard_map/ppermute | solution.py:349
  176.1 20.0 %collective-permute-start.20 = (f32[2,4,128,256]{3,2,1,0:T(8,128)}, f32[2,4,128,256]{3,2,1,0:T(8,128)}, u32[]{:S(2)}, u32[]{:S(2)}) collective-permute-start(f32[2,4,128,256]{3,2,1,0:T(8,128)} %get-tuple-element.52.refs_1_), channel_id=1, source_target_pairs={{0,1},{1,2},{2,3},{3,4},{4,5},{5,6},{6,7},{7,8},{8,9},{9,10},{10,1... | collective-permute-start | bytes 3145736 | tf_op jit(solution)/shard_map/ppermute | solution.py:349
  189.4 20.4 %collective-permute-start.35 = (f32[2,4,128,256]{3,2,1,0:T(8,128)}, f32[2,4,128,256]{3,2,1,0:T(8,128)}, u32[]{:S(2)}, u32[]{:S(2)}) collective-permute-start(f32[2,4,128,256]{3,2,1,0:T(8,128)} %get-tuple-element.62.refs_1_), channel_id=1, source_target_pairs={{0,1},{1,2},{2,3},{3,4},{4,5},{5,6},{6,7},{7,8},{8,9},{9,10},{10,1... | collective-permute-start | bytes 3145736 | tf_op jit(solution)/shard_map/ppermute | solution.py:349
  194.1 15.7 %collective-permute-start.36 = (f32[2,4,128,256]{3,2,1,0:T(8,128)}, f32[2,4,128,256]{3,2,1,0:T(8,128)}, u32[]{:S(2)}, u32[]{:S(2)}) collective-permute-start(f32[2,4,128,256]{3,2,1,0:T(8,128)} %get-tuple-element.62.refs_1_), channel_id=1, source_target_pairs={{1,0},{2,1},{3,2},{4,3},{5,4},{6,5},{7,6},{8,7},{9,8},{10,9},{11,1... | collective-permute-start | bytes 3145736 | tf_op jit(solution)/shard_map/ppermute | solution.py:349
  (40 other events, 323.7 us)

commit v3 on v2

--- a/solution.py
+++ b/solution.py
@@ -506,7 +506,7 @@
         mine = perturbations[g * each : (g + 1) * each]
         born[1][g] = taper * (mine * laps[0])
     born[1][1] = after(born[1][1], fields[2])
-    ahead = {(2, 1): fields[3]}
+    ahead = {(2, 1): fields[3], (3, 1): laps[3]}
     for t in (1, 2):
         for g in range(GROUPS):
             old = born[t - 1][g] if t > 1 else None

time: 270 us -> 258 us (0.956)
  waiting for transfers between devices: 58.3 us -> 41.7 us
  starting transfers between devices: 139 us -> 144 us
    ppermute x17, waiting for transfers between devices: 23.4 us -> 7.14 us  [halo(): lax.ppermute(block, 'slab', backward)]
    ppermute x17, starting transfers between devices: 81.7 us -> 85.9 us  [halo(): lax.ppermute(block, 'slab', forward)]
  transfers between devices with their start and end apart: 47 -> 47, of which waited for: 18 -> 17; matrix products, arithmetic and copies ran while one was open for 0% -> 0% of each run, Pallas kernels for 18% -> 19%
where the time goes in v3:
time: 258 us; the launch traced here: 256 us
  starting transfers between devices  144 us (56%)
  Pallas kernels  58.7 us (23%)
  waiting for transfers between devices  41.7 us (16%)
  local copies, waits for them, and re-layouts  10.5 us (4%)
    ppermute x17, starting transfers between devices, halo(): lax.ppermute(block, 'slab', forward)  85.9 us
    pallas_call x12, Pallas kernels, wave(): pl.pallas_call(functools.partial(wave_kernel, mode, old is not None), gri...  41.6 us
    ppermute x17, starting transfers between devices, halo(): lax.ppermute(block, 'slab', backward)  38.5 us
    ppermute x7, waiting for transfers between devices, add_up(): lax.ppermute(value, axis, [(i, i ^ stride) for i in range(size)])  22 us
    ppermute x6, starting transfers between devices, shards(): sketch.append(lax.ppermute(blocks[s], 'dirs', ring))  12.4 us
    ppermute x6, waiting for transfers between devices, shards(): sketch.append(lax.ppermute(blocks[s], 'dirs', ring))  10.6 us
    unnamed x34, local copies, waits for them, and re-layouts  10.5 us
    pallas_call x4, Pallas kernels, shards(): pl.pallas_call(functools.partial(background_kernel, source_weight(t), fir...  7.41 us
  transfers between devices with their start and end apart: 47, of which 17 were waited for; matrix products, arithmetic and copies ran while one was open for 0% of the time, Pallas kernels for 19%

profile of v3, /device:TPU:14, one launch (start us, length us, event | category | flops | bytes accessed | tf_op | source)
XLA Modules:
  0.0 256.4 jit_solution(3705291639047686796)
XLA Ops:
  2.6 3.6 %collective-permute-start.1 = (f32[4,128,256]{2,1,0:T(8,128)}, f32[4,128,256]{2,1,0:T(8,128)S(1)}, u32[]{:S(2)}, u32[]{:S(2)}) collective-permute-start(f32[4,128,256]{2,1,0:T(8,128)} %refs_2_.1), channel_id=1, source_target_pairs={{1,0},{2,1},{3,2},{4,3},{5,4},{6,5},{7,6},{8,7},{9,8},{10,9},{11,1... | collective-permute-start | bytes 1572872 | tf_op jit(solution)/shard_map/ppermute | solution.py:349
  8.1 3.6 %collective-permute-start.3 = (f32[4,128,256]{2,1,0:T(8,128)}, f32[4,128,256]{2,1,0:T(8,128)S(1)}, u32[]{:S(2)}, u32[]{:S(2)}) collective-permute-start(f32[4,128,256]{2,1,0:T(8,128)} %refs_1_.1), channel_id=1, source_target_pairs={{1,0},{2,1},{3,2},{4,3},{5,4},{6,5},{7,6},{8,7},{9,8},{10,9},{11,1... | collective-permute-start | bytes 1572872 | tf_op jit(solution)/shard_map/ppermute | solution.py:349
  22.5 6.4 %collective-permute-start.6 = (f32[4,128,256]{2,1,0:T(8,128)S(1)}, f32[4,128,256]{2,1,0:T(8,128)S(1)}, u32[]{:S(2)}, u32[]{:S(2)}) collective-permute-start(f32[4,128,256]{2,1,0:T(8,128)S(1)} %get-tuple-element.46.refs_1_.refs_10_), channel_id=1, source_target_pairs={{0,1},{1,2},{2,3},{3,4},{4,5},{5,6},{6,7},{7,8},{8,9},{9,10},{10,1... | collective-permute-start | bytes 1572872 | tf_op jit(solution)/shard_map/ppermute | solution.py:349
  39.3 7.3 %collective-permute-start.25 = (f32[2,4,128,256]{3,2,1,0:T(8,128)S(1)}, f32[2,4,128,256]{3,2,1,0:T(8,128)S(1)}, u32[]{:S(2)}, u32[]{:S(2)}) collective-permute-start(f32[2,4,128,256]{3,2,1,0:T(8,128)S(1)} %get-tuple-element.61.refs_1_.refs_3_.refs_12_), channel_id=1, source_target_pairs={{0,1},{1,2},{2,3},{3,4},{4,5},{5,6},{6,7},{7,8},{8,9},{9,10},{10,1... | collective-permute-start | bytes 3145736 | tf_op jit(solution)/shard_map/ppermute | solution.py:349
  57.0 5.1 %collective-permute-start.8 = (f32[2,4,128,256]{3,2,1,0:T(8,128)S(1)}, f32[2,4,128,256]{3,2,1,0:T(8,128)S(1)}, u32[]{:S(2)}, u32[]{:S(2)}) collective-permute-start(f32[2,4,128,256]{3,2,1,0:T(8,128)S(1)} %born.4.refs_1_.refs_3_.refs_10_), channel_id=1, source_target_pairs={{0,1},{1,2},{2,3},{3,4},{4,5},{5,6},{6,7},{7,8},{8,9},{9,10},{10,1... | collective-permute-start | bytes 3145736 | tf_op jit(solution)/shard_map/ppermute | solution.py:349
  71.1 8.8 %collective-permute-start.27 = (f32[2,4,128,256]{3,2,1,0:T(8,128)S(1)}, f32[2,4,128,256]{3,2,1,0:T(8,128)S(1)}, u32[]{:S(2)}, u32[]{:S(2)}) collective-permute-start(f32[2,4,128,256]{3,2,1,0:T(8,128)S(1)} %born.6.refs_1_.refs_3_.refs_10_), channel_id=1, source_target_pairs={{0,1},{1,2},{2,3},{3,4},{4,5},{5,6},{6,7},{7,8},{8,9},{9,10},{10,1... | collective-permute-start | bytes 3145736 | tf_op jit(solution)/shard_map/ppermute | solution.py:349
  90.5 4.0 %collective-permute-start.12 = (f32[2,4,128,256]{3,2,1,0:T(8,128)S(1)}, f32[2,4,128,256]{3,2,1,0:T(8,128)S(1)}, u32[]{:S(2)}, u32[]{:S(2)}) collective-permute-start(f32[2,4,128,256]{3,2,1,0:T(8,128)S(1)} %born.5.refs_1_.refs_9_), channel_id=1, source_target_pairs={{0,1},{1,2},{2,3},{3,4},{4,5},{5,6},{6,7},{7,8},{8,9},{9,10},{10,1... | collective-permute-start | bytes 3145736 | tf_op jit(solution)/shard_map/ppermute | solution.py:349
  104.4 5.9 %collective-permute-start.29 = (f32[2,4,128,256]{3,2,1,0:T(8,128)S(1)}, f32[2,4,128,256]{3,2,1,0:T(8,128)S(1)}, u32[]{:S(2)}, u32[]{:S(2)}) collective-permute-start(f32[2,4,128,256]{3,2,1,0:T(8,128)S(1)} %born.7.refs_1_.refs_9_), channel_id=1, source_target_pairs={{0,1},{1,2},{2,3},{3,4},{4,5},{5,6},{6,7},{7,8},{8,9},{9,10},{10,1... | collective-permute-start | bytes 3145736 | tf_op jit(solution)/shard_map/ppermute | solution.py:349
  115.4 6.2 %collective-permute-start.16 = (f32[2,4,128,256]{3,2,1,0:T(8,128)S(1)}, f32[2,4,128,256]{3,2,1,0:T(8,128)S(1)}, u32[]{:S(2)}, u32[]{:S(2)}) collective-permute-start(f32[2,4,128,256]{3,2,1,0:T(8,128)S(1)} %turn.2.refs_1_.refs_3_), channel_id=1, source_target_pairs={{0,1},{1,2},{2,3},{3,4},{4,5},{5,6},{6,7},{7,8},{8,9},{9,10},{10,1... | collective-permute-start | bytes 3145736 | tf_op jit(solution)/shard_map/ppermute | solution.py:349
  127.6 6.3 %collective-permute-start.31 = (f32[2,4,128,256]{3,2,1,0:T(8,128)S(1)}, f32[2,4,128,256]{3,2,1,0:T(8,128)S(1)}, u32[]{:S(2)}, u32[]{:S(2)}) collective-permute-start(f32[2,4,128,256]{3,2,1,0:T(8,128)S(1)} %turn.3.refs_1_.refs_3_), channel_id=1, source_target_pairs={{0,1},{1,2},{2,3},{3,4},{4,5},{5,6},{6,7},{7,8},{8,9},{9,10},{10,1... | collective-permute-start | bytes 3145736 | tf_op jit(solution)/shard_map/ppermute | solution.py:349
  138.8 6.2 %collective-permute-start.18 = (f32[2,4,128,256]{3,2,1,0:T(8,128)S(1)}, f32[2,4,128,256]{3,2,1,0:T(8,128)S(1)}, u32[]{:S(2)}, u32[]{:S(2)}) collective-permute-start(f32[2,4,128,256]{3,2,1,0:T(8,128)S(1)} %adjoint.2.refs_1_), channel_id=1, source_target_pairs={{0,1},{1,2},{2,3},{3,4},{4,5},{5,6},{6,7},{7,8},{8,9},{9,10},{10,1... | collective-permute-start | bytes 3145736 | tf_op jit(solution)/shard_map/ppermute | solution.py:349
  151.0 5.9 %collective-permute-start.33 = (f32[2,4,128,256]{3,2,1,0:T(8,128)S(1)}, f32[2,4,128,256]{3,2,1,0:T(8,128)S(1)}, u32[]{:S(2)}, u32[]{:S(2)}) collective-permute-start(f32[2,4,128,256]{3,2,1,0:T(8,128)S(1)} %adjoint.3.refs_1_), channel_id=1, source_target_pairs={{0,1},{1,2},{2,3},{3,4},{4,5},{5,6},{6,7},{7,8},{8,9},{9,10},{10,1... | collective-permute-start | bytes 3145736 | tf_op jit(solution)/shard_map/ppermute | solution.py:349
  159.3 4.5 %fold.2 = (f32[2,4,128,256]{3,2,1,0:T(8,128)}, f32[2,4,128,256]{3,2,1,0:T(8,128)S(1)}, f32[4,128,256]{2,1,0:T(8,128)S(1)}, f32[4,128,256]{2,1,0:T(8,128)S(1)}) custom-call(f32[2,4,128,256]{3,2,1,0:T(8,128)S(1)} %collective-permute-done.18.refs_0_, f32[2,4,128,256]{3,2,1,0:T(8,128)S(1)} %adjoint.2.refs_1_, ...), custom_call_target="tpu_custom_call" | custom-call | flops 15728640 | bytes 7340032 | tf_op jit(solution)/shard_map/fold/pallas_call | solution.py:481
  163.9 5.9 %collective-permute-start.20 = (f32[2,4,128,256]{3,2,1,0:T(8,128)}, f32[2,4,128,256]{3,2,1,0:T(8,128)}, u32[]{:S(2)}, u32[]{:S(2)}) collective-permute-start(f32[2,4,128,256]{3,2,1,0:T(8,128)} %get-tuple-element.53.refs_1_), channel_id=1, source_target_pairs={{0,1},{1,2},{2,3},{3,4},{4,5},{5,6},{6,7},{7,8},{8,9},{9,10},{10,1... | collective-permute-start | bytes 3145736 | tf_op jit(solution)/shard_map/ppermute | solution.py:349
  171.7 4.4 %fold.3 = (f32[2,4,128,256]{3,2,1,0:T(8,128)}, f32[2,4,128,256]{3,2,1,0:T(8,128)S(1)}) custom-call(f32[2,4,128,256]{3,2,1,0:T(8,128)S(1)} %collective-permute-done.33.refs_0_, f32[2,4,128,256]{3,2,1,0:T(8,128)S(1)} %adjoint.3.refs_1_, f32[2,4,128,256]{3,2,1,0:T(8,128)S(1)} %collective-permute-done.34.refs_2_, f32[2,4,128,256]{3,2,1,0:T(8,128)S(1)} %turn.3.refs_1_.refs_3_, ...), custom_call_target="tpu_custom_call" | custom-call | flops 15728640 | bytes 7340032 | tf_op jit(solution)/shard_map/fold/pallas_call | solution.py:481
  177.2 5.3 %collective-permute-start.35 = (f32[2,4,128,256]{3,2,1,0:T(8,128)}, f32[2,4,128,256]{3,2,1,0:T(8,128)}, u32[]{:S(2)}, u32[]{:S(2)}) collective-permute-start(f32[2,4,128,256]{3,2,1,0:T(8,128)} %get-tuple-element.64.refs_1_), channel_id=1, source_target_pairs={{0,1},{1,2},{2,3},{3,4},{4,5},{5,6},{6,7},{7,8},{8,9},{9,10},{10,1... | collective-permute-start | bytes 3145736 | tf_op jit(solution)/shard_map/ppermute | solution.py:349
  186.7 4.5 %image.2 = (f32[2,4,32,256]{3,2,1,0:T(8,128)S(1)}, f32[2,4,32,256]{3,2,1,0:T(8,128)S(1)}, f32[2,4,32,256]{3,2,1,0:T(8,128)S(1)}, f32[2,4,32,256]{3,2,1,0:T(8,128)S(1)}) custom-call(f32[2,4,128,256]{3,2,1,0:T(8,128)} %collective-permute-done.20.refs_0_, f32[2,4,128,256]{3,2,1,0:T(8,128)} %get-tuple-element.53.refs_1_, ...), custom_call_target="tpu_custom_call" | custom-call | flops 15728640 | bytes 7340032 | tf_op jit(solution)/shard_map/image/pallas_call | solution.py:481
  193.2 3.6 %collective-permute-start.23 = (f32[2,4,32,256]{3,2,1,0:T(8,128)S(1)}, f32[2,4,32,256]{3,2,1,0:T(8,128)S(1)}, u32[]{:S(2)}, u32[]{:S(2)}) collective-permute-start(f32[2,4,32,256]{3,2,1,0:T(8,128)S(1)} %get-tuple-element.59), channel_id=1, source_target_pairs={{0,64},{32,96},{64,0},{96,32},{1,65},{33,97},{65,1},{97,33},{2,66}... | collective-permute-start | bytes 786440 | tf_op jit(solution)/shard_map/ppermute | solution.py:537
  197.8 4.4 %image.3 = (f32[2,4,32,256]{3,2,1,0:T(8,128)S(1)}, f32[2,4,32,256]{3,2,1,0:T(8,128)S(1)}, f32[2,4,32,256]{3,2,1,0:T(8,128)S(1)}, f32[2,4,32,256]{3,2,1,0:T(8,128)S(1)}) custom-call(f32[2,4,128,256]{3,2,1,0:T(8,128)} %collective-permute-done.35.refs_0_, f32[2,4,128,256]{3,2,1,0:T(8,128)} %get-tuple-element.64.refs_1_, ...), custom_call_target="tpu_custom_call" | custom-call | flops 15728640 | bytes 7340032 | tf_op jit(solution)/shard_map/image/pallas_call | solution.py:481
  208.1 6.9 %collective-permute-done.37.refs_5_ = f32[2,4,32,256]{3,2,1,0:T(8,128)S(1)} collective-permute-done((f32[2,4,32,256]{3,2,1,0:T(8,128)S(1)}, f32[2,4,32,256]{3,2,1,0:T(8,128)S(1)}, u32[]{:S(2)}, u32[]{:S(2)}) %collective-permute-start.37) | collective-permute-done | bytes 262176 | tf_op jit(solution)/shard_map/ppermute | solution.py:537
  224.5 3.6 %collective-permute-done.41 = f32[16,16]{1,0:T(8,128)S(1)} collective-permute-done((f32[16,16]{1,0:T(8,128)S(1)}, f32[16,16]{1,0:T(8,128)S(1)}, u32[]{:S(2)}, u32[]{:S(2)}) %collective-permute-start.41) | collective-permute-done | bytes 1056 | tf_op jit(solution)/shard_map/ppermute | solution.py:361
  228.1 5.2 %collective-permute-done.42 = f32[16,16]{1,0:T(8,128)S(1)} collective-permute-done((f32[16,16]{1,0:T(8,128)S(1)}, f32[16,16]{1,0:T(8,128)S(1)}, u32[]{:S(2)}, u32[]{:S(2)}) %collective-permute-start.42) | collective-permute-done | bytes 1056 | tf_op jit(solution)/shard_map/ppermute | solution.py:361
  237.6 4.4 %collective-permute-done.44 = f32[16,16]{1,0:T(8,128)S(1)} collective-permute-done((f32[16,16]{1,0:T(8,128)S(1)}, f32[16,16]{1,0:T(8,128)S(1)}, u32[]{:S(2)}, u32[]{:S(2)}) %collective-permute-start.44) | collective-permute-done | bytes 1056 | tf_op jit(solution)/shard_map/ppermute | solution.py:361
  250.9 5.5 %basis.1 = (f32[16,4,32,256]{3,2,1,0:T(8,128)}, f32[16,16]{1,0:T(8,128)}) custom-call(f32[16,16]{1,0:T(8,128)S(1)} %add.68.gram_ref, f32[16,16]{1,0:T(8,128)S(1)} %get-tuple-element.73.sel_ref, f32[2,4,32,256]{3,2,1,0:T(8,128)S(1)} %get-tuple-element.57.refs_0_, f32[2,4,32,256]{3,2,1,0:T(8,128)S(1)} %collective-permute-done.22.refs_1_, ...), custom_call_target="tpu_custom_call" | custom-call | tf_op jit(solution)/shard_map/basis/pallas_call | solution.py:556
  (133 shorter events, 127.4 us)
Async XLA Ops:
  0.6 19.5 %collective-permute-start = (f32[4,128,256]{2,1,0:T(8,128)}, f32[4,128,256]{2,1,0:T(8,128)S(1)}, u32[]{:S(2)}, u32[]{:S(2)}) collective-permute-start(f32[4,128,256]{2,1,0:T(8,128)} %refs_2_.1), channel_id=1, source_target_pairs={{0,1},{1,2},{2,3},{3,4},{4,5},{5,6},{6,7},{7,8},{8,9},{9,10},{10,1... | collective-permute-start | bytes 1572872 | tf_op jit(solution)/shard_map/ppermute | solution.py:349
  2.6 17.6 %collective-permute-start.1 = (f32[4,128,256]{2,1,0:T(8,128)}, f32[4,128,256]{2,1,0:T(8,128)S(1)}, u32[]{:S(2)}, u32[]{:S(2)}) collective-permute-start(f32[4,128,256]{2,1,0:T(8,128)} %refs_2_.1), channel_id=1, source_target_pairs={{1,0},{2,1},{3,2},{4,3},{5,4},{6,5},{7,6},{8,7},{9,8},{10,9},{11,1... | collective-permute-start | bytes 1572872 | tf_op jit(solution)/shard_map/ppermute | solution.py:349
  31.1 20.4 %collective-permute-start.4 = (f32[2,4,128,256]{3,2,1,0:T(8,128)S(1)}, f32[2,4,128,256]{3,2,1,0:T(8,128)S(1)}, u32[]{:S(2)}, u32[]{:S(2)}) collective-permute-start(f32[2,4,128,256]{3,2,1,0:T(8,128)S(1)} %get-tuple-element.71.refs_1_.refs_3_.refs_12_), channel_id=1, source_target_pairs={{0,1},{1,2},{2,3},{3,4},{4,5},{5,6},{6,7},{7,8},{8,9},{9,10},{10,1... | collective-permute-start | bytes 3145736 | tf_op jit(solution)/shard_map/ppermute | solution.py:349
  34.4 19.7 %collective-permute-start.5 = (f32[2,4,128,256]{3,2,1,0:T(8,128)S(1)}, f32[2,4,128,256]{3,2,1,0:T(8,128)S(1)}, u32[]{:S(2)}, u32[]{:S(2)}) collective-permute-start(f32[2,4,128,256]{3,2,1,0:T(8,128)S(1)} %get-tuple-element.71.refs_1_.refs_3_.refs_12_), channel_id=1, source_target_pairs={{1,0},{2,1},{3,2},{4,3},{5,4},{6,5},{7,6},{8,7},{9,8},{10,9},{11,1... | collective-permute-start | bytes 3145736 | tf_op jit(solution)/shard_map/ppermute | solution.py:349
  39.3 28.9 %collective-permute-start.25 = (f32[2,4,128,256]{3,2,1,0:T(8,128)S(1)}, f32[2,4,128,256]{3,2,1,0:T(8,128)S(1)}, u32[]{:S(2)}, u32[]{:S(2)}) collective-permute-start(f32[2,4,128,256]{3,2,1,0:T(8,128)S(1)} %get-tuple-element.61.refs_1_.refs_3_.refs_12_), channel_id=1, source_target_pairs={{0,1},{1,2},{2,3},{3,4},{4,5},{5,6},{6,7},{7,8},{8,9},{9,10},{10,1... | collective-permute-start | bytes 3145736 | tf_op jit(solution)/shard_map/ppermute | solution.py:349
  46.5 21.6 %collective-permute-start.26 = (f32[2,4,128,256]{3,2,1,0:T(8,128)S(1)}, f32[2,4,128,256]{3,2,1,0:T(8,128)S(1)}, u32[]{:S(2)}, u32[]{:S(2)}) collective-permute-start(f32[2,4,128,256]{3,2,1,0:T(8,128)S(1)} %get-tuple-element.61.refs_1_.refs_3_.refs_12_), channel_id=1, source_target_pairs={{1,0},{2,1},{3,2},{4,3},{5,4},{6,5},{7,6},{8,7},{9,8},{10,9},{11,1... | collective-permute-start | bytes 3145736 | tf_op jit(solution)/shard_map/ppermute | solution.py:349
  48.5 15.6 %collective-permute-start.10 = (f32[4,128,256]{2,1,0:T(8,128)S(1)}, f32[4,128,256]{2,1,0:T(8,128)S(1)}, u32[]{:S(2)}, u32[]{:S(2)}) collective-permute-start(f32[4,128,256]{2,1,0:T(8,128)S(1)} %get-tuple-element.49.refs_1_), channel_id=1, source_target_pairs={{0,1},{1,2},{2,3},{3,4},{4,5},{5,6},{6,7},{7,8},{8,9},{9,10},{10,1... | collective-permute-start | bytes 1572872 | tf_op jit(solution)/shard_map/ppermute | solution.py:349
  57.0 27.2 %collective-permute-start.8 = (f32[2,4,128,256]{3,2,1,0:T(8,128)S(1)}, f32[2,4,128,256]{3,2,1,0:T(8,128)S(1)}, u32[]{:S(2)}, u32[]{:S(2)}) collective-permute-start(f32[2,4,128,256]{3,2,1,0:T(8,128)S(1)} %born.4.refs_1_.refs_3_.refs_10_), channel_id=1, source_target_pairs={{0,1},{1,2},{2,3},{3,4},{4,5},{5,6},{6,7},{7,8},{8,9},{9,10},{10,1... | collective-permute-start | bytes 3145736 | tf_op jit(solution)/shard_map/ppermute | solution.py:349
  64.0 23.4 %collective-permute-start.9 = (f32[2,4,128,256]{3,2,1,0:T(8,128)S(1)}, f32[2,4,128,256]{3,2,1,0:T(8,128)S(1)}, u32[]{:S(2)}, u32[]{:S(2)}) collective-permute-start(f32[2,4,128,256]{3,2,1,0:T(8,128)S(1)} %born.4.refs_1_.refs_3_.refs_10_), channel_id=1, source_target_pairs={{1,0},{2,1},{3,2},{4,3},{5,4},{6,5},{7,6},{8,7},{9,8},{10,9},{11,1... | collective-permute-start | bytes 3145736 | tf_op jit(solution)/shard_map/ppermute | solution.py:349
  71.1 30.2 %collective-permute-start.27 = (f32[2,4,128,256]{3,2,1,0:T(8,128)S(1)}, f32[2,4,128,256]{3,2,1,0:T(8,128)S(1)}, u32[]{:S(2)}, u32[]{:S(2)}) collective-permute-start(f32[2,4,128,256]{3,2,1,0:T(8,128)S(1)} %born.6.refs_1_.refs_3_.refs_10_), channel_id=1, source_target_pairs={{0,1},{1,2},{2,3},{3,4},{4,5},{5,6},{6,7},{7,8},{8,9},{9,10},{10,1... | collective-permute-start | bytes 3145736 | tf_op jit(solution)/shard_map/ppermute | solution.py:349
  79.9 21.5 %collective-permute-start.28 = (f32[2,4,128,256]{3,2,1,0:T(8,128)S(1)}, f32[2,4,128,256]{3,2,1,0:T(8,128)S(1)}, u32[]{:S(2)}, u32[]{:S(2)}) collective-permute-start(f32[2,4,128,256]{3,2,1,0:T(8,128)S(1)} %born.6.refs_1_.refs_3_.refs_10_), channel_id=1, source_target_pairs={{1,0},{2,1},{3,2},{4,3},{5,4},{6,5},{7,6},{8,7},{9,8},{10,9},{11,1... | collective-permute-start | bytes 3145736 | tf_op jit(solution)/shard_map/ppermute | solution.py:349
  84.3 15.5 %collective-permute-start.15 = (f32[4,128,256]{2,1,0:T(8,128)S(1)}, f32[4,128,256]{2,1,0:T(8,128)S(1)}, u32[]{:S(2)}, u32[]{:S(2)}) collective-permute-start(f32[4,128,256]{2,1,0:T(8,128)S(1)} %get-tuple-element.51.refs_1_), channel_id=1, source_target_pairs={{1,0},{2,1},{3,2},{4,3},{5,4},{6,5},{7,6},{8,7},{9,8},{10,9},{11,1... | collective-permute-start | bytes 1572872 | tf_op jit(solution)/shard_map/ppermute | solution.py:349
  90.5 21.8 %collective-permute-start.12 = (f32[2,4,128,256]{3,2,1,0:T(8,128)S(1)}, f32[2,4,128,256]{3,2,1,0:T(8,128)S(1)}, u32[]{:S(2)}, u32[]{:S(2)}) collective-permute-start(f32[2,4,128,256]{3,2,1,0:T(8,128)S(1)} %born.5.refs_1_.refs_9_), channel_id=1, source_target_pairs={{0,1},{1,2},{2,3},{3,4},{4,5},{5,6},{6,7},{7,8},{8,9},{9,10},{10,1... | collective-permute-start | bytes 3145736 | tf_op jit(solution)/shard_map/ppermute | solution.py:349
  94.5 17.8 %collective-permute-start.13 = (f32[2,4,128,256]{3,2,1,0:T(8,128)S(1)}, f32[2,4,128,256]{3,2,1,0:T(8,128)S(1)}, u32[]{:S(2)}, u32[]{:S(2)}) collective-permute-start(f32[2,4,128,256]{3,2,1,0:T(8,128)S(1)} %born.5.refs_1_.refs_9_), channel_id=1, source_target_pairs={{1,0},{2,1},{3,2},{4,3},{5,4},{6,5},{7,6},{8,7},{9,8},{10,9},{11,1... | collective-permute-start | bytes 3145736 | tf_op jit(solution)/shard_map/ppermute | solution.py:349
  104.4 19.1 %collective-permute-start.29 = (f32[2,4,128,256]{3,2,1,0:T(8,128)S(1)}, f32[2,4,128,256]{3,2,1,0:T(8,128)S(1)}, u32[]{:S(2)}, u32[]{:S(2)}) collective-permute-start(f32[2,4,128,256]{3,2,1,0:T(8,128)S(1)} %born.7.refs_1_.refs_9_), channel_id=1, source_target_pairs={{0,1},{1,2},{2,3},{3,4},{4,5},{5,6},{6,7},{7,8},{8,9},{9,10},{10,1... | collective-permute-start | bytes 3145736 | tf_op jit(solution)/shard_map/ppermute | solution.py:349
  115.4 20.5 %collective-permute-start.16 = (f32[2,4,128,256]{3,2,1,0:T(8,128)S(1)}, f32[2,4,128,256]{3,2,1,0:T(8,128)S(1)}, u32[]{:S(2)}, u32[]{:S(2)}) collective-permute-start(f32[2,4,128,256]{3,2,1,0:T(8,128)S(1)} %turn.2.refs_1_.refs_3_), channel_id=1, source_target_pairs={{0,1},{1,2},{2,3},{3,4},{4,5},{5,6},{6,7},{7,8},{8,9},{9,10},{10,1... | collective-permute-start | bytes 3145736 | tf_op jit(solution)/shard_map/ppermute | solution.py:349
  127.6 19.5 %collective-permute-start.31 = (f32[2,4,128,256]{3,2,1,0:T(8,128)S(1)}, f32[2,4,128,256]{3,2,1,0:T(8,128)S(1)}, u32[]{:S(2)}, u32[]{:S(2)}) collective-permute-start(f32[2,4,128,256]{3,2,1,0:T(8,128)S(1)} %turn.3.refs_1_.refs_3_), channel_id=1, source_target_pairs={{0,1},{1,2},{2,3},{3,4},{4,5},{5,6},{6,7},{7,8},{8,9},{9,10},{10,1... | collective-permute-start | bytes 3145736 | tf_op jit(solution)/shard_map/ppermute | solution.py:349
  138.8 20.1 %collective-permute-start.18 = (f32[2,4,128,256]{3,2,1,0:T(8,128)S(1)}, f32[2,4,128,256]{3,2,1,0:T(8,128)S(1)}, u32[]{:S(2)}, u32[]{:S(2)}) collective-permute-start(f32[2,4,128,256]{3,2,1,0:T(8,128)S(1)} %adjoint.2.refs_1_), channel_id=1, source_target_pairs={{0,1},{1,2},{2,3},{3,4},{4,5},{5,6},{6,7},{7,8},{8,9},{9,10},{10,1... | collective-permute-start | bytes 3145736 | tf_op jit(solution)/shard_map/ppermute | solution.py:349
  151.0 20.7 %collective-permute-start.33 = (f32[2,4,128,256]{3,2,1,0:T(8,128)S(1)}, f32[2,4,128,256]{3,2,1,0:T(8,128)S(1)}, u32[]{:S(2)}, u32[]{:S(2)}) collective-permute-start(f32[2,4,128,256]{3,2,1,0:T(8,128)S(1)} %adjoint.3.refs_1_), channel_id=1, source_target_pairs={{0,1},{1,2},{2,3},{3,4},{4,5},{5,6},{6,7},{7,8},{8,9},{9,10},{10,1... | collective-permute-start | bytes 3145736 | tf_op jit(solution)/shard_map/ppermute | solution.py:349
  163.9 20.6 %collective-permute-start.20 = (f32[2,4,128,256]{3,2,1,0:T(8,128)}, f32[2,4,128,256]{3,2,1,0:T(8,128)}, u32[]{:S(2)}, u32[]{:S(2)}) collective-permute-start(f32[2,4,128,256]{3,2,1,0:T(8,128)} %get-tuple-element.53.refs_1_), channel_id=1, source_target_pairs={{0,1},{1,2},{2,3},{3,4},{4,5},{5,6},{6,7},{7,8},{8,9},{9,10},{10,1... | collective-permute-start | bytes 3145736 | tf_op jit(solution)/shard_map/ppermute | solution.py:349
  177.2 20.6 %collective-permute-start.35 = (f32[2,4,128,256]{3,2,1,0:T(8,128)}, f32[2,4,128,256]{3,2,1,0:T(8,128)}, u32[]{:S(2)}, u32[]{:S(2)}) collective-permute-start(f32[2,4,128,256]{3,2,1,0:T(8,128)} %get-tuple-element.64.refs_1_), channel_id=1, source_target_pairs={{0,1},{1,2},{2,3},{3,4},{4,5},{5,6},{6,7},{7,8},{8,9},{9,10},{10,1... | collective-permute-start | bytes 3145736 | tf_op jit(solution)/shard_map/ppermute | solution.py:349
  182.5 15.3 %collective-permute-start.36 = (f32[2,4,128,256]{3,2,1,0:T(8,128)}, f32[2,4,128,256]{3,2,1,0:T(8,128)}, u32[]{:S(2)}, u32[]{:S(2)}) collective-permute-start(f32[2,4,128,256]{3,2,1,0:T(8,128)} %get-tuple-element.64.refs_1_), channel_id=1, source_target_pairs={{1,0},{2,1},{3,2},{4,3},{5,4},{6,5},{7,6},{8,7},{9,8},{10,9},{11,1... | collective-permute-start | bytes 3145736 | tf_op jit(solution)/shard_map/ppermute | solution.py:349
  191.2 15.8 %collective-permute-start.22 = (f32[2,4,32,256]{3,2,1,0:T(8,128)S(1)}, f32[2,4,32,256]{3,2,1,0:T(8,128)S(1)}, u32[]{:S(2)}, u32[]{:S(2)}) collective-permute-start(f32[2,4,32,256]{3,2,1,0:T(8,128)S(1)} %get-tuple-element.58), channel_id=1, source_target_pairs={{0,32},{32,64},{64,96},{96,0},{1,33},{33,65},{65,97},{97,1},{2,34}... | collective-permute-start | bytes 786440 | tf_op jit(solution)/shard_map/ppermute | solution.py:537
  193.2 14.9 %collective-permute-start.23 = (f32[2,4,32,256]{3,2,1,0:T(8,128)S(1)}, f32[2,4,32,256]{3,2,1,0:T(8,128)S(1)}, u32[]{:S(2)}, u32[]{:S(2)}) collective-permute-start(f32[2,4,32,256]{3,2,1,0:T(8,128)S(1)} %get-tuple-element.59), channel_id=1, source_target_pairs={{0,64},{32,96},{64,0},{96,32},{1,65},{33,97},{65,1},{97,33},{2,66}... | collective-permute-start | bytes 786440 | tf_op jit(solution)/shard_map/ppermute | solution.py:537
  (40 other events, 320.8 us)

commit v4 on v3

--- a/solution.py
+++ b/solution.py
@@ -123,6 +123,41 @@
     taper_ref[...] = 1.0 - DAMPING * mask_ref[...].astype(jnp.float32)
 
 
+def marks_kernel(cells_ref, line_ref, column_ref):
+    cells = cells_ref[...]
+    columns = column_ref.shape[0]
+    line = lax.broadcasted_iota(jnp.int32, line_ref.shape, 0) == cells // columns
+    column = lax.broadcasted_iota(jnp.int32, column_ref.shape, 0) == cells % columns
+    line_ref[...] = jnp.where(line, 1.0, 0.0).astype(jnp.bfloat16)
+    column_ref[...] = jnp.where(column, 1.0, 0.0)
+
+
+def halves(values):
+    high = values.astype(jnp.bfloat16)
+    return high, (values - high.astype(jnp.float32)).astype(jnp.bfloat16)
+
+
+def read_at(field, line_ref, column_ref):
+    total = None
+    for part in halves(field):
+        lines = lax.dot_general(
+            part, line_ref[...], (((0,), (0,)), ((), ())), preferred_element_type=jnp.float32
+        )
+        total = lines if total is None else total + lines
+    return jnp.sum(total * column_ref[...], axis=0, keepdims=True)
+
+
+def add_at(records, line_ref, column_ref):
+    total = None
+    for part in halves(records):
+        spread = (column_ref[...] * part.astype(jnp.float32)).astype(jnp.bfloat16)
+        field = lax.dot_general(
+            line_ref[...], spread, (((1,), (1,)), ((), ())), preferred_element_type=jnp.float32
+        )
+        total = field if total is None else total + field
+    return total
+
+
 def background_kernel(weight, first, last, *refs):
     refs = list(refs)
     u = [refs.pop(0) for _ in range(3)]
@@ -186,11 +221,20 @@
         sum_ref, me_ref, weight_ref, near_ref = (refs.pop(0) for _ in range(4))
     else:
         taper_ref, add_ref, lap_ref = (refs.pop(0) for _ in range(3))
-    count_ref = refs.pop(0) if mode == "turn" else None
+    if mode == "turn":
+        count_ref, line_ref, column_ref = (refs.pop(0) for _ in range(3))
+    if mode == "spread":
+        marks = [refs.pop(0) for _ in range(4)]
     if mode == "fold":
         first_ref = refs.pop(0)
         laps = [refs.pop(0) for _ in range(4)]
     mx_ref, my_ref = refs.pop(0), refs.pop(0)
+    if mode == "spread":
+        low_ref, high_ref = refs[-2:]
+        refs = refs[:-2]
+        low_ref[...] = add_at(p[0][...], *marks[:2]).reshape(low_ref.shape)
+        high_ref[...] = add_at(p[2][...], *marks[2:]).reshape(high_ref.shape)
+        p = [low_ref, p[1], high_ref]
     y_ref, a_ref = refs[-2:]
     outs = refs[:-2]
 
@@ -227,6 +271,7 @@
             else:
                 new = taper * total + added
             if mode == "turn":
+                a_ref[0, layer, at, columns] = new
                 new = count_ref[spot] * new
             outs[0][spot] = new
             if mode == "fold":
@@ -246,6 +291,8 @@
             tiles(per, columns, functools.partial(body, block), owner * per)
     else:
         tiles(rows, columns, functools.partial(body, 0))
+    if mode == "turn":
+        outs[1][...] = read_at(a_ref[0].reshape(-1, columns), line_ref, column_ref)
 
 
 def piece_of(pieces, parts, c):
@@ -446,12 +493,35 @@
         if first:
             dg = results.pop(0)
 
-    def wave(mode, group, p, old, add, lap, extra=()):
-        low, high = halo(p)
+    def marks(cells):
+        return pl.pallas_call(
+            marks_kernel,
+            out_shape=(
+                matrix(layers * rows, cells.shape[-1]),
+                jax.ShapeDtypeStruct((columns, cells.shape[-1]), f32),
+            ),
+            compiler_params=params(),
+            name="marks",
+        )(cells)
+
+    cells = receiver_cells.reshape(1, -1)
+    at_mine = marks(cells)
+    at_low, at_high = (marks(other) for other in halo(cells))
+    receivers = cells.shape[-1]
+
+    def after(value, earlier):
+        return lax.optimization_barrier((value, earlier))[0]
+
+    def wave(mode, group, p, old, add, lap, extra=(), records=None, wait=None):
+        low, high = halo(p if records is None else records)
+        if wait is not None:
+            low = after(low, wait)
         one = pl.BlockSpec((None, *shape), lambda d: (d, 0, 0, 0))
         shifted = pl.BlockSpec((None, *shape), lambda d: (d + group * each, 0, 0, 0))
         same = whole(shape)
-        operands, specs = [low, p, high], [one] * 3
+        heard = pl.BlockSpec((None, 1, receivers), lambda d: (d, 0, 0))
+        side = one if records is None else heard
+        operands, specs = [low, p, high], [side, one, side]
         if old is not None:
             operands.append(old)
             specs.append(one)
@@ -461,8 +531,11 @@
             operands += [taper, add, lap]
             specs += [same, shifted if mode in ("born", "turn") else one, same]
         if mode == "turn":
-            operands.append(counts)
-            specs.append(same)
+            operands += [counts, *at_mine]
+            specs += [same] + [whole(mark.shape) for mark in at_mine]
+        if mode == "spread":
+            operands += [*at_low, *at_high]
+            specs += [whole(mark.shape) for mark in at_low + at_high]
         if mode == "fold":
             specs += [one] + [same] * 4
         if mode == "image":
@@ -474,6 +547,9 @@
             out_shape, out_spec = out_shape * 2, out_spec * 2
             if group == 0:
                 out_shape, out_spec = out_shape + (field,) * 2, out_spec + [same] * 2
+        elif mode == "turn":
+            out_shape += (jax.ShapeDtypeStruct((each, 1, receivers), f32),)
+            out_spec = out_spec + [heard]
         elif mode == "image":
             split = (layers, rows // owners, columns)
             out_shape = (jax.ShapeDtypeStruct((each, *split), f32),) * owners
@@ -487,7 +563,8 @@
             scratch_shapes=[
                 pltpu.VMEM((2, layers, 2 * rows, columns), jnp.bfloat16),
                 pltpu.VMEM((2, layers, rows, columns), f32),
-            ],
+            ]
+            + [pltpu.VMEM(shape, f32)] * (2 if mode == "spread" else 0),
             compiler_params=params(),
             cost_estimate=pl.CostEstimate(
                 flops=60 * each * cells_here,
@@ -498,15 +575,12 @@
         )(*operands)
         return results[0] if len(results) == 1 else results
 
-    def after(value, earlier):
-        return lax.optimization_barrier((value, earlier))[0]
-
     born = [[None] * GROUPS for _ in range(STEPS + 1)]
     for g in range(GROUPS):
         mine = perturbations[g * each : (g + 1) * each]
         born[1][g] = taper * (mine * laps[0])
     born[1][1] = after(born[1][1], fields[2])
-    ahead = {(2, 1): fields[3], (3, 1): laps[3]}
+    ahead = {(2, 1): fields[3], (3, 1): (laps[3], at_mine, at_low, at_high)}
     for t in (1, 2):
         for g in range(GROUPS):
             old = born[t - 1][g] if t > 1 else None
@@ -516,9 +590,13 @@
             born[t + 1][g] = new
     adjoint = [[None] * GROUPS for _ in range(STEPS + 1)]
     for g in range(GROUPS):
-        adjoint[3][g] = wave("turn", g, born[3][g], born[2][g], perturbations, laps[3])
-    for g in range(GROUPS):
-        adjoint[2][g] = wave("adjoint", g, adjoint[3][g], None, born[3][g], counts)
+        wait = adjoint[2][g - 1] if g else None
+        adjoint[3][g], records = wave(
+            "turn", g, born[3][g], born[2][g], perturbations, laps[3], wait=wait
+        )
+        adjoint[2][g] = wave(
+            "spread", g, adjoint[3][g], None, born[3][g], counts, records=records
+        )
     known = [None] * GROUPS
     for g in range(GROUPS):
         adjoint[1][g], known[g], *rest = wave(

time: 258 us -> 280 us (1.085)
  Pallas kernels: 58.7 us -> 67.7 us
  waiting for transfers between devices: 41.7 us -> 49.8 us
  starting transfers between devices: 144 us -> 148 us
    pallas_call x12, Pallas kernels: 41.6 us -> 49.8 us  [wave(): pl.pallas_call(functools.partial(wave_kernel, mode, old is not None), gri...]
    ppermute x17 -> x18, starting transfers between devices: 38.5 us -> 42.9 us  [halo(): lax.ppermute(block, 'slab', backward)]
    ppermute x17 -> x18, waiting for transfers between devices: 1.9 us -> 5.35 us  [halo(): lax.ppermute(block, 'slab', forward)]
    ppermute x17 -> x18, waiting for transfers between devices: 7.14 us -> 9.84 us  [halo(): lax.ppermute(block, 'slab', backward)]
    ppermute x17 -> x18, starting transfers between devices: 85.9 us -> 87.9 us  [halo(): lax.ppermute(block, 'slab', forward)]
    unnamed x34 -> x36, local copies, waits for them, and re-layouts: 10.5 us -> 11.5 us
  transfers between devices with their start and end apart: 47 -> 49, of which waited for: 17 -> 19; matrix products, arithmetic and copies ran while one was open for 0% -> 0% of each run, Pallas kernels for 19% -> 20%
where the time goes in v4:
time: 280 us; the launch traced here: 279 us
  starting transfers between devices  148 us (53%)
  Pallas kernels  67.7 us (24%)
  waiting for transfers between devices  49.8 us (18%)
  local copies, waits for them, and re-layouts  11.5 us (4%)
    ppermute x18, starting transfers between devices, halo(): lax.ppermute(block, 'slab', forward)  87.9 us
    pallas_call x12, Pallas kernels, wave(): pl.pallas_call(functools.partial(wave_kernel, mode, old is not None), gri...  49.8 us
    ppermute x18, starting transfers between devices, halo(): lax.ppermute(block, 'slab', backward)  42.9 us
    ppermute x7, waiting for transfers between devices, add_up(): lax.ppermute(value, axis, [(i, i ^ stride) for i in range(size)])  22 us
    ppermute x6, waiting for transfers between devices, shards(): sketch.append(lax.ppermute(blocks[s], 'dirs', ring))  12.6 us
    ppermute x6, starting transfers between devices, shards(): sketch.append(lax.ppermute(blocks[s], 'dirs', ring))  11.8 us
    unnamed x36, local copies, waits for them, and re-layouts  11.5 us
    ppermute x18, waiting for transfers between devices, halo(): lax.ppermute(block, 'slab', backward)  9.84 us
  transfers between devices with their start and end apart: 49, of which 19 were waited for; matrix products, arithmetic and copies ran while one was open for 0% of the time, Pallas kernels for 20%

profile of v4, /device:TPU:14, one launch (start us, length us, event | category | flops | bytes accessed | tf_op | source)
XLA Modules:
  0.0 279.0 jit_solution(7686987768945359298)
XLA Ops:
  22.6 6.4 %collective-permute-start.6 = (f32[4,128,256]{2,1,0:T(8,128)S(1)}, f32[4,128,256]{2,1,0:T(8,128)S(1)}, u32[]{:S(2)}, u32[]{:S(2)}) collective-permute-start(f32[4,128,256]{2,1,0:T(8,128)S(1)} %get-tuple-element.57.refs_1_.refs_10_), channel_id=1, source_target_pairs={{0,1},{1,2},{2,3},{3,4},{4,5},{5,6},{6,7},{7,8},{8,9},{9,10},{10,1... | collective-permute-start | bytes 1572872 | tf_op jit(solution)/shard_map/ppermute | solution.py:396
  39.3 7.3 %collective-permute-start.27 = (f32[2,4,128,256]{3,2,1,0:T(8,128)S(1)}, f32[2,4,128,256]{3,2,1,0:T(8,128)S(1)}, u32[]{:S(2)}, u32[]{:S(2)}) collective-permute-start(f32[2,4,128,256]{3,2,1,0:T(8,128)S(1)} %get-tuple-element.80.refs_1_.refs_3_.refs_12_), channel_id=1, source_target_pairs={{0,1},{1,2},{2,3},{3,4},{4,5},{5,6},{6,7},{7,8},{8,9},{9,10},{10,1... | collective-permute-start | bytes 3145736 | tf_op jit(solution)/shard_map/ppermute | solution.py:396
  57.1 5.1 %collective-permute-start.8 = (f32[2,4,128,256]{3,2,1,0:T(8,128)S(1)}, f32[2,4,128,256]{3,2,1,0:T(8,128)S(1)}, u32[]{:S(2)}, u32[]{:S(2)}) collective-permute-start(f32[2,4,128,256]{3,2,1,0:T(8,128)S(1)} %born.4.refs_1_.refs_3_.refs_10_), channel_id=1, source_target_pairs={{0,1},{1,2},{2,3},{3,4},{4,5},{5,6},{6,7},{7,8},{8,9},{9,10},{10,1... | collective-permute-start | bytes 3145736 | tf_op jit(solution)/shard_map/ppermute | solution.py:396
  71.3 8.8 %collective-permute-start.29 = (f32[2,4,128,256]{3,2,1,0:T(8,128)S(1)}, f32[2,4,128,256]{3,2,1,0:T(8,128)S(1)}, u32[]{:S(2)}, u32[]{:S(2)}) collective-permute-start(f32[2,4,128,256]{3,2,1,0:T(8,128)S(1)} %born.6.refs_1_.refs_3_.refs_10_), channel_id=1, source_target_pairs={{0,1},{1,2},{2,3},{3,4},{4,5},{5,6},{6,7},{7,8},{8,9},{9,10},{10,1... | collective-permute-start | bytes 3145736 | tf_op jit(solution)/shard_map/ppermute | solution.py:396
  87.9 5.8 %collective-permute-start.14 = (f32[4,128,256]{2,1,0:T(8,128)S(1)}, f32[4,128,256]{2,1,0:T(8,128)S(1)}, u32[]{:S(2)}, u32[]{:S(2)}) collective-permute-start(f32[4,128,256]{2,1,0:T(8,128)S(1)} %get-tuple-element.62.refs_1_), channel_id=1, source_target_pairs={{0,1},{1,2},{2,3},{3,4},{4,5},{5,6},{6,7},{7,8},{8,9},{9,10},{10,1... | collective-permute-start | bytes 1572872 | tf_op jit(solution)/shard_map/ppermute | solution.py:396
  102.8 10.0 %collective-permute-start.12 = (f32[2,4,128,256]{3,2,1,0:T(8,128)S(1)}, f32[2,4,128,256]{3,2,1,0:T(8,128)S(1)}, u32[]{:S(2)}, u32[]{:S(2)}) collective-permute-start(f32[2,4,128,256]{3,2,1,0:T(8,128)S(1)} %born.5.refs_1_.refs_9_), channel_id=1, source_target_pairs={{0,1},{1,2},{2,3},{3,4},{4,5},{5,6},{6,7},{7,8},{8,9},{9,10},{10,1... | collective-permute-start | bytes 3145736 | tf_op jit(solution)/shard_map/ppermute | solution.py:396
  127.1 4.6 %turn.2 = (f32[2,4,128,256]{3,2,1,0:T(8,128)S(1)}, f32[2,1,1024]{2,1,0:T(1,128)S(1)}) custom-call(f32[2,4,128,256]{3,2,1,0:T(8,128)S(1)} %collective-permute-done.12.refs_0_, f32[2,4,128,256]{3,2,1,0:T(8,128)S(1)} %born.5.refs_1_.refs_9_, f32[2,4,128,256]{3,2,1,0:T(8,128)S(1)} %collective-permute-done.13.refs_2_, ...), custom_call_target="tpu_custom_call" | custom-call | flops 15728640 | bytes 7340032 | tf_op jit(solution)/shard_map/turn/pallas_call | solution.py:557
  131.8 5.9 %collective-permute-start.16 = (f32[2,1,1024]{2,1,0:T(1,128)S(1)}, f32[2,1,1024]{2,1,0:T(1,128)S(1)}, u32[]{:S(2)}, u32[]{:S(2)}) collective-permute-start(f32[2,1,1024]{2,1,0:T(1,128)S(1)} %get-tuple-element.66), channel_id=1, source_target_pairs={{0,1},{1,2},{2,3},{3,4},{4,5},{5,6},{6,7},{7,8},{8,9},{9,10},{10,1... | collective-permute-start | bytes 24584 | tf_op jit(solution)/shard_map/ppermute | solution.py:396
  141.1 5.3 %spread.2.refs_1_ = f32[2,4,128,256]{3,2,1,0:T(8,128)S(1)} custom-call(f32[2,1,1024]{2,1,0:T(1,128)S(1)} %collective-permute-done.16.refs_0_, f32[2,4,128,256]{3,2,1,0:T(8,128)S(1)} %get-tuple-element.67.refs_1_.refs_3_, f32[2,1,1024]{2,1,0:T(1,128)S(1)} %collective-permute-done.17.refs_2_, f32[4,128,256]{2,1,0:T(8,128)S(1)} %collective-permute-done.2.refs_3_.refs_4_, ...), custom_call_target="tpu_custom_call" | custom-call | flops 15728640 | bytes 7340032 | tf_op jit(solution)/shard_map/spread/pallas_call | solution.py:557
  146.4 6.4 %collective-permute-start.20 = (f32[2,4,128,256]{3,2,1,0:T(8,128)S(1)}, f32[2,4,128,256]{3,2,1,0:T(8,128)S(1)}, u32[]{:S(2)}, u32[]{:S(2)}) collective-permute-start(f32[2,4,128,256]{3,2,1,0:T(8,128)S(1)} %spread.2.refs_1_), channel_id=1, source_target_pairs={{0,1},{1,2},{2,3},{3,4},{4,5},{5,6},{6,7},{7,8},{8,9},{9,10},{10,1... | collective-permute-start | bytes 3145736 | tf_op jit(solution)/shard_map/ppermute | solution.py:396
  154.8 4.6 %turn.3 = (f32[2,4,128,256]{3,2,1,0:T(8,128)S(1)}, f32[2,1,1024]{2,1,0:T(1,128)S(1)}) custom-call(f32[2,4,128,256]{3,2,1,0:T(8,128)S(1)} %collective-permute-done.31.refs_0_, f32[2,4,128,256]{3,2,1,0:T(8,128)S(1)} %born.7.refs_1_.refs_9_, f32[2,4,128,256]{3,2,1,0:T(8,128)S(1)} %collective-permute-done.32.refs_2_, ...), custom_call_target="tpu_custom_call" | custom-call | flops 15728640 | bytes 7340032 | tf_op jit(solution)/shard_map/turn/pallas_call | solution.py:557
  167.8 5.3 %spread.3.refs_1_ = f32[2,4,128,256]{3,2,1,0:T(8,128)S(1)} custom-call(f32[2,1,1024]{2,1,0:T(1,128)S(1)} %collective-permute-done.33.refs_0_, f32[2,4,128,256]{3,2,1,0:T(8,128)S(1)} %get-tuple-element.85.refs_1_.refs_3_, f32[2,1,1024]{2,1,0:T(1,128)S(1)} %collective-permute-done.34.refs_2_, f32[4,128,256]{2,1,0:T(8,128)S(1)} %collective-permute-done.2.refs_3_.refs_4_, ...), custom_call_target="tpu_custom_call" | custom-call | flops 15728640 | bytes 7340032 | tf_op jit(solution)/shard_map/spread/pallas_call | solution.py:557
  173.0 6.4 %collective-permute-start.35 = (f32[2,4,128,256]{3,2,1,0:T(8,128)S(1)}, f32[2,4,128,256]{3,2,1,0:T(8,128)S(1)}, u32[]{:S(2)}, u32[]{:S(2)}) collective-permute-start(f32[2,4,128,256]{3,2,1,0:T(8,128)S(1)} %spread.3.refs_1_), channel_id=1, source_target_pairs={{0,1},{1,2},{2,3},{3,4},{4,5},{5,6},{6,7},{7,8},{8,9},{9,10},{10,1... | collective-permute-start | bytes 3145736 | tf_op jit(solution)/shard_map/ppermute | solution.py:396
  181.4 4.6 %fold.2 = (f32[2,4,128,256]{3,2,1,0:T(8,128)}, f32[2,4,128,256]{3,2,1,0:T(8,128)S(1)}, f32[4,128,256]{2,1,0:T(8,128)S(1)}, f32[4,128,256]{2,1,0:T(8,128)S(1)}) custom-call(f32[2,4,128,256]{3,2,1,0:T(8,128)S(1)} %collective-permute-done.20.refs_0_, f32[2,4,128,256]{3,2,1,0:T(8,128)S(1)} %spread.2.refs_1_, ...), custom_call_target="tpu_custom_call" | custom-call | flops 15728640 | bytes 7340032 | tf_op jit(solution)/shard_map/fold/pallas_call | solution.py:557
  193.7 4.4 %fold.3 = (f32[2,4,128,256]{3,2,1,0:T(8,128)}, f32[2,4,128,256]{3,2,1,0:T(8,128)S(1)}) custom-call(f32[2,4,128,256]{3,2,1,0:T(8,128)S(1)} %collective-permute-done.35.refs_0_, f32[2,4,128,256]{3,2,1,0:T(8,128)S(1)} %spread.3.refs_1_, f32[2,4,128,256]{3,2,1,0:T(8,128)S(1)} %collective-permute-done.36.refs_2_, ...), custom_call_target="tpu_custom_call" | custom-call | flops 15728640 | bytes 7340032 | tf_op jit(solution)/shard_map/fold/pallas_call | solution.py:557
  199.2 5.9 %collective-permute-start.37 = (f32[2,4,128,256]{3,2,1,0:T(8,128)}, f32[2,4,128,256]{3,2,1,0:T(8,128)}, u32[]{:S(2)}, u32[]{:S(2)}) collective-permute-start(f32[2,4,128,256]{3,2,1,0:T(8,128)} %get-tuple-element.86.refs_1_), channel_id=1, source_target_pairs={{0,1},{1,2},{2,3},{3,4},{4,5},{5,6},{6,7},{7,8},{8,9},{9,10},{10,1... | collective-permute-start | bytes 3145736 | tf_op jit(solution)/shard_map/ppermute | solution.py:396
  209.3 4.5 %image.2 = (f32[2,4,32,256]{3,2,1,0:T(8,128)S(1)}, f32[2,4,32,256]{3,2,1,0:T(8,128)S(1)}, f32[2,4,32,256]{3,2,1,0:T(8,128)S(1)}, f32[2,4,32,256]{3,2,1,0:T(8,128)S(1)}) custom-call(f32[2,4,128,256]{3,2,1,0:T(8,128)} %collective-permute-done.22.refs_0_, f32[2,4,128,256]{3,2,1,0:T(8,128)} %get-tuple-element.72.refs_1_, ...), custom_call_target="tpu_custom_call" | custom-call | flops 15728640 | bytes 7340032 | tf_op jit(solution)/shard_map/image/pallas_call | solution.py:557
  220.4 4.4 %image.3 = (f32[2,4,32,256]{3,2,1,0:T(8,128)S(1)}, f32[2,4,32,256]{3,2,1,0:T(8,128)S(1)}, f32[2,4,32,256]{3,2,1,0:T(8,128)S(1)}, f32[2,4,32,256]{3,2,1,0:T(8,128)S(1)}) custom-call(f32[2,4,128,256]{3,2,1,0:T(8,128)} %collective-permute-done.37.refs_0_, f32[2,4,128,256]{3,2,1,0:T(8,128)} %get-tuple-element.86.refs_1_, ...), custom_call_target="tpu_custom_call" | custom-call | flops 15728640 | bytes 7340032 | tf_op jit(solution)/shard_map/image/pallas_call | solution.py:557
  230.1 5.6 %collective-permute-done.40.refs_6_ = f32[2,4,32,256]{3,2,1,0:T(8,128)S(1)} collective-permute-done((f32[2,4,32,256]{3,2,1,0:T(8,128)S(1)}, f32[2,4,32,256]{3,2,1,0:T(8,128)S(1)}, u32[]{:S(2)}, u32[]{:S(2)}) %collective-permute-start.40) | collective-permute-done | bytes 262176 | tf_op jit(solution)/shard_map/ppermute | solution.py:615
  235.7 5.3 %collective-permute-done.41.refs_7_ = f32[2,4,32,256]{3,2,1,0:T(8,128)S(1)} collective-permute-done((f32[2,4,32,256]{3,2,1,0:T(8,128)S(1)}, f32[2,4,32,256]{3,2,1,0:T(8,128)S(1)}, u32[]{:S(2)}, u32[]{:S(2)}) %collective-permute-start.41) | collective-permute-done | bytes 262176 | tf_op jit(solution)/shard_map/ppermute | solution.py:615
  247.1 3.6 %collective-permute-done.43 = f32[16,16]{1,0:T(8,128)S(1)} collective-permute-done((f32[16,16]{1,0:T(8,128)S(1)}, f32[16,16]{1,0:T(8,128)S(1)}, u32[]{:S(2)}, u32[]{:S(2)}) %collective-permute-start.43) | collective-permute-done | bytes 1056 | tf_op jit(solution)/shard_map/ppermute | solution.py:408
  250.7 5.2 %collective-permute-done.44 = f32[16,16]{1,0:T(8,128)S(1)} collective-permute-done((f32[16,16]{1,0:T(8,128)S(1)}, f32[16,16]{1,0:T(8,128)S(1)}, u32[]{:S(2)}, u32[]{:S(2)}) %collective-permute-start.44) | collective-permute-done | bytes 1056 | tf_op jit(solution)/shard_map/ppermute | solution.py:408
  260.3 4.4 %collective-permute-done.46 = f32[16,16]{1,0:T(8,128)S(1)} collective-permute-done((f32[16,16]{1,0:T(8,128)S(1)}, f32[16,16]{1,0:T(8,128)S(1)}, u32[]{:S(2)}, u32[]{:S(2)}) %collective-permute-start.46) | collective-permute-done | bytes 1056 | tf_op jit(solution)/shard_map/ppermute | solution.py:408
  273.5 5.5 %basis.1 = (f32[16,4,32,256]{3,2,1,0:T(8,128)}, f32[16,16]{1,0:T(8,128)}) custom-call(f32[16,16]{1,0:T(8,128)S(1)} %add.68.gram_ref, f32[16,16]{1,0:T(8,128)S(1)} %get-tuple-element.95.sel_ref, f32[2,4,32,256]{3,2,1,0:T(8,128)S(1)} %get-tuple-element.76.refs_0_, f32[2,4,32,256]{3,2,1,0:T(8,128)S(1)} %collective-permute-done.24.refs_1_, ...), custom_call_target="tpu_custom_call" | custom-call | tf_op jit(solution)/shard_map/basis/pallas_call | solution.py:634
  (142 shorter events, 142.3 us)
Async XLA Ops:
  0.6 19.5 %collective-permute-start.2 = (f32[4,128,256]{2,1,0:T(8,128)}, f32[4,128,256]{2,1,0:T(8,128)S(1)}, u32[]{:S(2)}, u32[]{:S(2)}) collective-permute-start(f32[4,128,256]{2,1,0:T(8,128)} %refs_1_.1), channel_id=1, source_target_pairs={{0,1},{1,2},{2,3},{3,4},{4,5},{5,6},{6,7},{7,8},{8,9},{9,10},{10,1... | collective-permute-start | bytes 1572872 | tf_op jit(solution)/shard_map/ppermute | solution.py:396
  2.6 17.6 %collective-permute-start.3 = (f32[4,128,256]{2,1,0:T(8,128)}, f32[4,128,256]{2,1,0:T(8,128)S(1)}, u32[]{:S(2)}, u32[]{:S(2)}) collective-permute-start(f32[4,128,256]{2,1,0:T(8,128)} %refs_1_.1), channel_id=1, source_target_pairs={{1,0},{2,1},{3,2},{4,3},{5,4},{6,5},{7,6},{8,7},{9,8},{10,9},{11,1... | collective-permute-start | bytes 1572872 | tf_op jit(solution)/shard_map/ppermute | solution.py:396
  31.1 20.5 %collective-permute-start.4 = (f32[2,4,128,256]{3,2,1,0:T(8,128)S(1)}, f32[2,4,128,256]{3,2,1,0:T(8,128)S(1)}, u32[]{:S(2)}, u32[]{:S(2)}) collective-permute-start(f32[2,4,128,256]{3,2,1,0:T(8,128)S(1)} %get-tuple-element.93.refs_1_.refs_3_.refs_12_), channel_id=1, source_target_pairs={{0,1},{1,2},{2,3},{3,4},{4,5},{5,6},{6,7},{7,8},{8,9},{9,10},{10,1... | collective-permute-start | bytes 3145736 | tf_op jit(solution)/shard_map/ppermute | solution.py:396
  34.4 19.7 %collective-permute-start.5 = (f32[2,4,128,256]{3,2,1,0:T(8,128)S(1)}, f32[2,4,128,256]{3,2,1,0:T(8,128)S(1)}, u32[]{:S(2)}, u32[]{:S(2)}) collective-permute-start(f32[2,4,128,256]{3,2,1,0:T(8,128)S(1)} %get-tuple-element.93.refs_1_.refs_3_.refs_12_), channel_id=1, source_target_pairs={{1,0},{2,1},{3,2},{4,3},{5,4},{6,5},{7,6},{8,7},{9,8},{10,9},{11,1... | collective-permute-start | bytes 3145736 | tf_op jit(solution)/shard_map/ppermute | solution.py:396
  39.3 28.9 %collective-permute-start.27 = (f32[2,4,128,256]{3,2,1,0:T(8,128)S(1)}, f32[2,4,128,256]{3,2,1,0:T(8,128)S(1)}, u32[]{:S(2)}, u32[]{:S(2)}) collective-permute-start(f32[2,4,128,256]{3,2,1,0:T(8,128)S(1)} %get-tuple-element.80.refs_1_.refs_3_.refs_12_), channel_id=1, source_target_pairs={{0,1},{1,2},{2,3},{3,4},{4,5},{5,6},{6,7},{7,8},{8,9},{9,10},{10,1... | collective-permute-start | bytes 3145736 | tf_op jit(solution)/shard_map/ppermute | solution.py:396
  46.6 21.7 %collective-permute-start.28 = (f32[2,4,128,256]{3,2,1,0:T(8,128)S(1)}, f32[2,4,128,256]{3,2,1,0:T(8,128)S(1)}, u32[]{:S(2)}, u32[]{:S(2)}) collective-permute-start(f32[2,4,128,256]{3,2,1,0:T(8,128)S(1)} %get-tuple-element.80.refs_1_.refs_3_.refs_12_), channel_id=1, source_target_pairs={{1,0},{2,1},{3,2},{4,3},{5,4},{6,5},{7,6},{8,7},{9,8},{10,9},{11,1... | collective-permute-start | bytes 3145736 | tf_op jit(solution)/shard_map/ppermute | solution.py:396
  48.5 15.5 %collective-permute-start.10 = (f32[4,128,256]{2,1,0:T(8,128)S(1)}, f32[4,128,256]{2,1,0:T(8,128)S(1)}, u32[]{:S(2)}, u32[]{:S(2)}) collective-permute-start(f32[4,128,256]{2,1,0:T(8,128)S(1)} %get-tuple-element.60.refs_1_), channel_id=1, source_target_pairs={{0,1},{1,2},{2,3},{3,4},{4,5},{5,6},{6,7},{7,8},{8,9},{9,10},{10,1... | collective-permute-start | bytes 1572872 | tf_op jit(solution)/shard_map/ppermute | solution.py:396
  57.1 36.6 %collective-permute-start.8 = (f32[2,4,128,256]{3,2,1,0:T(8,128)S(1)}, f32[2,4,128,256]{3,2,1,0:T(8,128)S(1)}, u32[]{:S(2)}, u32[]{:S(2)}) collective-permute-start(f32[2,4,128,256]{3,2,1,0:T(8,128)S(1)} %born.4.refs_1_.refs_3_.refs_10_), channel_id=1, source_target_pairs={{0,1},{1,2},{2,3},{3,4},{4,5},{5,6},{6,7},{7,8},{8,9},{9,10},{10,1... | collective-permute-start | bytes 3145736 | tf_op jit(solution)/shard_map/ppermute | solution.py:396
  64.1 31.6 %collective-permute-start.9 = (f32[2,4,128,256]{3,2,1,0:T(8,128)S(1)}, f32[2,4,128,256]{3,2,1,0:T(8,128)S(1)}, u32[]{:S(2)}, u32[]{:S(2)}) collective-permute-start(f32[2,4,128,256]{3,2,1,0:T(8,128)S(1)} %born.4.refs_1_.refs_3_.refs_10_), channel_id=1, source_target_pairs={{1,0},{2,1},{3,2},{4,3},{5,4},{6,5},{7,6},{8,7},{9,8},{10,9},{11,1... | collective-permute-start | bytes 3145736 | tf_op jit(solution)/shard_map/ppermute | solution.py:396
  71.3 46.0 %collective-permute-start.29 = (f32[2,4,128,256]{3,2,1,0:T(8,128)S(1)}, f32[2,4,128,256]{3,2,1,0:T(8,128)S(1)}, u32[]{:S(2)}, u32[]{:S(2)}) collective-permute-start(f32[2,4,128,256]{3,2,1,0:T(8,128)S(1)} %born.6.refs_1_.refs_3_.refs_10_), channel_id=1, source_target_pairs={{0,1},{1,2},{2,3},{3,4},{4,5},{5,6},{6,7},{7,8},{8,9},{9,10},{10,1... | collective-permute-start | bytes 3145736 | tf_op jit(solution)/shard_map/ppermute | solution.py:396
  80.1 37.2 %collective-permute-start.30 = (f32[2,4,128,256]{3,2,1,0:T(8,128)S(1)}, f32[2,4,128,256]{3,2,1,0:T(8,128)S(1)}, u32[]{:S(2)}, u32[]{:S(2)}) collective-permute-start(f32[2,4,128,256]{3,2,1,0:T(8,128)S(1)} %born.6.refs_1_.refs_3_.refs_10_), channel_id=1, source_target_pairs={{1,0},{2,1},{3,2},{4,3},{5,4},{6,5},{7,6},{8,7},{9,8},{10,9},{11,1... | collective-permute-start | bytes 3145736 | tf_op jit(solution)/shard_map/ppermute | solution.py:396
  87.9 25.0 %collective-permute-start.14 = (f32[4,128,256]{2,1,0:T(8,128)S(1)}, f32[4,128,256]{2,1,0:T(8,128)S(1)}, u32[]{:S(2)}, u32[]{:S(2)}) collective-permute-start(f32[4,128,256]{2,1,0:T(8,128)S(1)} %get-tuple-element.62.refs_1_), channel_id=1, source_target_pairs={{0,1},{1,2},{2,3},{3,4},{4,5},{5,6},{6,7},{7,8},{8,9},{9,10},{10,1... | collective-permute-start | bytes 1572872 | tf_op jit(solution)/shard_map/ppermute | solution.py:396
  93.8 21.9 %collective-permute-start.15 = (f32[4,128,256]{2,1,0:T(8,128)S(1)}, f32[4,128,256]{2,1,0:T(8,128)S(1)}, u32[]{:S(2)}, u32[]{:S(2)}) collective-permute-start(f32[4,128,256]{2,1,0:T(8,128)S(1)} %get-tuple-element.62.refs_1_), channel_id=1, source_target_pairs={{1,0},{2,1},{3,2},{4,3},{5,4},{6,5},{7,6},{8,7},{9,8},{10,9},{11,1... | collective-permute-start | bytes 1572872 | tf_op jit(solution)/shard_map/ppermute | solution.py:396
  102.8 23.1 %collective-permute-start.12 = (f32[2,4,128,256]{3,2,1,0:T(8,128)S(1)}, f32[2,4,128,256]{3,2,1,0:T(8,128)S(1)}, u32[]{:S(2)}, u32[]{:S(2)}) collective-permute-start(f32[2,4,128,256]{3,2,1,0:T(8,128)S(1)} %born.5.refs_1_.refs_9_), channel_id=1, source_target_pairs={{0,1},{1,2},{2,3},{3,4},{4,5},{5,6},{6,7},{7,8},{8,9},{9,10},{10,1... | collective-permute-start | bytes 3145736 | tf_op jit(solution)/shard_map/ppermute | solution.py:396
  120.4 34.4 %collective-permute-start.31 = (f32[2,4,128,256]{3,2,1,0:T(8,128)S(1)}, f32[2,4,128,256]{3,2,1,0:T(8,128)S(1)}, u32[]{:S(2)}, u32[]{:S(2)}) collective-permute-start(f32[2,4,128,256]{3,2,1,0:T(8,128)S(1)} %born.7.refs_1_.refs_9_), channel_id=1, source_target_pairs={{0,1},{1,2},{2,3},{3,4},{4,5},{5,6},{6,7},{7,8},{8,9},{9,10},{10,1... | collective-permute-start | bytes 3145736 | tf_op jit(solution)/shard_map/ppermute | solution.py:396
  122.8 32.0 %collective-permute-start.32 = (f32[2,4,128,256]{3,2,1,0:T(8,128)S(1)}, f32[2,4,128,256]{3,2,1,0:T(8,128)S(1)}, u32[]{:S(2)}, u32[]{:S(2)}) collective-permute-start(f32[2,4,128,256]{3,2,1,0:T(8,128)S(1)} %born.7.refs_1_.refs_9_), channel_id=1, source_target_pairs={{1,0},{2,1},{3,2},{4,3},{5,4},{6,5},{7,6},{8,7},{9,8},{10,9},{11,1... | collective-permute-start | bytes 3145736 | tf_op jit(solution)/shard_map/ppermute | solution.py:396
  146.4 35.0 %collective-permute-start.20 = (f32[2,4,128,256]{3,2,1,0:T(8,128)S(1)}, f32[2,4,128,256]{3,2,1,0:T(8,128)S(1)}, u32[]{:S(2)}, u32[]{:S(2)}) collective-permute-start(f32[2,4,128,256]{3,2,1,0:T(8,128)S(1)} %spread.2.refs_1_), channel_id=1, source_target_pairs={{0,1},{1,2},{2,3},{3,4},{4,5},{5,6},{6,7},{7,8},{8,9},{9,10},{10,1... | collective-permute-start | bytes 3145736 | tf_op jit(solution)/shard_map/ppermute | solution.py:396
  152.8 28.6 %collective-permute-start.21 = (f32[2,4,128,256]{3,2,1,0:T(8,128)S(1)}, f32[2,4,128,256]{3,2,1,0:T(8,128)S(1)}, u32[]{:S(2)}, u32[]{:S(2)}) collective-permute-start(f32[2,4,128,256]{3,2,1,0:T(8,128)S(1)} %spread.2.refs_1_), channel_id=1, source_target_pairs={{1,0},{2,1},{3,2},{4,3},{5,4},{6,5},{7,6},{8,7},{9,8},{10,9},{11,1... | collective-permute-start | bytes 3145736 | tf_op jit(solution)/shard_map/ppermute | solution.py:396
  173.0 19.5 %collective-permute-start.35 = (f32[2,4,128,256]{3,2,1,0:T(8,128)S(1)}, f32[2,4,128,256]{3,2,1,0:T(8,128)S(1)}, u32[]{:S(2)}, u32[]{:S(2)}) collective-permute-start(f32[2,4,128,256]{3,2,1,0:T(8,128)S(1)} %spread.3.refs_1_), channel_id=1, source_target_pairs={{0,1},{1,2},{2,3},{3,4},{4,5},{5,6},{6,7},{7,8},{8,9},{9,10},{10,1... | collective-permute-start | bytes 3145736 | tf_op jit(solution)/shard_map/ppermute | solution.py:396
  187.0 20.1 %collective-permute-start.22 = (f32[2,4,128,256]{3,2,1,0:T(8,128)}, f32[2,4,128,256]{3,2,1,0:T(8,128)}, u32[]{:S(2)}, u32[]{:S(2)}) collective-permute-start(f32[2,4,128,256]{3,2,1,0:T(8,128)} %get-tuple-element.72.refs_1_), channel_id=1, source_target_pairs={{0,1},{1,2},{2,3},{3,4},{4,5},{5,6},{6,7},{7,8},{8,9},{9,10},{10,1... | collective-permute-start | bytes 3145736 | tf_op jit(solution)/shard_map/ppermute | solution.py:396
  189.4 17.7 %collective-permute-start.23 = (f32[2,4,128,256]{3,2,1,0:T(8,128)}, f32[2,4,128,256]{3,2,1,0:T(8,128)}, u32[]{:S(2)}, u32[]{:S(2)}) collective-permute-start(f32[2,4,128,256]{3,2,1,0:T(8,128)} %get-tuple-element.72.refs_1_), channel_id=1, source_target_pairs={{1,0},{2,1},{3,2},{4,3},{5,4},{6,5},{7,6},{8,7},{9,8},{10,9},{11,1... | collective-permute-start | bytes 3145736 | tf_op jit(solution)/shard_map/ppermute | solution.py:396
  199.2 21.2 %collective-permute-start.37 = (f32[2,4,128,256]{3,2,1,0:T(8,128)}, f32[2,4,128,256]{3,2,1,0:T(8,128)}, u32[]{:S(2)}, u32[]{:S(2)}) collective-permute-start(f32[2,4,128,256]{3,2,1,0:T(8,128)} %get-tuple-element.86.refs_1_), channel_id=1, source_target_pairs={{0,1},{1,2},{2,3},{3,4},{4,5},{5,6},{6,7},{7,8},{8,9},{9,10},{10,1... | collective-permute-start | bytes 3145736 | tf_op jit(solution)/shard_map/ppermute | solution.py:396
  205.1 15.3 %collective-permute-start.38 = (f32[2,4,128,256]{3,2,1,0:T(8,128)}, f32[2,4,128,256]{3,2,1,0:T(8,128)}, u32[]{:S(2)}, u32[]{:S(2)}) collective-permute-start(f32[2,4,128,256]{3,2,1,0:T(8,128)} %get-tuple-element.86.refs_1_), channel_id=1, source_target_pairs={{1,0},{2,1},{3,2},{4,3},{5,4},{6,5},{7,6},{8,7},{9,8},{10,9},{11,1... | collective-permute-start | bytes 3145736 | tf_op jit(solution)/shard_map/ppermute | solution.py:396
  213.8 14.9 %collective-permute-start.24 = (f32[2,4,32,256]{3,2,1,0:T(8,128)S(1)}, f32[2,4,32,256]{3,2,1,0:T(8,128)S(1)}, u32[]{:S(2)}, u32[]{:S(2)}) collective-permute-start(f32[2,4,32,256]{3,2,1,0:T(8,128)S(1)} %get-tuple-element.77), channel_id=1, source_target_pairs={{0,32},{32,64},{64,96},{96,0},{1,33},{33,65},{65,97},{97,1},{2,34}... | collective-permute-start | bytes 786440 | tf_op jit(solution)/shard_map/ppermute | solution.py:615
  (43 other events, 297.6 us)

commit v5 on v3

--- a/solution.py
+++ b/solution.py
@@ -137,7 +137,7 @@
     if not last:
         new_ref = refs.pop(0)
     if first:
-        dg_ref = refs.pop(0)
+        dg_ref, start_ref = refs.pop(0), refs.pop(0)
     y_ref, a_ref = refs
 
     def functions(layer, row, size):
@@ -162,6 +162,8 @@
             times = depth_part(both, layer) + a_ref[1, layer, at, columns]
             lap = HALF * (b_here * plain + times - here * dg)
             lap_ref[layer, at, columns] = lap
+            if first:
+                start_ref[layer, at, columns] = taper_ref[layer, at, columns] * lap
             if not last:
                 new_ref[layer, at, columns] = (
                     taper_ref[layer, at, columns]
@@ -191,6 +193,12 @@
         first_ref = refs.pop(0)
         laps = [refs.pop(0) for _ in range(4)]
     mx_ref, my_ref = refs.pop(0), refs.pop(0)
+    if mode == "start":
+        *refs, low_ref, high_ref = refs
+        starts = [refs.pop(0) for _ in range(3)]
+        for target, source, factor_ref in zip((low_ref, refs[1], high_ref), p, starts):
+            target[...] = source[...] * factor_ref[...]
+        p = [low_ref, refs[1], high_ref]
     y_ref, a_ref = refs[-2:]
     outs = refs[:-2]
 
@@ -222,7 +230,7 @@
                 total = total - old
             taper = taper_ref[spot]
             added = add_ref[spot] * lap_ref[spot]
-            if mode in ("born", "turn"):
+            if mode in ("start", "born", "turn"):
                 new = taper * (total + added)
             else:
                 new = taper * total + added
@@ -385,7 +393,7 @@
     field = jax.ShapeDtypeStruct(shape, f32)
     cells_here = layers * rows * columns
     b_low, b_high = halo(buoyancy)
-    u_low, u_high = halo(background_now)
+    u_low, u_high = u0_low, u0_high = halo(background_now)
 
     def matrix(*size):
         return jax.ShapeDtypeStruct(size, jnp.bfloat16)
@@ -427,7 +435,7 @@
         slots = 3 if first else 2
         results = pl.pallas_call(
             functools.partial(background_kernel, source_weight(t), first, last),
-            out_shape=(field,) * (1 + (not last) + first),
+            out_shape=(field,) * (1 + (not last) + 2 * first),
             scratch_shapes=[
                 pltpu.VMEM((slots, layers, 3 * rows, columns), jnp.bfloat16),
                 pltpu.VMEM((slots, layers, rows, columns), f32),
@@ -444,14 +452,15 @@
             older, current = current, results.pop(0)
             fields.append(current)
         if first:
-            dg = results.pop(0)
-
-    def wave(mode, group, p, old, add, lap, extra=()):
-        low, high = halo(p)
+            dg, start = results
+            start_low, start_high = halo(start)
+
+    def wave(mode, group, p, old, add, lap, extra=(), ends=None):
+        low, high = halo(p) if mode != "start" else ends
         one = pl.BlockSpec((None, *shape), lambda d: (d, 0, 0, 0))
         shifted = pl.BlockSpec((None, *shape), lambda d: (d + group * each, 0, 0, 0))
         same = whole(shape)
-        operands, specs = [low, p, high], [one] * 3
+        operands, specs = [low, p, high], [one, shifted if mode == "start" else one, one]
         if old is not None:
             operands.append(old)
             specs.append(one)
@@ -459,7 +468,7 @@
         specs += [same] * 5
         if mode != "image":
             operands += [taper, add, lap]
-            specs += [same, shifted if mode in ("born", "turn") else one, same]
+            specs += [same, shifted if mode in ("start", "born", "turn") else one, same]
         if mode == "turn":
             operands.append(counts)
             specs.append(same)
@@ -469,12 +478,17 @@
             specs += [one, pl.BlockSpec(memory_space=pltpu.SMEM)] + [same] * 2
         operands += [*extra, mx, my2]
         specs += [whole(mx.shape), whole(my2.shape)]
+        if mode == "start":
+            operands += [start_low, start, start_high]
+            specs += [same] * 3
         out_shape, out_spec = (jax.ShapeDtypeStruct((each, *shape), f32),), [one]
+        if mode == "start":
+            out_shape, out_spec = out_shape * 2, out_spec * 2
         if mode == "fold":
             out_shape, out_spec = out_shape * 2, out_spec * 2
             if group == 0:
                 out_shape, out_spec = out_shape + (field,) * 2, out_spec + [same] * 2
-        elif mode == "image":
+        if mode == "image":
             split = (layers, rows // owners, columns)
             out_shape = (jax.ShapeDtypeStruct((each, *split), f32),) * owners
             out_spec = [pl.BlockSpec((None, *split), lambda d: (d, 0, 0, 0))] * owners
@@ -487,7 +501,8 @@
             scratch_shapes=[
                 pltpu.VMEM((2, layers, 2 * rows, columns), jnp.bfloat16),
                 pltpu.VMEM((2, layers, rows, columns), f32),
-            ],
+            ]
+            + [pltpu.VMEM(shape, f32)] * (2 if mode == "start" else 0),
             compiler_params=params(),
             cost_estimate=pl.CostEstimate(
                 flops=60 * each * cells_here,
@@ -502,15 +517,17 @@
         return lax.optimization_barrier((value, earlier))[0]
 
     born = [[None] * GROUPS for _ in range(STEPS + 1)]
-    for g in range(GROUPS):
-        mine = perturbations[g * each : (g + 1) * each]
-        born[1][g] = taper * (mine * laps[0])
-    born[1][1] = after(born[1][1], fields[2])
+    first_after = [(b_low, b_high, u0_low, u0_high), fields[2]]
     ahead = {(2, 1): fields[3], (3, 1): laps[3]}
     for t in (1, 2):
         for g in range(GROUPS):
-            old = born[t - 1][g] if t > 1 else None
-            new = wave("born", g, born[t][g], old, perturbations, laps[t])
+            if t == 1:
+                mine = after(perturbations[g * each : (g + 1) * each], first_after[g])
+                new, born[1][g] = wave(
+                    "start", g, perturbations, None, perturbations, laps[1], ends=halo(mine)
+                )
+            else:
+                new = wave("born", g, born[t][g], born[t - 1][g], perturbations, laps[t])
             if (t + 1, g) in ahead:
                 new = after(new, ahead[t + 1, g])
             born[t + 1][g] = new

time: 258 us -> 266 us (1.031)
  waiting for transfers between devices: 41.7 us -> 46.5 us
    ppermute x17 -> x18, waiting for transfers between devices: 1.9 us -> 10.2 us  [halo(): lax.ppermute(block, 'slab', forward)]
    ppermute x17 -> x18, waiting for transfers between devices: 7.14 us -> 2.66 us  [halo(): lax.ppermute(block, 'slab', backward)]
    ppermute x17 -> x18, starting transfers between devices: 38.5 us -> 41 us  [halo(): lax.ppermute(block, 'slab', backward)]
    ppermute x17 -> x18, starting transfers between devices: 85.9 us -> 85.9 us  [halo(): lax.ppermute(block, 'slab', forward)]
  transfers between devices with their start and end apart: 47 -> 49, of which waited for: 17 -> 20; matrix products, arithmetic and copies ran while one was open for 0% -> 0% of each run, Pallas kernels for 19% -> 18%
where the time goes in v5:
time: 266 us; the launch traced here: 263 us
  starting transfers between devices  146 us (55%)
  Pallas kernels  59.1 us (22%)
  waiting for transfers between devices  46.5 us (17%)
  local copies, waits for them, and re-layouts  10.7 us (4%)
    ppermute x18, starting transfers between devices, halo(): lax.ppermute(block, 'slab', forward)  85.9 us
    pallas_call x12, Pallas kernels, wave(): pl.pallas_call(functools.partial(wave_kernel, mode, old is not None), gri...  42 us
    ppermute x18, starting transfers between devices, halo(): lax.ppermute(block, 'slab', backward)  41 us
    ppermute x7, waiting for transfers between devices, add_up(): lax.ppermute(value, axis, [(i, i ^ stride) for i in range(size)])  20.9 us
    ppermute x6, waiting for transfers between devices, shards(): sketch.append(lax.ppermute(blocks[s], 'dirs', ring))  12.8 us
    unnamed x34, local copies, waits for them, and re-layouts  10.5 us
    ppermute x6, starting transfers between devices, shards(): sketch.append(lax.ppermute(blocks[s], 'dirs', ring))  10.4 us
    ppermute x18, waiting for transfers between devices, halo(): lax.ppermute(block, 'slab', forward)  10.2 us
  transfers between devices with their start and end apart: 49, of which 20 were waited for; matrix products, arithmetic and copies ran while one was open for 0% of the time, Pallas kernels for 18%

profile of v5, /device:TPU:14, one launch (start us, length us, event | category | flops | bytes accessed | tf_op | source)
XLA Modules:
  0.0 263.3 jit_solution(5252100345423150097)
XLA Ops:
  2.6 3.6 %collective-permute-start.3 = (f32[4,128,256]{2,1,0:T(8,128)}, f32[4,128,256]{2,1,0:T(8,128)S(1)}, u32[]{:S(2)}, u32[]{:S(2)}) collective-permute-start(f32[4,128,256]{2,1,0:T(8,128)} %refs_2_.1), channel_id=1, source_target_pairs={{1,0},{2,1},{3,2},{4,3},{5,4},{6,5},{7,6},{8,7},{9,8},{10,9},{11,1... | collective-permute-start | bytes 1572872 | tf_op jit(solution)/shard_map/ppermute | solution.py:357
  8.1 3.6 %collective-permute-start.1 = (f32[4,128,256]{2,1,0:T(8,128)}, f32[4,128,256]{2,1,0:T(8,128)S(1)}, u32[]{:S(2)}, u32[]{:S(2)}) collective-permute-start(f32[4,128,256]{2,1,0:T(8,128)} %refs_1_.3), channel_id=1, source_target_pairs={{1,0},{2,1},{3,2},{4,3},{5,4},{6,5},{7,6},{8,7},{9,8},{10,9},{11,1... | collective-permute-start | bytes 1572872 | tf_op jit(solution)/shard_map/ppermute | solution.py:357
  24.9 6.0 %collective-permute-start.6 = (f32[4,128,256]{2,1,0:T(8,128)S(1)}, f32[4,128,256]{2,1,0:T(8,128)S(1)}, u32[]{:S(2)}, u32[]{:S(2)}) collective-permute-start(f32[4,128,256]{2,1,0:T(8,128)S(1)} %get-tuple-element.52.refs_1_.refs_10_), channel_id=1, source_target_pairs={{0,1},{1,2},{2,3},{3,4},{4,5},{5,6},{6,7},{7,8},{8,9},{9,10},{10,1... | collective-permute-start | bytes 1572872 | tf_op jit(solution)/shard_map/ppermute | solution.py:357
  33.0 5.8 %collective-permute-start.4 = (f32[2,4,128,256]{3,2,1,0:T(8,128)S(1)}, f32[2,4,128,256]{3,2,1,0:T(8,128)S(1)}, u32[]{:S(2)}, u32[]{:S(2)}) collective-permute-start(f32[2,4,128,256]{3,2,1,0:T(8,128)S(1)} %get-tuple-element.42), channel_id=1, source_target_pairs={{0,1},{1,2},{2,3},{3,4},{4,5},{5,6},{6,7},{7,8},{8,9},{9,10},{10,1... | collective-permute-start | bytes 3145736 | tf_op jit(solution)/shard_map/ppermute | solution.py:357
  40.7 5.8 %collective-permute-start.8 = (f32[4,128,256]{2,1,0:T(8,128)S(1)}, f32[4,128,256]{2,1,0:T(8,128)S(1)}, u32[]{:S(2)}, u32[]{:S(2)}) collective-permute-start(f32[4,128,256]{2,1,0:T(8,128)S(1)} %get-tuple-element.55.refs_14_), channel_id=1, source_target_pairs={{0,1},{1,2},{2,3},{3,4},{4,5},{5,6},{6,7},{7,8},{8,9},{9,10},{10,1... | collective-permute-start | bytes 1572872 | tf_op jit(solution)/shard_map/ppermute | solution.py:357
  50.9 9.7 %collective-permute-start.27 = (f32[2,4,128,256]{3,2,1,0:T(8,128)S(1)}, f32[2,4,128,256]{3,2,1,0:T(8,128)S(1)}, u32[]{:S(2)}, u32[]{:S(2)}) collective-permute-start(f32[2,4,128,256]{3,2,1,0:T(8,128)S(1)} %get-tuple-element.71), channel_id=1, source_target_pairs={{0,1},{1,2},{2,3},{3,4},{4,5},{5,6},{6,7},{7,8},{8,9},{9,10},{10,1... | collective-permute-start | bytes 3145736 | tf_op jit(solution)/shard_map/ppermute | solution.py:357
  71.4 6.4 %collective-permute-start.10 = (f32[2,4,128,256]{3,2,1,0:T(8,128)S(1)}, f32[2,4,128,256]{3,2,1,0:T(8,128)S(1)}, u32[]{:S(2)}, u32[]{:S(2)}) collective-permute-start(f32[2,4,128,256]{3,2,1,0:T(8,128)S(1)} %get-tuple-element.56.refs_1_.refs_3_.refs_10_), channel_id=1, source_target_pairs={{0,1},{1,2},{2,3},{3,4},{4,5},{5,6},{6,7},{7,8},{8,9},{9,10},{10,1... | collective-permute-start | bytes 3145736 | tf_op jit(solution)/shard_map/ppermute | solution.py:357
  90.3 5.5 %collective-permute-start.16 = (f32[4,128,256]{2,1,0:T(8,128)S(1)}, f32[4,128,256]{2,1,0:T(8,128)S(1)}, u32[]{:S(2)}, u32[]{:S(2)}) collective-permute-start(f32[4,128,256]{2,1,0:T(8,128)S(1)} %get-tuple-element.60.refs_1_), channel_id=1, source_target_pairs={{0,1},{1,2},{2,3},{3,4},{4,5},{5,6},{6,7},{7,8},{8,9},{9,10},{10,1... | collective-permute-start | bytes 1572872 | tf_op jit(solution)/shard_map/ppermute | solution.py:357
  102.6 7.3 %collective-permute-start.14 = (f32[2,4,128,256]{3,2,1,0:T(8,128)S(1)}, f32[2,4,128,256]{3,2,1,0:T(8,128)S(1)}, u32[]{:S(2)}, u32[]{:S(2)}) collective-permute-start(f32[2,4,128,256]{3,2,1,0:T(8,128)S(1)} %born.2.refs_1_.refs_9_), channel_id=1, source_target_pairs={{0,1},{1,2},{2,3},{3,4},{4,5},{5,6},{6,7},{7,8},{8,9},{9,10},{10,1... | collective-permute-start | bytes 3145736 | tf_op jit(solution)/shard_map/ppermute | solution.py:357
  125.2 4.4 %collective-permute-start.18 = (f32[2,4,128,256]{3,2,1,0:T(8,128)S(1)}, f32[2,4,128,256]{3,2,1,0:T(8,128)S(1)}, u32[]{:S(2)}, u32[]{:S(2)}) collective-permute-start(f32[2,4,128,256]{3,2,1,0:T(8,128)S(1)} %turn.2.refs_1_.refs_3_), channel_id=1, source_target_pairs={{0,1},{1,2},{2,3},{3,4},{4,5},{5,6},{6,7},{7,8},{8,9},{9,10},{10,1... | collective-permute-start | bytes 3145736 | tf_op jit(solution)/shard_map/ppermute | solution.py:357
  137.6 3.8 %collective-permute-start.33 = (f32[2,4,128,256]{3,2,1,0:T(8,128)S(1)}, f32[2,4,128,256]{3,2,1,0:T(8,128)S(1)}, u32[]{:S(2)}, u32[]{:S(2)}) collective-permute-start(f32[2,4,128,256]{3,2,1,0:T(8,128)S(1)} %turn.3.refs_1_.refs_3_), channel_id=1, source_target_pairs={{0,1},{1,2},{2,3},{3,4},{4,5},{5,6},{6,7},{7,8},{8,9},{9,10},{10,1... | collective-permute-start | bytes 3145736 | tf_op jit(solution)/shard_map/ppermute | solution.py:357
  148.7 4.1 %collective-permute-start.20 = (f32[2,4,128,256]{3,2,1,0:T(8,128)S(1)}, f32[2,4,128,256]{3,2,1,0:T(8,128)S(1)}, u32[]{:S(2)}, u32[]{:S(2)}) collective-permute-start(f32[2,4,128,256]{3,2,1,0:T(8,128)S(1)} %adjoint.2.refs_1_), channel_id=1, source_target_pairs={{0,1},{1,2},{2,3},{3,4},{4,5},{5,6},{6,7},{7,8},{8,9},{9,10},{10,1... | collective-permute-start | bytes 3145736 | tf_op jit(solution)/shard_map/ppermute | solution.py:357
  160.0 4.4 %collective-permute-start.35 = (f32[2,4,128,256]{3,2,1,0:T(8,128)S(1)}, f32[2,4,128,256]{3,2,1,0:T(8,128)S(1)}, u32[]{:S(2)}, u32[]{:S(2)}) collective-permute-start(f32[2,4,128,256]{3,2,1,0:T(8,128)S(1)} %adjoint.3.refs_1_), channel_id=1, source_target_pairs={{0,1},{1,2},{2,3},{3,4},{4,5},{5,6},{6,7},{7,8},{8,9},{9,10},{10,1... | collective-permute-start | bytes 3145736 | tf_op jit(solution)/shard_map/ppermute | solution.py:357
  166.4 4.5 %fold.2 = (f32[2,4,128,256]{3,2,1,0:T(8,128)}, f32[2,4,128,256]{3,2,1,0:T(8,128)S(1)}, f32[4,128,256]{2,1,0:T(8,128)S(1)}, f32[4,128,256]{2,1,0:T(8,128)S(1)}) custom-call(f32[2,4,128,256]{3,2,1,0:T(8,128)S(1)} %collective-permute-done.20.refs_0_, f32[2,4,128,256]{3,2,1,0:T(8,128)S(1)} %adjoint.2.refs_1_, ...), custom_call_target="tpu_custom_call" | custom-call | flops 15728640 | bytes 7340032 | tf_op jit(solution)/shard_map/fold/pallas_call | solution.py:495
  172.8 4.6 %collective-permute-start.22 = (f32[2,4,128,256]{3,2,1,0:T(8,128)}, f32[2,4,128,256]{3,2,1,0:T(8,128)}, u32[]{:S(2)}, u32[]{:S(2)}) collective-permute-start(f32[2,4,128,256]{3,2,1,0:T(8,128)} %get-tuple-element.63.refs_1_), channel_id=1, source_target_pairs={{0,1},{1,2},{2,3},{3,4},{4,5},{5,6},{6,7},{7,8},{8,9},{9,10},{10,1... | collective-permute-start | bytes 3145736 | tf_op jit(solution)/shard_map/ppermute | solution.py:357
  177.6 4.4 %fold.3 = (f32[2,4,128,256]{3,2,1,0:T(8,128)}, f32[2,4,128,256]{3,2,1,0:T(8,128)S(1)}) custom-call(f32[2,4,128,256]{3,2,1,0:T(8,128)S(1)} %collective-permute-done.35.refs_0_, f32[2,4,128,256]{3,2,1,0:T(8,128)S(1)} %adjoint.3.refs_1_, f32[2,4,128,256]{3,2,1,0:T(8,128)S(1)} %collective-permute-done.36.refs_2_, f32[2,4,128,256]{3,2,1,0:T(8,128)S(1)} %turn.3.refs_1_.refs_3_, ...), custom_call_target="tpu_custom_call" | custom-call | flops 15728640 | bytes 7340032 | tf_op jit(solution)/shard_map/fold/pallas_call | solution.py:495
  185.0 6.2 %collective-permute-start.37 = (f32[2,4,128,256]{3,2,1,0:T(8,128)}, f32[2,4,128,256]{3,2,1,0:T(8,128)}, u32[]{:S(2)}, u32[]{:S(2)}) collective-permute-start(f32[2,4,128,256]{3,2,1,0:T(8,128)} %get-tuple-element.76.refs_1_), channel_id=1, source_target_pairs={{0,1},{1,2},{2,3},{3,4},{4,5},{5,6},{6,7},{7,8},{8,9},{9,10},{10,1... | collective-permute-start | bytes 3145736 | tf_op jit(solution)/shard_map/ppermute | solution.py:357
  193.4 4.5 %image.2 = (f32[2,4,32,256]{3,2,1,0:T(8,128)S(1)}, f32[2,4,32,256]{3,2,1,0:T(8,128)S(1)}, f32[2,4,32,256]{3,2,1,0:T(8,128)S(1)}, f32[2,4,32,256]{3,2,1,0:T(8,128)S(1)}) custom-call(f32[2,4,128,256]{3,2,1,0:T(8,128)} %collective-permute-done.22.refs_0_, f32[2,4,128,256]{3,2,1,0:T(8,128)} %get-tuple-element.63.refs_1_, ...), custom_call_target="tpu_custom_call" | custom-call | flops 15728640 | bytes 7340032 | tf_op jit(solution)/shard_map/image/pallas_call | solution.py:495
  199.8 3.6 %collective-permute-start.25 = (f32[2,4,32,256]{3,2,1,0:T(8,128)S(1)}, f32[2,4,32,256]{3,2,1,0:T(8,128)S(1)}, u32[]{:S(2)}, u32[]{:S(2)}) collective-permute-start(f32[2,4,32,256]{3,2,1,0:T(8,128)S(1)} %get-tuple-element.69), channel_id=1, source_target_pairs={{0,64},{32,96},{64,0},{96,32},{1,65},{33,97},{65,1},{97,33},{2,66}... | collective-permute-start | bytes 786440 | tf_op jit(solution)/shard_map/ppermute | solution.py:554
  204.5 4.4 %image.3 = (f32[2,4,32,256]{3,2,1,0:T(8,128)S(1)}, f32[2,4,32,256]{3,2,1,0:T(8,128)S(1)}, f32[2,4,32,256]{3,2,1,0:T(8,128)S(1)}, f32[2,4,32,256]{3,2,1,0:T(8,128)S(1)}) custom-call(f32[2,4,128,256]{3,2,1,0:T(8,128)} %collective-permute-done.37.refs_0_, f32[2,4,128,256]{3,2,1,0:T(8,128)} %get-tuple-element.76.refs_1_, ...), custom_call_target="tpu_custom_call" | custom-call | flops 15728640 | bytes 7340032 | tf_op jit(solution)/shard_map/image/pallas_call | solution.py:495
  213.8 8.6 %collective-permute-done.39.refs_5_ = f32[2,4,32,256]{3,2,1,0:T(8,128)S(1)} collective-permute-done((f32[2,4,32,256]{3,2,1,0:T(8,128)S(1)}, f32[2,4,32,256]{3,2,1,0:T(8,128)S(1)}, u32[]{:S(2)}, u32[]{:S(2)}) %collective-permute-start.39) | collective-permute-done | bytes 262176 | tf_op jit(solution)/shard_map/ppermute | solution.py:554
  231.3 3.6 %collective-permute-done.43 = f32[16,16]{1,0:T(8,128)S(1)} collective-permute-done((f32[16,16]{1,0:T(8,128)S(1)}, f32[16,16]{1,0:T(8,128)S(1)}, u32[]{:S(2)}, u32[]{:S(2)}) %collective-permute-start.43) | collective-permute-done | bytes 1056 | tf_op jit(solution)/shard_map/ppermute | solution.py:369
  244.5 4.4 %collective-permute-done.46 = f32[16,16]{1,0:T(8,128)S(1)} collective-permute-done((f32[16,16]{1,0:T(8,128)S(1)}, f32[16,16]{1,0:T(8,128)S(1)}, u32[]{:S(2)}, u32[]{:S(2)}) %collective-permute-start.46) | collective-permute-done | bytes 1056 | tf_op jit(solution)/shard_map/ppermute | solution.py:369
  257.8 5.5 %basis.1 = (f32[16,4,32,256]{3,2,1,0:T(8,128)}, f32[16,16]{1,0:T(8,128)}) custom-call(f32[16,16]{1,0:T(8,128)S(1)} %add.68.gram_ref, f32[16,16]{1,0:T(8,128)S(1)} %get-tuple-element.85.sel_ref, f32[2,4,32,256]{3,2,1,0:T(8,128)S(1)} %get-tuple-element.67.refs_0_, f32[2,4,32,256]{3,2,1,0:T(8,128)S(1)} %collective-permute-done.24.refs_1_, ...), custom_call_target="tpu_custom_call" | custom-call | tf_op jit(solution)/shard_map/basis/pallas_call | solution.py:573
  (137 shorter events, 137.2 us)
Async XLA Ops:
  0.6 19.5 %collective-permute-start.2 = (f32[4,128,256]{2,1,0:T(8,128)}, f32[4,128,256]{2,1,0:T(8,128)S(1)}, u32[]{:S(2)}, u32[]{:S(2)}) collective-permute-start(f32[4,128,256]{2,1,0:T(8,128)} %refs_2_.1), channel_id=1, source_target_pairs={{0,1},{1,2},{2,3},{3,4},{4,5},{5,6},{6,7},{7,8},{8,9},{9,10},{10,1... | collective-permute-start | bytes 1572872 | tf_op jit(solution)/shard_map/ppermute | solution.py:357
  2.6 17.6 %collective-permute-start.3 = (f32[4,128,256]{2,1,0:T(8,128)}, f32[4,128,256]{2,1,0:T(8,128)S(1)}, u32[]{:S(2)}, u32[]{:S(2)}) collective-permute-start(f32[4,128,256]{2,1,0:T(8,128)} %refs_2_.1), channel_id=1, source_target_pairs={{1,0},{2,1},{3,2},{4,3},{5,4},{6,5},{7,6},{8,7},{9,8},{10,9},{11,1... | collective-permute-start | bytes 1572872 | tf_op jit(solution)/shard_map/ppermute | solution.py:357
  22.5 18.1 %collective-permute-start.7 = (f32[4,128,256]{2,1,0:T(8,128)S(1)}, f32[4,128,256]{2,1,0:T(8,128)S(1)}, u32[]{:S(2)}, u32[]{:S(2)}) collective-permute-start(f32[4,128,256]{2,1,0:T(8,128)S(1)} %get-tuple-element.52.refs_1_.refs_10_), channel_id=1, source_target_pairs={{1,0},{2,1},{3,2},{4,3},{5,4},{6,5},{7,6},{8,7},{9,8},{10,9},{11,1... | collective-permute-start | bytes 1572872 | tf_op jit(solution)/shard_map/ppermute | solution.py:357
  24.9 21.6 %collective-permute-start.6 = (f32[4,128,256]{2,1,0:T(8,128)S(1)}, f32[4,128,256]{2,1,0:T(8,128)S(1)}, u32[]{:S(2)}, u32[]{:S(2)}) collective-permute-start(f32[4,128,256]{2,1,0:T(8,128)S(1)} %get-tuple-element.52.refs_1_.refs_10_), channel_id=1, source_target_pairs={{0,1},{1,2},{2,3},{3,4},{4,5},{5,6},{6,7},{7,8},{8,9},{9,10},{10,1... | collective-permute-start | bytes 1572872 | tf_op jit(solution)/shard_map/ppermute | solution.py:357
  31.1 31.5 %collective-permute-start.5 = (f32[2,4,128,256]{3,2,1,0:T(8,128)S(1)}, f32[2,4,128,256]{3,2,1,0:T(8,128)S(1)}, u32[]{:S(2)}, u32[]{:S(2)}) collective-permute-start(f32[2,4,128,256]{3,2,1,0:T(8,128)S(1)} %get-tuple-element.42), channel_id=1, source_target_pairs={{1,0},{2,1},{3,2},{4,3},{5,4},{6,5},{7,6},{8,7},{9,8},{10,9},{11,1... | collective-permute-start | bytes 3145736 | tf_op jit(solution)/shard_map/ppermute | solution.py:357
  33.0 32.0 %collective-permute-start.4 = (f32[2,4,128,256]{3,2,1,0:T(8,128)S(1)}, f32[2,4,128,256]{3,2,1,0:T(8,128)S(1)}, u32[]{:S(2)}, u32[]{:S(2)}) collective-permute-start(f32[2,4,128,256]{3,2,1,0:T(8,128)S(1)} %get-tuple-element.42), channel_id=1, source_target_pairs={{0,1},{1,2},{2,3},{3,4},{4,5},{5,6},{6,7},{7,8},{8,9},{9,10},{10,1... | collective-permute-start | bytes 3145736 | tf_op jit(solution)/shard_map/ppermute | solution.py:357
  40.7 20.0 %collective-permute-start.8 = (f32[4,128,256]{2,1,0:T(8,128)S(1)}, f32[4,128,256]{2,1,0:T(8,128)S(1)}, u32[]{:S(2)}, u32[]{:S(2)}) collective-permute-start(f32[4,128,256]{2,1,0:T(8,128)S(1)} %get-tuple-element.55.refs_14_), channel_id=1, source_target_pairs={{0,1},{1,2},{2,3},{3,4},{4,5},{5,6},{6,7},{7,8},{8,9},{9,10},{10,1... | collective-permute-start | bytes 1572872 | tf_op jit(solution)/shard_map/ppermute | solution.py:357
  48.2 31.4 %collective-permute-start.28 = (f32[2,4,128,256]{3,2,1,0:T(8,128)S(1)}, f32[2,4,128,256]{3,2,1,0:T(8,128)S(1)}, u32[]{:S(2)}, u32[]{:S(2)}) collective-permute-start(f32[2,4,128,256]{3,2,1,0:T(8,128)S(1)} %get-tuple-element.71), channel_id=1, source_target_pairs={{1,0},{2,1},{3,2},{4,3},{5,4},{6,5},{7,6},{8,7},{9,8},{10,9},{11,1... | collective-permute-start | bytes 3145736 | tf_op jit(solution)/shard_map/ppermute | solution.py:357
  50.9 28.7 %collective-permute-start.27 = (f32[2,4,128,256]{3,2,1,0:T(8,128)S(1)}, f32[2,4,128,256]{3,2,1,0:T(8,128)S(1)}, u32[]{:S(2)}, u32[]{:S(2)}) collective-permute-start(f32[2,4,128,256]{3,2,1,0:T(8,128)S(1)} %get-tuple-element.71), channel_id=1, source_target_pairs={{0,1},{1,2},{2,3},{3,4},{4,5},{5,6},{6,7},{7,8},{8,9},{9,10},{10,1... | collective-permute-start | bytes 3145736 | tf_op jit(solution)/shard_map/ppermute | solution.py:357
  68.2 22.1 %collective-permute-start.11 = (f32[2,4,128,256]{3,2,1,0:T(8,128)S(1)}, f32[2,4,128,256]{3,2,1,0:T(8,128)S(1)}, u32[]{:S(2)}, u32[]{:S(2)}) collective-permute-start(f32[2,4,128,256]{3,2,1,0:T(8,128)S(1)} %get-tuple-element.56.refs_1_.refs_3_.refs_10_), channel_id=1, source_target_pairs={{1,0},{2,1},{3,2},{4,3},{5,4},{6,5},{7,6},{8,7},{9,8},{10,9},{11,1... | collective-permute-start | bytes 3145736 | tf_op jit(solution)/shard_map/ppermute | solution.py:357
  71.4 24.4 %collective-permute-start.10 = (f32[2,4,128,256]{3,2,1,0:T(8,128)S(1)}, f32[2,4,128,256]{3,2,1,0:T(8,128)S(1)}, u32[]{:S(2)}, u32[]{:S(2)}) collective-permute-start(f32[2,4,128,256]{3,2,1,0:T(8,128)S(1)} %get-tuple-element.56.refs_1_.refs_3_.refs_10_), channel_id=1, source_target_pairs={{0,1},{1,2},{2,3},{3,4},{4,5},{5,6},{6,7},{7,8},{8,9},{9,10},{10,1... | collective-permute-start | bytes 3145736 | tf_op jit(solution)/shard_map/ppermute | solution.py:357
  82.8 28.8 %collective-permute-start.30 = (f32[2,4,128,256]{3,2,1,0:T(8,128)S(1)}, f32[2,4,128,256]{3,2,1,0:T(8,128)S(1)}, u32[]{:S(2)}, u32[]{:S(2)}) collective-permute-start(f32[2,4,128,256]{3,2,1,0:T(8,128)S(1)} %get-tuple-element.73.refs_1_.refs_3_.refs_10_), channel_id=1, source_target_pairs={{1,0},{2,1},{3,2},{4,3},{5,4},{6,5},{7,6},{8,7},{9,8},{10,9},{11,1... | collective-permute-start | bytes 3145736 | tf_op jit(solution)/shard_map/ppermute | solution.py:357
  84.7 26.9 %collective-permute-start.29 = (f32[2,4,128,256]{3,2,1,0:T(8,128)S(1)}, f32[2,4,128,256]{3,2,1,0:T(8,128)S(1)}, u32[]{:S(2)}, u32[]{:S(2)}) collective-permute-start(f32[2,4,128,256]{3,2,1,0:T(8,128)S(1)} %get-tuple-element.73.refs_1_.refs_3_.refs_10_), channel_id=1, source_target_pairs={{0,1},{1,2},{2,3},{3,4},{4,5},{5,6},{6,7},{7,8},{8,9},{9,10},{10,1... | collective-permute-start | bytes 3145736 | tf_op jit(solution)/shard_map/ppermute | solution.py:357
  90.3 19.7 %collective-permute-start.16 = (f32[4,128,256]{2,1,0:T(8,128)S(1)}, f32[4,128,256]{2,1,0:T(8,128)S(1)}, u32[]{:S(2)}, u32[]{:S(2)}) collective-permute-start(f32[4,128,256]{2,1,0:T(8,128)S(1)} %get-tuple-element.60.refs_1_), channel_id=1, source_target_pairs={{0,1},{1,2},{2,3},{3,4},{4,5},{5,6},{6,7},{7,8},{8,9},{9,10},{10,1... | collective-permute-start | bytes 1572872 | tf_op jit(solution)/shard_map/ppermute | solution.py:357
  98.8 20.2 %collective-permute-start.15 = (f32[2,4,128,256]{3,2,1,0:T(8,128)S(1)}, f32[2,4,128,256]{3,2,1,0:T(8,128)S(1)}, u32[]{:S(2)}, u32[]{:S(2)}) collective-permute-start(f32[2,4,128,256]{3,2,1,0:T(8,128)S(1)} %born.2.refs_1_.refs_9_), channel_id=1, source_target_pairs={{1,0},{2,1},{3,2},{4,3},{5,4},{6,5},{7,6},{8,7},{9,8},{10,9},{11,1... | collective-permute-start | bytes 3145736 | tf_op jit(solution)/shard_map/ppermute | solution.py:357
  122.2 19.3 %collective-permute-start.19 = (f32[2,4,128,256]{3,2,1,0:T(8,128)S(1)}, f32[2,4,128,256]{3,2,1,0:T(8,128)S(1)}, u32[]{:S(2)}, u32[]{:S(2)}) collective-permute-start(f32[2,4,128,256]{3,2,1,0:T(8,128)S(1)} %turn.2.refs_1_.refs_3_), channel_id=1, source_target_pairs={{1,0},{2,1},{3,2},{4,3},{5,4},{6,5},{7,6},{8,7},{9,8},{10,9},{11,1... | collective-permute-start | bytes 3145736 | tf_op jit(solution)/shard_map/ppermute | solution.py:357
  125.2 18.7 %collective-permute-start.18 = (f32[2,4,128,256]{3,2,1,0:T(8,128)S(1)}, f32[2,4,128,256]{3,2,1,0:T(8,128)S(1)}, u32[]{:S(2)}, u32[]{:S(2)}) collective-permute-start(f32[2,4,128,256]{3,2,1,0:T(8,128)S(1)} %turn.2.refs_1_.refs_3_), channel_id=1, source_target_pairs={{0,1},{1,2},{2,3},{3,4},{4,5},{5,6},{6,7},{7,8},{8,9},{9,10},{10,1... | collective-permute-start | bytes 3145736 | tf_op jit(solution)/shard_map/ppermute | solution.py:357
  148.7 17.6 %collective-permute-start.20 = (f32[2,4,128,256]{3,2,1,0:T(8,128)S(1)}, f32[2,4,128,256]{3,2,1,0:T(8,128)S(1)}, u32[]{:S(2)}, u32[]{:S(2)}) collective-permute-start(f32[2,4,128,256]{3,2,1,0:T(8,128)S(1)} %adjoint.2.refs_1_), channel_id=1, source_target_pairs={{0,1},{1,2},{2,3},{3,4},{4,5},{5,6},{6,7},{7,8},{8,9},{9,10},{10,1... | collective-permute-start | bytes 3145736 | tf_op jit(solution)/shard_map/ppermute | solution.py:357
  158.1 19.3 %collective-permute-start.36 = (f32[2,4,128,256]{3,2,1,0:T(8,128)S(1)}, f32[2,4,128,256]{3,2,1,0:T(8,128)S(1)}, u32[]{:S(2)}, u32[]{:S(2)}) collective-permute-start(f32[2,4,128,256]{3,2,1,0:T(8,128)S(1)} %adjoint.3.refs_1_), channel_id=1, source_target_pairs={{1,0},{2,1},{3,2},{4,3},{5,4},{6,5},{7,6},{8,7},{9,8},{10,9},{11,1... | collective-permute-start | bytes 3145736 | tf_op jit(solution)/shard_map/ppermute | solution.py:357
  160.0 17.6 %collective-permute-start.35 = (f32[2,4,128,256]{3,2,1,0:T(8,128)S(1)}, f32[2,4,128,256]{3,2,1,0:T(8,128)S(1)}, u32[]{:S(2)}, u32[]{:S(2)}) collective-permute-start(f32[2,4,128,256]{3,2,1,0:T(8,128)S(1)} %adjoint.3.refs_1_), channel_id=1, source_target_pairs={{0,1},{1,2},{2,3},{3,4},{4,5},{5,6},{6,7},{7,8},{8,9},{9,10},{10,1... | collective-permute-start | bytes 3145736 | tf_op jit(solution)/shard_map/ppermute | solution.py:357
  170.9 20.2 %collective-permute-start.23 = (f32[2,4,128,256]{3,2,1,0:T(8,128)}, f32[2,4,128,256]{3,2,1,0:T(8,128)}, u32[]{:S(2)}, u32[]{:S(2)}) collective-permute-start(f32[2,4,128,256]{3,2,1,0:T(8,128)} %get-tuple-element.63.refs_1_), channel_id=1, source_target_pairs={{1,0},{2,1},{3,2},{4,3},{5,4},{6,5},{7,6},{8,7},{9,8},{10,9},{11,1... | collective-permute-start | bytes 3145736 | tf_op jit(solution)/shard_map/ppermute | solution.py:357
  172.8 18.3 %collective-permute-start.22 = (f32[2,4,128,256]{3,2,1,0:T(8,128)}, f32[2,4,128,256]{3,2,1,0:T(8,128)}, u32[]{:S(2)}, u32[]{:S(2)}) collective-permute-start(f32[2,4,128,256]{3,2,1,0:T(8,128)} %get-tuple-element.63.refs_1_), channel_id=1, source_target_pairs={{0,1},{1,2},{2,3},{3,4},{4,5},{5,6},{6,7},{7,8},{8,9},{9,10},{10,1... | collective-permute-start | bytes 3145736 | tf_op jit(solution)/shard_map/ppermute | solution.py:357
  183.0 21.4 %collective-permute-start.38 = (f32[2,4,128,256]{3,2,1,0:T(8,128)}, f32[2,4,128,256]{3,2,1,0:T(8,128)}, u32[]{:S(2)}, u32[]{:S(2)}) collective-permute-start(f32[2,4,128,256]{3,2,1,0:T(8,128)} %get-tuple-element.76.refs_1_), channel_id=1, source_target_pairs={{1,0},{2,1},{3,2},{4,3},{5,4},{6,5},{7,6},{8,7},{9,8},{10,9},{11,1... | collective-permute-start | bytes 3145736 | tf_op jit(solution)/shard_map/ppermute | solution.py:357
  185.0 19.5 %collective-permute-start.37 = (f32[2,4,128,256]{3,2,1,0:T(8,128)}, f32[2,4,128,256]{3,2,1,0:T(8,128)}, u32[]{:S(2)}, u32[]{:S(2)}) collective-permute-start(f32[2,4,128,256]{3,2,1,0:T(8,128)} %get-tuple-element.76.refs_1_), channel_id=1, source_target_pairs={{0,1},{1,2},{2,3},{3,4},{4,5},{5,6},{6,7},{7,8},{8,9},{9,10},{10,1... | collective-permute-start | bytes 3145736 | tf_op jit(solution)/shard_map/ppermute | solution.py:357
  (42 other events, 361.1 us)

commit v6 on v5

--- a/solution.py
+++ b/solution.py
@@ -134,10 +134,11 @@
         taper_ref, src_ref, older_ref = (refs.pop(0) for _ in range(3))
     mx_ref, my_ref = refs.pop(0), refs.pop(0)
     lap_ref = refs.pop(0)
-    if not last:
+    if first:
+        pair_ref, dg_ref = refs.pop(0), refs.pop(0)
+        new_ref, start_ref = pair_ref.at[0], pair_ref.at[1]
+    elif not last:
         new_ref = refs.pop(0)
-    if first:
-        dg_ref, start_ref = refs.pop(0), refs.pop(0)
     y_ref, a_ref = refs
 
     def functions(layer, row, size):
@@ -392,8 +393,15 @@
     f32 = jnp.float32
     field = jax.ShapeDtypeStruct(shape, f32)
     cells_here = layers * rows * columns
-    b_low, b_high = halo(buoyancy)
-    u_low, u_high = u0_low, u0_high = halo(background_now)
+    def after(value, earlier):
+        return lax.optimization_barrier((value, earlier))[0]
+
+    def view(array, index):
+        return array, pl.BlockSpec((None, *shape), lambda *_: (index, 0, 0, 0))
+
+    low, high = halo(jnp.stack([buoyancy, background_now]))
+    b_low, u_low = view(low, 0), view(low, 1)
+    b_high, u_high = view(high, 0), view(high, 1)
 
     def matrix(*size):
         return jax.ShapeDtypeStruct(size, jnp.bfloat16)
@@ -418,24 +426,35 @@
         *copied,
     )
 
-    buoy = (b_low, b_mid, b_high)
-    fields = [current]
+    def flat(array):
+        return array, whole(array.shape)
+
+    ends = halo(after(perturbations, counts))
+    buoy = (b_low, flat(b_mid), b_high)
+    current, older = flat(current), flat(older)
+    fields = [None]
     laps = []
     dg = None
     for t in range(STEPS):
         first, last = t == 0, t == STEPS - 1
+        if t > 1:
+            u_low, u_high = (flat(end) for end in halo(current[0]))
+        operands = [u_low, current, u_high, *buoy, flat(stiffness)]
         if not first:
-            u_low, u_high = halo(current)
-        operands = [u_low, current, u_high, *buoy, stiffness]
-        if not first:
-            operands.append(dg)
+            operands.append(flat(dg))
         if not last:
-            operands += [taper, source_field, older]
-        operands += [mx, my3]
+            operands += [flat(taper), flat(source_field), older]
+        operands += [flat(mx), flat(my3)]
         slots = 3 if first else 2
+        out_shape = (field,) if last else (field, field)
+        if first:
+            out_shape = (field, jax.ShapeDtypeStruct((2, *shape), f32), field)
         results = pl.pallas_call(
             functools.partial(background_kernel, source_weight(t), first, last),
-            out_shape=(field,) * (1 + (not last) + 2 * first),
+            grid=(1,),
+            in_specs=[spec for _, spec in operands],
+            out_specs=[whole(out.shape) for out in out_shape],
+            out_shape=out_shape,
             scratch_shapes=[
                 pltpu.VMEM((slots, layers, 3 * rows, columns), jnp.bfloat16),
                 pltpu.VMEM((slots, layers, rows, columns), f32),
@@ -445,27 +464,31 @@
                 flops=60 * cells_here, bytes_accessed=56 * cells_here, transcendentals=0
             ),
             name=f"background{t}",
-        )(*operands)
-        results = list(results)
-        laps.append(results.pop(0))
+        )(*[array for array, _ in operands])
+        laps.append(results[0])
         if not last:
-            older, current = current, results.pop(0)
-            fields.append(current)
+            older = current
+            fields.append(results[1])
         if first:
-            dg, start = results
-            start_low, start_high = halo(start)
-
-    def wave(mode, group, p, old, add, lap, extra=(), ends=None):
-        low, high = halo(p) if mode != "start" else ends
+            pair, dg = results[1], results[2]
+            low, high = halo(pair)
+            current, start = view(pair, 0), view(pair, 1)
+            u_low, start_low = view(low, 0), view(low, 1)
+            u_high, start_high = view(high, 0), view(high, 1)
+        elif not last:
+            current = flat(results[1])
+
+    def wave(mode, group, p, old, add, lap, extra=()):
+        low, high = ends if mode == "start" else halo(p)
         one = pl.BlockSpec((None, *shape), lambda d: (d, 0, 0, 0))
         shifted = pl.BlockSpec((None, *shape), lambda d: (d + group * each, 0, 0, 0))
         same = whole(shape)
-        operands, specs = [low, p, high], [one, shifted if mode == "start" else one, one]
+        operands, specs = [low, p, high], [shifted if mode == "start" else one] * 3
         if old is not None:
             operands.append(old)
             specs.append(one)
-        operands += [*buoy, dg, stiffness]
-        specs += [same] * 5
+        operands += [array for array, _ in buoy] + [dg, stiffness]
+        specs += [spec for _, spec in buoy] + [same] * 2
         if mode != "image":
             operands += [taper, add, lap]
             specs += [same, shifted if mode in ("start", "born", "turn") else one, same]
@@ -479,8 +502,8 @@
         operands += [*extra, mx, my2]
         specs += [whole(mx.shape), whole(my2.shape)]
         if mode == "start":
-            operands += [start_low, start, start_high]
-            specs += [same] * 3
+            operands += [array for array, _ in (start_low, start, start_high)]
+            specs += [spec for _, spec in (start_low, start, start_high)]
         out_shape, out_spec = (jax.ShapeDtypeStruct((each, *shape), f32),), [one]
         if mode == "start":
             out_shape, out_spec = out_shape * 2, out_spec * 2
@@ -513,18 +536,13 @@
         )(*operands)
         return results[0] if len(results) == 1 else results
 
-    def after(value, earlier):
-        return lax.optimization_barrier((value, earlier))[0]
-
     born = [[None] * GROUPS for _ in range(STEPS + 1)]
-    first_after = [(b_low, b_high, u0_low, u0_high), fields[2]]
     ahead = {(2, 1): fields[3], (3, 1): laps[3]}
     for t in (1, 2):
         for g in range(GROUPS):
             if t == 1:
-                mine = after(perturbations[g * each : (g + 1) * each], first_after[g])
                 new, born[1][g] = wave(
-                    "start", g, perturbations, None, perturbations, laps[1], ends=halo(mine)
+                    "start", g, perturbations, None, perturbations, laps[1]
                 )
             else:
                 new = wave("born", g, born[t][g], born[t - 1][g], perturbations, laps[t])

time: 266 us -> 266 us (level)
  starting transfers between devices: 146 us -> 119 us
  waiting for transfers between devices: 46.5 us -> 73.5 us
    ppermute x18 -> x15, waiting for transfers between devices: 2.66 us -> 22.5 us  [halo(): lax.ppermute(block, 'slab', backward)]
    ppermute x18 -> x15, starting transfers between devices: 85.9 us -> 69 us  [halo(): lax.ppermute(block, 'slab', forward)]
    ppermute x18 -> x15, starting transfers between devices: 41 us -> 32.2 us  [halo(): lax.ppermute(block, 'slab', backward)]
    ppermute x18 -> x15, waiting for transfers between devices: 10.2 us -> 16.6 us  [halo(): lax.ppermute(block, 'slab', forward)]
    unnamed x34 -> x44, local copies, waits for them, and re-layouts: 10.5 us -> 9.41 us
  transfers between devices with their start and end apart: 49 -> 43, of which waited for: 20 -> 19; matrix products, arithmetic and copies ran while one was open for 0% -> 0% of each run, Pallas kernels for 18% -> 19%
where the time goes in v6:
time: 266 us; the launch traced here: 264 us
  starting transfers between devices  119 us (45%)
  waiting for transfers between devices  73.5 us (28%)
  Pallas kernels  59.1 us (22%)
  local copies, waits for them, and re-layouts  9.41 us (4%)
    ppermute x15, starting transfers between devices, halo(): lax.ppermute(block, 'slab', forward)  69 us
    pallas_call x12, Pallas kernels, wave(): pl.pallas_call(functools.partial(wave_kernel, mode, old is not None), gri...  42 us
    ppermute x15, starting transfers between devices, halo(): lax.ppermute(block, 'slab', backward)  32.2 us
    ppermute x15, waiting for transfers between devices, halo(): lax.ppermute(block, 'slab', backward)  22.5 us
    ppermute x7, waiting for transfers between devices, add_up(): lax.ppermute(value, axis, [(i, i ^ stride) for i in range(size)])  21.4 us
    ppermute x15, waiting for transfers between devices, halo(): lax.ppermute(block, 'slab', forward)  16.6 us
    ppermute x6, waiting for transfers between devices, shards(): sketch.append(lax.ppermute(blocks[s], 'dirs', ring))  13.1 us
    ppermute x6, starting transfers between devices, shards(): sketch.append(lax.ppermute(blocks[s], 'dirs', ring))  10.4 us
  transfers between devices with their start and end apart: 43, of which 19 were waited for; matrix products, arithmetic and copies ran while one was open for 0% of the time, Pallas kernels for 19%

profile of v6, /device:TPU:14, one launch (start us, length us, event | category | flops | bytes accessed | tf_op | source)
XLA Modules:
  0.0 264.1 jit_solution(2347672017451198512)
XLA Ops:
  14.2 3.6 %collective-permute-start = (f32[4,4,128,256]{3,2,1,0:T(8,128)S(1)}, f32[4,4,128,256]{3,2,1,0:T(8,128)S(1)}, u32[]{:S(2)}, u32[]{:S(2)}) collective-permute-start(f32[4,4,128,256]{3,2,1,0:T(8,128)S(1)} %copy-done), channel_id=1, source_target_pairs={{0,1},{1,2},{2,3},{3,4},{4,5},{5,6},{6,7},{7,8},{8,9},{9,10},{10,1... | collective-permute-start | bytes 6291464 | tf_op jit(solution)/shard_map/ppermute | solution.py:358
  27.9 22.5 %collective-permute-done.5.refs_2_.refs_15_ = f32[2,4,128,256]{3,2,1,0:T(8,128)S(1)} collective-permute-done((f32[2,4,128,256]{3,2,1,0:T(8,128)S(1)}, f32[2,4,128,256]{3,2,1,0:T(8,128)S(1)}, u32[]{:S(2)}, u32[]{:S(2)}) %collective-permute-start.5) | collective-permute-done | bytes 1048608 | tf_op jit(solution)/shard_map/ppermute | solution.py:358
  50.4 3.8 %collective-permute-done.4.refs_0_.refs_13_ = f32[2,4,128,256]{3,2,1,0:T(8,128)S(1)} collective-permute-done((f32[2,4,128,256]{3,2,1,0:T(8,128)S(1)}, f32[2,4,128,256]{3,2,1,0:T(8,128)S(1)}, u32[]{:S(2)}, u32[]{:S(2)}) %collective-permute-start.4) | collective-permute-done | bytes 1048608 | tf_op jit(solution)/shard_map/ppermute | solution.py:358
  57.9 3.5 %collective-permute-start.8 = (f32[4,128,256]{2,1,0:T(8,128)S(1)}, f32[4,128,256]{2,1,0:T(8,128)S(1)}, u32[]{:S(2)}, u32[]{:S(2)}) collective-permute-start(f32[4,128,256]{2,1,0:T(8,128)S(1)} %get-tuple-element.56.refs_1_), channel_id=1, source_target_pairs={{0,1},{1,2},{2,3},{3,4},{4,5},{5,6},{6,7},{7,8},{8,9},{9,10},{10,1... | collective-permute-start | bytes 1572872 | tf_op jit(solution)/shard_map/ppermute | solution.py:358
  66.7 6.4 %collective-permute-start.6 = (f32[2,4,128,256]{3,2,1,0:T(8,128)S(1)}, f32[2,4,128,256]{3,2,1,0:T(8,128)S(1)}, u32[]{:S(2)}, u32[]{:S(2)}) collective-permute-start(f32[2,4,128,256]{3,2,1,0:T(8,128)S(1)} %get-tuple-element.54.refs_1_.refs_3_.refs_10_), channel_id=1, source_target_pairs={{0,1},{1,2},{2,3},{3,4},{4,5},{5,6},{6,7},{7,8},{8,9},{9,10},{10,1... | collective-permute-start | bytes 3145736 | tf_op jit(solution)/shard_map/ppermute | solution.py:358
  79.9 5.8 %collective-permute-start.23 = (f32[2,4,128,256]{3,2,1,0:T(8,128)S(1)}, f32[2,4,128,256]{3,2,1,0:T(8,128)S(1)}, u32[]{:S(2)}, u32[]{:S(2)}) collective-permute-start(f32[2,4,128,256]{3,2,1,0:T(8,128)S(1)} %get-tuple-element.69.refs_1_.refs_3_.refs_10_), channel_id=1, source_target_pairs={{0,1},{1,2},{2,3},{3,4},{4,5},{5,6},{6,7},{7,8},{8,9},{9,10},{10,1... | collective-permute-start | bytes 3145736 | tf_op jit(solution)/shard_map/ppermute | solution.py:358
  87.6 5.8 %collective-permute-start.12 = (f32[4,128,256]{2,1,0:T(8,128)S(1)}, f32[4,128,256]{2,1,0:T(8,128)S(1)}, u32[]{:S(2)}, u32[]{:S(2)}) collective-permute-start(f32[4,128,256]{2,1,0:T(8,128)S(1)} %get-tuple-element.58.refs_1_), channel_id=1, source_target_pairs={{0,1},{1,2},{2,3},{3,4},{4,5},{5,6},{6,7},{7,8},{8,9},{9,10},{10,1... | collective-permute-start | bytes 1572872 | tf_op jit(solution)/shard_map/ppermute | solution.py:358
  98.4 9.2 %collective-permute-start.10 = (f32[2,4,128,256]{3,2,1,0:T(8,128)S(1)}, f32[2,4,128,256]{3,2,1,0:T(8,128)S(1)}, u32[]{:S(2)}, u32[]{:S(2)}) collective-permute-start(f32[2,4,128,256]{3,2,1,0:T(8,128)S(1)} %born.2.refs_1_.refs_9_), channel_id=1, source_target_pairs={{0,1},{1,2},{2,3},{3,4},{4,5},{5,6},{6,7},{7,8},{8,9},{9,10},{10,1... | collective-permute-start | bytes 3145736 | tf_op jit(solution)/shard_map/ppermute | solution.py:358
  122.8 4.4 %collective-permute-start.14 = (f32[2,4,128,256]{3,2,1,0:T(8,128)S(1)}, f32[2,4,128,256]{3,2,1,0:T(8,128)S(1)}, u32[]{:S(2)}, u32[]{:S(2)}) collective-permute-start(f32[2,4,128,256]{3,2,1,0:T(8,128)S(1)} %turn.2.refs_1_.refs_3_), channel_id=1, source_target_pairs={{0,1},{1,2},{2,3},{3,4},{4,5},{5,6},{6,7},{7,8},{8,9},{9,10},{10,1... | collective-permute-start | bytes 3145736 | tf_op jit(solution)/shard_map/ppermute | solution.py:358
  135.3 3.6 %collective-permute-start.27 = (f32[2,4,128,256]{3,2,1,0:T(8,128)S(1)}, f32[2,4,128,256]{3,2,1,0:T(8,128)S(1)}, u32[]{:S(2)}, u32[]{:S(2)}) collective-permute-start(f32[2,4,128,256]{3,2,1,0:T(8,128)S(1)} %turn.3.refs_1_.refs_3_), channel_id=1, source_target_pairs={{0,1},{1,2},{2,3},{3,4},{4,5},{5,6},{6,7},{7,8},{8,9},{9,10},{10,1... | collective-permute-start | bytes 3145736 | tf_op jit(solution)/shard_map/ppermute | solution.py:358
  146.6 3.9 %collective-permute-start.16 = (f32[2,4,128,256]{3,2,1,0:T(8,128)S(1)}, f32[2,4,128,256]{3,2,1,0:T(8,128)S(1)}, u32[]{:S(2)}, u32[]{:S(2)}) collective-permute-start(f32[2,4,128,256]{3,2,1,0:T(8,128)S(1)} %adjoint.2.refs_1_), channel_id=1, source_target_pairs={{0,1},{1,2},{2,3},{3,4},{4,5},{5,6},{6,7},{7,8},{8,9},{9,10},{10,1... | collective-permute-start | bytes 3145736 | tf_op jit(solution)/shard_map/ppermute | solution.py:358
  157.6 4.3 %collective-permute-start.29 = (f32[2,4,128,256]{3,2,1,0:T(8,128)S(1)}, f32[2,4,128,256]{3,2,1,0:T(8,128)S(1)}, u32[]{:S(2)}, u32[]{:S(2)}) collective-permute-start(f32[2,4,128,256]{3,2,1,0:T(8,128)S(1)} %adjoint.3.refs_1_), channel_id=1, source_target_pairs={{0,1},{1,2},{2,3},{3,4},{4,5},{5,6},{6,7},{7,8},{8,9},{9,10},{10,1... | collective-permute-start | bytes 3145736 | tf_op jit(solution)/shard_map/ppermute | solution.py:358
  164.0 4.5 %fold.2 = (f32[2,4,128,256]{3,2,1,0:T(8,128)}, f32[2,4,128,256]{3,2,1,0:T(8,128)S(1)}, f32[4,128,256]{2,1,0:T(8,128)S(1)}, f32[4,128,256]{2,1,0:T(8,128)S(1)}) custom-call(f32[2,4,128,256]{3,2,1,0:T(8,128)S(1)} %collective-permute-done.16.refs_0_, f32[2,4,128,256]{3,2,1,0:T(8,128)S(1)} %adjoint.2.refs_1_, ...), custom_call_target="tpu_custom_call" | custom-call | flops 15728640 | bytes 7340032 | tf_op jit(solution)/shard_map/fold/pallas_call | solution.py:518
  171.4 4.5 %collective-permute-start.18 = (f32[2,4,128,256]{3,2,1,0:T(8,128)}, f32[2,4,128,256]{3,2,1,0:T(8,128)}, u32[]{:S(2)}, u32[]{:S(2)}) collective-permute-start(f32[2,4,128,256]{3,2,1,0:T(8,128)} %get-tuple-element.60.refs_1_), channel_id=1, source_target_pairs={{0,1},{1,2},{2,3},{3,4},{4,5},{5,6},{6,7},{7,8},{8,9},{9,10},{10,1... | collective-permute-start | bytes 3145736 | tf_op jit(solution)/shard_map/ppermute | solution.py:358
  176.0 4.5 %fold.3 = (f32[2,4,128,256]{3,2,1,0:T(8,128)}, f32[2,4,128,256]{3,2,1,0:T(8,128)S(1)}) custom-call(f32[2,4,128,256]{3,2,1,0:T(8,128)S(1)} %collective-permute-done.29.refs_0_, f32[2,4,128,256]{3,2,1,0:T(8,128)S(1)} %adjoint.3.refs_1_, f32[2,4,128,256]{3,2,1,0:T(8,128)S(1)} %collective-permute-done.30.refs_2_, f32[2,4,128,256]{3,2,1,0:T(8,128)S(1)} %turn.3.refs_1_.refs_3_, ...), custom_call_target="tpu_custom_call" | custom-call | flops 15728640 | bytes 7340032 | tf_op jit(solution)/shard_map/fold/pallas_call | solution.py:518
  183.4 6.4 %collective-permute-start.31 = (f32[2,4,128,256]{3,2,1,0:T(8,128)}, f32[2,4,128,256]{3,2,1,0:T(8,128)}, u32[]{:S(2)}, u32[]{:S(2)}) collective-permute-start(f32[2,4,128,256]{3,2,1,0:T(8,128)} %get-tuple-element.72.refs_1_), channel_id=1, source_target_pairs={{0,1},{1,2},{2,3},{3,4},{4,5},{5,6},{6,7},{7,8},{8,9},{9,10},{10,1... | collective-permute-start | bytes 3145736 | tf_op jit(solution)/shard_map/ppermute | solution.py:358
  194.1 4.5 %image.2 = (f32[2,4,32,256]{3,2,1,0:T(8,128)S(1)}, f32[2,4,32,256]{3,2,1,0:T(8,128)S(1)}, f32[2,4,32,256]{3,2,1,0:T(8,128)S(1)}, f32[2,4,32,256]{3,2,1,0:T(8,128)S(1)}) custom-call(f32[2,4,128,256]{3,2,1,0:T(8,128)} %collective-permute-done.18.refs_0_, f32[2,4,128,256]{3,2,1,0:T(8,128)} %get-tuple-element.60.refs_1_, ...), custom_call_target="tpu_custom_call" | custom-call | flops 15728640 | bytes 7340032 | tf_op jit(solution)/shard_map/image/pallas_call | solution.py:518
  200.6 3.6 %collective-permute-start.21 = (f32[2,4,32,256]{3,2,1,0:T(8,128)S(1)}, f32[2,4,32,256]{3,2,1,0:T(8,128)S(1)}, u32[]{:S(2)}, u32[]{:S(2)}) collective-permute-start(f32[2,4,32,256]{3,2,1,0:T(8,128)S(1)} %get-tuple-element.66), channel_id=1, source_target_pairs={{0,64},{32,96},{64,0},{96,32},{1,65},{33,97},{65,1},{97,33},{2,66}... | collective-permute-start | bytes 786440 | tf_op jit(solution)/shard_map/ppermute | solution.py:572
  205.3 4.4 %image.3 = (f32[2,4,32,256]{3,2,1,0:T(8,128)S(1)}, f32[2,4,32,256]{3,2,1,0:T(8,128)S(1)}, f32[2,4,32,256]{3,2,1,0:T(8,128)S(1)}, f32[2,4,32,256]{3,2,1,0:T(8,128)S(1)}) custom-call(f32[2,4,128,256]{3,2,1,0:T(8,128)} %collective-permute-done.31.refs_0_, f32[2,4,128,256]{3,2,1,0:T(8,128)} %get-tuple-element.72.refs_1_, ...), custom_call_target="tpu_custom_call" | custom-call | flops 15728640 | bytes 7340032 | tf_op jit(solution)/shard_map/image/pallas_call | solution.py:518
  214.6 9.2 %collective-permute-done.33.refs_5_ = f32[2,4,32,256]{3,2,1,0:T(8,128)S(1)} collective-permute-done((f32[2,4,32,256]{3,2,1,0:T(8,128)S(1)}, f32[2,4,32,256]{3,2,1,0:T(8,128)S(1)}, u32[]{:S(2)}, u32[]{:S(2)}) %collective-permute-start.33) | collective-permute-done | bytes 262176 | tf_op jit(solution)/shard_map/ppermute | solution.py:572
  232.1 3.6 %collective-permute-done.37 = f32[16,16]{1,0:T(8,128)S(1)} collective-permute-done((f32[16,16]{1,0:T(8,128)S(1)}, f32[16,16]{1,0:T(8,128)S(1)}, u32[]{:S(2)}, u32[]{:S(2)}) %collective-permute-start.37) | collective-permute-done | bytes 1056 | tf_op jit(solution)/shard_map/ppermute | solution.py:370
  236.6 4.3 %collective-permute-done.38 = f32[16,16]{1,0:T(8,128)S(1)} collective-permute-done((f32[16,16]{1,0:T(8,128)S(1)}, f32[16,16]{1,0:T(8,128)S(1)}, u32[]{:S(2)}, u32[]{:S(2)}) %collective-permute-start.38) | collective-permute-done | bytes 1056 | tf_op jit(solution)/shard_map/ppermute | solution.py:370
  245.6 4.1 %collective-permute-done.40 = f32[16,16]{1,0:T(8,128)S(1)} collective-permute-done((f32[16,16]{1,0:T(8,128)S(1)}, f32[16,16]{1,0:T(8,128)S(1)}, u32[]{:S(2)}, u32[]{:S(2)}) %collective-permute-start.40) | collective-permute-done | bytes 1056 | tf_op jit(solution)/shard_map/ppermute | solution.py:370
  258.6 5.5 %basis.1 = (f32[16,4,32,256]{3,2,1,0:T(8,128)}, f32[16,16]{1,0:T(8,128)}) custom-call(f32[16,16]{1,0:T(8,128)S(1)} %add.68.gram_ref, f32[16,16]{1,0:T(8,128)S(1)} %get-tuple-element.79.sel_ref, f32[2,4,32,256]{3,2,1,0:T(8,128)S(1)} %get-tuple-element.64.refs_0_, f32[2,4,32,256]{3,2,1,0:T(8,128)S(1)} %collective-permute-done.20.refs_1_, ...), custom_call_target="tpu_custom_call" | custom-call | tf_op jit(solution)/shard_map/basis/pallas_call | solution.py:591
  (135 shorter events, 126.8 us)
Async XLA Ops:
  10.8 50.7 %collective-permute-start.1 = (f32[4,4,128,256]{3,2,1,0:T(8,128)S(1)}, f32[4,4,128,256]{3,2,1,0:T(8,128)S(1)}, u32[]{:S(2)}, u32[]{:S(2)}) collective-permute-start(f32[4,4,128,256]{3,2,1,0:T(8,128)S(1)} %copy-done), channel_id=1, source_target_pairs={{1,0},{2,1},{3,2},{4,3},{5,4},{6,5},{7,6},{8,7},{9,8},{10,9},{11,1... | collective-permute-start | bytes 6291464 | tf_op jit(solution)/shard_map/ppermute | solution.py:358
  14.2 47.2 %collective-permute-start = (f32[4,4,128,256]{3,2,1,0:T(8,128)S(1)}, f32[4,4,128,256]{3,2,1,0:T(8,128)S(1)}, u32[]{:S(2)}, u32[]{:S(2)}) collective-permute-start(f32[4,4,128,256]{3,2,1,0:T(8,128)S(1)} %copy-done), channel_id=1, source_target_pairs={{0,1},{1,2},{2,3},{3,4},{4,5},{5,6},{6,7},{7,8},{8,9},{9,10},{10,1... | collective-permute-start | bytes 6291464 | tf_op jit(solution)/shard_map/ppermute | solution.py:358
  22.9 27.5 %collective-permute-start.5 = (f32[2,4,128,256]{3,2,1,0:T(8,128)S(1)}, f32[2,4,128,256]{3,2,1,0:T(8,128)S(1)}, u32[]{:S(2)}, u32[]{:S(2)}) collective-permute-start(f32[2,4,128,256]{3,2,1,0:T(8,128)S(1)} %get-tuple-element.51.refs_1_.refs_14_.refs_10_), channel_id=1, source_target_pairs={{1,0},{2,1},{3,2},{4,3},{5,4},{6,5},{7,6},{8,7},{9,8},{10,9},{11,1... | collective-permute-start | bytes 3145736 | tf_op jit(solution)/shard_map/ppermute | solution.py:358
  24.9 29.4 %collective-permute-start.4 = (f32[2,4,128,256]{3,2,1,0:T(8,128)S(1)}, f32[2,4,128,256]{3,2,1,0:T(8,128)S(1)}, u32[]{:S(2)}, u32[]{:S(2)}) collective-permute-start(f32[2,4,128,256]{3,2,1,0:T(8,128)S(1)} %get-tuple-element.51.refs_1_.refs_14_.refs_10_), channel_id=1, source_target_pairs={{0,1},{1,2},{2,3},{3,4},{4,5},{5,6},{6,7},{7,8},{8,9},{9,10},{10,1... | collective-permute-start | bytes 3145736 | tf_op jit(solution)/shard_map/ppermute | solution.py:358
  56.0 20.2 %collective-permute-start.9 = (f32[4,128,256]{2,1,0:T(8,128)S(1)}, f32[4,128,256]{2,1,0:T(8,128)S(1)}, u32[]{:S(2)}, u32[]{:S(2)}) collective-permute-start(f32[4,128,256]{2,1,0:T(8,128)S(1)} %get-tuple-element.56.refs_1_), channel_id=1, source_target_pairs={{1,0},{2,1},{3,2},{4,3},{5,4},{6,5},{7,6},{8,7},{9,8},{10,9},{11,1... | collective-permute-start | bytes 1572872 | tf_op jit(solution)/shard_map/ppermute | solution.py:358
  57.9 18.3 %collective-permute-start.8 = (f32[4,128,256]{2,1,0:T(8,128)S(1)}, f32[4,128,256]{2,1,0:T(8,128)S(1)}, u32[]{:S(2)}, u32[]{:S(2)}) collective-permute-start(f32[4,128,256]{2,1,0:T(8,128)S(1)} %get-tuple-element.56.refs_1_), channel_id=1, source_target_pairs={{0,1},{1,2},{2,3},{3,4},{4,5},{5,6},{6,7},{7,8},{8,9},{9,10},{10,1... | collective-permute-start | bytes 1572872 | tf_op jit(solution)/shard_map/ppermute | solution.py:358
  64.7 23.0 %collective-permute-start.7 = (f32[2,4,128,256]{3,2,1,0:T(8,128)S(1)}, f32[2,4,128,256]{3,2,1,0:T(8,128)S(1)}, u32[]{:S(2)}, u32[]{:S(2)}) collective-permute-start(f32[2,4,128,256]{3,2,1,0:T(8,128)S(1)} %get-tuple-element.54.refs_1_.refs_3_.refs_10_), channel_id=1, source_target_pairs={{1,0},{2,1},{3,2},{4,3},{5,4},{6,5},{7,6},{8,7},{9,8},{10,9},{11,1... | collective-permute-start | bytes 3145736 | tf_op jit(solution)/shard_map/ppermute | solution.py:358
  66.7 26.7 %collective-permute-start.6 = (f32[2,4,128,256]{3,2,1,0:T(8,128)S(1)}, f32[2,4,128,256]{3,2,1,0:T(8,128)S(1)}, u32[]{:S(2)}, u32[]{:S(2)}) collective-permute-start(f32[2,4,128,256]{3,2,1,0:T(8,128)S(1)} %get-tuple-element.54.refs_1_.refs_3_.refs_10_), channel_id=1, source_target_pairs={{0,1},{1,2},{2,3},{3,4},{4,5},{5,6},{6,7},{7,8},{8,9},{9,10},{10,1... | collective-permute-start | bytes 3145736 | tf_op jit(solution)/shard_map/ppermute | solution.py:358
  78.0 31.2 %collective-permute-start.24 = (f32[2,4,128,256]{3,2,1,0:T(8,128)S(1)}, f32[2,4,128,256]{3,2,1,0:T(8,128)S(1)}, u32[]{:S(2)}, u32[]{:S(2)}) collective-permute-start(f32[2,4,128,256]{3,2,1,0:T(8,128)S(1)} %get-tuple-element.69.refs_1_.refs_3_.refs_10_), channel_id=1, source_target_pairs={{1,0},{2,1},{3,2},{4,3},{5,4},{6,5},{7,6},{8,7},{9,8},{10,9},{11,1... | collective-permute-start | bytes 3145736 | tf_op jit(solution)/shard_map/ppermute | solution.py:358
  79.9 29.3 %collective-permute-start.23 = (f32[2,4,128,256]{3,2,1,0:T(8,128)S(1)}, f32[2,4,128,256]{3,2,1,0:T(8,128)S(1)}, u32[]{:S(2)}, u32[]{:S(2)}) collective-permute-start(f32[2,4,128,256]{3,2,1,0:T(8,128)S(1)} %get-tuple-element.69.refs_1_.refs_3_.refs_10_), channel_id=1, source_target_pairs={{0,1},{1,2},{2,3},{3,4},{4,5},{5,6},{6,7},{7,8},{8,9},{9,10},{10,1... | collective-permute-start | bytes 3145736 | tf_op jit(solution)/shard_map/ppermute | solution.py:358
  87.6 20.0 %collective-permute-start.12 = (f32[4,128,256]{2,1,0:T(8,128)S(1)}, f32[4,128,256]{2,1,0:T(8,128)S(1)}, u32[]{:S(2)}, u32[]{:S(2)}) collective-permute-start(f32[4,128,256]{2,1,0:T(8,128)S(1)} %get-tuple-element.58.refs_1_), channel_id=1, source_target_pairs={{0,1},{1,2},{2,3},{3,4},{4,5},{5,6},{6,7},{7,8},{8,9},{9,10},{10,1... | collective-permute-start | bytes 1572872 | tf_op jit(solution)/shard_map/ppermute | solution.py:358
  96.4 20.2 %collective-permute-start.11 = (f32[2,4,128,256]{3,2,1,0:T(8,128)S(1)}, f32[2,4,128,256]{3,2,1,0:T(8,128)S(1)}, u32[]{:S(2)}, u32[]{:S(2)}) collective-permute-start(f32[2,4,128,256]{3,2,1,0:T(8,128)S(1)} %born.2.refs_1_.refs_9_), channel_id=1, source_target_pairs={{1,0},{2,1},{3,2},{4,3},{5,4},{6,5},{7,6},{8,7},{9,8},{10,9},{11,1... | collective-permute-start | bytes 3145736 | tf_op jit(solution)/shard_map/ppermute | solution.py:358
  98.4 18.2 %collective-permute-start.10 = (f32[2,4,128,256]{3,2,1,0:T(8,128)S(1)}, f32[2,4,128,256]{3,2,1,0:T(8,128)S(1)}, u32[]{:S(2)}, u32[]{:S(2)}) collective-permute-start(f32[2,4,128,256]{3,2,1,0:T(8,128)S(1)} %born.2.refs_1_.refs_9_), channel_id=1, source_target_pairs={{0,1},{1,2},{2,3},{3,4},{4,5},{5,6},{6,7},{7,8},{8,9},{9,10},{10,1... | collective-permute-start | bytes 3145736 | tf_op jit(solution)/shard_map/ppermute | solution.py:358
  119.7 19.2 %collective-permute-start.15 = (f32[2,4,128,256]{3,2,1,0:T(8,128)S(1)}, f32[2,4,128,256]{3,2,1,0:T(8,128)S(1)}, u32[]{:S(2)}, u32[]{:S(2)}) collective-permute-start(f32[2,4,128,256]{3,2,1,0:T(8,128)S(1)} %turn.2.refs_1_.refs_3_), channel_id=1, source_target_pairs={{1,0},{2,1},{3,2},{4,3},{5,4},{6,5},{7,6},{8,7},{9,8},{10,9},{11,1... | collective-permute-start | bytes 3145736 | tf_op jit(solution)/shard_map/ppermute | solution.py:358
  122.8 18.7 %collective-permute-start.14 = (f32[2,4,128,256]{3,2,1,0:T(8,128)S(1)}, f32[2,4,128,256]{3,2,1,0:T(8,128)S(1)}, u32[]{:S(2)}, u32[]{:S(2)}) collective-permute-start(f32[2,4,128,256]{3,2,1,0:T(8,128)S(1)} %turn.2.refs_1_.refs_3_), channel_id=1, source_target_pairs={{0,1},{1,2},{2,3},{3,4},{4,5},{5,6},{6,7},{7,8},{8,9},{9,10},{10,1... | collective-permute-start | bytes 3145736 | tf_op jit(solution)/shard_map/ppermute | solution.py:358
  135.3 17.5 %collective-permute-start.27 = (f32[2,4,128,256]{3,2,1,0:T(8,128)S(1)}, f32[2,4,128,256]{3,2,1,0:T(8,128)S(1)}, u32[]{:S(2)}, u32[]{:S(2)}) collective-permute-start(f32[2,4,128,256]{3,2,1,0:T(8,128)S(1)} %turn.3.refs_1_.refs_3_), channel_id=1, source_target_pairs={{0,1},{1,2},{2,3},{3,4},{4,5},{5,6},{6,7},{7,8},{8,9},{9,10},{10,1... | collective-permute-start | bytes 3145736 | tf_op jit(solution)/shard_map/ppermute | solution.py:358
  144.5 17.5 %collective-permute-start.17 = (f32[2,4,128,256]{3,2,1,0:T(8,128)S(1)}, f32[2,4,128,256]{3,2,1,0:T(8,128)S(1)}, u32[]{:S(2)}, u32[]{:S(2)}) collective-permute-start(f32[2,4,128,256]{3,2,1,0:T(8,128)S(1)} %adjoint.2.refs_1_), channel_id=1, source_target_pairs={{1,0},{2,1},{3,2},{4,3},{5,4},{6,5},{7,6},{8,7},{9,8},{10,9},{11,1... | collective-permute-start | bytes 3145736 | tf_op jit(solution)/shard_map/ppermute | solution.py:358
  146.6 17.4 %collective-permute-start.16 = (f32[2,4,128,256]{3,2,1,0:T(8,128)S(1)}, f32[2,4,128,256]{3,2,1,0:T(8,128)S(1)}, u32[]{:S(2)}, u32[]{:S(2)}) collective-permute-start(f32[2,4,128,256]{3,2,1,0:T(8,128)S(1)} %adjoint.2.refs_1_), channel_id=1, source_target_pairs={{0,1},{1,2},{2,3},{3,4},{4,5},{5,6},{6,7},{7,8},{8,9},{9,10},{10,1... | collective-permute-start | bytes 3145736 | tf_op jit(solution)/shard_map/ppermute | solution.py:358
  155.7 20.3 %collective-permute-start.30 = (f32[2,4,128,256]{3,2,1,0:T(8,128)S(1)}, f32[2,4,128,256]{3,2,1,0:T(8,128)S(1)}, u32[]{:S(2)}, u32[]{:S(2)}) collective-permute-start(f32[2,4,128,256]{3,2,1,0:T(8,128)S(1)} %adjoint.3.refs_1_), channel_id=1, source_target_pairs={{1,0},{2,1},{3,2},{4,3},{5,4},{6,5},{7,6},{8,7},{9,8},{10,9},{11,1... | collective-permute-start | bytes 3145736 | tf_op jit(solution)/shard_map/ppermute | solution.py:358
  157.6 18.4 %collective-permute-start.29 = (f32[2,4,128,256]{3,2,1,0:T(8,128)S(1)}, f32[2,4,128,256]{3,2,1,0:T(8,128)S(1)}, u32[]{:S(2)}, u32[]{:S(2)}) collective-permute-start(f32[2,4,128,256]{3,2,1,0:T(8,128)S(1)} %adjoint.3.refs_1_), channel_id=1, source_target_pairs={{0,1},{1,2},{2,3},{3,4},{4,5},{5,6},{6,7},{7,8},{8,9},{9,10},{10,1... | collective-permute-start | bytes 3145736 | tf_op jit(solution)/shard_map/ppermute | solution.py:358
  169.5 20.3 %collective-permute-start.19 = (f32[2,4,128,256]{3,2,1,0:T(8,128)}, f32[2,4,128,256]{3,2,1,0:T(8,128)}, u32[]{:S(2)}, u32[]{:S(2)}) collective-permute-start(f32[2,4,128,256]{3,2,1,0:T(8,128)} %get-tuple-element.60.refs_1_), channel_id=1, source_target_pairs={{1,0},{2,1},{3,2},{4,3},{5,4},{6,5},{7,6},{8,7},{9,8},{10,9},{11,1... | collective-permute-start | bytes 3145736 | tf_op jit(solution)/shard_map/ppermute | solution.py:358
  171.4 18.3 %collective-permute-start.18 = (f32[2,4,128,256]{3,2,1,0:T(8,128)}, f32[2,4,128,256]{3,2,1,0:T(8,128)}, u32[]{:S(2)}, u32[]{:S(2)}) collective-permute-start(f32[2,4,128,256]{3,2,1,0:T(8,128)} %get-tuple-element.60.refs_1_), channel_id=1, source_target_pairs={{0,1},{1,2},{2,3},{3,4},{4,5},{5,6},{6,7},{7,8},{8,9},{9,10},{10,1... | collective-permute-start | bytes 3145736 | tf_op jit(solution)/shard_map/ppermute | solution.py:358
  181.5 23.8 %collective-permute-start.32 = (f32[2,4,128,256]{3,2,1,0:T(8,128)}, f32[2,4,128,256]{3,2,1,0:T(8,128)}, u32[]{:S(2)}, u32[]{:S(2)}) collective-permute-start(f32[2,4,128,256]{3,2,1,0:T(8,128)} %get-tuple-element.72.refs_1_), channel_id=1, source_target_pairs={{1,0},{2,1},{3,2},{4,3},{5,4},{6,5},{7,6},{8,7},{9,8},{10,9},{11,1... | collective-permute-start | bytes 3145736 | tf_op jit(solution)/shard_map/ppermute | solution.py:358
  183.4 21.9 %collective-permute-start.31 = (f32[2,4,128,256]{3,2,1,0:T(8,128)}, f32[2,4,128,256]{3,2,1,0:T(8,128)}, u32[]{:S(2)}, u32[]{:S(2)}) collective-permute-start(f32[2,4,128,256]{3,2,1,0:T(8,128)} %get-tuple-element.72.refs_1_), channel_id=1, source_target_pairs={{0,1},{1,2},{2,3},{3,4},{4,5},{5,6},{6,7},{7,8},{8,9},{9,10},{10,1... | collective-permute-start | bytes 3145736 | tf_op jit(solution)/shard_map/ppermute | solution.py:358
  (41 other events, 462.1 us)

commit v7 on v6

--- a/solution.py
+++ b/solution.py
@@ -134,11 +134,10 @@
         taper_ref, src_ref, older_ref = (refs.pop(0) for _ in range(3))
     mx_ref, my_ref = refs.pop(0), refs.pop(0)
     lap_ref = refs.pop(0)
+    if not last:
+        new_ref = refs.pop(0)
     if first:
-        pair_ref, dg_ref = refs.pop(0), refs.pop(0)
-        new_ref, start_ref = pair_ref.at[0], pair_ref.at[1]
-    elif not last:
-        new_ref = refs.pop(0)
+        dg_ref = refs.pop(0)
     y_ref, a_ref = refs
 
     def functions(layer, row, size):
@@ -163,8 +162,6 @@
             times = depth_part(both, layer) + a_ref[1, layer, at, columns]
             lap = HALF * (b_here * plain + times - here * dg)
             lap_ref[layer, at, columns] = lap
-            if first:
-                start_ref[layer, at, columns] = taper_ref[layer, at, columns] * lap
             if not last:
                 new_ref[layer, at, columns] = (
                     taper_ref[layer, at, columns]
@@ -194,12 +191,6 @@
         first_ref = refs.pop(0)
         laps = [refs.pop(0) for _ in range(4)]
     mx_ref, my_ref = refs.pop(0), refs.pop(0)
-    if mode == "start":
-        *refs, low_ref, high_ref = refs
-        starts = [refs.pop(0) for _ in range(3)]
-        for target, source, factor_ref in zip((low_ref, refs[1], high_ref), p, starts):
-            target[...] = source[...] * factor_ref[...]
-        p = [low_ref, refs[1], high_ref]
     y_ref, a_ref = refs[-2:]
     outs = refs[:-2]
 
@@ -231,7 +222,7 @@
                 total = total - old
             taper = taper_ref[spot]
             added = add_ref[spot] * lap_ref[spot]
-            if mode in ("start", "born", "turn"):
+            if mode in ("born", "turn"):
                 new = taper * (total + added)
             else:
                 new = taper * total + added
@@ -406,13 +397,13 @@
     def matrix(*size):
         return jax.ShapeDtypeStruct(size, jnp.bfloat16)
 
-    copied = (stiffness, buoyancy, background_now, background_prev)
+    copied = (stiffness, buoyancy, background_now, background_prev, perturbations)
     matrices = (matrix(columns, columns), matrix(rows, 2 * rows), matrix(rows, 3 * rows))
     (
-        counts, source_field, taper, mx, my2, my3, stiffness, b_mid, current, older
+        counts, source_field, taper, mx, my2, my3, stiffness, b_mid, current, older, perturbations
     ) = pl.pallas_call(
         functools.partial(place_kernel, len(copied)),
-        out_shape=(field,) * 3 + matrices + (field,) * len(copied),
+        out_shape=(field,) * 3 + matrices + (*[field] * 4, jax.ShapeDtypeStruct(perturbations.shape, f32)),
         compiler_params=params(),
         cost_estimate=pl.CostEstimate(
             flops=40 * cells_here, bytes_accessed=16 * cells_here, transcendentals=0
@@ -429,7 +420,6 @@
     def flat(array):
         return array, whole(array.shape)
 
-    ends = halo(after(perturbations, counts))
     buoy = (b_low, flat(b_mid), b_high)
     current, older = flat(current), flat(older)
     fields = [None]
@@ -437,7 +427,7 @@
     dg = None
     for t in range(STEPS):
         first, last = t == 0, t == STEPS - 1
-        if t > 1:
+        if not first:
             u_low, u_high = (flat(end) for end in halo(current[0]))
         operands = [u_low, current, u_high, *buoy, flat(stiffness)]
         if not first:
@@ -446,9 +436,7 @@
             operands += [flat(taper), flat(source_field), older]
         operands += [flat(mx), flat(my3)]
         slots = 3 if first else 2
-        out_shape = (field,) if last else (field, field)
-        if first:
-            out_shape = (field, jax.ShapeDtypeStruct((2, *shape), f32), field)
+        out_shape = (field,) * (1 + (not last) + first)
         results = pl.pallas_call(
             functools.partial(background_kernel, source_weight(t), first, last),
             grid=(1,),
@@ -467,46 +455,35 @@
         )(*[array for array, _ in operands])
         laps.append(results[0])
         if not last:
-            older = current
+            older, current = current, flat(results[1])
             fields.append(results[1])
         if first:
-            pair, dg = results[1], results[2]
-            low, high = halo(pair)
-            current, start = view(pair, 0), view(pair, 1)
-            u_low, start_low = view(low, 0), view(low, 1)
-            u_high, start_high = view(high, 0), view(high, 1)
-        elif not last:
-            current = flat(results[1])
-
-    def wave(mode, group, p, old, add, lap, extra=()):
-        low, high = ends if mode == "start" else halo(p)
+            dg = results[2]
+
+    def wave(mode, group, p, old, add, lap, extra=(), ends=None):
+        low, high = ends or halo(p)
         one = pl.BlockSpec((None, *shape), lambda d: (d, 0, 0, 0))
         shifted = pl.BlockSpec((None, *shape), lambda d: (d + group * each, 0, 0, 0))
         same = whole(shape)
-        operands, specs = [low, p, high], [shifted if mode == "start" else one] * 3
+        operands, specs = [low, p, high], [shifted if ends else one] * 3
         if old is not None:
             operands.append(old)
-            specs.append(one)
+            specs.append(one if old.shape[0] == each else shifted)
         operands += [array for array, _ in buoy] + [dg, stiffness]
         specs += [spec for _, spec in buoy] + [same] * 2
         if mode != "image":
             operands += [taper, add, lap]
-            specs += [same, shifted if mode in ("start", "born", "turn") else one, same]
+            specs += [same, shifted if mode in ("born", "turn") else one, same]
         if mode == "turn":
             operands.append(counts)
             specs.append(same)
         if mode == "fold":
-            specs += [one] + [same] * 4
+            specs += [shifted] + [same] * 4
         if mode == "image":
             specs += [one, pl.BlockSpec(memory_space=pltpu.SMEM)] + [same] * 2
         operands += [*extra, mx, my2]
         specs += [whole(mx.shape), whole(my2.shape)]
-        if mode == "start":
-            operands += [array for array, _ in (start_low, start, start_high)]
-            specs += [spec for _, spec in (start_low, start, start_high)]
         out_shape, out_spec = (jax.ShapeDtypeStruct((each, *shape), f32),), [one]
-        if mode == "start":
-            out_shape, out_spec = out_shape * 2, out_spec * 2
         if mode == "fold":
             out_shape, out_spec = out_shape * 2, out_spec * 2
             if group == 0:
@@ -524,8 +501,7 @@
             scratch_shapes=[
                 pltpu.VMEM((2, layers, 2 * rows, columns), jnp.bfloat16),
                 pltpu.VMEM((2, layers, rows, columns), f32),
-            ]
-            + [pltpu.VMEM(shape, f32)] * (2 if mode == "start" else 0),
+            ],
             compiler_params=params(),
             cost_estimate=pl.CostEstimate(
                 flops=60 * each * cells_here,
@@ -537,15 +513,16 @@
         return results[0] if len(results) == 1 else results
 
     born = [[None] * GROUPS for _ in range(STEPS + 1)]
-    ahead = {(2, 1): fields[3], (3, 1): laps[3]}
+    begun = taper * (perturbations * laps[0])
+    ends = halo(begun)
+    ahead = {(3, 0): fields[3], (3, 1): laps[3]}
     for t in (1, 2):
         for g in range(GROUPS):
             if t == 1:
-                new, born[1][g] = wave(
-                    "start", g, perturbations, None, perturbations, laps[1]
-                )
+                new = wave("born", g, begun, None, perturbations, laps[1], ends=ends)
             else:
-                new = wave("born", g, born[t][g], born[t - 1][g], perturbations, laps[t])
+                old = begun if t == 2 else born[t - 1][g]
+                new = wave("born", g, born[t][g], old, perturbations, laps[t])
             if (t + 1, g) in ahead:
                 new = after(new, ahead[t + 1, g])
             born[t + 1][g] = new
@@ -557,7 +534,7 @@
     known = [None] * GROUPS
     for g in range(GROUPS):
         adjoint[1][g], known[g], *rest = wave(
-            "fold", g, adjoint[2][g], adjoint[3][g], born[2][g], counts, (born[1][g], *laps)
+            "fold", g, adjoint[2][g], adjoint[3][g], born[2][g], counts, (begun, *laps)
         )
         if g == 0:
             weight, near = rest

time: 266 us -> 273 us (1.026)
  starting transfers between devices: 119 us -> 134 us
  waiting for transfers between devices: 73.5 us -> 63 us
    ppermute x15, starting transfers between devices: 69 us -> 84.2 us  [halo(): lax.ppermute(block, 'slab', forward)]
    ppermute x15, waiting for transfers between devices: 16.6 us -> 7.68 us  [halo(): lax.ppermute(block, 'slab', forward)]
  transfers between devices with their start and end apart: 43 -> 43, of which waited for: 19 -> 16; matrix products, arithmetic and copies ran while one was open for 0% -> 0% of each run, Pallas kernels for 19% -> 17%
where the time goes in v7:
time: 273 us; the launch traced here: 269 us
  starting transfers between devices  134 us (49%)
  waiting for transfers between devices  63 us (23%)
  Pallas kernels  59 us (22%)
  local copies, waits for them, and re-layouts  10.5 us (4%)
    ppermute x15, starting transfers between devices, halo(): lax.ppermute(block, 'slab', forward)  84.2 us
    pallas_call x12, Pallas kernels, wave(): pl.pallas_call(functools.partial(wave_kernel, mode, old is not None), gri...  41.8 us
    ppermute x15, starting transfers between devices, halo(): lax.ppermute(block, 'slab', backward)  31 us
    ppermute x15, waiting for transfers between devices, halo(): lax.ppermute(block, 'slab', backward)  21.5 us
    ppermute x7, waiting for transfers between devices, add_up(): lax.ppermute(value, axis, [(i, i ^ stride) for i in range(size)])  20.7 us
    ppermute x6, waiting for transfers between devices, shards(): sketch.append(lax.ppermute(blocks[s], 'dirs', ring))  13.1 us
    unnamed x44, local copies, waits for them, and re-layouts  10.5 us
    ppermute x6, starting transfers between devices, shards(): sketch.append(lax.ppermute(blocks[s], 'dirs', ring))  10.4 us
  transfers between devices with their start and end apart: 43, of which 16 were waited for; matrix products, arithmetic and copies ran while one was open for 0% of the time, Pallas kernels for 17%

profile of v7, /device:TPU:14, one launch (start us, length us, event | category | flops | bytes accessed | tf_op | source)
XLA Modules:
  0.0 269.4 jit_solution(18083466227832194250)
XLA Ops:
  16.6 3.8 %collective-permute-done.refs_0_.refs_3_.refs_4_ = f32[2,4,128,256]{3,2,1,0:T(8,128)S(1)} collective-permute-done((f32[2,4,128,256]{3,2,1,0:T(8,128)S(1)}, f32[2,4,128,256]{3,2,1,0:T(8,128)S(1)}, u32[]{:S(2)}, u32[]{:S(2)}) %collective-permute-start) | collective-permute-done | bytes 1048608 | tf_op jit(solution)/shard_map/ppermute | solution.py:349
  30.5 5.7 %collective-permute-start.4 = (f32[4,128,256]{2,1,0:T(8,128)S(1)}, f32[4,128,256]{2,1,0:T(8,128)S(1)}, u32[]{:S(2)}, u32[]{:S(2)}) collective-permute-start(f32[4,128,256]{2,1,0:T(8,128)S(1)} %get-tuple-element.47.refs_1_.refs_10_), channel_id=1, source_target_pairs={{0,1},{1,2},{2,3},{3,4},{4,5},{5,6},{6,7},{7,8},{8,9},{9,10},{10,1... | collective-permute-start | bytes 1572872 | tf_op jit(solution)/shard_map/ppermute | solution.py:349
  36.2 17.9 %collective-permute-done.5.refs_2_ = f32[4,128,256]{2,1,0:T(8,128)S(1)} collective-permute-done((f32[4,128,256]{2,1,0:T(8,128)S(1)}, f32[4,128,256]{2,1,0:T(8,128)S(1)}, u32[]{:S(2)}, u32[]{:S(2)}) %collective-permute-start.5) | collective-permute-done | bytes 524320 | tf_op jit(solution)/shard_map/ppermute | solution.py:349
  54.1 3.8 %collective-permute-done.4.refs_0_ = f32[4,128,256]{2,1,0:T(8,128)S(1)} collective-permute-done((f32[4,128,256]{2,1,0:T(8,128)S(1)}, f32[4,128,256]{2,1,0:T(8,128)S(1)}, u32[]{:S(2)}, u32[]{:S(2)}) %collective-permute-start.4) | collective-permute-done | bytes 524320 | tf_op jit(solution)/shard_map/ppermute | solution.py:349
  67.2 4.3 %collective-permute-start.6 = (f32[2,4,128,256]{3,2,1,0:T(8,128)S(1)}, f32[2,4,128,256]{3,2,1,0:T(8,128)S(1)}, u32[]{:S(2)}, u32[]{:S(2)}) collective-permute-start(f32[2,4,128,256]{3,2,1,0:T(8,128)S(1)} %born.4.refs_1_.refs_3_.refs_10_), channel_id=1, source_target_pairs={{0,1},{1,2},{2,3},{3,4},{4,5},{5,6},{6,7},{7,8},{8,9},{9,10},{10,1... | collective-permute-start | bytes 3145736 | tf_op jit(solution)/shard_map/ppermute | solution.py:349
  71.5 6.5 %collective-permute-start.8 = (f32[4,128,256]{2,1,0:T(8,128)S(1)}, f32[4,128,256]{2,1,0:T(8,128)S(1)}, u32[]{:S(2)}, u32[]{:S(2)}) collective-permute-start(f32[4,128,256]{2,1,0:T(8,128)S(1)} %get-tuple-element.50.refs_1_), channel_id=1, source_target_pairs={{0,1},{1,2},{2,3},{3,4},{4,5},{5,6},{6,7},{7,8},{8,9},{9,10},{10,1... | collective-permute-start | bytes 1572872 | tf_op jit(solution)/shard_map/ppermute | solution.py:349
  82.9 9.3 %collective-permute-start.23 = (f32[2,4,128,256]{3,2,1,0:T(8,128)S(1)}, f32[2,4,128,256]{3,2,1,0:T(8,128)S(1)}, u32[]{:S(2)}, u32[]{:S(2)}) collective-permute-start(f32[2,4,128,256]{3,2,1,0:T(8,128)S(1)} %born.6.refs_1_.refs_3_.refs_10_), channel_id=1, source_target_pairs={{0,1},{1,2},{2,3},{3,4},{4,5},{5,6},{6,7},{7,8},{8,9},{9,10},{10,1... | collective-permute-start | bytes 3145736 | tf_op jit(solution)/shard_map/ppermute | solution.py:349
  104.5 6.0 %collective-permute-start.10 = (f32[2,4,128,256]{3,2,1,0:T(8,128)S(1)}, f32[2,4,128,256]{3,2,1,0:T(8,128)S(1)}, u32[]{:S(2)}, u32[]{:S(2)}) collective-permute-start(f32[2,4,128,256]{3,2,1,0:T(8,128)S(1)} %born.5.refs_1_.refs_9_), channel_id=1, source_target_pairs={{0,1},{1,2},{2,3},{3,4},{4,5},{5,6},{6,7},{7,8},{8,9},{9,10},{10,1... | collective-permute-start | bytes 3145736 | tf_op jit(solution)/shard_map/ppermute | solution.py:349
  117.0 5.8 %collective-permute-start.25 = (f32[2,4,128,256]{3,2,1,0:T(8,128)S(1)}, f32[2,4,128,256]{3,2,1,0:T(8,128)S(1)}, u32[]{:S(2)}, u32[]{:S(2)}) collective-permute-start(f32[2,4,128,256]{3,2,1,0:T(8,128)S(1)} %born.7.refs_1_.refs_9_), channel_id=1, source_target_pairs={{0,1},{1,2},{2,3},{3,4},{4,5},{5,6},{6,7},{7,8},{8,9},{9,10},{10,1... | collective-permute-start | bytes 3145736 | tf_op jit(solution)/shard_map/ppermute | solution.py:349
  127.8 5.8 %collective-permute-start.14 = (f32[2,4,128,256]{3,2,1,0:T(8,128)S(1)}, f32[2,4,128,256]{3,2,1,0:T(8,128)S(1)}, u32[]{:S(2)}, u32[]{:S(2)}) collective-permute-start(f32[2,4,128,256]{3,2,1,0:T(8,128)S(1)} %turn.2.refs_1_.refs_3_), channel_id=1, source_target_pairs={{0,1},{1,2},{2,3},{3,4},{4,5},{5,6},{6,7},{7,8},{8,9},{9,10},{10,1... | collective-permute-start | bytes 3145736 | tf_op jit(solution)/shard_map/ppermute | solution.py:349
  138.6 6.7 %collective-permute-start.27 = (f32[2,4,128,256]{3,2,1,0:T(8,128)S(1)}, f32[2,4,128,256]{3,2,1,0:T(8,128)S(1)}, u32[]{:S(2)}, u32[]{:S(2)}) collective-permute-start(f32[2,4,128,256]{3,2,1,0:T(8,128)S(1)} %turn.3.refs_1_.refs_3_), channel_id=1, source_target_pairs={{0,1},{1,2},{2,3},{3,4},{4,5},{5,6},{6,7},{7,8},{8,9},{9,10},{10,1... | collective-permute-start | bytes 3145736 | tf_op jit(solution)/shard_map/ppermute | solution.py:349
  150.1 6.7 %collective-permute-start.16 = (f32[2,4,128,256]{3,2,1,0:T(8,128)S(1)}, f32[2,4,128,256]{3,2,1,0:T(8,128)S(1)}, u32[]{:S(2)}, u32[]{:S(2)}) collective-permute-start(f32[2,4,128,256]{3,2,1,0:T(8,128)S(1)} %adjoint.2.refs_1_), channel_id=1, source_target_pairs={{0,1},{1,2},{2,3},{3,4},{4,5},{5,6},{6,7},{7,8},{8,9},{9,10},{10,1... | collective-permute-start | bytes 3145736 | tf_op jit(solution)/shard_map/ppermute | solution.py:349
  161.7 6.6 %collective-permute-start.29 = (f32[2,4,128,256]{3,2,1,0:T(8,128)S(1)}, f32[2,4,128,256]{3,2,1,0:T(8,128)S(1)}, u32[]{:S(2)}, u32[]{:S(2)}) collective-permute-start(f32[2,4,128,256]{3,2,1,0:T(8,128)S(1)} %adjoint.3.refs_1_), channel_id=1, source_target_pairs={{0,1},{1,2},{2,3},{3,4},{4,5},{5,6},{6,7},{7,8},{8,9},{9,10},{10,1... | collective-permute-start | bytes 3145736 | tf_op jit(solution)/shard_map/ppermute | solution.py:349
  168.4 4.6 %fold.2 = (f32[2,4,128,256]{3,2,1,0:T(8,128)}, f32[2,4,128,256]{3,2,1,0:T(8,128)S(1)}, f32[4,128,256]{2,1,0:T(8,128)S(1)}, f32[4,128,256]{2,1,0:T(8,128)S(1)}) custom-call(f32[2,4,128,256]{3,2,1,0:T(8,128)S(1)} %collective-permute-done.16.refs_0_, f32[2,4,128,256]{3,2,1,0:T(8,128)S(1)} %adjoint.2.refs_1_, ...), custom_call_target="tpu_custom_call" | custom-call | flops 15728640 | bytes 7340032 | tf_op jit(solution)/shard_map/fold/pallas_call | solution.py:495
  174.9 6.5 %collective-permute-start.18 = (f32[2,4,128,256]{3,2,1,0:T(8,128)}, f32[2,4,128,256]{3,2,1,0:T(8,128)}, u32[]{:S(2)}, u32[]{:S(2)}) collective-permute-start(f32[2,4,128,256]{3,2,1,0:T(8,128)} %get-tuple-element.55.refs_1_), channel_id=1, source_target_pairs={{0,1},{1,2},{2,3},{3,4},{4,5},{5,6},{6,7},{7,8},{8,9},{9,10},{10,1... | collective-permute-start | bytes 3145736 | tf_op jit(solution)/shard_map/ppermute | solution.py:349
  181.5 4.4 %fold.3 = (f32[2,4,128,256]{3,2,1,0:T(8,128)}, f32[2,4,128,256]{3,2,1,0:T(8,128)S(1)}) custom-call(f32[2,4,128,256]{3,2,1,0:T(8,128)S(1)} %collective-permute-done.29.refs_0_, f32[2,4,128,256]{3,2,1,0:T(8,128)S(1)} %adjoint.3.refs_1_, f32[2,4,128,256]{3,2,1,0:T(8,128)S(1)} %collective-permute-done.30.refs_2_, f32[2,4,128,256]{3,2,1,0:T(8,128)S(1)} %turn.3.refs_1_.refs_3_, ...), custom_call_target="tpu_custom_call" | custom-call | flops 15728640 | bytes 7340032 | tf_op jit(solution)/shard_map/fold/pallas_call | solution.py:495
  188.7 6.4 %collective-permute-start.31 = (f32[2,4,128,256]{3,2,1,0:T(8,128)}, f32[2,4,128,256]{3,2,1,0:T(8,128)}, u32[]{:S(2)}, u32[]{:S(2)}) collective-permute-start(f32[2,4,128,256]{3,2,1,0:T(8,128)} %get-tuple-element.64.refs_1_), channel_id=1, source_target_pairs={{0,1},{1,2},{2,3},{3,4},{4,5},{5,6},{6,7},{7,8},{8,9},{9,10},{10,1... | collective-permute-start | bytes 3145736 | tf_op jit(solution)/shard_map/ppermute | solution.py:349
  199.5 4.5 %image.2 = (f32[2,4,32,256]{3,2,1,0:T(8,128)S(1)}, f32[2,4,32,256]{3,2,1,0:T(8,128)S(1)}, f32[2,4,32,256]{3,2,1,0:T(8,128)S(1)}, f32[2,4,32,256]{3,2,1,0:T(8,128)S(1)}) custom-call(f32[2,4,128,256]{3,2,1,0:T(8,128)} %collective-permute-done.18.refs_0_, f32[2,4,128,256]{3,2,1,0:T(8,128)} %get-tuple-element.55.refs_1_, ...), custom_call_target="tpu_custom_call" | custom-call | flops 15728640 | bytes 7340032 | tf_op jit(solution)/shard_map/image/pallas_call | solution.py:495
  210.6 4.4 %image.3 = (f32[2,4,32,256]{3,2,1,0:T(8,128)S(1)}, f32[2,4,32,256]{3,2,1,0:T(8,128)S(1)}, f32[2,4,32,256]{3,2,1,0:T(8,128)S(1)}, f32[2,4,32,256]{3,2,1,0:T(8,128)S(1)}) custom-call(f32[2,4,128,256]{3,2,1,0:T(8,128)} %collective-permute-done.31.refs_0_, f32[2,4,128,256]{3,2,1,0:T(8,128)} %get-tuple-element.64.refs_1_, ...), custom_call_target="tpu_custom_call" | custom-call | flops 15728640 | bytes 7340032 | tf_op jit(solution)/shard_map/image/pallas_call | solution.py:495
  220.0 9.2 %collective-permute-done.33.refs_5_ = f32[2,4,32,256]{3,2,1,0:T(8,128)S(1)} collective-permute-done((f32[2,4,32,256]{3,2,1,0:T(8,128)S(1)}, f32[2,4,32,256]{3,2,1,0:T(8,128)S(1)}, u32[]{:S(2)}, u32[]{:S(2)}) %collective-permute-start.33) | collective-permute-done | bytes 262176 | tf_op jit(solution)/shard_map/ppermute | solution.py:549
  237.5 3.6 %collective-permute-done.37 = f32[16,16]{1,0:T(8,128)S(1)} collective-permute-done((f32[16,16]{1,0:T(8,128)S(1)}, f32[16,16]{1,0:T(8,128)S(1)}, u32[]{:S(2)}, u32[]{:S(2)}) %collective-permute-start.37) | collective-permute-done | bytes 1056 | tf_op jit(solution)/shard_map/ppermute | solution.py:361
  242.6 3.7 %collective-permute-done.38 = f32[16,16]{1,0:T(8,128)S(1)} collective-permute-done((f32[16,16]{1,0:T(8,128)S(1)}, f32[16,16]{1,0:T(8,128)S(1)}, u32[]{:S(2)}, u32[]{:S(2)}) %collective-permute-start.38) | collective-permute-done | bytes 1056 | tf_op jit(solution)/shard_map/ppermute | solution.py:361
  251.0 4.1 %collective-permute-done.40 = f32[16,16]{1,0:T(8,128)S(1)} collective-permute-done((f32[16,16]{1,0:T(8,128)S(1)}, f32[16,16]{1,0:T(8,128)S(1)}, u32[]{:S(2)}, u32[]{:S(2)}) %collective-permute-start.40) | collective-permute-done | bytes 1056 | tf_op jit(solution)/shard_map/ppermute | solution.py:361
  263.9 5.5 %basis.1 = (f32[16,4,32,256]{3,2,1,0:T(8,128)}, f32[16,16]{1,0:T(8,128)}) custom-call(f32[16,16]{1,0:T(8,128)S(1)} %add.68.gram_ref, f32[16,16]{1,0:T(8,128)S(1)} %get-tuple-element.71.sel_ref, f32[2,4,32,256]{3,2,1,0:T(8,128)S(1)} %get-tuple-element.59.refs_0_, f32[2,4,32,256]{3,2,1,0:T(8,128)S(1)} %collective-permute-done.20.refs_1_, ...), custom_call_target="tpu_custom_call" | custom-call | tf_op jit(solution)/shard_map/basis/pallas_call | solution.py:568
  (136 shorter events, 122.4 us)
Async XLA Ops:
  23.0 36.7 %collective-permute-start.3 = (f32[4,4,128,256]{3,2,1,0:T(8,128)S(1)}, f32[4,4,128,256]{3,2,1,0:T(8,128)S(1)}, u32[]{:S(2)}, u32[]{:S(2)}) collective-permute-start(f32[4,4,128,256]{3,2,1,0:T(8,128)S(1)} %multiply_multiply_fusion.refs_1_.refs_3_.refs_12_), channel_id=1, source_target_pairs={{1,0},{2,1},{3,2},{4,3},{5,4},{6,5},{7,6},{8,7},{9,8},{10,9},{11,1... | collective-permute-start | bytes 6291464 | tf_op jit(solution)/shard_map/ppermute | solution.py:349
  24.9 34.7 %collective-permute-start.2 = (f32[4,4,128,256]{3,2,1,0:T(8,128)S(1)}, f32[4,4,128,256]{3,2,1,0:T(8,128)S(1)}, u32[]{:S(2)}, u32[]{:S(2)}) collective-permute-start(f32[4,4,128,256]{3,2,1,0:T(8,128)S(1)} %multiply_multiply_fusion.refs_1_.refs_3_.refs_12_), channel_id=1, source_target_pairs={{0,1},{1,2},{2,3},{3,4},{4,5},{5,6},{6,7},{7,8},{8,9},{9,10},{10,1... | collective-permute-start | bytes 6291464 | tf_op jit(solution)/shard_map/ppermute | solution.py:349
  27.8 26.3 %collective-permute-start.5 = (f32[4,128,256]{2,1,0:T(8,128)S(1)}, f32[4,128,256]{2,1,0:T(8,128)S(1)}, u32[]{:S(2)}, u32[]{:S(2)}) collective-permute-start(f32[4,128,256]{2,1,0:T(8,128)S(1)} %get-tuple-element.47.refs_1_.refs_10_), channel_id=1, source_target_pairs={{1,0},{2,1},{3,2},{4,3},{5,4},{6,5},{7,6},{8,7},{9,8},{10,9},{11,1... | collective-permute-start | bytes 1572872 | tf_op jit(solution)/shard_map/ppermute | solution.py:349
  30.5 27.4 %collective-permute-start.4 = (f32[4,128,256]{2,1,0:T(8,128)S(1)}, f32[4,128,256]{2,1,0:T(8,128)S(1)}, u32[]{:S(2)}, u32[]{:S(2)}) collective-permute-start(f32[4,128,256]{2,1,0:T(8,128)S(1)} %get-tuple-element.47.refs_1_.refs_10_), channel_id=1, source_target_pairs={{0,1},{1,2},{2,3},{3,4},{4,5},{5,6},{6,7},{7,8},{8,9},{9,10},{10,1... | collective-permute-start | bytes 1572872 | tf_op jit(solution)/shard_map/ppermute | solution.py:349
  62.6 33.3 %collective-permute-start.7 = (f32[2,4,128,256]{3,2,1,0:T(8,128)S(1)}, f32[2,4,128,256]{3,2,1,0:T(8,128)S(1)}, u32[]{:S(2)}, u32[]{:S(2)}) collective-permute-start(f32[2,4,128,256]{3,2,1,0:T(8,128)S(1)} %born.4.refs_1_.refs_3_.refs_10_), channel_id=1, source_target_pairs={{1,0},{2,1},{3,2},{4,3},{5,4},{6,5},{7,6},{8,7},{9,8},{10,9},{11,1... | collective-permute-start | bytes 3145736 | tf_op jit(solution)/shard_map/ppermute | solution.py:349
  64.6 18.3 %collective-permute-start.9 = (f32[4,128,256]{2,1,0:T(8,128)S(1)}, f32[4,128,256]{2,1,0:T(8,128)S(1)}, u32[]{:S(2)}, u32[]{:S(2)}) collective-permute-start(f32[4,128,256]{2,1,0:T(8,128)S(1)} %get-tuple-element.50.refs_1_), channel_id=1, source_target_pairs={{1,0},{2,1},{3,2},{4,3},{5,4},{6,5},{7,6},{8,7},{9,8},{10,9},{11,1... | collective-permute-start | bytes 1572872 | tf_op jit(solution)/shard_map/ppermute | solution.py:349
  67.2 31.9 %collective-permute-start.6 = (f32[2,4,128,256]{3,2,1,0:T(8,128)S(1)}, f32[2,4,128,256]{3,2,1,0:T(8,128)S(1)}, u32[]{:S(2)}, u32[]{:S(2)}) collective-permute-start(f32[2,4,128,256]{3,2,1,0:T(8,128)S(1)} %born.4.refs_1_.refs_3_.refs_10_), channel_id=1, source_target_pairs={{0,1},{1,2},{2,3},{3,4},{4,5},{5,6},{6,7},{7,8},{8,9},{9,10},{10,1... | collective-permute-start | bytes 3145736 | tf_op jit(solution)/shard_map/ppermute | solution.py:349
  71.5 20.7 %collective-permute-start.8 = (f32[4,128,256]{2,1,0:T(8,128)S(1)}, f32[4,128,256]{2,1,0:T(8,128)S(1)}, u32[]{:S(2)}, u32[]{:S(2)}) collective-permute-start(f32[4,128,256]{2,1,0:T(8,128)S(1)} %get-tuple-element.50.refs_1_), channel_id=1, source_target_pairs={{0,1},{1,2},{2,3},{3,4},{4,5},{5,6},{6,7},{7,8},{8,9},{9,10},{10,1... | collective-permute-start | bytes 1572872 | tf_op jit(solution)/shard_map/ppermute | solution.py:349
  80.9 31.2 %collective-permute-start.24 = (f32[2,4,128,256]{3,2,1,0:T(8,128)S(1)}, f32[2,4,128,256]{3,2,1,0:T(8,128)S(1)}, u32[]{:S(2)}, u32[]{:S(2)}) collective-permute-start(f32[2,4,128,256]{3,2,1,0:T(8,128)S(1)} %born.6.refs_1_.refs_3_.refs_10_), channel_id=1, source_target_pairs={{1,0},{2,1},{3,2},{4,3},{5,4},{6,5},{7,6},{8,7},{9,8},{10,9},{11,1... | collective-permute-start | bytes 3145736 | tf_op jit(solution)/shard_map/ppermute | solution.py:349
  82.9 29.2 %collective-permute-start.23 = (f32[2,4,128,256]{3,2,1,0:T(8,128)S(1)}, f32[2,4,128,256]{3,2,1,0:T(8,128)S(1)}, u32[]{:S(2)}, u32[]{:S(2)}) collective-permute-start(f32[2,4,128,256]{3,2,1,0:T(8,128)S(1)} %born.6.refs_1_.refs_3_.refs_10_), channel_id=1, source_target_pairs={{0,1},{1,2},{2,3},{3,4},{4,5},{5,6},{6,7},{7,8},{8,9},{9,10},{10,1... | collective-permute-start | bytes 3145736 | tf_op jit(solution)/shard_map/ppermute | solution.py:349
  102.0 20.8 %collective-permute-start.11 = (f32[2,4,128,256]{3,2,1,0:T(8,128)S(1)}, f32[2,4,128,256]{3,2,1,0:T(8,128)S(1)}, u32[]{:S(2)}, u32[]{:S(2)}) collective-permute-start(f32[2,4,128,256]{3,2,1,0:T(8,128)S(1)} %born.5.refs_1_.refs_9_), channel_id=1, source_target_pairs={{1,0},{2,1},{3,2},{4,3},{5,4},{6,5},{7,6},{8,7},{9,8},{10,9},{11,1... | collective-permute-start | bytes 3145736 | tf_op jit(solution)/shard_map/ppermute | solution.py:349
  104.5 18.3 %collective-permute-start.10 = (f32[2,4,128,256]{3,2,1,0:T(8,128)S(1)}, f32[2,4,128,256]{3,2,1,0:T(8,128)S(1)}, u32[]{:S(2)}, u32[]{:S(2)}) collective-permute-start(f32[2,4,128,256]{3,2,1,0:T(8,128)S(1)} %born.5.refs_1_.refs_9_), channel_id=1, source_target_pairs={{0,1},{1,2},{2,3},{3,4},{4,5},{5,6},{6,7},{7,8},{8,9},{9,10},{10,1... | collective-permute-start | bytes 3145736 | tf_op jit(solution)/shard_map/ppermute | solution.py:349
  115.1 18.5 %collective-permute-start.26 = (f32[2,4,128,256]{3,2,1,0:T(8,128)S(1)}, f32[2,4,128,256]{3,2,1,0:T(8,128)S(1)}, u32[]{:S(2)}, u32[]{:S(2)}) collective-permute-start(f32[2,4,128,256]{3,2,1,0:T(8,128)S(1)} %born.7.refs_1_.refs_9_), channel_id=1, source_target_pairs={{1,0},{2,1},{3,2},{4,3},{5,4},{6,5},{7,6},{8,7},{9,8},{10,9},{11,1... | collective-permute-start | bytes 3145736 | tf_op jit(solution)/shard_map/ppermute | solution.py:349
  125.9 19.4 %collective-permute-start.15 = (f32[2,4,128,256]{3,2,1,0:T(8,128)S(1)}, f32[2,4,128,256]{3,2,1,0:T(8,128)S(1)}, u32[]{:S(2)}, u32[]{:S(2)}) collective-permute-start(f32[2,4,128,256]{3,2,1,0:T(8,128)S(1)} %turn.2.refs_1_.refs_3_), channel_id=1, source_target_pairs={{1,0},{2,1},{3,2},{4,3},{5,4},{6,5},{7,6},{8,7},{9,8},{10,9},{11,1... | collective-permute-start | bytes 3145736 | tf_op jit(solution)/shard_map/ppermute | solution.py:349
  136.7 20.2 %collective-permute-start.28 = (f32[2,4,128,256]{3,2,1,0:T(8,128)S(1)}, f32[2,4,128,256]{3,2,1,0:T(8,128)S(1)}, u32[]{:S(2)}, u32[]{:S(2)}) collective-permute-start(f32[2,4,128,256]{3,2,1,0:T(8,128)S(1)} %turn.3.refs_1_.refs_3_), channel_id=1, source_target_pairs={{1,0},{2,1},{3,2},{4,3},{5,4},{6,5},{7,6},{8,7},{9,8},{10,9},{11,1... | collective-permute-start | bytes 3145736 | tf_op jit(solution)/shard_map/ppermute | solution.py:349
  138.6 18.3 %collective-permute-start.27 = (f32[2,4,128,256]{3,2,1,0:T(8,128)S(1)}, f32[2,4,128,256]{3,2,1,0:T(8,128)S(1)}, u32[]{:S(2)}, u32[]{:S(2)}) collective-permute-start(f32[2,4,128,256]{3,2,1,0:T(8,128)S(1)} %turn.3.refs_1_.refs_3_), channel_id=1, source_target_pairs={{0,1},{1,2},{2,3},{3,4},{4,5},{5,6},{6,7},{7,8},{8,9},{9,10},{10,1... | collective-permute-start | bytes 3145736 | tf_op jit(solution)/shard_map/ppermute | solution.py:349
  148.2 20.1 %collective-permute-start.17 = (f32[2,4,128,256]{3,2,1,0:T(8,128)S(1)}, f32[2,4,128,256]{3,2,1,0:T(8,128)S(1)}, u32[]{:S(2)}, u32[]{:S(2)}) collective-permute-start(f32[2,4,128,256]{3,2,1,0:T(8,128)S(1)} %adjoint.2.refs_1_), channel_id=1, source_target_pairs={{1,0},{2,1},{3,2},{4,3},{5,4},{6,5},{7,6},{8,7},{9,8},{10,9},{11,1... | collective-permute-start | bytes 3145736 | tf_op jit(solution)/shard_map/ppermute | solution.py:349
  150.1 18.2 %collective-permute-start.16 = (f32[2,4,128,256]{3,2,1,0:T(8,128)S(1)}, f32[2,4,128,256]{3,2,1,0:T(8,128)S(1)}, u32[]{:S(2)}, u32[]{:S(2)}) collective-permute-start(f32[2,4,128,256]{3,2,1,0:T(8,128)S(1)} %adjoint.2.refs_1_), channel_id=1, source_target_pairs={{0,1},{1,2},{2,3},{3,4},{4,5},{5,6},{6,7},{7,8},{8,9},{9,10},{10,1... | collective-permute-start | bytes 3145736 | tf_op jit(solution)/shard_map/ppermute | solution.py:349
  159.8 21.6 %collective-permute-start.30 = (f32[2,4,128,256]{3,2,1,0:T(8,128)S(1)}, f32[2,4,128,256]{3,2,1,0:T(8,128)S(1)}, u32[]{:S(2)}, u32[]{:S(2)}) collective-permute-start(f32[2,4,128,256]{3,2,1,0:T(8,128)S(1)} %adjoint.3.refs_1_), channel_id=1, source_target_pairs={{1,0},{2,1},{3,2},{4,3},{5,4},{6,5},{7,6},{8,7},{9,8},{10,9},{11,1... | collective-permute-start | bytes 3145736 | tf_op jit(solution)/shard_map/ppermute | solution.py:349
  161.7 19.7 %collective-permute-start.29 = (f32[2,4,128,256]{3,2,1,0:T(8,128)S(1)}, f32[2,4,128,256]{3,2,1,0:T(8,128)S(1)}, u32[]{:S(2)}, u32[]{:S(2)}) collective-permute-start(f32[2,4,128,256]{3,2,1,0:T(8,128)S(1)} %adjoint.3.refs_1_), channel_id=1, source_target_pairs={{0,1},{1,2},{2,3},{3,4},{4,5},{5,6},{6,7},{7,8},{8,9},{9,10},{10,1... | collective-permute-start | bytes 3145736 | tf_op jit(solution)/shard_map/ppermute | solution.py:349
  173.0 22.1 %collective-permute-start.19 = (f32[2,4,128,256]{3,2,1,0:T(8,128)}, f32[2,4,128,256]{3,2,1,0:T(8,128)}, u32[]{:S(2)}, u32[]{:S(2)}) collective-permute-start(f32[2,4,128,256]{3,2,1,0:T(8,128)} %get-tuple-element.55.refs_1_), channel_id=1, source_target_pairs={{1,0},{2,1},{3,2},{4,3},{5,4},{6,5},{7,6},{8,7},{9,8},{10,9},{11,1... | collective-permute-start | bytes 3145736 | tf_op jit(solution)/shard_map/ppermute | solution.py:349
  174.9 20.2 %collective-permute-start.18 = (f32[2,4,128,256]{3,2,1,0:T(8,128)}, f32[2,4,128,256]{3,2,1,0:T(8,128)}, u32[]{:S(2)}, u32[]{:S(2)}) collective-permute-start(f32[2,4,128,256]{3,2,1,0:T(8,128)} %get-tuple-element.55.refs_1_), channel_id=1, source_target_pairs={{0,1},{1,2},{2,3},{3,4},{4,5},{5,6},{6,7},{7,8},{8,9},{9,10},{10,1... | collective-permute-start | bytes 3145736 | tf_op jit(solution)/shard_map/ppermute | solution.py:349
  186.8 23.8 %collective-permute-start.32 = (f32[2,4,128,256]{3,2,1,0:T(8,128)}, f32[2,4,128,256]{3,2,1,0:T(8,128)}, u32[]{:S(2)}, u32[]{:S(2)}) collective-permute-start(f32[2,4,128,256]{3,2,1,0:T(8,128)} %get-tuple-element.64.refs_1_), channel_id=1, source_target_pairs={{1,0},{2,1},{3,2},{4,3},{5,4},{6,5},{7,6},{8,7},{9,8},{10,9},{11,1... | collective-permute-start | bytes 3145736 | tf_op jit(solution)/shard_map/ppermute | solution.py:349
  188.7 21.9 %collective-permute-start.31 = (f32[2,4,128,256]{3,2,1,0:T(8,128)}, f32[2,4,128,256]{3,2,1,0:T(8,128)}, u32[]{:S(2)}, u32[]{:S(2)}) collective-permute-start(f32[2,4,128,256]{3,2,1,0:T(8,128)} %get-tuple-element.64.refs_1_), channel_id=1, source_target_pairs={{0,1},{1,2},{2,3},{3,4},{4,5},{5,6},{6,7},{7,8},{8,9},{9,10},{10,1... | collective-permute-start | bytes 3145736 | tf_op jit(solution)/shard_map/ppermute | solution.py:349
  (41 other events, 471.7 us)

commit v8 on v7

--- a/solution.py
+++ b/solution.py
@@ -123,6 +123,41 @@
     taper_ref[...] = 1.0 - DAMPING * mask_ref[...].astype(jnp.float32)
 
 
+def marks_kernel(cells_ref, line_ref, column_ref):
+    cells = cells_ref[...]
+    columns = column_ref.shape[0]
+    line = lax.broadcasted_iota(jnp.int32, line_ref.shape, 0) == cells // columns
+    column = lax.broadcasted_iota(jnp.int32, column_ref.shape, 0) == cells % columns
+    line_ref[...] = jnp.where(line, 1.0, 0.0).astype(jnp.bfloat16)
+    column_ref[...] = jnp.where(column, 1.0, 0.0)
+
+
+def halves(values):
+    high = values.astype(jnp.bfloat16)
+    return high, (values - high.astype(jnp.float32)).astype(jnp.bfloat16)
+
+
+def read_at(field, line_ref, column_ref):
+    total = None
+    for part in halves(field):
+        lines = lax.dot_general(
+            part, line_ref[...], (((0,), (0,)), ((), ())), preferred_element_type=jnp.float32
+        )
+        total = lines if total is None else total + lines
+    return jnp.sum(total * column_ref[...], axis=0, keepdims=True)
+
+
+def add_at(records, line_ref, column_ref):
+    total = None
+    for part in halves(records):
+        spread = (column_ref[...] * part.astype(jnp.float32)).astype(jnp.bfloat16)
+        field = lax.dot_general(
+            line_ref[...], spread, (((1,), (1,)), ((), ())), preferred_element_type=jnp.float32
+        )
+        total = field if total is None else total + field
+    return total
+
+
 def background_kernel(weight, first, last, *refs):
     refs = list(refs)
     u = [refs.pop(0) for _ in range(3)]
@@ -186,11 +221,21 @@
         sum_ref, me_ref, weight_ref, near_ref = (refs.pop(0) for _ in range(4))
     else:
         taper_ref, add_ref, lap_ref = (refs.pop(0) for _ in range(3))
-    count_ref = refs.pop(0) if mode == "turn" else None
+    if mode in ("turn", "read"):
+        count_ref = refs.pop(0)
+    if mode == "read":
+        line_ref, column_ref = refs.pop(0), refs.pop(0)
+    if mode == "spread":
+        marks = [refs.pop(0) for _ in range(4)]
     if mode == "fold":
         first_ref = refs.pop(0)
         laps = [refs.pop(0) for _ in range(4)]
     mx_ref, my_ref = refs.pop(0), refs.pop(0)
+    if mode == "spread":
+        *refs, low_ref, high_ref = refs
+        low_ref[...] = add_at(p[0][...], *marks[:2]).reshape(low_ref.shape)
+        high_ref[...] = add_at(p[2][...], *marks[2:]).reshape(high_ref.shape)
+        p = [low_ref, p[1], high_ref]
     y_ref, a_ref = refs[-2:]
     outs = refs[:-2]
 
@@ -222,11 +267,13 @@
                 total = total - old
             taper = taper_ref[spot]
             added = add_ref[spot] * lap_ref[spot]
-            if mode in ("born", "turn"):
+            if mode in ("born", "turn", "read"):
                 new = taper * (total + added)
             else:
                 new = taper * total + added
-            if mode == "turn":
+            if mode == "read":
+                a_ref[0, layer, at, columns] = new
+            if mode in ("turn", "read"):
                 new = count_ref[spot] * new
             outs[0][spot] = new
             if mode == "fold":
@@ -246,6 +293,8 @@
             tiles(per, columns, functools.partial(body, block), owner * per)
     else:
         tiles(rows, columns, functools.partial(body, 0))
+    if mode == "read":
+        outs[1][...] = read_at(a_ref[0].reshape(-1, columns), line_ref, column_ref)
 
 
 def piece_of(pieces, parts, c):
@@ -416,6 +465,22 @@
         absorb_mask,
         *copied,
     )
+
+    def marks(cells):
+        return pl.pallas_call(
+            marks_kernel,
+            out_shape=(
+                matrix(layers * rows, receivers),
+                jax.ShapeDtypeStruct((columns, receivers), f32),
+            ),
+            compiler_params=params(),
+            name="marks",
+        )(cells)
+
+    cells = receiver_cells.reshape(1, -1)
+    receivers = cells.shape[-1]
+    at_mine = marks(cells)
+    at_low, at_high = (marks(other) for other in halo(cells))
 
     def flat(array):
         return array, whole(array.shape)
@@ -458,27 +523,37 @@
             older, current = current, flat(results[1])
             fields.append(results[1])
         if first:
-            dg = results[2]
-
-    def wave(mode, group, p, old, add, lap, extra=(), ends=None):
-        low, high = ends or halo(p)
+            dg = after(results[2], (at_mine, at_low, at_high))
+
+    def wave(mode, group, p, old, add, lap, extra=(), records=None, wait=None):
+        low, high = halo(p if records is None else records)
+        if wait is not None:
+            low = after(low, wait)
         one = pl.BlockSpec((None, *shape), lambda d: (d, 0, 0, 0))
         shifted = pl.BlockSpec((None, *shape), lambda d: (d + group * each, 0, 0, 0))
         same = whole(shape)
-        operands, specs = [low, p, high], [shifted if ends else one] * 3
+        heard = pl.BlockSpec((None, 1, receivers), lambda d: (d, 0, 0))
+        side = one if records is None else heard
+        operands, specs = [low, p, high], [side, one, side]
         if old is not None:
             operands.append(old)
-            specs.append(one if old.shape[0] == each else shifted)
+            specs.append(one)
         operands += [array for array, _ in buoy] + [dg, stiffness]
         specs += [spec for _, spec in buoy] + [same] * 2
         if mode != "image":
             operands += [taper, add, lap]
-            specs += [same, shifted if mode in ("born", "turn") else one, same]
-        if mode == "turn":
+            specs += [same, shifted if mode in ("born", "turn", "read") else one, same]
+        if mode in ("turn", "read"):
             operands.append(counts)
             specs.append(same)
+        if mode == "read":
+            operands += at_mine
+            specs += [whole(mark.shape) for mark in at_mine]
+        if mode == "spread":
+            operands += [*at_low, *at_high]
+            specs += [whole(mark.shape) for mark in (*at_low, *at_high)]
         if mode == "fold":
-            specs += [shifted] + [same] * 4
+            specs += [one] + [same] * 4
         if mode == "image":
             specs += [one, pl.BlockSpec(memory_space=pltpu.SMEM)] + [same] * 2
         operands += [*extra, mx, my2]
@@ -488,6 +563,9 @@
             out_shape, out_spec = out_shape * 2, out_spec * 2
             if group == 0:
                 out_shape, out_spec = out_shape + (field,) * 2, out_spec + [same] * 2
+        if mode == "read":
+            out_shape += (jax.ShapeDtypeStruct((each, 1, receivers), f32),)
+            out_spec = out_spec + [heard]
         if mode == "image":
             split = (layers, rows // owners, columns)
             out_shape = (jax.ShapeDtypeStruct((each, *split), f32),) * owners
@@ -501,7 +579,8 @@
             scratch_shapes=[
                 pltpu.VMEM((2, layers, 2 * rows, columns), jnp.bfloat16),
                 pltpu.VMEM((2, layers, rows, columns), f32),
-            ],
+            ]
+            + [pltpu.VMEM(shape, f32)] * (2 if mode == "spread" else 0),
             compiler_params=params(),
             cost_estimate=pl.CostEstimate(
                 flops=60 * each * cells_here,
@@ -513,28 +592,30 @@
         return results[0] if len(results) == 1 else results
 
     born = [[None] * GROUPS for _ in range(STEPS + 1)]
-    begun = taper * (perturbations * laps[0])
-    ends = halo(begun)
-    ahead = {(3, 0): fields[3], (3, 1): laps[3]}
+    for g in range(GROUPS):
+        born[1][g] = taper * (perturbations[g * each : (g + 1) * each] * laps[0])
+    born[1][1] = after(born[1][1], fields[2])
+    ahead = {(2, 1): fields[3], (3, 1): laps[3]}
     for t in (1, 2):
         for g in range(GROUPS):
-            if t == 1:
-                new = wave("born", g, begun, None, perturbations, laps[1], ends=ends)
-            else:
-                old = begun if t == 2 else born[t - 1][g]
-                new = wave("born", g, born[t][g], old, perturbations, laps[t])
+            old = born[t - 1][g] if t > 1 else None
+            new = wave("born", g, born[t][g], old, perturbations, laps[t])
             if (t + 1, g) in ahead:
                 new = after(new, ahead[t + 1, g])
             born[t + 1][g] = new
     adjoint = [[None] * GROUPS for _ in range(STEPS + 1)]
-    for g in range(GROUPS):
-        adjoint[3][g] = wave("turn", g, born[3][g], born[2][g], perturbations, laps[3])
-    for g in range(GROUPS):
-        adjoint[2][g] = wave("adjoint", g, adjoint[3][g], None, born[3][g], counts)
+    adjoint[3][0] = wave("turn", 0, born[3][0], born[2][0], perturbations, laps[3])
+    adjoint[3][1], records = wave("read", 1, born[3][1], born[2][1], perturbations, laps[3])
+    adjoint[2][0] = wave("adjoint", 0, adjoint[3][0], None, born[3][0], counts)
+    adjoint[2][1] = wave(
+        "spread", 1, adjoint[3][1], None, born[3][1], counts,
+        records=records, wait=adjoint[2][0],
+    )
     known = [None] * GROUPS
     for g in range(GROUPS):
         adjoint[1][g], known[g], *rest = wave(
-            "fold", g, adjoint[2][g], adjoint[3][g], born[2][g], counts, (begun, *laps)
+            "fold", g, adjoint[2][g], adjoint[3][g], born[2][g], counts, (born[1][g], *laps),
+            wait=adjoint[1][g - 1] if g else None,
         )
         if g == 0:
             weight, near = rest

time: 273 us -> 309 us (1.13)
  waiting for transfers between devices: 63 us -> 102 us
  starting transfers between devices: 134 us -> 127 us
  Pallas kernels: 59 us -> 63.5 us
    ppermute x15 -> x17, waiting for transfers between devices: 21.5 us -> 52.8 us  [halo(): lax.ppermute(block, 'slab', backward)]
    ppermute x15 -> x17, starting transfers between devices: 84.2 us -> 64.5 us  [halo(): lax.ppermute(block, 'slab', forward)]
    ppermute x15 -> x17, starting transfers between devices: 31 us -> 45.7 us  [halo(): lax.ppermute(block, 'slab', backward)]
    ppermute x15 -> x17, waiting for transfers between devices: 7.68 us -> 13.9 us  [halo(): lax.ppermute(block, 'slab', forward)]
    pallas_call x12, Pallas kernels: 41.8 us -> 45.5 us  [wave(): pl.pallas_call(functools.partial(wave_kernel, mode, old is not None), gri...]
    unnamed x44 -> x40, local copies, waits for them, and re-layouts: 10.5 us -> 11.6 us
  transfers between devices with their start and end apart: 43 -> 47, of which waited for: 16 -> 25; matrix products, arithmetic and copies ran while one was open for 0% -> 0% of each run, Pallas kernels for 17% -> 16%
where the time goes in v8:
time: 309 us; the launch traced here: 308 us
  starting transfers between devices  127 us (41%)
  waiting for transfers between devices  102 us (33%)
  Pallas kernels  63.5 us (21%)
  local copies, waits for them, and re-layouts  11.6 us (4%)
    ppermute x17, starting transfers between devices, halo(): lax.ppermute(block, 'slab', forward)  64.5 us
    ppermute x17, waiting for transfers between devices, halo(): lax.ppermute(block, 'slab', backward)  52.8 us
    ppermute x17, starting transfers between devices, halo(): lax.ppermute(block, 'slab', backward)  45.7 us
    pallas_call x12, Pallas kernels, wave(): pl.pallas_call(functools.partial(wave_kernel, mode, old is not None), gri...  45.5 us
    ppermute x7, waiting for transfers between devices, add_up(): lax.ppermute(value, axis, [(i, i ^ stride) for i in range(size)])  22.6 us
    ppermute x17, waiting for transfers between devices, halo(): lax.ppermute(block, 'slab', forward)  13.9 us
    ppermute x6, waiting for transfers between devices, shards(): sketch.append(lax.ppermute(blocks[s], 'dirs', ring))  13.1 us
    unnamed x40, local copies, waits for them, and re-layouts  11.6 us
  transfers between devices with their start and end apart: 47, of which 25 were waited for; matrix products, arithmetic and copies ran while one was open for 0% of the time, Pallas kernels for 16%

profile of v8, /device:TPU:14, one launch (start us, length us, event | category | flops | bytes accessed | tf_op | source)
XLA Modules:
  0.0 307.6 jit_solution(4816191355061830751)
XLA Ops:
  14.2 4.0 %collective-permute-done.refs_0_.refs_3_.refs_4_ = f32[2,4,128,256]{3,2,1,0:T(8,128)S(1)} collective-permute-done((f32[2,4,128,256]{3,2,1,0:T(8,128)S(1)}, f32[2,4,128,256]{3,2,1,0:T(8,128)S(1)}, u32[]{:S(2)}, u32[]{:S(2)}) %collective-permute-start) | collective-permute-done | bytes 1048608 | tf_op jit(solution)/shard_map/ppermute | solution.py:398
  22.5 5.8 %collective-permute-start.2 = (f32[2,4,128,256]{3,2,1,0:T(8,128)S(1)}, f32[2,4,128,256]{3,2,1,0:T(8,128)S(1)}, u32[]{:S(2)}, u32[]{:S(2)}) collective-permute-start(f32[2,4,128,256]{3,2,1,0:T(8,128)S(1)} %get-tuple-element.95.refs_1_.refs_3_.refs_12_), channel_id=1, source_target_pairs={{0,1},{1,2},{2,3},{3,4},{4,5},{5,6},{6,7},{7,8},{8,9},{9,10},{10,1... | collective-permute-start | bytes 3145736 | tf_op jit(solution)/shard_map/ppermute | solution.py:398
  35.8 4.0 %collective-permute-start.4 = (s32[1,1024]{1,0:T(1,128)S(1)}, s32[1,1024]{1,0:T(1,128)S(1)}, u32[]{:S(2)}, u32[]{:S(2)}) collective-permute-start(s32[1,1024]{1,0:T(1,128)S(1)} %bitcast.25), channel_id=1, source_target_pairs={{0,1},{1,2},{2,3},{3,4},{4,5},{5,6},{6,7},{7,8},{8,9},{9,10},{10,1... | collective-permute-start | bytes 12296 | tf_op jit(solution)/shard_map/ppermute | solution.py:398
  39.9 4.6 %collective-permute-done.4.cells_ref = s32[1,1024]{1,0:T(1,128)S(1)} collective-permute-done((s32[1,1024]{1,0:T(1,128)S(1)}, s32[1,1024]{1,0:T(1,128)S(1)}, u32[]{:S(2)}, u32[]{:S(2)}) %collective-permute-start.4) | collective-permute-done | bytes 4128 | tf_op jit(solution)/shard_map/ppermute | solution.py:398
  50.3 7.1 %collective-permute-start.10 = (f32[4,128,256]{2,1,0:T(8,128)S(1)}, f32[4,128,256]{2,1,0:T(8,128)S(1)}, u32[]{:S(2)}, u32[]{:S(2)}) collective-permute-start(f32[4,128,256]{2,1,0:T(8,128)S(1)} %get-tuple-element.69.refs_1_), channel_id=1, source_target_pairs={{0,1},{1,2},{2,3},{3,4},{4,5},{5,6},{6,7},{7,8},{8,9},{9,10},{10,1... | collective-permute-start | bytes 1572872 | tf_op jit(solution)/shard_map/ppermute | solution.py:398
  73.6 18.6 %collective-permute-done.11.refs_2_ = f32[4,128,256]{2,1,0:T(8,128)S(1)} collective-permute-done((f32[4,128,256]{2,1,0:T(8,128)S(1)}, f32[4,128,256]{2,1,0:T(8,128)S(1)}, u32[]{:S(2)}, u32[]{:S(2)}) %collective-permute-start.11) | collective-permute-done | bytes 524320 | tf_op jit(solution)/shard_map/ppermute | solution.py:398
  94.0 4.2 %collective-permute-start.14 = (f32[4,128,256]{2,1,0:T(8,128)S(1)}, f32[4,128,256]{2,1,0:T(8,128)S(1)}, u32[]{:S(2)}, u32[]{:S(2)}) collective-permute-start(f32[4,128,256]{2,1,0:T(8,128)S(1)} %get-tuple-element.71.refs_1_), channel_id=1, source_target_pairs={{0,1},{1,2},{2,3},{3,4},{4,5},{5,6},{6,7},{7,8},{8,9},{9,10},{10,1... | collective-permute-start | bytes 1572872 | tf_op jit(solution)/shard_map/ppermute | solution.py:398
  117.3 18.6 %collective-permute-done.15.refs_2_ = f32[4,128,256]{2,1,0:T(8,128)S(1)} collective-permute-done((f32[4,128,256]{2,1,0:T(8,128)S(1)}, f32[4,128,256]{2,1,0:T(8,128)S(1)}, u32[]{:S(2)}, u32[]{:S(2)}) %collective-permute-start.15) | collective-permute-done | bytes 524320 | tf_op jit(solution)/shard_map/ppermute | solution.py:398
  140.6 4.2 %collective-permute-start.29 = (f32[2,4,128,256]{3,2,1,0:T(8,128)S(1)}, f32[2,4,128,256]{3,2,1,0:T(8,128)S(1)}, u32[]{:S(2)}, u32[]{:S(2)}) collective-permute-start(f32[2,4,128,256]{3,2,1,0:T(8,128)S(1)} %born.7.refs_1_.refs_9_), channel_id=1, source_target_pairs={{0,1},{1,2},{2,3},{3,4},{4,5},{5,6},{6,7},{7,8},{8,9},{9,10},{10,1... | collective-permute-start | bytes 3145736 | tf_op jit(solution)/shard_map/ppermute | solution.py:398
  159.0 4.6 %read.1 = (f32[2,4,128,256]{3,2,1,0:T(8,128)S(1)}, f32[2,1,1024]{2,1,0:T(1,128)S(1)}) custom-call(f32[2,4,128,256]{3,2,1,0:T(8,128)S(1)} %collective-permute-done.29.refs_0_, f32[2,4,128,256]{3,2,1,0:T(8,128)S(1)} %born.7.refs_1_.refs_9_, f32[2,4,128,256]{3,2,1,0:T(8,128)S(1)} %collective-permute-done.30.refs_2_, ...), custom_call_target="tpu_custom_call" | custom-call | flops 15728640 | bytes 7340032 | tf_op jit(solution)/shard_map/read/pallas_call | solution.py:573
  163.6 5.9 %collective-permute-start.31 = (f32[2,1,1024]{2,1,0:T(1,128)S(1)}, f32[2,1,1024]{2,1,0:T(1,128)S(1)}, u32[]{:S(2)}, u32[]{:S(2)}) collective-permute-start(f32[2,1,1024]{2,1,0:T(1,128)S(1)} %get-tuple-element.84), channel_id=1, source_target_pairs={{0,1},{1,2},{2,3},{3,4},{4,5},{5,6},{6,7},{7,8},{8,9},{9,10},{10,1... | collective-permute-start | bytes 24584 | tf_op jit(solution)/shard_map/ppermute | solution.py:398
  174.4 4.7 %collective-permute-start.18 = (f32[2,4,128,256]{3,2,1,0:T(8,128)S(1)}, f32[2,4,128,256]{3,2,1,0:T(8,128)S(1)}, u32[]{:S(2)}, u32[]{:S(2)}) collective-permute-start(f32[2,4,128,256]{3,2,1,0:T(8,128)S(1)} %adjoint.1.refs_1_), channel_id=1, source_target_pairs={{0,1},{1,2},{2,3},{3,4},{4,5},{5,6},{6,7},{7,8},{8,9},{9,10},{10,1... | collective-permute-start | bytes 3145736 | tf_op jit(solution)/shard_map/ppermute | solution.py:398
  181.1 5.2 %spread.1.refs_1_ = f32[2,4,128,256]{3,2,1,0:T(8,128)S(1)} custom-call(f32[2,1,1024]{2,1,0:T(1,128)S(1)} %collective-permute-done.31.refs_0_, f32[2,4,128,256]{3,2,1,0:T(8,128)S(1)} %get-tuple-element.86.refs_1_.refs_3_, f32[2,1,1024]{2,1,0:T(1,128)S(1)} %collective-permute-done.32.refs_2_, ...), custom_call_target="tpu_custom_call" | custom-call | flops 15728640 | bytes 7340032 | tf_op jit(solution)/shard_map/spread/pallas_call | solution.py:573
  193.3 4.5 %fold.2 = (f32[2,4,128,256]{3,2,1,0:T(8,128)}, f32[2,4,128,256]{3,2,1,0:T(8,128)S(1)}, f32[4,128,256]{2,1,0:T(8,128)S(1)}, f32[4,128,256]{2,1,0:T(8,128)S(1)}) custom-call(f32[2,4,128,256]{3,2,1,0:T(8,128)S(1)} %collective-permute-done.18.refs_0_, f32[2,4,128,256]{3,2,1,0:T(8,128)S(1)} %adjoint.1.refs_1_, ...), custom_call_target="tpu_custom_call" | custom-call | flops 15728640 | bytes 7340032 | tf_op jit(solution)/shard_map/fold/pallas_call | solution.py:573
  204.6 4.4 %fold.3 = (f32[2,4,128,256]{3,2,1,0:T(8,128)}, f32[2,4,128,256]{3,2,1,0:T(8,128)S(1)}) custom-call(f32[2,4,128,256]{3,2,1,0:T(8,128)S(1)} %collective-permute-done.33.refs_0_, f32[2,4,128,256]{3,2,1,0:T(8,128)S(1)} %spread.1.refs_1_, f32[2,4,128,256]{3,2,1,0:T(8,128)S(1)} %collective-permute-done.34.refs_2_, ...), custom_call_target="tpu_custom_call" | custom-call | flops 15728640 | bytes 7340032 | tf_op jit(solution)/shard_map/fold/pallas_call | solution.py:573
  210.0 8.7 %collective-permute-start.35 = (f32[2,4,128,256]{3,2,1,0:T(8,128)}, f32[2,4,128,256]{3,2,1,0:T(8,128)}, u32[]{:S(2)}, u32[]{:S(2)}) collective-permute-start(f32[2,4,128,256]{3,2,1,0:T(8,128)} %get-tuple-element.88.refs_1_), channel_id=1, source_target_pairs={{0,1},{1,2},{2,3},{3,4},{4,5},{5,6},{6,7},{7,8},{8,9},{9,10},{10,1... | collective-permute-start | bytes 3145736 | tf_op jit(solution)/shard_map/ppermute | solution.py:398
  226.6 6.7 %collective-permute-done.36.refs_2_ = f32[2,4,128,256]{3,2,1,0:T(8,128)} collective-permute-done((f32[2,4,128,256]{3,2,1,0:T(8,128)}, f32[2,4,128,256]{3,2,1,0:T(8,128)}, u32[]{:S(2)}, u32[]{:S(2)}) %collective-permute-start.36) | collective-permute-done | bytes 1048608 | tf_op jit(solution)/shard_map/ppermute | solution.py:398
  237.6 4.4 %image.3 = (f32[2,4,32,256]{3,2,1,0:T(8,128)S(1)}, f32[2,4,32,256]{3,2,1,0:T(8,128)S(1)}, f32[2,4,32,256]{3,2,1,0:T(8,128)S(1)}, f32[2,4,32,256]{3,2,1,0:T(8,128)S(1)}) custom-call(f32[2,4,128,256]{3,2,1,0:T(8,128)} %collective-permute-done.35.refs_0_, f32[2,4,128,256]{3,2,1,0:T(8,128)} %get-tuple-element.88.refs_1_, ...), custom_call_target="tpu_custom_call" | custom-call | flops 15728640 | bytes 7340032 | tf_op jit(solution)/shard_map/image/pallas_call | solution.py:573
  248.7 4.4 %image.2 = (f32[2,4,32,256]{3,2,1,0:T(8,128)S(1)}, f32[2,4,32,256]{3,2,1,0:T(8,128)S(1)}, f32[2,4,32,256]{3,2,1,0:T(8,128)S(1)}, f32[2,4,32,256]{3,2,1,0:T(8,128)S(1)}) custom-call(f32[2,4,128,256]{3,2,1,0:T(8,128)} %collective-permute-done.20.refs_0_, f32[2,4,128,256]{3,2,1,0:T(8,128)} %get-tuple-element.73.refs_1_, ...), custom_call_target="tpu_custom_call" | custom-call | flops 15728640 | bytes 7340032 | tf_op jit(solution)/shard_map/image/pallas_call | solution.py:573
  257.8 9.6 %collective-permute-done.22.refs_1_ = f32[2,4,32,256]{3,2,1,0:T(8,128)S(1)} collective-permute-done((f32[2,4,32,256]{3,2,1,0:T(8,128)S(1)}, f32[2,4,32,256]{3,2,1,0:T(8,128)S(1)}, u32[]{:S(2)}, u32[]{:S(2)}) %collective-permute-start.22) | collective-permute-done | bytes 262176 | tf_op jit(solution)/shard_map/ppermute | solution.py:630
  275.6 3.6 %collective-permute-done.41 = f32[16,16]{1,0:T(8,128)S(1)} collective-permute-done((f32[16,16]{1,0:T(8,128)S(1)}, f32[16,16]{1,0:T(8,128)S(1)}, u32[]{:S(2)}, u32[]{:S(2)}) %collective-permute-start.41) | collective-permute-done | bytes 1056 | tf_op jit(solution)/shard_map/ppermute | solution.py:410
  279.3 5.2 %collective-permute-done.42 = f32[16,16]{1,0:T(8,128)S(1)} collective-permute-done((f32[16,16]{1,0:T(8,128)S(1)}, f32[16,16]{1,0:T(8,128)S(1)}, u32[]{:S(2)}, u32[]{:S(2)}) %collective-permute-start.42) | collective-permute-done | bytes 1056 | tf_op jit(solution)/shard_map/ppermute | solution.py:410
  288.8 4.4 %collective-permute-done.44 = f32[16,16]{1,0:T(8,128)S(1)} collective-permute-done((f32[16,16]{1,0:T(8,128)S(1)}, f32[16,16]{1,0:T(8,128)S(1)}, u32[]{:S(2)}, u32[]{:S(2)}) %collective-permute-start.44) | collective-permute-done | bytes 1056 | tf_op jit(solution)/shard_map/ppermute | solution.py:410
  302.1 5.5 %basis.1 = (f32[16,4,32,256]{3,2,1,0:T(8,128)}, f32[16,16]{1,0:T(8,128)}) custom-call(f32[16,16]{1,0:T(8,128)S(1)} %add.68.gram_ref, f32[16,16]{1,0:T(8,128)S(1)} %get-tuple-element.97.sel_ref, f32[2,4,32,256]{3,2,1,0:T(8,128)S(1)} %get-tuple-element.77.refs_0_, f32[2,4,32,256]{3,2,1,0:T(8,128)S(1)} %collective-permute-done.22.refs_1_, ...), custom_call_target="tpu_custom_call" | custom-call | tf_op jit(solution)/shard_map/basis/pallas_call | solution.py:649
  (143 shorter events, 153.2 us)
Async XLA Ops:
  2.1 16.1 %collective-permute-start = (f32[2,4,128,256]{3,2,1,0:T(8,128)S(1)}, f32[2,4,128,256]{3,2,1,0:T(8,128)S(1)}, u32[]{:S(2)}, u32[]{:S(2)}) collective-permute-start(f32[2,4,128,256]{3,2,1,0:T(8,128)S(1)} %pad_maximum_fusion), channel_id=1, source_target_pairs={{0,1},{1,2},{2,3},{3,4},{4,5},{5,6},{6,7},{7,8},{8,9},{9,10},{10,1... | collective-permute-start | bytes 3145736 | tf_op jit(solution)/shard_map/ppermute | solution.py:398
  22.5 40.5 %collective-permute-start.2 = (f32[2,4,128,256]{3,2,1,0:T(8,128)S(1)}, f32[2,4,128,256]{3,2,1,0:T(8,128)S(1)}, u32[]{:S(2)}, u32[]{:S(2)}) collective-permute-start(f32[2,4,128,256]{3,2,1,0:T(8,128)S(1)} %get-tuple-element.95.refs_1_.refs_3_.refs_12_), channel_id=1, source_target_pairs={{0,1},{1,2},{2,3},{3,4},{4,5},{5,6},{6,7},{7,8},{8,9},{9,10},{10,1... | collective-permute-start | bytes 3145736 | tf_op jit(solution)/shard_map/ppermute | solution.py:398
  28.3 34.7 %collective-permute-start.3 = (f32[2,4,128,256]{3,2,1,0:T(8,128)S(1)}, f32[2,4,128,256]{3,2,1,0:T(8,128)S(1)}, u32[]{:S(2)}, u32[]{:S(2)}) collective-permute-start(f32[2,4,128,256]{3,2,1,0:T(8,128)S(1)} %get-tuple-element.95.refs_1_.refs_3_.refs_12_), channel_id=1, source_target_pairs={{1,0},{2,1},{3,2},{4,3},{5,4},{6,5},{7,6},{8,7},{9,8},{10,9},{11,1... | collective-permute-start | bytes 3145736 | tf_op jit(solution)/shard_map/ppermute | solution.py:398
  30.3 18.3 %collective-permute-start.6 = (f32[4,128,256]{2,1,0:T(8,128)S(1)}, f32[4,128,256]{2,1,0:T(8,128)S(1)}, u32[]{:S(2)}, u32[]{:S(2)}) collective-permute-start(f32[4,128,256]{2,1,0:T(8,128)S(1)} %get-tuple-element.66.refs_1_.refs_10_), channel_id=1, source_target_pairs={{0,1},{1,2},{2,3},{3,4},{4,5},{5,6},{6,7},{7,8},{8,9},{9,10},{10,1... | collective-permute-start | bytes 1572872 | tf_op jit(solution)/shard_map/ppermute | solution.py:398
  50.3 21.3 %collective-permute-start.10 = (f32[4,128,256]{2,1,0:T(8,128)S(1)}, f32[4,128,256]{2,1,0:T(8,128)S(1)}, u32[]{:S(2)}, u32[]{:S(2)}) collective-permute-start(f32[4,128,256]{2,1,0:T(8,128)S(1)} %get-tuple-element.69.refs_1_), channel_id=1, source_target_pairs={{0,1},{1,2},{2,3},{3,4},{4,5},{5,6},{6,7},{7,8},{8,9},{9,10},{10,1... | collective-permute-start | bytes 1572872 | tf_op jit(solution)/shard_map/ppermute | solution.py:398
  57.5 40.7 %collective-permute-start.25 = (f32[2,4,128,256]{3,2,1,0:T(8,128)S(1)}, f32[2,4,128,256]{3,2,1,0:T(8,128)S(1)}, u32[]{:S(2)}, u32[]{:S(2)}) collective-permute-start(f32[2,4,128,256]{3,2,1,0:T(8,128)S(1)} %get-tuple-element.81.refs_1_.refs_3_.refs_12_), channel_id=1, source_target_pairs={{0,1},{1,2},{2,3},{3,4},{4,5},{5,6},{6,7},{7,8},{8,9},{9,10},{10,1... | collective-permute-start | bytes 3145736 | tf_op jit(solution)/shard_map/ppermute | solution.py:398
  59.4 38.8 %collective-permute-start.26 = (f32[2,4,128,256]{3,2,1,0:T(8,128)S(1)}, f32[2,4,128,256]{3,2,1,0:T(8,128)S(1)}, u32[]{:S(2)}, u32[]{:S(2)}) collective-permute-start(f32[2,4,128,256]{3,2,1,0:T(8,128)S(1)} %get-tuple-element.81.refs_1_.refs_3_.refs_12_), channel_id=1, source_target_pairs={{1,0},{2,1},{3,2},{4,3},{5,4},{6,5},{7,6},{8,7},{9,8},{10,9},{11,1... | collective-permute-start | bytes 3145736 | tf_op jit(solution)/shard_map/ppermute | solution.py:398
  66.0 40.7 %collective-permute-start.8 = (f32[2,4,128,256]{3,2,1,0:T(8,128)S(1)}, f32[2,4,128,256]{3,2,1,0:T(8,128)S(1)}, u32[]{:S(2)}, u32[]{:S(2)}) collective-permute-start(f32[2,4,128,256]{3,2,1,0:T(8,128)S(1)} %born.4.refs_1_.refs_3_.refs_10_), channel_id=1, source_target_pairs={{0,1},{1,2},{2,3},{3,4},{4,5},{5,6},{6,7},{7,8},{8,9},{9,10},{10,1... | collective-permute-start | bytes 3145736 | tf_op jit(solution)/shard_map/ppermute | solution.py:398
  68.0 38.8 %collective-permute-start.9 = (f32[2,4,128,256]{3,2,1,0:T(8,128)S(1)}, f32[2,4,128,256]{3,2,1,0:T(8,128)S(1)}, u32[]{:S(2)}, u32[]{:S(2)}) collective-permute-start(f32[2,4,128,256]{3,2,1,0:T(8,128)S(1)} %born.4.refs_1_.refs_3_.refs_10_), channel_id=1, source_target_pairs={{1,0},{2,1},{3,2},{4,3},{5,4},{6,5},{7,6},{8,7},{9,8},{10,9},{11,1... | collective-permute-start | bytes 3145736 | tf_op jit(solution)/shard_map/ppermute | solution.py:398
  71.6 20.6 %collective-permute-start.11 = (f32[4,128,256]{2,1,0:T(8,128)S(1)}, f32[4,128,256]{2,1,0:T(8,128)S(1)}, u32[]{:S(2)}, u32[]{:S(2)}) collective-permute-start(f32[4,128,256]{2,1,0:T(8,128)S(1)} %get-tuple-element.69.refs_1_), channel_id=1, source_target_pairs={{1,0},{2,1},{3,2},{4,3},{5,4},{6,5},{7,6},{8,7},{9,8},{10,9},{11,1... | collective-permute-start | bytes 1572872 | tf_op jit(solution)/shard_map/ppermute | solution.py:398
  94.0 21.4 %collective-permute-start.14 = (f32[4,128,256]{2,1,0:T(8,128)S(1)}, f32[4,128,256]{2,1,0:T(8,128)S(1)}, u32[]{:S(2)}, u32[]{:S(2)}) collective-permute-start(f32[4,128,256]{2,1,0:T(8,128)S(1)} %get-tuple-element.71.refs_1_), channel_id=1, source_target_pairs={{0,1},{1,2},{2,3},{3,4},{4,5},{5,6},{6,7},{7,8},{8,9},{9,10},{10,1... | collective-permute-start | bytes 1572872 | tf_op jit(solution)/shard_map/ppermute | solution.py:398
  101.2 36.3 %collective-permute-start.27 = (f32[2,4,128,256]{3,2,1,0:T(8,128)S(1)}, f32[2,4,128,256]{3,2,1,0:T(8,128)S(1)}, u32[]{:S(2)}, u32[]{:S(2)}) collective-permute-start(f32[2,4,128,256]{3,2,1,0:T(8,128)S(1)} %born.6.refs_1_.refs_3_.refs_10_), channel_id=1, source_target_pairs={{0,1},{1,2},{2,3},{3,4},{4,5},{5,6},{6,7},{7,8},{8,9},{9,10},{10,1... | collective-permute-start | bytes 3145736 | tf_op jit(solution)/shard_map/ppermute | solution.py:398
  103.1 34.4 %collective-permute-start.28 = (f32[2,4,128,256]{3,2,1,0:T(8,128)S(1)}, f32[2,4,128,256]{3,2,1,0:T(8,128)S(1)}, u32[]{:S(2)}, u32[]{:S(2)}) collective-permute-start(f32[2,4,128,256]{3,2,1,0:T(8,128)S(1)} %born.6.refs_1_.refs_3_.refs_10_), channel_id=1, source_target_pairs={{1,0},{2,1},{3,2},{4,3},{5,4},{6,5},{7,6},{8,7},{9,8},{10,9},{11,1... | collective-permute-start | bytes 3145736 | tf_op jit(solution)/shard_map/ppermute | solution.py:398
  109.8 36.9 %collective-permute-start.12 = (f32[2,4,128,256]{3,2,1,0:T(8,128)S(1)}, f32[2,4,128,256]{3,2,1,0:T(8,128)S(1)}, u32[]{:S(2)}, u32[]{:S(2)}) collective-permute-start(f32[2,4,128,256]{3,2,1,0:T(8,128)S(1)} %born.5.refs_1_.refs_9_), channel_id=1, source_target_pairs={{0,1},{1,2},{2,3},{3,4},{4,5},{5,6},{6,7},{7,8},{8,9},{9,10},{10,1... | collective-permute-start | bytes 3145736 | tf_op jit(solution)/shard_map/ppermute | solution.py:398
  111.7 35.0 %collective-permute-start.13 = (f32[2,4,128,256]{3,2,1,0:T(8,128)S(1)}, f32[2,4,128,256]{3,2,1,0:T(8,128)S(1)}, u32[]{:S(2)}, u32[]{:S(2)}) collective-permute-start(f32[2,4,128,256]{3,2,1,0:T(8,128)S(1)} %born.5.refs_1_.refs_9_), channel_id=1, source_target_pairs={{1,0},{2,1},{3,2},{4,3},{5,4},{6,5},{7,6},{8,7},{9,8},{10,9},{11,1... | collective-permute-start | bytes 3145736 | tf_op jit(solution)/shard_map/ppermute | solution.py:398
  115.4 20.5 %collective-permute-start.15 = (f32[4,128,256]{2,1,0:T(8,128)S(1)}, f32[4,128,256]{2,1,0:T(8,128)S(1)}, u32[]{:S(2)}, u32[]{:S(2)}) collective-permute-start(f32[4,128,256]{2,1,0:T(8,128)S(1)} %get-tuple-element.71.refs_1_), channel_id=1, source_target_pairs={{1,0},{2,1},{3,2},{4,3},{5,4},{6,5},{7,6},{8,7},{9,8},{10,9},{11,1... | collective-permute-start | bytes 1572872 | tf_op jit(solution)/shard_map/ppermute | solution.py:398
  140.6 16.3 %collective-permute-start.29 = (f32[2,4,128,256]{3,2,1,0:T(8,128)S(1)}, f32[2,4,128,256]{3,2,1,0:T(8,128)S(1)}, u32[]{:S(2)}, u32[]{:S(2)}) collective-permute-start(f32[2,4,128,256]{3,2,1,0:T(8,128)S(1)} %born.7.refs_1_.refs_9_), channel_id=1, source_target_pairs={{0,1},{1,2},{2,3},{3,4},{4,5},{5,6},{6,7},{7,8},{8,9},{9,10},{10,1... | collective-permute-start | bytes 3145736 | tf_op jit(solution)/shard_map/ppermute | solution.py:398
  149.8 21.7 %collective-permute-start.16 = (f32[2,4,128,256]{3,2,1,0:T(8,128)S(1)}, f32[2,4,128,256]{3,2,1,0:T(8,128)S(1)}, u32[]{:S(2)}, u32[]{:S(2)}) collective-permute-start(f32[2,4,128,256]{3,2,1,0:T(8,128)S(1)} %turn.1.refs_1_.refs_3_), channel_id=1, source_target_pairs={{0,1},{1,2},{2,3},{3,4},{4,5},{5,6},{6,7},{7,8},{8,9},{9,10},{10,1... | collective-permute-start | bytes 3145736 | tf_op jit(solution)/shard_map/ppermute | solution.py:398
  152.2 19.3 %collective-permute-start.17 = (f32[2,4,128,256]{3,2,1,0:T(8,128)S(1)}, f32[2,4,128,256]{3,2,1,0:T(8,128)S(1)}, u32[]{:S(2)}, u32[]{:S(2)}) collective-permute-start(f32[2,4,128,256]{3,2,1,0:T(8,128)S(1)} %turn.1.refs_1_.refs_3_), channel_id=1, source_target_pairs={{1,0},{2,1},{3,2},{4,3},{5,4},{6,5},{7,6},{8,7},{9,8},{10,9},{11,1... | collective-permute-start | bytes 3145736 | tf_op jit(solution)/shard_map/ppermute | solution.py:398
  163.6 17.4 %collective-permute-start.31 = (f32[2,1,1024]{2,1,0:T(1,128)S(1)}, f32[2,1,1024]{2,1,0:T(1,128)S(1)}, u32[]{:S(2)}, u32[]{:S(2)}) collective-permute-start(f32[2,1,1024]{2,1,0:T(1,128)S(1)} %get-tuple-element.84), channel_id=1, source_target_pairs={{0,1},{1,2},{2,3},{3,4},{4,5},{5,6},{6,7},{7,8},{8,9},{9,10},{10,1... | collective-permute-start | bytes 24584 | tf_op jit(solution)/shard_map/ppermute | solution.py:398
  174.4 17.4 %collective-permute-start.18 = (f32[2,4,128,256]{3,2,1,0:T(8,128)S(1)}, f32[2,4,128,256]{3,2,1,0:T(8,128)S(1)}, u32[]{:S(2)}, u32[]{:S(2)}) collective-permute-start(f32[2,4,128,256]{3,2,1,0:T(8,128)S(1)} %adjoint.1.refs_1_), channel_id=1, source_target_pairs={{0,1},{1,2},{2,3},{3,4},{4,5},{5,6},{6,7},{7,8},{8,9},{9,10},{10,1... | collective-permute-start | bytes 3145736 | tf_op jit(solution)/shard_map/ppermute | solution.py:398
  210.0 16.6 %collective-permute-start.35 = (f32[2,4,128,256]{3,2,1,0:T(8,128)}, f32[2,4,128,256]{3,2,1,0:T(8,128)}, u32[]{:S(2)}, u32[]{:S(2)}) collective-permute-start(f32[2,4,128,256]{3,2,1,0:T(8,128)} %get-tuple-element.88.refs_1_), channel_id=1, source_target_pairs={{0,1},{1,2},{2,3},{3,4},{4,5},{5,6},{6,7},{7,8},{8,9},{9,10},{10,1... | collective-permute-start | bytes 3145736 | tf_op jit(solution)/shard_map/ppermute | solution.py:398
  220.7 28.0 %collective-permute-start.20 = (f32[2,4,128,256]{3,2,1,0:T(8,128)}, f32[2,4,128,256]{3,2,1,0:T(8,128)}, u32[]{:S(2)}, u32[]{:S(2)}) collective-permute-start(f32[2,4,128,256]{3,2,1,0:T(8,128)} %get-tuple-element.73.refs_1_), channel_id=1, source_target_pairs={{0,1},{1,2},{2,3},{3,4},{4,5},{5,6},{6,7},{7,8},{8,9},{9,10},{10,1... | collective-permute-start | bytes 3145736 | tf_op jit(solution)/shard_map/ppermute | solution.py:398
  223.1 25.6 %collective-permute-start.21 = (f32[2,4,128,256]{3,2,1,0:T(8,128)}, f32[2,4,128,256]{3,2,1,0:T(8,128)}, u32[]{:S(2)}, u32[]{:S(2)}) collective-permute-start(f32[2,4,128,256]{3,2,1,0:T(8,128)} %get-tuple-element.73.refs_1_), channel_id=1, source_target_pairs={{1,0},{2,1},{3,2},{4,3},{5,4},{6,5},{7,6},{8,7},{9,8},{10,9},{11,1... | collective-permute-start | bytes 3145736 | tf_op jit(solution)/shard_map/ppermute | solution.py:398
  (43 other events, 500.9 us)

commit v9 on v3

--- a/solution.py
+++ b/solution.py
@@ -16,6 +16,7 @@
 GROUPS = 2
 VMEM = 22 * 1024 * 1024
 LANE = 128
+WHOLE = ("born", "turn", "adjoint", "fold", "image")
 
 
 def band(shape, period):
@@ -248,6 +249,12 @@
         tiles(rows, columns, functools.partial(body, 0))
 
 
+def all_waves(mode, has_old, picks, each, *refs):
+    for d in range(each):
+        views = [ref if at is None else ref.at[d + at] for ref, at in zip(refs, picks)]
+        wave_kernel(mode, has_old, *views, *refs[len(picks) :])
+
+
 def piece_of(pieces, parts, c):
     each = pieces[0].shape[0]
     block, rest = divmod(c, parts * each)
@@ -478,11 +485,23 @@
             split = (layers, rows // owners, columns)
             out_shape = (jax.ShapeDtypeStruct((each, *split), f32),) * owners
             out_spec = [pl.BlockSpec((None, *split), lambda d: (d, 0, 0, 0))] * owners
+        kernel, how = functools.partial(wave_kernel, mode, old is not None), {}
+        if mode in WHOLE:
+            picks = [
+                None
+                if not spec.block_shape or spec.block_shape[0] is not None
+                else group * each if spec is shifted else 0
+                for spec in [*specs, *out_spec]
+            ]
+            kernel = functools.partial(all_waves, mode, old is not None, picks, each)
+            memory = [spec.memory_space or pltpu.VMEM for spec in specs]
+            how["in_specs"] = [pl.BlockSpec(memory_space=space) for space in memory]
+            how["out_specs"] = [pl.BlockSpec(memory_space=pltpu.VMEM)] * len(out_spec)
+        else:
+            how = {"grid": (each,), "in_specs": specs, "out_specs": out_spec}
         results = pl.pallas_call(
-            functools.partial(wave_kernel, mode, old is not None),
-            grid=(each,),
-            in_specs=specs,
-            out_specs=out_spec,
+            kernel,
+            **how,
             out_shape=out_shape,
             scratch_shapes=[
                 pltpu.VMEM((2, layers, 2 * rows, columns), jnp.bfloat16),

time: 258 us -> 259 us (level)
  no operation moved by 1% of the time
where the time goes in v9:
time: 259 us; the launch traced here: 257 us
  starting transfers between devices  143 us (55%)
  Pallas kernels  60 us (23%)
  waiting for transfers between devices  41.7 us (16%)
  local copies, waits for them, and re-layouts  10.5 us (4%)
    ppermute x17, starting transfers between devices, halo(): lax.ppermute(block, 'slab', forward)  85.6 us
    pallas_call x12, Pallas kernels, wave(): pl.pallas_call(kernel, **how, out_shape=out_shape, scratch_shapes=[pltpu....  42.9 us
    ppermute x17, starting transfers between devices, halo(): lax.ppermute(block, 'slab', backward)  38.5 us
    ppermute x7, waiting for transfers between devices, add_up(): lax.ppermute(value, axis, [(i, i ^ stride) for i in range(size)])  22 us
    ppermute x6, starting transfers between devices, shards(): sketch.append(lax.ppermute(blocks[s], 'dirs', ring))  11.9 us
    unnamed x34, local copies, waits for them, and re-layouts  10.5 us
    ppermute x6, waiting for transfers between devices, shards(): sketch.append(lax.ppermute(blocks[s], 'dirs', ring))  10.4 us
    pallas_call x4, Pallas kernels, shards(): pl.pallas_call(functools.partial(background_kernel, source_weight(t), fir...  7.41 us
  transfers between devices with their start and end apart: 47, of which 17 were waited for; matrix products, arithmetic and copies ran while one was open for 0% of the time, Pallas kernels for 19%

profile of v9, /device:TPU:14, one launch (start us, length us, event | category | flops | bytes accessed | tf_op | source)
XLA Modules:
  0.0 257.1 jit_solution(1020823016027367390)
XLA Ops:
  2.6 3.6 %collective-permute-start.1 = (f32[4,128,256]{2,1,0:T(8,128)}, f32[4,128,256]{2,1,0:T(8,128)S(1)}, u32[]{:S(2)}, u32[]{:S(2)}) collective-permute-start(f32[4,128,256]{2,1,0:T(8,128)} %refs_2_.1), channel_id=1, source_target_pairs={{1,0},{2,1},{3,2},{4,3},{5,4},{6,5},{7,6},{8,7},{9,8},{10,9},{11,1... | collective-permute-start | bytes 1572872 | tf_op jit(solution)/shard_map/ppermute | solution.py:356
  8.1 3.6 %collective-permute-start.3 = (f32[4,128,256]{2,1,0:T(8,128)}, f32[4,128,256]{2,1,0:T(8,128)S(1)}, u32[]{:S(2)}, u32[]{:S(2)}) collective-permute-start(f32[4,128,256]{2,1,0:T(8,128)} %refs_1_.1), channel_id=1, source_target_pairs={{1,0},{2,1},{3,2},{4,3},{5,4},{6,5},{7,6},{8,7},{9,8},{10,9},{11,1... | collective-permute-start | bytes 1572872 | tf_op jit(solution)/shard_map/ppermute | solution.py:356
  22.5 6.4 %collective-permute-start.6 = (f32[4,128,256]{2,1,0:T(8,128)S(1)}, f32[4,128,256]{2,1,0:T(8,128)S(1)}, u32[]{:S(2)}, u32[]{:S(2)}) collective-permute-start(f32[4,128,256]{2,1,0:T(8,128)S(1)} %get-tuple-element.46.refs_1_.refs_10_), channel_id=1, source_target_pairs={{0,1},{1,2},{2,3},{3,4},{4,5},{5,6},{6,7},{7,8},{8,9},{9,10},{10,1... | collective-permute-start | bytes 1572872 | tf_op jit(solution)/shard_map/ppermute | solution.py:356
  39.3 7.3 %collective-permute-start.25 = (f32[2,4,128,256]{3,2,1,0:T(8,128)S(1)}, f32[2,4,128,256]{3,2,1,0:T(8,128)S(1)}, u32[]{:S(2)}, u32[]{:S(2)}) collective-permute-start(f32[2,4,128,256]{3,2,1,0:T(8,128)S(1)} %get-tuple-element.61.refs_1_.refs_3_.refs_12_), channel_id=1, source_target_pairs={{0,1},{1,2},{2,3},{3,4},{4,5},{5,6},{6,7},{7,8},{8,9},{9,10},{10,1... | collective-permute-start | bytes 3145736 | tf_op jit(solution)/shard_map/ppermute | solution.py:356
  57.0 5.1 %collective-permute-start.8 = (f32[2,4,128,256]{3,2,1,0:T(8,128)S(1)}, f32[2,4,128,256]{3,2,1,0:T(8,128)S(1)}, u32[]{:S(2)}, u32[]{:S(2)}) collective-permute-start(f32[2,4,128,256]{3,2,1,0:T(8,128)S(1)} %born.4.refs_1_.refs_3_.refs_10_), channel_id=1, source_target_pairs={{0,1},{1,2},{2,3},{3,4},{4,5},{5,6},{6,7},{7,8},{8,9},{9,10},{10,1... | collective-permute-start | bytes 3145736 | tf_op jit(solution)/shard_map/ppermute | solution.py:356
  71.1 8.8 %collective-permute-start.27 = (f32[2,4,128,256]{3,2,1,0:T(8,128)S(1)}, f32[2,4,128,256]{3,2,1,0:T(8,128)S(1)}, u32[]{:S(2)}, u32[]{:S(2)}) collective-permute-start(f32[2,4,128,256]{3,2,1,0:T(8,128)S(1)} %born.6.refs_1_.refs_3_.refs_10_), channel_id=1, source_target_pairs={{0,1},{1,2},{2,3},{3,4},{4,5},{5,6},{6,7},{7,8},{8,9},{9,10},{10,1... | collective-permute-start | bytes 3145736 | tf_op jit(solution)/shard_map/ppermute | solution.py:356
  90.4 4.0 %collective-permute-start.12 = (f32[2,4,128,256]{3,2,1,0:T(8,128)S(1)}, f32[2,4,128,256]{3,2,1,0:T(8,128)S(1)}, u32[]{:S(2)}, u32[]{:S(2)}) collective-permute-start(f32[2,4,128,256]{3,2,1,0:T(8,128)S(1)} %born.5.refs_1_.refs_9_), channel_id=1, source_target_pairs={{0,1},{1,2},{2,3},{3,4},{4,5},{5,6},{6,7},{7,8},{8,9},{9,10},{10,1... | collective-permute-start | bytes 3145736 | tf_op jit(solution)/shard_map/ppermute | solution.py:356
  104.4 5.9 %collective-permute-start.29 = (f32[2,4,128,256]{3,2,1,0:T(8,128)S(1)}, f32[2,4,128,256]{3,2,1,0:T(8,128)S(1)}, u32[]{:S(2)}, u32[]{:S(2)}) collective-permute-start(f32[2,4,128,256]{3,2,1,0:T(8,128)S(1)} %born.7.refs_1_.refs_9_), channel_id=1, source_target_pairs={{0,1},{1,2},{2,3},{3,4},{4,5},{5,6},{6,7},{7,8},{8,9},{9,10},{10,1... | collective-permute-start | bytes 3145736 | tf_op jit(solution)/shard_map/ppermute | solution.py:356
  115.5 6.0 %collective-permute-start.16 = (f32[2,4,128,256]{3,2,1,0:T(8,128)S(1)}, f32[2,4,128,256]{3,2,1,0:T(8,128)S(1)}, u32[]{:S(2)}, u32[]{:S(2)}) collective-permute-start(f32[2,4,128,256]{3,2,1,0:T(8,128)S(1)} %turn.2.refs_1_.refs_3_), channel_id=1, source_target_pairs={{0,1},{1,2},{2,3},{3,4},{4,5},{5,6},{6,7},{7,8},{8,9},{9,10},{10,1... | collective-permute-start | bytes 3145736 | tf_op jit(solution)/shard_map/ppermute | solution.py:356
  127.6 6.2 %collective-permute-start.31 = (f32[2,4,128,256]{3,2,1,0:T(8,128)S(1)}, f32[2,4,128,256]{3,2,1,0:T(8,128)S(1)}, u32[]{:S(2)}, u32[]{:S(2)}) collective-permute-start(f32[2,4,128,256]{3,2,1,0:T(8,128)S(1)} %turn.3.refs_1_.refs_3_), channel_id=1, source_target_pairs={{0,1},{1,2},{2,3},{3,4},{4,5},{5,6},{6,7},{7,8},{8,9},{9,10},{10,1... | collective-permute-start | bytes 3145736 | tf_op jit(solution)/shard_map/ppermute | solution.py:356
  138.7 6.2 %collective-permute-start.18 = (f32[2,4,128,256]{3,2,1,0:T(8,128)S(1)}, f32[2,4,128,256]{3,2,1,0:T(8,128)S(1)}, u32[]{:S(2)}, u32[]{:S(2)}) collective-permute-start(f32[2,4,128,256]{3,2,1,0:T(8,128)S(1)} %adjoint.2.refs_1_), channel_id=1, source_target_pairs={{0,1},{1,2},{2,3},{3,4},{4,5},{5,6},{6,7},{7,8},{8,9},{9,10},{10,1... | collective-permute-start | bytes 3145736 | tf_op jit(solution)/shard_map/ppermute | solution.py:356
  151.0 5.9 %collective-permute-start.33 = (f32[2,4,128,256]{3,2,1,0:T(8,128)S(1)}, f32[2,4,128,256]{3,2,1,0:T(8,128)S(1)}, u32[]{:S(2)}, u32[]{:S(2)}) collective-permute-start(f32[2,4,128,256]{3,2,1,0:T(8,128)S(1)} %adjoint.3.refs_1_), channel_id=1, source_target_pairs={{0,1},{1,2},{2,3},{3,4},{4,5},{5,6},{6,7},{7,8},{8,9},{9,10},{10,1... | collective-permute-start | bytes 3145736 | tf_op jit(solution)/shard_map/ppermute | solution.py:356
  159.3 4.7 %fold.2 = (f32[2,4,128,256]{3,2,1,0:T(8,128)}, f32[2,4,128,256]{3,2,1,0:T(8,128)S(1)}, f32[4,128,256]{2,1,0:T(8,128)S(1)}, f32[4,128,256]{2,1,0:T(8,128)S(1)}) custom-call(f32[2,4,128,256]{3,2,1,0:T(8,128)S(1)} %collective-permute-done.18.refs_0_, f32[2,4,128,256]{3,2,1,0:T(8,128)S(1)} %adjoint.2.refs_1_, ...), custom_call_target="tpu_custom_call" | custom-call | flops 15728640 | bytes 7340032 | tf_op jit(solution)/shard_map/fold/pallas_call | solution.py:502
  164.0 5.9 %collective-permute-start.20 = (f32[2,4,128,256]{3,2,1,0:T(8,128)}, f32[2,4,128,256]{3,2,1,0:T(8,128)}, u32[]{:S(2)}, u32[]{:S(2)}) collective-permute-start(f32[2,4,128,256]{3,2,1,0:T(8,128)} %get-tuple-element.53.refs_1_), channel_id=1, source_target_pairs={{0,1},{1,2},{2,3},{3,4},{4,5},{5,6},{6,7},{7,8},{8,9},{9,10},{10,1... | collective-permute-start | bytes 3145736 | tf_op jit(solution)/shard_map/ppermute | solution.py:356
  171.9 4.6 %fold.3 = (f32[2,4,128,256]{3,2,1,0:T(8,128)}, f32[2,4,128,256]{3,2,1,0:T(8,128)S(1)}) custom-call(f32[2,4,128,256]{3,2,1,0:T(8,128)S(1)} %collective-permute-done.33.refs_0_, f32[2,4,128,256]{3,2,1,0:T(8,128)S(1)} %adjoint.3.refs_1_, f32[2,4,128,256]{3,2,1,0:T(8,128)S(1)} %collective-permute-done.34.refs_2_, f32[2,4,128,256]{3,2,1,0:T(8,128)S(1)} %turn.3.refs_1_.refs_3_, ...), custom_call_target="tpu_custom_call" | custom-call | flops 15728640 | bytes 7340032 | tf_op jit(solution)/shard_map/fold/pallas_call | solution.py:502
  177.5 5.2 %collective-permute-start.35 = (f32[2,4,128,256]{3,2,1,0:T(8,128)}, f32[2,4,128,256]{3,2,1,0:T(8,128)}, u32[]{:S(2)}, u32[]{:S(2)}) collective-permute-start(f32[2,4,128,256]{3,2,1,0:T(8,128)} %get-tuple-element.64.refs_1_), channel_id=1, source_target_pairs={{0,1},{1,2},{2,3},{3,4},{4,5},{5,6},{6,7},{7,8},{8,9},{9,10},{10,1... | collective-permute-start | bytes 3145736 | tf_op jit(solution)/shard_map/ppermute | solution.py:356
  186.9 5.0 %image.2 = (f32[2,4,32,256]{3,2,1,0:T(8,128)S(1)}, f32[2,4,32,256]{3,2,1,0:T(8,128)S(1)}, f32[2,4,32,256]{3,2,1,0:T(8,128)S(1)}, f32[2,4,32,256]{3,2,1,0:T(8,128)S(1)}) custom-call(f32[2,4,128,256]{3,2,1,0:T(8,128)} %collective-permute-done.20.refs_0_, f32[2,4,128,256]{3,2,1,0:T(8,128)} %get-tuple-element.53.refs_1_, ...), custom_call_target="tpu_custom_call" | custom-call | flops 15728640 | bytes 7340032 | tf_op jit(solution)/shard_map/image/pallas_call | solution.py:502
  193.9 3.6 %collective-permute-start.23 = (f32[2,4,32,256]{3,2,1,0:T(8,128)S(1)}, f32[2,4,32,256]{3,2,1,0:T(8,128)S(1)}, u32[]{:S(2)}, u32[]{:S(2)}) collective-permute-start(f32[2,4,32,256]{3,2,1,0:T(8,128)S(1)} %get-tuple-element.59), channel_id=1, source_target_pairs={{0,64},{32,96},{64,0},{96,32},{1,65},{33,97},{65,1},{97,33},{2,66}... | collective-permute-start | bytes 786440 | tf_op jit(solution)/shard_map/ppermute | solution.py:556
  198.5 4.9 %image.3 = (f32[2,4,32,256]{3,2,1,0:T(8,128)S(1)}, f32[2,4,32,256]{3,2,1,0:T(8,128)S(1)}, f32[2,4,32,256]{3,2,1,0:T(8,128)S(1)}, f32[2,4,32,256]{3,2,1,0:T(8,128)S(1)}) custom-call(f32[2,4,128,256]{3,2,1,0:T(8,128)} %collective-permute-done.35.refs_0_, f32[2,4,128,256]{3,2,1,0:T(8,128)} %get-tuple-element.64.refs_1_, ...), custom_call_target="tpu_custom_call" | custom-call | flops 15728640 | bytes 7340032 | tf_op jit(solution)/shard_map/image/pallas_call | solution.py:502
  208.8 6.8 %collective-permute-done.37.refs_5_ = f32[2,4,32,256]{3,2,1,0:T(8,128)S(1)} collective-permute-done((f32[2,4,32,256]{3,2,1,0:T(8,128)S(1)}, f32[2,4,32,256]{3,2,1,0:T(8,128)S(1)}, u32[]{:S(2)}, u32[]{:S(2)}) %collective-permute-start.37) | collective-permute-done | bytes 262176 | tf_op jit(solution)/shard_map/ppermute | solution.py:556
  225.1 3.6 %collective-permute-done.41 = f32[16,16]{1,0:T(8,128)S(1)} collective-permute-done((f32[16,16]{1,0:T(8,128)S(1)}, f32[16,16]{1,0:T(8,128)S(1)}, u32[]{:S(2)}, u32[]{:S(2)}) %collective-permute-start.41) | collective-permute-done | bytes 1056 | tf_op jit(solution)/shard_map/ppermute | solution.py:368
  228.8 5.2 %collective-permute-done.42 = f32[16,16]{1,0:T(8,128)S(1)} collective-permute-done((f32[16,16]{1,0:T(8,128)S(1)}, f32[16,16]{1,0:T(8,128)S(1)}, u32[]{:S(2)}, u32[]{:S(2)}) %collective-permute-start.42) | collective-permute-done | bytes 1056 | tf_op jit(solution)/shard_map/ppermute | solution.py:368
  238.3 4.4 %collective-permute-done.44 = f32[16,16]{1,0:T(8,128)S(1)} collective-permute-done((f32[16,16]{1,0:T(8,128)S(1)}, f32[16,16]{1,0:T(8,128)S(1)}, u32[]{:S(2)}, u32[]{:S(2)}) %collective-permute-start.44) | collective-permute-done | bytes 1056 | tf_op jit(solution)/shard_map/ppermute | solution.py:368
  251.6 5.5 %basis.1 = (f32[16,4,32,256]{3,2,1,0:T(8,128)}, f32[16,16]{1,0:T(8,128)}) custom-call(f32[16,16]{1,0:T(8,128)S(1)} %add.68.gram_ref, f32[16,16]{1,0:T(8,128)S(1)} %get-tuple-element.73.sel_ref, f32[2,4,32,256]{3,2,1,0:T(8,128)S(1)} %get-tuple-element.57.refs_0_, f32[2,4,32,256]{3,2,1,0:T(8,128)S(1)} %collective-permute-done.22.refs_1_, ...), custom_call_target="tpu_custom_call" | custom-call | tf_op jit(solution)/shard_map/basis/pallas_call | solution.py:575
  (133 shorter events, 127.2 us)
Async XLA Ops:
  0.6 19.5 %collective-permute-start = (f32[4,128,256]{2,1,0:T(8,128)}, f32[4,128,256]{2,1,0:T(8,128)S(1)}, u32[]{:S(2)}, u32[]{:S(2)}) collective-permute-start(f32[4,128,256]{2,1,0:T(8,128)} %refs_2_.1), channel_id=1, source_target_pairs={{0,1},{1,2},{2,3},{3,4},{4,5},{5,6},{6,7},{7,8},{8,9},{9,10},{10,1... | collective-permute-start | bytes 1572872 | tf_op jit(solution)/shard_map/ppermute | solution.py:356
  2.6 17.6 %collective-permute-start.1 = (f32[4,128,256]{2,1,0:T(8,128)}, f32[4,128,256]{2,1,0:T(8,128)S(1)}, u32[]{:S(2)}, u32[]{:S(2)}) collective-permute-start(f32[4,128,256]{2,1,0:T(8,128)} %refs_2_.1), channel_id=1, source_target_pairs={{1,0},{2,1},{3,2},{4,3},{5,4},{6,5},{7,6},{8,7},{9,8},{10,9},{11,1... | collective-permute-start | bytes 1572872 | tf_op jit(solution)/shard_map/ppermute | solution.py:356
  31.1 20.4 %collective-permute-start.4 = (f32[2,4,128,256]{3,2,1,0:T(8,128)S(1)}, f32[2,4,128,256]{3,2,1,0:T(8,128)S(1)}, u32[]{:S(2)}, u32[]{:S(2)}) collective-permute-start(f32[2,4,128,256]{3,2,1,0:T(8,128)S(1)} %get-tuple-element.71.refs_1_.refs_3_.refs_12_), channel_id=1, source_target_pairs={{0,1},{1,2},{2,3},{3,4},{4,5},{5,6},{6,7},{7,8},{8,9},{9,10},{10,1... | collective-permute-start | bytes 3145736 | tf_op jit(solution)/shard_map/ppermute | solution.py:356
  34.4 19.7 %collective-permute-start.5 = (f32[2,4,128,256]{3,2,1,0:T(8,128)S(1)}, f32[2,4,128,256]{3,2,1,0:T(8,128)S(1)}, u32[]{:S(2)}, u32[]{:S(2)}) collective-permute-start(f32[2,4,128,256]{3,2,1,0:T(8,128)S(1)} %get-tuple-element.71.refs_1_.refs_3_.refs_12_), channel_id=1, source_target_pairs={{1,0},{2,1},{3,2},{4,3},{5,4},{6,5},{7,6},{8,7},{9,8},{10,9},{11,1... | collective-permute-start | bytes 3145736 | tf_op jit(solution)/shard_map/ppermute | solution.py:356
  39.3 28.9 %collective-permute-start.25 = (f32[2,4,128,256]{3,2,1,0:T(8,128)S(1)}, f32[2,4,128,256]{3,2,1,0:T(8,128)S(1)}, u32[]{:S(2)}, u32[]{:S(2)}) collective-permute-start(f32[2,4,128,256]{3,2,1,0:T(8,128)S(1)} %get-tuple-element.61.refs_1_.refs_3_.refs_12_), channel_id=1, source_target_pairs={{0,1},{1,2},{2,3},{3,4},{4,5},{5,6},{6,7},{7,8},{8,9},{9,10},{10,1... | collective-permute-start | bytes 3145736 | tf_op jit(solution)/shard_map/ppermute | solution.py:356
  46.5 21.6 %collective-permute-start.26 = (f32[2,4,128,256]{3,2,1,0:T(8,128)S(1)}, f32[2,4,128,256]{3,2,1,0:T(8,128)S(1)}, u32[]{:S(2)}, u32[]{:S(2)}) collective-permute-start(f32[2,4,128,256]{3,2,1,0:T(8,128)S(1)} %get-tuple-element.61.refs_1_.refs_3_.refs_12_), channel_id=1, source_target_pairs={{1,0},{2,1},{3,2},{4,3},{5,4},{6,5},{7,6},{8,7},{9,8},{10,9},{11,1... | collective-permute-start | bytes 3145736 | tf_op jit(solution)/shard_map/ppermute | solution.py:356
  48.5 15.6 %collective-permute-start.10 = (f32[4,128,256]{2,1,0:T(8,128)S(1)}, f32[4,128,256]{2,1,0:T(8,128)S(1)}, u32[]{:S(2)}, u32[]{:S(2)}) collective-permute-start(f32[4,128,256]{2,1,0:T(8,128)S(1)} %get-tuple-element.49.refs_1_), channel_id=1, source_target_pairs={{0,1},{1,2},{2,3},{3,4},{4,5},{5,6},{6,7},{7,8},{8,9},{9,10},{10,1... | collective-permute-start | bytes 1572872 | tf_op jit(solution)/shard_map/ppermute | solution.py:356
  57.0 27.2 %collective-permute-start.8 = (f32[2,4,128,256]{3,2,1,0:T(8,128)S(1)}, f32[2,4,128,256]{3,2,1,0:T(8,128)S(1)}, u32[]{:S(2)}, u32[]{:S(2)}) collective-permute-start(f32[2,4,128,256]{3,2,1,0:T(8,128)S(1)} %born.4.refs_1_.refs_3_.refs_10_), channel_id=1, source_target_pairs={{0,1},{1,2},{2,3},{3,4},{4,5},{5,6},{6,7},{7,8},{8,9},{9,10},{10,1... | collective-permute-start | bytes 3145736 | tf_op jit(solution)/shard_map/ppermute | solution.py:356
  64.0 23.4 %collective-permute-start.9 = (f32[2,4,128,256]{3,2,1,0:T(8,128)S(1)}, f32[2,4,128,256]{3,2,1,0:T(8,128)S(1)}, u32[]{:S(2)}, u32[]{:S(2)}) collective-permute-start(f32[2,4,128,256]{3,2,1,0:T(8,128)S(1)} %born.4.refs_1_.refs_3_.refs_10_), channel_id=1, source_target_pairs={{1,0},{2,1},{3,2},{4,3},{5,4},{6,5},{7,6},{8,7},{9,8},{10,9},{11,1... | collective-permute-start | bytes 3145736 | tf_op jit(solution)/shard_map/ppermute | solution.py:356
  71.1 30.2 %collective-permute-start.27 = (f32[2,4,128,256]{3,2,1,0:T(8,128)S(1)}, f32[2,4,128,256]{3,2,1,0:T(8,128)S(1)}, u32[]{:S(2)}, u32[]{:S(2)}) collective-permute-start(f32[2,4,128,256]{3,2,1,0:T(8,128)S(1)} %born.6.refs_1_.refs_3_.refs_10_), channel_id=1, source_target_pairs={{0,1},{1,2},{2,3},{3,4},{4,5},{5,6},{6,7},{7,8},{8,9},{9,10},{10,1... | collective-permute-start | bytes 3145736 | tf_op jit(solution)/shard_map/ppermute | solution.py:356
  79.9 21.5 %collective-permute-start.28 = (f32[2,4,128,256]{3,2,1,0:T(8,128)S(1)}, f32[2,4,128,256]{3,2,1,0:T(8,128)S(1)}, u32[]{:S(2)}, u32[]{:S(2)}) collective-permute-start(f32[2,4,128,256]{3,2,1,0:T(8,128)S(1)} %born.6.refs_1_.refs_3_.refs_10_), channel_id=1, source_target_pairs={{1,0},{2,1},{3,2},{4,3},{5,4},{6,5},{7,6},{8,7},{9,8},{10,9},{11,1... | collective-permute-start | bytes 3145736 | tf_op jit(solution)/shard_map/ppermute | solution.py:356
  84.3 15.5 %collective-permute-start.15 = (f32[4,128,256]{2,1,0:T(8,128)S(1)}, f32[4,128,256]{2,1,0:T(8,128)S(1)}, u32[]{:S(2)}, u32[]{:S(2)}) collective-permute-start(f32[4,128,256]{2,1,0:T(8,128)S(1)} %get-tuple-element.51.refs_1_), channel_id=1, source_target_pairs={{1,0},{2,1},{3,2},{4,3},{5,4},{6,5},{7,6},{8,7},{9,8},{10,9},{11,1... | collective-permute-start | bytes 1572872 | tf_op jit(solution)/shard_map/ppermute | solution.py:356
  90.4 22.0 %collective-permute-start.12 = (f32[2,4,128,256]{3,2,1,0:T(8,128)S(1)}, f32[2,4,128,256]{3,2,1,0:T(8,128)S(1)}, u32[]{:S(2)}, u32[]{:S(2)}) collective-permute-start(f32[2,4,128,256]{3,2,1,0:T(8,128)S(1)} %born.5.refs_1_.refs_9_), channel_id=1, source_target_pairs={{0,1},{1,2},{2,3},{3,4},{4,5},{5,6},{6,7},{7,8},{8,9},{9,10},{10,1... | collective-permute-start | bytes 3145736 | tf_op jit(solution)/shard_map/ppermute | solution.py:356
  94.5 17.9 %collective-permute-start.13 = (f32[2,4,128,256]{3,2,1,0:T(8,128)S(1)}, f32[2,4,128,256]{3,2,1,0:T(8,128)S(1)}, u32[]{:S(2)}, u32[]{:S(2)}) collective-permute-start(f32[2,4,128,256]{3,2,1,0:T(8,128)S(1)} %born.5.refs_1_.refs_9_), channel_id=1, source_target_pairs={{1,0},{2,1},{3,2},{4,3},{5,4},{6,5},{7,6},{8,7},{9,8},{10,9},{11,1... | collective-permute-start | bytes 3145736 | tf_op jit(solution)/shard_map/ppermute | solution.py:356
  104.4 19.1 %collective-permute-start.29 = (f32[2,4,128,256]{3,2,1,0:T(8,128)S(1)}, f32[2,4,128,256]{3,2,1,0:T(8,128)S(1)}, u32[]{:S(2)}, u32[]{:S(2)}) collective-permute-start(f32[2,4,128,256]{3,2,1,0:T(8,128)S(1)} %born.7.refs_1_.refs_9_), channel_id=1, source_target_pairs={{0,1},{1,2},{2,3},{3,4},{4,5},{5,6},{6,7},{7,8},{8,9},{9,10},{10,1... | collective-permute-start | bytes 3145736 | tf_op jit(solution)/shard_map/ppermute | solution.py:356
  115.5 20.3 %collective-permute-start.16 = (f32[2,4,128,256]{3,2,1,0:T(8,128)S(1)}, f32[2,4,128,256]{3,2,1,0:T(8,128)S(1)}, u32[]{:S(2)}, u32[]{:S(2)}) collective-permute-start(f32[2,4,128,256]{3,2,1,0:T(8,128)S(1)} %turn.2.refs_1_.refs_3_), channel_id=1, source_target_pairs={{0,1},{1,2},{2,3},{3,4},{4,5},{5,6},{6,7},{7,8},{8,9},{9,10},{10,1... | collective-permute-start | bytes 3145736 | tf_op jit(solution)/shard_map/ppermute | solution.py:356
  127.6 19.3 %collective-permute-start.31 = (f32[2,4,128,256]{3,2,1,0:T(8,128)S(1)}, f32[2,4,128,256]{3,2,1,0:T(8,128)S(1)}, u32[]{:S(2)}, u32[]{:S(2)}) collective-permute-start(f32[2,4,128,256]{3,2,1,0:T(8,128)S(1)} %turn.3.refs_1_.refs_3_), channel_id=1, source_target_pairs={{0,1},{1,2},{2,3},{3,4},{4,5},{5,6},{6,7},{7,8},{8,9},{9,10},{10,1... | collective-permute-start | bytes 3145736 | tf_op jit(solution)/shard_map/ppermute | solution.py:356
  138.7 20.1 %collective-permute-start.18 = (f32[2,4,128,256]{3,2,1,0:T(8,128)S(1)}, f32[2,4,128,256]{3,2,1,0:T(8,128)S(1)}, u32[]{:S(2)}, u32[]{:S(2)}) collective-permute-start(f32[2,4,128,256]{3,2,1,0:T(8,128)S(1)} %adjoint.2.refs_1_), channel_id=1, source_target_pairs={{0,1},{1,2},{2,3},{3,4},{4,5},{5,6},{6,7},{7,8},{8,9},{9,10},{10,1... | collective-permute-start | bytes 3145736 | tf_op jit(solution)/shard_map/ppermute | solution.py:356
  151.0 20.9 %collective-permute-start.33 = (f32[2,4,128,256]{3,2,1,0:T(8,128)S(1)}, f32[2,4,128,256]{3,2,1,0:T(8,128)S(1)}, u32[]{:S(2)}, u32[]{:S(2)}) collective-permute-start(f32[2,4,128,256]{3,2,1,0:T(8,128)S(1)} %adjoint.3.refs_1_), channel_id=1, source_target_pairs={{0,1},{1,2},{2,3},{3,4},{4,5},{5,6},{6,7},{7,8},{8,9},{9,10},{10,1... | collective-permute-start | bytes 3145736 | tf_op jit(solution)/shard_map/ppermute | solution.py:356
  156.9 14.9 %collective-permute-start.34 = (f32[2,4,128,256]{3,2,1,0:T(8,128)S(1)}, f32[2,4,128,256]{3,2,1,0:T(8,128)S(1)}, u32[]{:S(2)}, u32[]{:S(2)}) collective-permute-start(f32[2,4,128,256]{3,2,1,0:T(8,128)S(1)} %adjoint.3.refs_1_), channel_id=1, source_target_pairs={{1,0},{2,1},{3,2},{4,3},{5,4},{6,5},{7,6},{8,7},{9,8},{10,9},{11,1... | collective-permute-start | bytes 3145736 | tf_op jit(solution)/shard_map/ppermute | solution.py:356
  164.0 20.6 %collective-permute-start.20 = (f32[2,4,128,256]{3,2,1,0:T(8,128)}, f32[2,4,128,256]{3,2,1,0:T(8,128)}, u32[]{:S(2)}, u32[]{:S(2)}) collective-permute-start(f32[2,4,128,256]{3,2,1,0:T(8,128)} %get-tuple-element.53.refs_1_), channel_id=1, source_target_pairs={{0,1},{1,2},{2,3},{3,4},{4,5},{5,6},{6,7},{7,8},{8,9},{9,10},{10,1... | collective-permute-start | bytes 3145736 | tf_op jit(solution)/shard_map/ppermute | solution.py:356
  177.5 21.0 %collective-permute-start.35 = (f32[2,4,128,256]{3,2,1,0:T(8,128)}, f32[2,4,128,256]{3,2,1,0:T(8,128)}, u32[]{:S(2)}, u32[]{:S(2)}) collective-permute-start(f32[2,4,128,256]{3,2,1,0:T(8,128)} %get-tuple-element.64.refs_1_), channel_id=1, source_target_pairs={{0,1},{1,2},{2,3},{3,4},{4,5},{5,6},{6,7},{7,8},{8,9},{9,10},{10,1... | collective-permute-start | bytes 3145736 | tf_op jit(solution)/shard_map/ppermute | solution.py:356
  182.7 15.8 %collective-permute-start.36 = (f32[2,4,128,256]{3,2,1,0:T(8,128)}, f32[2,4,128,256]{3,2,1,0:T(8,128)}, u32[]{:S(2)}, u32[]{:S(2)}) collective-permute-start(f32[2,4,128,256]{3,2,1,0:T(8,128)} %get-tuple-element.64.refs_1_), channel_id=1, source_target_pairs={{1,0},{2,1},{3,2},{4,3},{5,4},{6,5},{7,6},{8,7},{9,8},{10,9},{11,1... | collective-permute-start | bytes 3145736 | tf_op jit(solution)/shard_map/ppermute | solution.py:356
  191.9 15.8 %collective-permute-start.22 = (f32[2,4,32,256]{3,2,1,0:T(8,128)S(1)}, f32[2,4,32,256]{3,2,1,0:T(8,128)S(1)}, u32[]{:S(2)}, u32[]{:S(2)}) collective-permute-start(f32[2,4,32,256]{3,2,1,0:T(8,128)S(1)} %get-tuple-element.58), channel_id=1, source_target_pairs={{0,32},{32,64},{64,96},{96,0},{1,33},{33,65},{65,97},{97,1},{2,34}... | collective-permute-start | bytes 786440 | tf_op jit(solution)/shard_map/ppermute | solution.py:556
  (40 other events, 321.1 us)

commit v10 on v3

--- a/solution.py
+++ b/solution.py
@@ -81,7 +81,7 @@
             body(i, at, slice(column, column + LANE))
         return carry
 
-    lax.fori_loop(0, rows // 8, step, 0)
+    lax.fori_loop(0, rows // 8, step, 0, unroll=2)
 
 
 def place_kernel(copies, rc_ref, sc_ref, amp_ref, mask_ref, *refs):

time: 258 us -> 256 us (level)
  Pallas kernels: 58.7 us -> 55.4 us
    pallas_call x12, Pallas kernels: 41.6 us -> 38.8 us  [wave(): pl.pallas_call(functools.partial(wave_kernel, mode, old is not None), gri...]
  transfers between devices with their start and end apart: 47 -> 47, of which waited for: 17 -> 19; matrix products, arithmetic and copies ran while one was open for 0% -> 0% of each run, Pallas kernels for 19% -> 18%
where the time goes in v10:
time: 256 us; the launch traced here: 255 us
  starting transfers between devices  144 us (56%)
  Pallas kernels  55.4 us (22%)
  waiting for transfers between devices  43.3 us (17%)
  local copies, waits for them, and re-layouts  10.5 us (4%)
    ppermute x17, starting transfers between devices, halo(): lax.ppermute(block, 'slab', forward)  85.7 us
    pallas_call x12, Pallas kernels, wave(): pl.pallas_call(functools.partial(wave_kernel, mode, old is not None), gri...  38.8 us
    ppermute x17, starting transfers between devices, halo(): lax.ppermute(block, 'slab', backward)  38.5 us
    ppermute x7, waiting for transfers between devices, add_up(): lax.ppermute(value, axis, [(i, i ^ stride) for i in range(size)])  22 us
    ppermute x6, starting transfers between devices, shards(): sketch.append(lax.ppermute(blocks[s], 'dirs', ring))  12.5 us
    ppermute x6, waiting for transfers between devices, shards(): sketch.append(lax.ppermute(blocks[s], 'dirs', ring))  10.9 us
    unnamed x34, local copies, waits for them, and re-layouts  10.5 us
    ppermute x17, waiting for transfers between devices, halo(): lax.ppermute(block, 'slab', backward)  8.17 us
  transfers between devices with their start and end apart: 47, of which 19 were waited for; matrix products, arithmetic and copies ran while one was open for 0% of the time, Pallas kernels for 18%

profile of v10, /device:TPU:14, one launch (start us, length us, event | category | flops | bytes accessed | tf_op | source)
XLA Modules:
  0.0 254.5 jit_solution(17392932249963768734)
XLA Ops:
  2.6 3.6 %collective-permute-start.1 = (f32[4,128,256]{2,1,0:T(8,128)}, f32[4,128,256]{2,1,0:T(8,128)S(1)}, u32[]{:S(2)}, u32[]{:S(2)}) collective-permute-start(f32[4,128,256]{2,1,0:T(8,128)} %refs_2_.1), channel_id=1, source_target_pairs={{1,0},{2,1},{3,2},{4,3},{5,4},{6,5},{7,6},{8,7},{9,8},{10,9},{11,1... | collective-permute-start | bytes 1572872 | tf_op jit(solution)/shard_map/ppermute | solution.py:349
  8.1 3.6 %collective-permute-start.3 = (f32[4,128,256]{2,1,0:T(8,128)}, f32[4,128,256]{2,1,0:T(8,128)S(1)}, u32[]{:S(2)}, u32[]{:S(2)}) collective-permute-start(f32[4,128,256]{2,1,0:T(8,128)} %refs_1_.1), channel_id=1, source_target_pairs={{1,0},{2,1},{3,2},{4,3},{5,4},{6,5},{7,6},{8,7},{9,8},{10,9},{11,1... | collective-permute-start | bytes 1572872 | tf_op jit(solution)/shard_map/ppermute | solution.py:349
  22.4 6.4 %collective-permute-start.6 = (f32[4,128,256]{2,1,0:T(8,128)S(1)}, f32[4,128,256]{2,1,0:T(8,128)S(1)}, u32[]{:S(2)}, u32[]{:S(2)}) collective-permute-start(f32[4,128,256]{2,1,0:T(8,128)S(1)} %get-tuple-element.46.refs_1_.refs_10_), channel_id=1, source_target_pairs={{0,1},{1,2},{2,3},{3,4},{4,5},{5,6},{6,7},{7,8},{8,9},{9,10},{10,1... | collective-permute-start | bytes 1572872 | tf_op jit(solution)/shard_map/ppermute | solution.py:349
  39.1 7.3 %collective-permute-start.25 = (f32[2,4,128,256]{3,2,1,0:T(8,128)S(1)}, f32[2,4,128,256]{3,2,1,0:T(8,128)S(1)}, u32[]{:S(2)}, u32[]{:S(2)}) collective-permute-start(f32[2,4,128,256]{3,2,1,0:T(8,128)S(1)} %get-tuple-element.61.refs_1_.refs_3_.refs_12_), channel_id=1, source_target_pairs={{0,1},{1,2},{2,3},{3,4},{4,5},{5,6},{6,7},{7,8},{8,9},{9,10},{10,1... | collective-permute-start | bytes 3145736 | tf_op jit(solution)/shard_map/ppermute | solution.py:349
  56.6 5.1 %collective-permute-start.8 = (f32[2,4,128,256]{3,2,1,0:T(8,128)S(1)}, f32[2,4,128,256]{3,2,1,0:T(8,128)S(1)}, u32[]{:S(2)}, u32[]{:S(2)}) collective-permute-start(f32[2,4,128,256]{3,2,1,0:T(8,128)S(1)} %born.4.refs_1_.refs_3_.refs_10_), channel_id=1, source_target_pairs={{0,1},{1,2},{2,3},{3,4},{4,5},{5,6},{6,7},{7,8},{8,9},{9,10},{10,1... | collective-permute-start | bytes 3145736 | tf_op jit(solution)/shard_map/ppermute | solution.py:349
  70.6 8.9 %collective-permute-start.27 = (f32[2,4,128,256]{3,2,1,0:T(8,128)S(1)}, f32[2,4,128,256]{3,2,1,0:T(8,128)S(1)}, u32[]{:S(2)}, u32[]{:S(2)}) collective-permute-start(f32[2,4,128,256]{3,2,1,0:T(8,128)S(1)} %born.6.refs_1_.refs_3_.refs_10_), channel_id=1, source_target_pairs={{0,1},{1,2},{2,3},{3,4},{4,5},{5,6},{6,7},{7,8},{8,9},{9,10},{10,1... | collective-permute-start | bytes 3145736 | tf_op jit(solution)/shard_map/ppermute | solution.py:349
  89.8 4.0 %collective-permute-start.12 = (f32[2,4,128,256]{3,2,1,0:T(8,128)S(1)}, f32[2,4,128,256]{3,2,1,0:T(8,128)S(1)}, u32[]{:S(2)}, u32[]{:S(2)}) collective-permute-start(f32[2,4,128,256]{3,2,1,0:T(8,128)S(1)} %born.5.refs_1_.refs_9_), channel_id=1, source_target_pairs={{0,1},{1,2},{2,3},{3,4},{4,5},{5,6},{6,7},{7,8},{8,9},{9,10},{10,1... | collective-permute-start | bytes 3145736 | tf_op jit(solution)/shard_map/ppermute | solution.py:349
  103.6 5.9 %collective-permute-start.29 = (f32[2,4,128,256]{3,2,1,0:T(8,128)S(1)}, f32[2,4,128,256]{3,2,1,0:T(8,128)S(1)}, u32[]{:S(2)}, u32[]{:S(2)}) collective-permute-start(f32[2,4,128,256]{3,2,1,0:T(8,128)S(1)} %born.7.refs_1_.refs_9_), channel_id=1, source_target_pairs={{0,1},{1,2},{2,3},{3,4},{4,5},{5,6},{6,7},{7,8},{8,9},{9,10},{10,1... | collective-permute-start | bytes 3145736 | tf_op jit(solution)/shard_map/ppermute | solution.py:349
  114.3 6.3 %collective-permute-start.16 = (f32[2,4,128,256]{3,2,1,0:T(8,128)S(1)}, f32[2,4,128,256]{3,2,1,0:T(8,128)S(1)}, u32[]{:S(2)}, u32[]{:S(2)}) collective-permute-start(f32[2,4,128,256]{3,2,1,0:T(8,128)S(1)} %turn.2.refs_1_.refs_3_), channel_id=1, source_target_pairs={{0,1},{1,2},{2,3},{3,4},{4,5},{5,6},{6,7},{7,8},{8,9},{9,10},{10,1... | collective-permute-start | bytes 3145736 | tf_op jit(solution)/shard_map/ppermute | solution.py:349
  126.6 6.0 %collective-permute-start.31 = (f32[2,4,128,256]{3,2,1,0:T(8,128)S(1)}, f32[2,4,128,256]{3,2,1,0:T(8,128)S(1)}, u32[]{:S(2)}, u32[]{:S(2)}) collective-permute-start(f32[2,4,128,256]{3,2,1,0:T(8,128)S(1)} %turn.3.refs_1_.refs_3_), channel_id=1, source_target_pairs={{0,1},{1,2},{2,3},{3,4},{4,5},{5,6},{6,7},{7,8},{8,9},{9,10},{10,1... | collective-permute-start | bytes 3145736 | tf_op jit(solution)/shard_map/ppermute | solution.py:349
  137.7 6.0 %collective-permute-start.18 = (f32[2,4,128,256]{3,2,1,0:T(8,128)S(1)}, f32[2,4,128,256]{3,2,1,0:T(8,128)S(1)}, u32[]{:S(2)}, u32[]{:S(2)}) collective-permute-start(f32[2,4,128,256]{3,2,1,0:T(8,128)S(1)} %adjoint.2.refs_1_), channel_id=1, source_target_pairs={{0,1},{1,2},{2,3},{3,4},{4,5},{5,6},{6,7},{7,8},{8,9},{9,10},{10,1... | collective-permute-start | bytes 3145736 | tf_op jit(solution)/shard_map/ppermute | solution.py:349
  149.5 5.9 %collective-permute-start.33 = (f32[2,4,128,256]{3,2,1,0:T(8,128)S(1)}, f32[2,4,128,256]{3,2,1,0:T(8,128)S(1)}, u32[]{:S(2)}, u32[]{:S(2)}) collective-permute-start(f32[2,4,128,256]{3,2,1,0:T(8,128)S(1)} %adjoint.3.refs_1_), channel_id=1, source_target_pairs={{0,1},{1,2},{2,3},{3,4},{4,5},{5,6},{6,7},{7,8},{8,9},{9,10},{10,1... | collective-permute-start | bytes 3145736 | tf_op jit(solution)/shard_map/ppermute | solution.py:349
  158.1 4.2 %fold.2 = (f32[2,4,128,256]{3,2,1,0:T(8,128)}, f32[2,4,128,256]{3,2,1,0:T(8,128)S(1)}, f32[4,128,256]{2,1,0:T(8,128)S(1)}, f32[4,128,256]{2,1,0:T(8,128)S(1)}) custom-call(f32[2,4,128,256]{3,2,1,0:T(8,128)S(1)} %collective-permute-done.18.refs_0_, f32[2,4,128,256]{3,2,1,0:T(8,128)S(1)} %adjoint.2.refs_1_, ...), custom_call_target="tpu_custom_call" | custom-call | flops 15728640 | bytes 7340032 | tf_op jit(solution)/shard_map/fold/pallas_call | solution.py:481
  162.3 5.9 %collective-permute-start.20 = (f32[2,4,128,256]{3,2,1,0:T(8,128)}, f32[2,4,128,256]{3,2,1,0:T(8,128)}, u32[]{:S(2)}, u32[]{:S(2)}) collective-permute-start(f32[2,4,128,256]{3,2,1,0:T(8,128)} %get-tuple-element.53.refs_1_), channel_id=1, source_target_pairs={{0,1},{1,2},{2,3},{3,4},{4,5},{5,6},{6,7},{7,8},{8,9},{9,10},{10,1... | collective-permute-start | bytes 3145736 | tf_op jit(solution)/shard_map/ppermute | solution.py:349
  170.2 4.2 %fold.3 = (f32[2,4,128,256]{3,2,1,0:T(8,128)}, f32[2,4,128,256]{3,2,1,0:T(8,128)S(1)}) custom-call(f32[2,4,128,256]{3,2,1,0:T(8,128)S(1)} %collective-permute-done.33.refs_0_, f32[2,4,128,256]{3,2,1,0:T(8,128)S(1)} %adjoint.3.refs_1_, f32[2,4,128,256]{3,2,1,0:T(8,128)S(1)} %collective-permute-done.34.refs_2_, f32[2,4,128,256]{3,2,1,0:T(8,128)S(1)} %turn.3.refs_1_.refs_3_, ...), custom_call_target="tpu_custom_call" | custom-call | flops 15728640 | bytes 7340032 | tf_op jit(solution)/shard_map/fold/pallas_call | solution.py:481
  175.4 5.4 %collective-permute-start.35 = (f32[2,4,128,256]{3,2,1,0:T(8,128)}, f32[2,4,128,256]{3,2,1,0:T(8,128)}, u32[]{:S(2)}, u32[]{:S(2)}) collective-permute-start(f32[2,4,128,256]{3,2,1,0:T(8,128)} %get-tuple-element.64.refs_1_), channel_id=1, source_target_pairs={{0,1},{1,2},{2,3},{3,4},{4,5},{5,6},{6,7},{7,8},{8,9},{9,10},{10,1... | collective-permute-start | bytes 3145736 | tf_op jit(solution)/shard_map/ppermute | solution.py:349
  185.0 4.3 %image.2 = (f32[2,4,32,256]{3,2,1,0:T(8,128)S(1)}, f32[2,4,32,256]{3,2,1,0:T(8,128)S(1)}, f32[2,4,32,256]{3,2,1,0:T(8,128)S(1)}, f32[2,4,32,256]{3,2,1,0:T(8,128)S(1)}) custom-call(f32[2,4,128,256]{3,2,1,0:T(8,128)} %collective-permute-done.20.refs_0_, f32[2,4,128,256]{3,2,1,0:T(8,128)} %get-tuple-element.53.refs_1_, ...), custom_call_target="tpu_custom_call" | custom-call | flops 15728640 | bytes 7340032 | tf_op jit(solution)/shard_map/image/pallas_call | solution.py:481
  191.3 3.6 %collective-permute-start.23 = (f32[2,4,32,256]{3,2,1,0:T(8,128)S(1)}, f32[2,4,32,256]{3,2,1,0:T(8,128)S(1)}, u32[]{:S(2)}, u32[]{:S(2)}) collective-permute-start(f32[2,4,32,256]{3,2,1,0:T(8,128)S(1)} %get-tuple-element.59), channel_id=1, source_target_pairs={{0,64},{32,96},{64,0},{96,32},{1,65},{33,97},{65,1},{97,33},{2,66}... | collective-permute-start | bytes 786440 | tf_op jit(solution)/shard_map/ppermute | solution.py:537
  195.9 4.2 %image.3 = (f32[2,4,32,256]{3,2,1,0:T(8,128)S(1)}, f32[2,4,32,256]{3,2,1,0:T(8,128)S(1)}, f32[2,4,32,256]{3,2,1,0:T(8,128)S(1)}, f32[2,4,32,256]{3,2,1,0:T(8,128)S(1)}) custom-call(f32[2,4,128,256]{3,2,1,0:T(8,128)} %collective-permute-done.35.refs_0_, f32[2,4,128,256]{3,2,1,0:T(8,128)} %get-tuple-element.64.refs_1_, ...), custom_call_target="tpu_custom_call" | custom-call | flops 15728640 | bytes 7340032 | tf_op jit(solution)/shard_map/image/pallas_call | solution.py:481
  206.1 7.1 %collective-permute-done.37.refs_5_ = f32[2,4,32,256]{3,2,1,0:T(8,128)S(1)} collective-permute-done((f32[2,4,32,256]{3,2,1,0:T(8,128)S(1)}, f32[2,4,32,256]{3,2,1,0:T(8,128)S(1)}, u32[]{:S(2)}, u32[]{:S(2)}) %collective-permute-start.37) | collective-permute-done | bytes 262176 | tf_op jit(solution)/shard_map/ppermute | solution.py:537
  222.6 3.6 %collective-permute-done.41 = f32[16,16]{1,0:T(8,128)S(1)} collective-permute-done((f32[16,16]{1,0:T(8,128)S(1)}, f32[16,16]{1,0:T(8,128)S(1)}, u32[]{:S(2)}, u32[]{:S(2)}) %collective-permute-start.41) | collective-permute-done | bytes 1056 | tf_op jit(solution)/shard_map/ppermute | solution.py:361
  226.2 5.2 %collective-permute-done.42 = f32[16,16]{1,0:T(8,128)S(1)} collective-permute-done((f32[16,16]{1,0:T(8,128)S(1)}, f32[16,16]{1,0:T(8,128)S(1)}, u32[]{:S(2)}, u32[]{:S(2)}) %collective-permute-start.42) | collective-permute-done | bytes 1056 | tf_op jit(solution)/shard_map/ppermute | solution.py:361
  235.8 4.4 %collective-permute-done.44 = f32[16,16]{1,0:T(8,128)S(1)} collective-permute-done((f32[16,16]{1,0:T(8,128)S(1)}, f32[16,16]{1,0:T(8,128)S(1)}, u32[]{:S(2)}, u32[]{:S(2)}) %collective-permute-start.44) | collective-permute-done | bytes 1056 | tf_op jit(solution)/shard_map/ppermute | solution.py:361
  249.0 5.5 %basis.1 = (f32[16,4,32,256]{3,2,1,0:T(8,128)}, f32[16,16]{1,0:T(8,128)}) custom-call(f32[16,16]{1,0:T(8,128)S(1)} %add.68.gram_ref, f32[16,16]{1,0:T(8,128)S(1)} %get-tuple-element.73.sel_ref, f32[2,4,32,256]{3,2,1,0:T(8,128)S(1)} %get-tuple-element.57.refs_0_, f32[2,4,32,256]{3,2,1,0:T(8,128)S(1)} %collective-permute-done.22.refs_1_, ...), custom_call_target="tpu_custom_call" | custom-call | tf_op jit(solution)/shard_map/basis/pallas_call | solution.py:556
  (133 shorter events, 126.5 us)
Async XLA Ops:
  0.6 19.5 %collective-permute-start = (f32[4,128,256]{2,1,0:T(8,128)}, f32[4,128,256]{2,1,0:T(8,128)S(1)}, u32[]{:S(2)}, u32[]{:S(2)}) collective-permute-start(f32[4,128,256]{2,1,0:T(8,128)} %refs_2_.1), channel_id=1, source_target_pairs={{0,1},{1,2},{2,3},{3,4},{4,5},{5,6},{6,7},{7,8},{8,9},{9,10},{10,1... | collective-permute-start | bytes 1572872 | tf_op jit(solution)/shard_map/ppermute | solution.py:349
  2.6 17.6 %collective-permute-start.1 = (f32[4,128,256]{2,1,0:T(8,128)}, f32[4,128,256]{2,1,0:T(8,128)S(1)}, u32[]{:S(2)}, u32[]{:S(2)}) collective-permute-start(f32[4,128,256]{2,1,0:T(8,128)} %refs_2_.1), channel_id=1, source_target_pairs={{1,0},{2,1},{3,2},{4,3},{5,4},{6,5},{7,6},{8,7},{9,8},{10,9},{11,1... | collective-permute-start | bytes 1572872 | tf_op jit(solution)/shard_map/ppermute | solution.py:349
  31.0 20.3 %collective-permute-start.4 = (f32[2,4,128,256]{3,2,1,0:T(8,128)S(1)}, f32[2,4,128,256]{3,2,1,0:T(8,128)S(1)}, u32[]{:S(2)}, u32[]{:S(2)}) collective-permute-start(f32[2,4,128,256]{3,2,1,0:T(8,128)S(1)} %get-tuple-element.71.refs_1_.refs_3_.refs_12_), channel_id=1, source_target_pairs={{0,1},{1,2},{2,3},{3,4},{4,5},{5,6},{6,7},{7,8},{8,9},{9,10},{10,1... | collective-permute-start | bytes 3145736 | tf_op jit(solution)/shard_map/ppermute | solution.py:349
  34.3 19.6 %collective-permute-start.5 = (f32[2,4,128,256]{3,2,1,0:T(8,128)S(1)}, f32[2,4,128,256]{3,2,1,0:T(8,128)S(1)}, u32[]{:S(2)}, u32[]{:S(2)}) collective-permute-start(f32[2,4,128,256]{3,2,1,0:T(8,128)S(1)} %get-tuple-element.71.refs_1_.refs_3_.refs_12_), channel_id=1, source_target_pairs={{1,0},{2,1},{3,2},{4,3},{5,4},{6,5},{7,6},{8,7},{9,8},{10,9},{11,1... | collective-permute-start | bytes 3145736 | tf_op jit(solution)/shard_map/ppermute | solution.py:349
  39.1 28.8 %collective-permute-start.25 = (f32[2,4,128,256]{3,2,1,0:T(8,128)S(1)}, f32[2,4,128,256]{3,2,1,0:T(8,128)S(1)}, u32[]{:S(2)}, u32[]{:S(2)}) collective-permute-start(f32[2,4,128,256]{3,2,1,0:T(8,128)S(1)} %get-tuple-element.61.refs_1_.refs_3_.refs_12_), channel_id=1, source_target_pairs={{0,1},{1,2},{2,3},{3,4},{4,5},{5,6},{6,7},{7,8},{8,9},{9,10},{10,1... | collective-permute-start | bytes 3145736 | tf_op jit(solution)/shard_map/ppermute | solution.py:349
  46.3 21.5 %collective-permute-start.26 = (f32[2,4,128,256]{3,2,1,0:T(8,128)S(1)}, f32[2,4,128,256]{3,2,1,0:T(8,128)S(1)}, u32[]{:S(2)}, u32[]{:S(2)}) collective-permute-start(f32[2,4,128,256]{3,2,1,0:T(8,128)S(1)} %get-tuple-element.61.refs_1_.refs_3_.refs_12_), channel_id=1, source_target_pairs={{1,0},{2,1},{3,2},{4,3},{5,4},{6,5},{7,6},{8,7},{9,8},{10,9},{11,1... | collective-permute-start | bytes 3145736 | tf_op jit(solution)/shard_map/ppermute | solution.py:349
  48.3 15.7 %collective-permute-start.10 = (f32[4,128,256]{2,1,0:T(8,128)S(1)}, f32[4,128,256]{2,1,0:T(8,128)S(1)}, u32[]{:S(2)}, u32[]{:S(2)}) collective-permute-start(f32[4,128,256]{2,1,0:T(8,128)S(1)} %get-tuple-element.49.refs_1_), channel_id=1, source_target_pairs={{0,1},{1,2},{2,3},{3,4},{4,5},{5,6},{6,7},{7,8},{8,9},{9,10},{10,1... | collective-permute-start | bytes 1572872 | tf_op jit(solution)/shard_map/ppermute | solution.py:349
  56.6 27.2 %collective-permute-start.8 = (f32[2,4,128,256]{3,2,1,0:T(8,128)S(1)}, f32[2,4,128,256]{3,2,1,0:T(8,128)S(1)}, u32[]{:S(2)}, u32[]{:S(2)}) collective-permute-start(f32[2,4,128,256]{3,2,1,0:T(8,128)S(1)} %born.4.refs_1_.refs_3_.refs_10_), channel_id=1, source_target_pairs={{0,1},{1,2},{2,3},{3,4},{4,5},{5,6},{6,7},{7,8},{8,9},{9,10},{10,1... | collective-permute-start | bytes 3145736 | tf_op jit(solution)/shard_map/ppermute | solution.py:349
  64.0 23.0 %collective-permute-start.9 = (f32[2,4,128,256]{3,2,1,0:T(8,128)S(1)}, f32[2,4,128,256]{3,2,1,0:T(8,128)S(1)}, u32[]{:S(2)}, u32[]{:S(2)}) collective-permute-start(f32[2,4,128,256]{3,2,1,0:T(8,128)S(1)} %born.4.refs_1_.refs_3_.refs_10_), channel_id=1, source_target_pairs={{1,0},{2,1},{3,2},{4,3},{5,4},{6,5},{7,6},{8,7},{9,8},{10,9},{11,1... | collective-permute-start | bytes 3145736 | tf_op jit(solution)/shard_map/ppermute | solution.py:349
  70.6 30.2 %collective-permute-start.27 = (f32[2,4,128,256]{3,2,1,0:T(8,128)S(1)}, f32[2,4,128,256]{3,2,1,0:T(8,128)S(1)}, u32[]{:S(2)}, u32[]{:S(2)}) collective-permute-start(f32[2,4,128,256]{3,2,1,0:T(8,128)S(1)} %born.6.refs_1_.refs_3_.refs_10_), channel_id=1, source_target_pairs={{0,1},{1,2},{2,3},{3,4},{4,5},{5,6},{6,7},{7,8},{8,9},{9,10},{10,1... | collective-permute-start | bytes 3145736 | tf_op jit(solution)/shard_map/ppermute | solution.py:349
  79.5 21.4 %collective-permute-start.28 = (f32[2,4,128,256]{3,2,1,0:T(8,128)S(1)}, f32[2,4,128,256]{3,2,1,0:T(8,128)S(1)}, u32[]{:S(2)}, u32[]{:S(2)}) collective-permute-start(f32[2,4,128,256]{3,2,1,0:T(8,128)S(1)} %born.6.refs_1_.refs_3_.refs_10_), channel_id=1, source_target_pairs={{1,0},{2,1},{3,2},{4,3},{5,4},{6,5},{7,6},{8,7},{9,8},{10,9},{11,1... | collective-permute-start | bytes 3145736 | tf_op jit(solution)/shard_map/ppermute | solution.py:349
  83.8 15.5 %collective-permute-start.15 = (f32[4,128,256]{2,1,0:T(8,128)S(1)}, f32[4,128,256]{2,1,0:T(8,128)S(1)}, u32[]{:S(2)}, u32[]{:S(2)}) collective-permute-start(f32[4,128,256]{2,1,0:T(8,128)S(1)} %get-tuple-element.51.refs_1_), channel_id=1, source_target_pairs={{1,0},{2,1},{3,2},{4,3},{5,4},{6,5},{7,6},{8,7},{9,8},{10,9},{11,1... | collective-permute-start | bytes 1572872 | tf_op jit(solution)/shard_map/ppermute | solution.py:349
  89.8 21.7 %collective-permute-start.12 = (f32[2,4,128,256]{3,2,1,0:T(8,128)S(1)}, f32[2,4,128,256]{3,2,1,0:T(8,128)S(1)}, u32[]{:S(2)}, u32[]{:S(2)}) collective-permute-start(f32[2,4,128,256]{3,2,1,0:T(8,128)S(1)} %born.5.refs_1_.refs_9_), channel_id=1, source_target_pairs={{0,1},{1,2},{2,3},{3,4},{4,5},{5,6},{6,7},{7,8},{8,9},{9,10},{10,1... | collective-permute-start | bytes 3145736 | tf_op jit(solution)/shard_map/ppermute | solution.py:349
  93.8 17.7 %collective-permute-start.13 = (f32[2,4,128,256]{3,2,1,0:T(8,128)S(1)}, f32[2,4,128,256]{3,2,1,0:T(8,128)S(1)}, u32[]{:S(2)}, u32[]{:S(2)}) collective-permute-start(f32[2,4,128,256]{3,2,1,0:T(8,128)S(1)} %born.5.refs_1_.refs_9_), channel_id=1, source_target_pairs={{1,0},{2,1},{3,2},{4,3},{5,4},{6,5},{7,6},{8,7},{9,8},{10,9},{11,1... | collective-permute-start | bytes 3145736 | tf_op jit(solution)/shard_map/ppermute | solution.py:349
  103.6 18.9 %collective-permute-start.29 = (f32[2,4,128,256]{3,2,1,0:T(8,128)S(1)}, f32[2,4,128,256]{3,2,1,0:T(8,128)S(1)}, u32[]{:S(2)}, u32[]{:S(2)}) collective-permute-start(f32[2,4,128,256]{3,2,1,0:T(8,128)S(1)} %born.7.refs_1_.refs_9_), channel_id=1, source_target_pairs={{0,1},{1,2},{2,3},{3,4},{4,5},{5,6},{6,7},{7,8},{8,9},{9,10},{10,1... | collective-permute-start | bytes 3145736 | tf_op jit(solution)/shard_map/ppermute | solution.py:349
  114.3 20.4 %collective-permute-start.16 = (f32[2,4,128,256]{3,2,1,0:T(8,128)S(1)}, f32[2,4,128,256]{3,2,1,0:T(8,128)S(1)}, u32[]{:S(2)}, u32[]{:S(2)}) collective-permute-start(f32[2,4,128,256]{3,2,1,0:T(8,128)S(1)} %turn.2.refs_1_.refs_3_), channel_id=1, source_target_pairs={{0,1},{1,2},{2,3},{3,4},{4,5},{5,6},{6,7},{7,8},{8,9},{9,10},{10,1... | collective-permute-start | bytes 3145736 | tf_op jit(solution)/shard_map/ppermute | solution.py:349
  126.6 19.1 %collective-permute-start.31 = (f32[2,4,128,256]{3,2,1,0:T(8,128)S(1)}, f32[2,4,128,256]{3,2,1,0:T(8,128)S(1)}, u32[]{:S(2)}, u32[]{:S(2)}) collective-permute-start(f32[2,4,128,256]{3,2,1,0:T(8,128)S(1)} %turn.3.refs_1_.refs_3_), channel_id=1, source_target_pairs={{0,1},{1,2},{2,3},{3,4},{4,5},{5,6},{6,7},{7,8},{8,9},{9,10},{10,1... | collective-permute-start | bytes 3145736 | tf_op jit(solution)/shard_map/ppermute | solution.py:349
  137.7 19.7 %collective-permute-start.18 = (f32[2,4,128,256]{3,2,1,0:T(8,128)S(1)}, f32[2,4,128,256]{3,2,1,0:T(8,128)S(1)}, u32[]{:S(2)}, u32[]{:S(2)}) collective-permute-start(f32[2,4,128,256]{3,2,1,0:T(8,128)S(1)} %adjoint.2.refs_1_), channel_id=1, source_target_pairs={{0,1},{1,2},{2,3},{3,4},{4,5},{5,6},{6,7},{7,8},{8,9},{9,10},{10,1... | collective-permute-start | bytes 3145736 | tf_op jit(solution)/shard_map/ppermute | solution.py:349
  149.5 20.6 %collective-permute-start.33 = (f32[2,4,128,256]{3,2,1,0:T(8,128)S(1)}, f32[2,4,128,256]{3,2,1,0:T(8,128)S(1)}, u32[]{:S(2)}, u32[]{:S(2)}) collective-permute-start(f32[2,4,128,256]{3,2,1,0:T(8,128)S(1)} %adjoint.3.refs_1_), channel_id=1, source_target_pairs={{0,1},{1,2},{2,3},{3,4},{4,5},{5,6},{6,7},{7,8},{8,9},{9,10},{10,1... | collective-permute-start | bytes 3145736 | tf_op jit(solution)/shard_map/ppermute | solution.py:349
  162.3 20.4 %collective-permute-start.20 = (f32[2,4,128,256]{3,2,1,0:T(8,128)}, f32[2,4,128,256]{3,2,1,0:T(8,128)}, u32[]{:S(2)}, u32[]{:S(2)}) collective-permute-start(f32[2,4,128,256]{3,2,1,0:T(8,128)} %get-tuple-element.53.refs_1_), channel_id=1, source_target_pairs={{0,1},{1,2},{2,3},{3,4},{4,5},{5,6},{6,7},{7,8},{8,9},{9,10},{10,1... | collective-permute-start | bytes 3145736 | tf_op jit(solution)/shard_map/ppermute | solution.py:349
  175.4 20.5 %collective-permute-start.35 = (f32[2,4,128,256]{3,2,1,0:T(8,128)}, f32[2,4,128,256]{3,2,1,0:T(8,128)}, u32[]{:S(2)}, u32[]{:S(2)}) collective-permute-start(f32[2,4,128,256]{3,2,1,0:T(8,128)} %get-tuple-element.64.refs_1_), channel_id=1, source_target_pairs={{0,1},{1,2},{2,3},{3,4},{4,5},{5,6},{6,7},{7,8},{8,9},{9,10},{10,1... | collective-permute-start | bytes 3145736 | tf_op jit(solution)/shard_map/ppermute | solution.py:349
  180.7 15.2 %collective-permute-start.36 = (f32[2,4,128,256]{3,2,1,0:T(8,128)}, f32[2,4,128,256]{3,2,1,0:T(8,128)}, u32[]{:S(2)}, u32[]{:S(2)}) collective-permute-start(f32[2,4,128,256]{3,2,1,0:T(8,128)} %get-tuple-element.64.refs_1_), channel_id=1, source_target_pairs={{1,0},{2,1},{3,2},{4,3},{5,4},{6,5},{7,6},{8,7},{9,8},{10,9},{11,1... | collective-permute-start | bytes 3145736 | tf_op jit(solution)/shard_map/ppermute | solution.py:349
  189.3 15.7 %collective-permute-start.22 = (f32[2,4,32,256]{3,2,1,0:T(8,128)S(1)}, f32[2,4,32,256]{3,2,1,0:T(8,128)S(1)}, u32[]{:S(2)}, u32[]{:S(2)}) collective-permute-start(f32[2,4,32,256]{3,2,1,0:T(8,128)S(1)} %get-tuple-element.58), channel_id=1, source_target_pairs={{0,32},{32,64},{64,96},{96,0},{1,33},{33,65},{65,97},{97,1},{2,34}... | collective-permute-start | bytes 786440 | tf_op jit(solution)/shard_map/ppermute | solution.py:537
  201.4 15.1 %collective-permute-start.38 = (f32[2,4,32,256]{3,2,1,0:T(8,128)S(1)}, f32[2,4,32,256]{3,2,1,0:T(8,128)S(1)}, u32[]{:S(2)}, u32[]{:S(2)}) collective-permute-start(f32[2,4,32,256]{3,2,1,0:T(8,128)S(1)} %get-tuple-element.68), channel_id=1, source_target_pairs={{0,64},{32,96},{64,0},{96,32},{1,65},{33,97},{65,1},{97,33},{2,66}... | collective-permute-start | bytes 786440 | tf_op jit(solution)/shard_map/ppermute | solution.py:537
  (40 other events, 319.6 us)

commit v11 on v10

--- a/solution.py
+++ b/solution.py
@@ -81,7 +81,7 @@
             body(i, at, slice(column, column + LANE))
         return carry
 
-    lax.fori_loop(0, rows // 8, step, 0, unroll=2)
+    lax.fori_loop(0, rows // 8, step, 0, unroll=4)
 
 
 def place_kernel(copies, rc_ref, sc_ref, amp_ref, mask_ref, *refs):

time: 256 us -> 256 us (level)
  no operation moved by 1% of the time
where the time goes in v11:
time: 256 us; the launch traced here: 255 us
  starting transfers between devices  143 us (56%)
  Pallas kernels  56.3 us (22%)
  waiting for transfers between devices  43.2 us (17%)
  local copies, waits for them, and re-layouts  10.5 us (4%)
    ppermute x17, starting transfers between devices, halo(): lax.ppermute(block, 'slab', forward)  85.8 us
    pallas_call x12, Pallas kernels, wave(): pl.pallas_call(functools.partial(wave_kernel, mode, old is not None), gri...  39.7 us
    ppermute x17, starting transfers between devices, halo(): lax.ppermute(block, 'slab', backward)  38.5 us
    ppermute x7, waiting for transfers between devices, add_up(): lax.ppermute(value, axis, [(i, i ^ stride) for i in range(size)])  22 us
    ppermute x6, starting transfers between devices, shards(): sketch.append(lax.ppermute(blocks[s], 'dirs', ring))  12.1 us
    ppermute x6, waiting for transfers between devices, shards(): sketch.append(lax.ppermute(blocks[s], 'dirs', ring))  11 us
    unnamed x34, local copies, waits for them, and re-layouts  10.5 us
    ppermute x17, waiting for transfers between devices, halo(): lax.ppermute(block, 'slab', backward)  8 us
  transfers between devices with their start and end apart: 47, of which 19 were waited for; matrix products, arithmetic and copies ran while one was open for 0% of the time, Pallas kernels for 18%

profile of v11, /device:TPU:14, one launch (start us, length us, event | category | flops | bytes accessed | tf_op | source)
XLA Modules:
  0.0 255.0 jit_solution(10576390813851952148)
XLA Ops:
  2.6 3.6 %collective-permute-start.1 = (f32[4,128,256]{2,1,0:T(8,128)}, f32[4,128,256]{2,1,0:T(8,128)S(1)}, u32[]{:S(2)}, u32[]{:S(2)}) collective-permute-start(f32[4,128,256]{2,1,0:T(8,128)} %refs_2_.1), channel_id=1, source_target_pairs={{1,0},{2,1},{3,2},{4,3},{5,4},{6,5},{7,6},{8,7},{9,8},{10,9},{11,1... | collective-permute-start | bytes 1572872 | tf_op jit(solution)/shard_map/ppermute | solution.py:349
  8.1 3.6 %collective-permute-start.3 = (f32[4,128,256]{2,1,0:T(8,128)}, f32[4,128,256]{2,1,0:T(8,128)S(1)}, u32[]{:S(2)}, u32[]{:S(2)}) collective-permute-start(f32[4,128,256]{2,1,0:T(8,128)} %refs_1_.1), channel_id=1, source_target_pairs={{1,0},{2,1},{3,2},{4,3},{5,4},{6,5},{7,6},{8,7},{9,8},{10,9},{11,1... | collective-permute-start | bytes 1572872 | tf_op jit(solution)/shard_map/ppermute | solution.py:349
  22.4 6.4 %collective-permute-start.6 = (f32[4,128,256]{2,1,0:T(8,128)S(1)}, f32[4,128,256]{2,1,0:T(8,128)S(1)}, u32[]{:S(2)}, u32[]{:S(2)}) collective-permute-start(f32[4,128,256]{2,1,0:T(8,128)S(1)} %get-tuple-element.46.refs_1_.refs_10_), channel_id=1, source_target_pairs={{0,1},{1,2},{2,3},{3,4},{4,5},{5,6},{6,7},{7,8},{8,9},{9,10},{10,1... | collective-permute-start | bytes 1572872 | tf_op jit(solution)/shard_map/ppermute | solution.py:349
  39.0 7.3 %collective-permute-start.25 = (f32[2,4,128,256]{3,2,1,0:T(8,128)S(1)}, f32[2,4,128,256]{3,2,1,0:T(8,128)S(1)}, u32[]{:S(2)}, u32[]{:S(2)}) collective-permute-start(f32[2,4,128,256]{3,2,1,0:T(8,128)S(1)} %get-tuple-element.61.refs_1_.refs_3_.refs_12_), channel_id=1, source_target_pairs={{0,1},{1,2},{2,3},{3,4},{4,5},{5,6},{6,7},{7,8},{8,9},{9,10},{10,1... | collective-permute-start | bytes 3145736 | tf_op jit(solution)/shard_map/ppermute | solution.py:349
  56.6 5.1 %collective-permute-start.8 = (f32[2,4,128,256]{3,2,1,0:T(8,128)S(1)}, f32[2,4,128,256]{3,2,1,0:T(8,128)S(1)}, u32[]{:S(2)}, u32[]{:S(2)}) collective-permute-start(f32[2,4,128,256]{3,2,1,0:T(8,128)S(1)} %born.4.refs_1_.refs_3_.refs_10_), channel_id=1, source_target_pairs={{0,1},{1,2},{2,3},{3,4},{4,5},{5,6},{6,7},{7,8},{8,9},{9,10},{10,1... | collective-permute-start | bytes 3145736 | tf_op jit(solution)/shard_map/ppermute | solution.py:349
  70.6 8.9 %collective-permute-start.27 = (f32[2,4,128,256]{3,2,1,0:T(8,128)S(1)}, f32[2,4,128,256]{3,2,1,0:T(8,128)S(1)}, u32[]{:S(2)}, u32[]{:S(2)}) collective-permute-start(f32[2,4,128,256]{3,2,1,0:T(8,128)S(1)} %born.6.refs_1_.refs_3_.refs_10_), channel_id=1, source_target_pairs={{0,1},{1,2},{2,3},{3,4},{4,5},{5,6},{6,7},{7,8},{8,9},{9,10},{10,1... | collective-permute-start | bytes 3145736 | tf_op jit(solution)/shard_map/ppermute | solution.py:349
  89.8 4.0 %collective-permute-start.12 = (f32[2,4,128,256]{3,2,1,0:T(8,128)S(1)}, f32[2,4,128,256]{3,2,1,0:T(8,128)S(1)}, u32[]{:S(2)}, u32[]{:S(2)}) collective-permute-start(f32[2,4,128,256]{3,2,1,0:T(8,128)S(1)} %born.5.refs_1_.refs_9_), channel_id=1, source_target_pairs={{0,1},{1,2},{2,3},{3,4},{4,5},{5,6},{6,7},{7,8},{8,9},{9,10},{10,1... | collective-permute-start | bytes 3145736 | tf_op jit(solution)/shard_map/ppermute | solution.py:349
  103.7 5.9 %collective-permute-start.29 = (f32[2,4,128,256]{3,2,1,0:T(8,128)S(1)}, f32[2,4,128,256]{3,2,1,0:T(8,128)S(1)}, u32[]{:S(2)}, u32[]{:S(2)}) collective-permute-start(f32[2,4,128,256]{3,2,1,0:T(8,128)S(1)} %born.7.refs_1_.refs_9_), channel_id=1, source_target_pairs={{0,1},{1,2},{2,3},{3,4},{4,5},{5,6},{6,7},{7,8},{8,9},{9,10},{10,1... | collective-permute-start | bytes 3145736 | tf_op jit(solution)/shard_map/ppermute | solution.py:349
  114.4 6.3 %collective-permute-start.16 = (f32[2,4,128,256]{3,2,1,0:T(8,128)S(1)}, f32[2,4,128,256]{3,2,1,0:T(8,128)S(1)}, u32[]{:S(2)}, u32[]{:S(2)}) collective-permute-start(f32[2,4,128,256]{3,2,1,0:T(8,128)S(1)} %turn.2.refs_1_.refs_3_), channel_id=1, source_target_pairs={{0,1},{1,2},{2,3},{3,4},{4,5},{5,6},{6,7},{7,8},{8,9},{9,10},{10,1... | collective-permute-start | bytes 3145736 | tf_op jit(solution)/shard_map/ppermute | solution.py:349
  126.7 6.1 %collective-permute-start.31 = (f32[2,4,128,256]{3,2,1,0:T(8,128)S(1)}, f32[2,4,128,256]{3,2,1,0:T(8,128)S(1)}, u32[]{:S(2)}, u32[]{:S(2)}) collective-permute-start(f32[2,4,128,256]{3,2,1,0:T(8,128)S(1)} %turn.3.refs_1_.refs_3_), channel_id=1, source_target_pairs={{0,1},{1,2},{2,3},{3,4},{4,5},{5,6},{6,7},{7,8},{8,9},{9,10},{10,1... | collective-permute-start | bytes 3145736 | tf_op jit(solution)/shard_map/ppermute | solution.py:349
  137.8 6.1 %collective-permute-start.18 = (f32[2,4,128,256]{3,2,1,0:T(8,128)S(1)}, f32[2,4,128,256]{3,2,1,0:T(8,128)S(1)}, u32[]{:S(2)}, u32[]{:S(2)}) collective-permute-start(f32[2,4,128,256]{3,2,1,0:T(8,128)S(1)} %adjoint.2.refs_1_), channel_id=1, source_target_pairs={{0,1},{1,2},{2,3},{3,4},{4,5},{5,6},{6,7},{7,8},{8,9},{9,10},{10,1... | collective-permute-start | bytes 3145736 | tf_op jit(solution)/shard_map/ppermute | solution.py:349
  149.7 5.9 %collective-permute-start.33 = (f32[2,4,128,256]{3,2,1,0:T(8,128)S(1)}, f32[2,4,128,256]{3,2,1,0:T(8,128)S(1)}, u32[]{:S(2)}, u32[]{:S(2)}) collective-permute-start(f32[2,4,128,256]{3,2,1,0:T(8,128)S(1)} %adjoint.3.refs_1_), channel_id=1, source_target_pairs={{0,1},{1,2},{2,3},{3,4},{4,5},{5,6},{6,7},{7,8},{8,9},{9,10},{10,1... | collective-permute-start | bytes 3145736 | tf_op jit(solution)/shard_map/ppermute | solution.py:349
  158.2 4.2 %fold.2 = (f32[2,4,128,256]{3,2,1,0:T(8,128)}, f32[2,4,128,256]{3,2,1,0:T(8,128)S(1)}, f32[4,128,256]{2,1,0:T(8,128)S(1)}, f32[4,128,256]{2,1,0:T(8,128)S(1)}) custom-call(f32[2,4,128,256]{3,2,1,0:T(8,128)S(1)} %collective-permute-done.18.refs_0_, f32[2,4,128,256]{3,2,1,0:T(8,128)S(1)} %adjoint.2.refs_1_, ...), custom_call_target="tpu_custom_call" | custom-call | flops 15728640 | bytes 7340032 | tf_op jit(solution)/shard_map/fold/pallas_call | solution.py:481
  162.4 5.9 %collective-permute-start.20 = (f32[2,4,128,256]{3,2,1,0:T(8,128)}, f32[2,4,128,256]{3,2,1,0:T(8,128)}, u32[]{:S(2)}, u32[]{:S(2)}) collective-permute-start(f32[2,4,128,256]{3,2,1,0:T(8,128)} %get-tuple-element.53.refs_1_), channel_id=1, source_target_pairs={{0,1},{1,2},{2,3},{3,4},{4,5},{5,6},{6,7},{7,8},{8,9},{9,10},{10,1... | collective-permute-start | bytes 3145736 | tf_op jit(solution)/shard_map/ppermute | solution.py:349
  170.3 4.1 %fold.3 = (f32[2,4,128,256]{3,2,1,0:T(8,128)}, f32[2,4,128,256]{3,2,1,0:T(8,128)S(1)}) custom-call(f32[2,4,128,256]{3,2,1,0:T(8,128)S(1)} %collective-permute-done.33.refs_0_, f32[2,4,128,256]{3,2,1,0:T(8,128)S(1)} %adjoint.3.refs_1_, f32[2,4,128,256]{3,2,1,0:T(8,128)S(1)} %collective-permute-done.34.refs_2_, f32[2,4,128,256]{3,2,1,0:T(8,128)S(1)} %turn.3.refs_1_.refs_3_, ...), custom_call_target="tpu_custom_call" | custom-call | flops 15728640 | bytes 7340032 | tf_op jit(solution)/shard_map/fold/pallas_call | solution.py:481
  175.4 5.4 %collective-permute-start.35 = (f32[2,4,128,256]{3,2,1,0:T(8,128)}, f32[2,4,128,256]{3,2,1,0:T(8,128)}, u32[]{:S(2)}, u32[]{:S(2)}) collective-permute-start(f32[2,4,128,256]{3,2,1,0:T(8,128)} %get-tuple-element.64.refs_1_), channel_id=1, source_target_pairs={{0,1},{1,2},{2,3},{3,4},{4,5},{5,6},{6,7},{7,8},{8,9},{9,10},{10,1... | collective-permute-start | bytes 3145736 | tf_op jit(solution)/shard_map/ppermute | solution.py:349
  185.2 4.6 %image.2 = (f32[2,4,32,256]{3,2,1,0:T(8,128)S(1)}, f32[2,4,32,256]{3,2,1,0:T(8,128)S(1)}, f32[2,4,32,256]{3,2,1,0:T(8,128)S(1)}, f32[2,4,32,256]{3,2,1,0:T(8,128)S(1)}) custom-call(f32[2,4,128,256]{3,2,1,0:T(8,128)} %collective-permute-done.20.refs_0_, f32[2,4,128,256]{3,2,1,0:T(8,128)} %get-tuple-element.53.refs_1_, ...), custom_call_target="tpu_custom_call" | custom-call | flops 15728640 | bytes 7340032 | tf_op jit(solution)/shard_map/image/pallas_call | solution.py:481
  191.8 3.6 %collective-permute-start.23 = (f32[2,4,32,256]{3,2,1,0:T(8,128)S(1)}, f32[2,4,32,256]{3,2,1,0:T(8,128)S(1)}, u32[]{:S(2)}, u32[]{:S(2)}) collective-permute-start(f32[2,4,32,256]{3,2,1,0:T(8,128)S(1)} %get-tuple-element.59), channel_id=1, source_target_pairs={{0,64},{32,96},{64,0},{96,32},{1,65},{33,97},{65,1},{97,33},{2,66}... | collective-permute-start | bytes 786440 | tf_op jit(solution)/shard_map/ppermute | solution.py:537
  196.4 4.5 %image.3 = (f32[2,4,32,256]{3,2,1,0:T(8,128)S(1)}, f32[2,4,32,256]{3,2,1,0:T(8,128)S(1)}, f32[2,4,32,256]{3,2,1,0:T(8,128)S(1)}, f32[2,4,32,256]{3,2,1,0:T(8,128)S(1)}) custom-call(f32[2,4,128,256]{3,2,1,0:T(8,128)} %collective-permute-done.35.refs_0_, f32[2,4,128,256]{3,2,1,0:T(8,128)} %get-tuple-element.64.refs_1_, ...), custom_call_target="tpu_custom_call" | custom-call | flops 15728640 | bytes 7340032 | tf_op jit(solution)/shard_map/image/pallas_call | solution.py:481
  206.6 7.2 %collective-permute-done.37.refs_5_ = f32[2,4,32,256]{3,2,1,0:T(8,128)S(1)} collective-permute-done((f32[2,4,32,256]{3,2,1,0:T(8,128)S(1)}, f32[2,4,32,256]{3,2,1,0:T(8,128)S(1)}, u32[]{:S(2)}, u32[]{:S(2)}) %collective-permute-start.37) | collective-permute-done | bytes 262176 | tf_op jit(solution)/shard_map/ppermute | solution.py:537
  223.0 3.6 %collective-permute-done.41 = f32[16,16]{1,0:T(8,128)S(1)} collective-permute-done((f32[16,16]{1,0:T(8,128)S(1)}, f32[16,16]{1,0:T(8,128)S(1)}, u32[]{:S(2)}, u32[]{:S(2)}) %collective-permute-start.41) | collective-permute-done | bytes 1056 | tf_op jit(solution)/shard_map/ppermute | solution.py:361
  226.7 5.2 %collective-permute-done.42 = f32[16,16]{1,0:T(8,128)S(1)} collective-permute-done((f32[16,16]{1,0:T(8,128)S(1)}, f32[16,16]{1,0:T(8,128)S(1)}, u32[]{:S(2)}, u32[]{:S(2)}) %collective-permute-start.42) | collective-permute-done | bytes 1056 | tf_op jit(solution)/shard_map/ppermute | solution.py:361
  236.2 4.4 %collective-permute-done.44 = f32[16,16]{1,0:T(8,128)S(1)} collective-permute-done((f32[16,16]{1,0:T(8,128)S(1)}, f32[16,16]{1,0:T(8,128)S(1)}, u32[]{:S(2)}, u32[]{:S(2)}) %collective-permute-start.44) | collective-permute-done | bytes 1056 | tf_op jit(solution)/shard_map/ppermute | solution.py:361
  249.5 5.5 %basis.1 = (f32[16,4,32,256]{3,2,1,0:T(8,128)}, f32[16,16]{1,0:T(8,128)}) custom-call(f32[16,16]{1,0:T(8,128)S(1)} %add.68.gram_ref, f32[16,16]{1,0:T(8,128)S(1)} %get-tuple-element.73.sel_ref, f32[2,4,32,256]{3,2,1,0:T(8,128)S(1)} %get-tuple-element.57.refs_0_, f32[2,4,32,256]{3,2,1,0:T(8,128)S(1)} %collective-permute-done.22.refs_1_, ...), custom_call_target="tpu_custom_call" | custom-call | tf_op jit(solution)/shard_map/basis/pallas_call | solution.py:556
  (133 shorter events, 126.1 us)
Async XLA Ops:
  0.6 19.5 %collective-permute-start = (f32[4,128,256]{2,1,0:T(8,128)}, f32[4,128,256]{2,1,0:T(8,128)S(1)}, u32[]{:S(2)}, u32[]{:S(2)}) collective-permute-start(f32[4,128,256]{2,1,0:T(8,128)} %refs_2_.1), channel_id=1, source_target_pairs={{0,1},{1,2},{2,3},{3,4},{4,5},{5,6},{6,7},{7,8},{8,9},{9,10},{10,1... | collective-permute-start | bytes 1572872 | tf_op jit(solution)/shard_map/ppermute | solution.py:349
  2.6 17.6 %collective-permute-start.1 = (f32[4,128,256]{2,1,0:T(8,128)}, f32[4,128,256]{2,1,0:T(8,128)S(1)}, u32[]{:S(2)}, u32[]{:S(2)}) collective-permute-start(f32[4,128,256]{2,1,0:T(8,128)} %refs_2_.1), channel_id=1, source_target_pairs={{1,0},{2,1},{3,2},{4,3},{5,4},{6,5},{7,6},{8,7},{9,8},{10,9},{11,1... | collective-permute-start | bytes 1572872 | tf_op jit(solution)/shard_map/ppermute | solution.py:349
  31.0 20.3 %collective-permute-start.4 = (f32[2,4,128,256]{3,2,1,0:T(8,128)S(1)}, f32[2,4,128,256]{3,2,1,0:T(8,128)S(1)}, u32[]{:S(2)}, u32[]{:S(2)}) collective-permute-start(f32[2,4,128,256]{3,2,1,0:T(8,128)S(1)} %get-tuple-element.71.refs_1_.refs_3_.refs_12_), channel_id=1, source_target_pairs={{0,1},{1,2},{2,3},{3,4},{4,5},{5,6},{6,7},{7,8},{8,9},{9,10},{10,1... | collective-permute-start | bytes 3145736 | tf_op jit(solution)/shard_map/ppermute | solution.py:349
  34.2 19.6 %collective-permute-start.5 = (f32[2,4,128,256]{3,2,1,0:T(8,128)S(1)}, f32[2,4,128,256]{3,2,1,0:T(8,128)S(1)}, u32[]{:S(2)}, u32[]{:S(2)}) collective-permute-start(f32[2,4,128,256]{3,2,1,0:T(8,128)S(1)} %get-tuple-element.71.refs_1_.refs_3_.refs_12_), channel_id=1, source_target_pairs={{1,0},{2,1},{3,2},{4,3},{5,4},{6,5},{7,6},{8,7},{9,8},{10,9},{11,1... | collective-permute-start | bytes 3145736 | tf_op jit(solution)/shard_map/ppermute | solution.py:349
  39.0 28.8 %collective-permute-start.25 = (f32[2,4,128,256]{3,2,1,0:T(8,128)S(1)}, f32[2,4,128,256]{3,2,1,0:T(8,128)S(1)}, u32[]{:S(2)}, u32[]{:S(2)}) collective-permute-start(f32[2,4,128,256]{3,2,1,0:T(8,128)S(1)} %get-tuple-element.61.refs_1_.refs_3_.refs_12_), channel_id=1, source_target_pairs={{0,1},{1,2},{2,3},{3,4},{4,5},{5,6},{6,7},{7,8},{8,9},{9,10},{10,1... | collective-permute-start | bytes 3145736 | tf_op jit(solution)/shard_map/ppermute | solution.py:349
  46.3 21.5 %collective-permute-start.26 = (f32[2,4,128,256]{3,2,1,0:T(8,128)S(1)}, f32[2,4,128,256]{3,2,1,0:T(8,128)S(1)}, u32[]{:S(2)}, u32[]{:S(2)}) collective-permute-start(f32[2,4,128,256]{3,2,1,0:T(8,128)S(1)} %get-tuple-element.61.refs_1_.refs_3_.refs_12_), channel_id=1, source_target_pairs={{1,0},{2,1},{3,2},{4,3},{5,4},{6,5},{7,6},{8,7},{9,8},{10,9},{11,1... | collective-permute-start | bytes 3145736 | tf_op jit(solution)/shard_map/ppermute | solution.py:349
  48.3 15.7 %collective-permute-start.10 = (f32[4,128,256]{2,1,0:T(8,128)S(1)}, f32[4,128,256]{2,1,0:T(8,128)S(1)}, u32[]{:S(2)}, u32[]{:S(2)}) collective-permute-start(f32[4,128,256]{2,1,0:T(8,128)S(1)} %get-tuple-element.49.refs_1_), channel_id=1, source_target_pairs={{0,1},{1,2},{2,3},{3,4},{4,5},{5,6},{6,7},{7,8},{8,9},{9,10},{10,1... | collective-permute-start | bytes 1572872 | tf_op jit(solution)/shard_map/ppermute | solution.py:349
  56.6 27.2 %collective-permute-start.8 = (f32[2,4,128,256]{3,2,1,0:T(8,128)S(1)}, f32[2,4,128,256]{3,2,1,0:T(8,128)S(1)}, u32[]{:S(2)}, u32[]{:S(2)}) collective-permute-start(f32[2,4,128,256]{3,2,1,0:T(8,128)S(1)} %born.4.refs_1_.refs_3_.refs_10_), channel_id=1, source_target_pairs={{0,1},{1,2},{2,3},{3,4},{4,5},{5,6},{6,7},{7,8},{8,9},{9,10},{10,1... | collective-permute-start | bytes 3145736 | tf_op jit(solution)/shard_map/ppermute | solution.py:349
  63.9 23.1 %collective-permute-start.9 = (f32[2,4,128,256]{3,2,1,0:T(8,128)S(1)}, f32[2,4,128,256]{3,2,1,0:T(8,128)S(1)}, u32[]{:S(2)}, u32[]{:S(2)}) collective-permute-start(f32[2,4,128,256]{3,2,1,0:T(8,128)S(1)} %born.4.refs_1_.refs_3_.refs_10_), channel_id=1, source_target_pairs={{1,0},{2,1},{3,2},{4,3},{5,4},{6,5},{7,6},{8,7},{9,8},{10,9},{11,1... | collective-permute-start | bytes 3145736 | tf_op jit(solution)/shard_map/ppermute | solution.py:349
  70.6 30.3 %collective-permute-start.27 = (f32[2,4,128,256]{3,2,1,0:T(8,128)S(1)}, f32[2,4,128,256]{3,2,1,0:T(8,128)S(1)}, u32[]{:S(2)}, u32[]{:S(2)}) collective-permute-start(f32[2,4,128,256]{3,2,1,0:T(8,128)S(1)} %born.6.refs_1_.refs_3_.refs_10_), channel_id=1, source_target_pairs={{0,1},{1,2},{2,3},{3,4},{4,5},{5,6},{6,7},{7,8},{8,9},{9,10},{10,1... | collective-permute-start | bytes 3145736 | tf_op jit(solution)/shard_map/ppermute | solution.py:349
  79.5 21.3 %collective-permute-start.28 = (f32[2,4,128,256]{3,2,1,0:T(8,128)S(1)}, f32[2,4,128,256]{3,2,1,0:T(8,128)S(1)}, u32[]{:S(2)}, u32[]{:S(2)}) collective-permute-start(f32[2,4,128,256]{3,2,1,0:T(8,128)S(1)} %born.6.refs_1_.refs_3_.refs_10_), channel_id=1, source_target_pairs={{1,0},{2,1},{3,2},{4,3},{5,4},{6,5},{7,6},{8,7},{9,8},{10,9},{11,1... | collective-permute-start | bytes 3145736 | tf_op jit(solution)/shard_map/ppermute | solution.py:349
  83.9 15.5 %collective-permute-start.15 = (f32[4,128,256]{2,1,0:T(8,128)S(1)}, f32[4,128,256]{2,1,0:T(8,128)S(1)}, u32[]{:S(2)}, u32[]{:S(2)}) collective-permute-start(f32[4,128,256]{2,1,0:T(8,128)S(1)} %get-tuple-element.51.refs_1_), channel_id=1, source_target_pairs={{1,0},{2,1},{3,2},{4,3},{5,4},{6,5},{7,6},{8,7},{9,8},{10,9},{11,1... | collective-permute-start | bytes 1572872 | tf_op jit(solution)/shard_map/ppermute | solution.py:349
  89.8 21.7 %collective-permute-start.12 = (f32[2,4,128,256]{3,2,1,0:T(8,128)S(1)}, f32[2,4,128,256]{3,2,1,0:T(8,128)S(1)}, u32[]{:S(2)}, u32[]{:S(2)}) collective-permute-start(f32[2,4,128,256]{3,2,1,0:T(8,128)S(1)} %born.5.refs_1_.refs_9_), channel_id=1, source_target_pairs={{0,1},{1,2},{2,3},{3,4},{4,5},{5,6},{6,7},{7,8},{8,9},{9,10},{10,1... | collective-permute-start | bytes 3145736 | tf_op jit(solution)/shard_map/ppermute | solution.py:349
  93.9 17.7 %collective-permute-start.13 = (f32[2,4,128,256]{3,2,1,0:T(8,128)S(1)}, f32[2,4,128,256]{3,2,1,0:T(8,128)S(1)}, u32[]{:S(2)}, u32[]{:S(2)}) collective-permute-start(f32[2,4,128,256]{3,2,1,0:T(8,128)S(1)} %born.5.refs_1_.refs_9_), channel_id=1, source_target_pairs={{1,0},{2,1},{3,2},{4,3},{5,4},{6,5},{7,6},{8,7},{9,8},{10,9},{11,1... | collective-permute-start | bytes 3145736 | tf_op jit(solution)/shard_map/ppermute | solution.py:349
  103.7 19.2 %collective-permute-start.29 = (f32[2,4,128,256]{3,2,1,0:T(8,128)S(1)}, f32[2,4,128,256]{3,2,1,0:T(8,128)S(1)}, u32[]{:S(2)}, u32[]{:S(2)}) collective-permute-start(f32[2,4,128,256]{3,2,1,0:T(8,128)S(1)} %born.7.refs_1_.refs_9_), channel_id=1, source_target_pairs={{0,1},{1,2},{2,3},{3,4},{4,5},{5,6},{6,7},{7,8},{8,9},{9,10},{10,1... | collective-permute-start | bytes 3145736 | tf_op jit(solution)/shard_map/ppermute | solution.py:349
  114.4 20.2 %collective-permute-start.16 = (f32[2,4,128,256]{3,2,1,0:T(8,128)S(1)}, f32[2,4,128,256]{3,2,1,0:T(8,128)S(1)}, u32[]{:S(2)}, u32[]{:S(2)}) collective-permute-start(f32[2,4,128,256]{3,2,1,0:T(8,128)S(1)} %turn.2.refs_1_.refs_3_), channel_id=1, source_target_pairs={{0,1},{1,2},{2,3},{3,4},{4,5},{5,6},{6,7},{7,8},{8,9},{9,10},{10,1... | collective-permute-start | bytes 3145736 | tf_op jit(solution)/shard_map/ppermute | solution.py:349
  126.7 19.1 %collective-permute-start.31 = (f32[2,4,128,256]{3,2,1,0:T(8,128)S(1)}, f32[2,4,128,256]{3,2,1,0:T(8,128)S(1)}, u32[]{:S(2)}, u32[]{:S(2)}) collective-permute-start(f32[2,4,128,256]{3,2,1,0:T(8,128)S(1)} %turn.3.refs_1_.refs_3_), channel_id=1, source_target_pairs={{0,1},{1,2},{2,3},{3,4},{4,5},{5,6},{6,7},{7,8},{8,9},{9,10},{10,1... | collective-permute-start | bytes 3145736 | tf_op jit(solution)/shard_map/ppermute | solution.py:349
  137.8 19.8 %collective-permute-start.18 = (f32[2,4,128,256]{3,2,1,0:T(8,128)S(1)}, f32[2,4,128,256]{3,2,1,0:T(8,128)S(1)}, u32[]{:S(2)}, u32[]{:S(2)}) collective-permute-start(f32[2,4,128,256]{3,2,1,0:T(8,128)S(1)} %adjoint.2.refs_1_), channel_id=1, source_target_pairs={{0,1},{1,2},{2,3},{3,4},{4,5},{5,6},{6,7},{7,8},{8,9},{9,10},{10,1... | collective-permute-start | bytes 3145736 | tf_op jit(solution)/shard_map/ppermute | solution.py:349
  149.7 20.6 %collective-permute-start.33 = (f32[2,4,128,256]{3,2,1,0:T(8,128)S(1)}, f32[2,4,128,256]{3,2,1,0:T(8,128)S(1)}, u32[]{:S(2)}, u32[]{:S(2)}) collective-permute-start(f32[2,4,128,256]{3,2,1,0:T(8,128)S(1)} %adjoint.3.refs_1_), channel_id=1, source_target_pairs={{0,1},{1,2},{2,3},{3,4},{4,5},{5,6},{6,7},{7,8},{8,9},{9,10},{10,1... | collective-permute-start | bytes 3145736 | tf_op jit(solution)/shard_map/ppermute | solution.py:349
  162.4 20.3 %collective-permute-start.20 = (f32[2,4,128,256]{3,2,1,0:T(8,128)}, f32[2,4,128,256]{3,2,1,0:T(8,128)}, u32[]{:S(2)}, u32[]{:S(2)}) collective-permute-start(f32[2,4,128,256]{3,2,1,0:T(8,128)} %get-tuple-element.53.refs_1_), channel_id=1, source_target_pairs={{0,1},{1,2},{2,3},{3,4},{4,5},{5,6},{6,7},{7,8},{8,9},{9,10},{10,1... | collective-permute-start | bytes 3145736 | tf_op jit(solution)/shard_map/ppermute | solution.py:349
  175.4 20.9 %collective-permute-start.35 = (f32[2,4,128,256]{3,2,1,0:T(8,128)}, f32[2,4,128,256]{3,2,1,0:T(8,128)}, u32[]{:S(2)}, u32[]{:S(2)}) collective-permute-start(f32[2,4,128,256]{3,2,1,0:T(8,128)} %get-tuple-element.64.refs_1_), channel_id=1, source_target_pairs={{0,1},{1,2},{2,3},{3,4},{4,5},{5,6},{6,7},{7,8},{8,9},{9,10},{10,1... | collective-permute-start | bytes 3145736 | tf_op jit(solution)/shard_map/ppermute | solution.py:349
  180.8 15.5 %collective-permute-start.36 = (f32[2,4,128,256]{3,2,1,0:T(8,128)}, f32[2,4,128,256]{3,2,1,0:T(8,128)}, u32[]{:S(2)}, u32[]{:S(2)}) collective-permute-start(f32[2,4,128,256]{3,2,1,0:T(8,128)} %get-tuple-element.64.refs_1_), channel_id=1, source_target_pairs={{1,0},{2,1},{3,2},{4,3},{5,4},{6,5},{7,6},{8,7},{9,8},{10,9},{11,1... | collective-permute-start | bytes 3145736 | tf_op jit(solution)/shard_map/ppermute | solution.py:349
  189.8 15.7 %collective-permute-start.22 = (f32[2,4,32,256]{3,2,1,0:T(8,128)S(1)}, f32[2,4,32,256]{3,2,1,0:T(8,128)S(1)}, u32[]{:S(2)}, u32[]{:S(2)}) collective-permute-start(f32[2,4,32,256]{3,2,1,0:T(8,128)S(1)} %get-tuple-element.58), channel_id=1, source_target_pairs={{0,32},{32,64},{64,96},{96,0},{1,33},{33,65},{65,97},{97,1},{2,34}... | collective-permute-start | bytes 786440 | tf_op jit(solution)/shard_map/ppermute | solution.py:537
  202.0 15.0 %collective-permute-start.38 = (f32[2,4,32,256]{3,2,1,0:T(8,128)S(1)}, f32[2,4,32,256]{3,2,1,0:T(8,128)S(1)}, u32[]{:S(2)}, u32[]{:S(2)}) collective-permute-start(f32[2,4,32,256]{3,2,1,0:T(8,128)S(1)} %get-tuple-element.68), channel_id=1, source_target_pairs={{0,64},{32,96},{64,0},{96,32},{1,65},{33,97},{65,1},{97,33},{2,66}... | collective-permute-start | bytes 786440 | tf_op jit(solution)/shard_map/ppermute | solution.py:537
  (40 other events, 319.7 us)
